TPU v7x, 512 devices: a whole 4x8x8 slice. The times are simulated.
512 devices in a mesh: group: 8 (over y_hi, core), node: 8 (over y_lo, x), gpu: 8 (over z).
Axes of the slice: x: 4, y: 8 (y_hi: 4, y_lo: 2; y = y_hi * 2 + y_lo), z: 8, core: 2. Of those that a mesh axis runs over, the one named last changes fastest.
Arguments:
- tokens: bfloat16 [65536, 12288], P(('group', 'node', 'gpu')), may hold values from -24 to 24
- weight: bfloat16 [12288, 256], P(('node', 'gpu')), may hold values from -0.0546875 to 0.0546875
- grad_out: bfloat16 [65536, 256], P(('group', 'node', 'gpu')), may hold values from -0.0625 to 0.0625
Outputs:
- output: bfloat16 [65536, 256], P(('group', 'node', 'gpu'))
- weight_grad: float32 [12288, 256], P(('node', 'gpu'))
All inputs are finite; a program needn't handle non-finite values.
Results may differ from a plain program's by a relative error of at most 0.0029.
Values may be sent and summed in bfloat16 or wider, within the bound.
No kernel may reach another device: no remote copies, remote signals or barrier semaphores. Data moves between devices by JAX's collectives and lax.ppermute only.
A program may use at most 128 MiB of HBM per device.

v0:
```python
import jax
import jax.numpy as jnp
from jax import lax
from jax.sharding import PartitionSpec as P


def sum_middle(received):
    return jnp.sum(received, axis=1, dtype=jnp.float32)


def local(tokens, weight, grad_out):
    tok_rows, model_width = tokens.shape
    shard_rows, out_cols = weight.shape
    projected = jnp.dot(
        tokens,
        lax.all_gather(weight, ("node", "gpu"), axis=0, tiled=True),
        preferred_element_type=jnp.float32,
    )
    local_term = lax.dot_general(
        tokens, grad_out, (((0,), (0,)), ((), ())), preferred_element_type=jnp.float32
    ).astype(jnp.bfloat16)
    stacked = local_term.reshape(model_width, 1, out_cols)
    own_shard = sum_middle(
        lax.all_to_all(stacked, ("node", "gpu"), split_axis=0, concat_axis=1, tiled=True)
    )
    output = projected.astype(jnp.bfloat16)
    weight_grad = lax.psum(own_shard, "group")
    return (output, weight_grad)


def solution(mesh):
    placed = (
        P(("group", "node", "gpu"), None),
        P(("node", "gpu"), None),
        P(("group", "node", "gpu"), None),
    )
    return jax.shard_map(
        local,
        mesh=mesh,
        in_specs=placed,
        out_specs=(P(("group", "node", "gpu"), None), P(("node", "gpu"), None)),
        check_vma=False,
    )
```

profile of v0, /device:TPU:24, one launch (start us, length us, event | category | flops | bytes accessed | tf_op | source)
XLA Modules:
  0.0 462.1 jit_solution(13978750002914948384)
XLA Ops:
  8.0 0.0 copy-start
  8.0 1.9 copy-done
  9.9 5.3 %fusion = bf16[12288,1,256]{2,0,1:T(8,128)(2,1)} fusion(bf16[128,12288]{1,0:T(8,128)(2,1)S(1)} %copy-done, bf16[128,256]{1,0:T(8,128)(2,1)} %param.5), kind=kOutput, calls=%fused_computation.1 | convolution fusion | flops 808452096 | bytes 9502720 | tf_op jit(solution)/shard_map/dot_general | solution.py:19
  15.2 0.5 broadcast
  15.7 8.9 %reduce.3 = bf16[12288,256]{1,0:T(8,128)(2,1)} reduce(bf16[12288,1,256]{2,0,1:T(8,128)(2,1)} %fusion, bf16[]{:T(256)} %broadcast), dimensions={1}, to_apply=%copy.5.reduce_sub_computation | reduce | bytes 12582914 | tf_op jit(solution)/shard_map/reshape | solution.py:22
  24.6 14.2 %reshape.13 = bf16[64,2,24576]{2,1,0:T(2,128)(2,1)} reshape(bf16[12288,256]{1,0:T(8,128)(2,1)} %reduce.3) | data formatting | bytes 12582912
  38.8 15.1 %all-to-all-start = ((bf16[64,2,24576]{2,1,0:T(2,128)(2,1)}), bf16[64,2,24576]{2,1,0:T(2,128)(2,1)}, u32[]{:S(2)}, u32[]{:S(2)}) async-start(bf16[64,2,24576]{2,1,0:T(2,128)(2,1)} %reshape.13), calls=%async_computation | async-start | bytes 12582912 | tf_op jit(solution)/shard_map/all_to_all | solution.py:24
  53.9 0.0 all-gather.2.cloned.1.call-start
  54.0 0.7 all-gather.2.cloned.1.call-update
  54.7 0.0 all-reduce.2.cloned.1.call-start
  54.7 158.8 %all-to-all-done = bf16[64,2,24576]{2,1,0:T(2,128)(2,1)} async-done(((bf16[64,2,24576]{2,1,0:T(2,128)(2,1)}), bf16[64,2,24576]{2,1,0:T(2,128)(2,1)}, u32[]{:S(2)}, u32[]{:S(2)}) %all-to-all-start) | async-done | bytes 6291488 | tf_op jit(solution)/shard_map/all_to_all | solution.py:24
  213.5 36.8 %reshape.14 = bf16[12288,1,256]{2,1,0:T(2,128)(2,1)} reshape(bf16[64,2,24576]{2,1,0:T(2,128)(2,1)} %all-to-all-done) | data formatting | bytes 12582912
  250.3 11.4 %copy.6 = f32[12288,1,256]{2,0,1:T(8,128)} copy(bf16[12288,1,256]{2,1,0:T(2,128)(2,1)} %reshape.14) | data formatting | bytes 18874368
  261.7 6.1 %reduce_sum.9 = f32[192,256]{1,0:T(8,128)} reduce(f32[64,192,256]{2,1,0:T(8,128)} %bitcast.7, f32[]{:T(128)} %constant.0.clone.1), dimensions={0}, to_apply=%region_0.0 | reduce | flops 3096576 | bytes 12779524 | tf_op jit(solution)/shard_map/reduce_sum | solution.py:8
  267.8 0.0 all-reduce.2.cloned.1.call-update
  267.8 180.8 %all-gather.2.cloned.1.call-done = bf16[12288,256]{1,0:T(8,128)(2,1)} async-done(((bf16[192,256]{1,0:T(8,128)(2,1)}), bf16[12288,256]{1,0:T(8,128)(2,1)}) %all-gather.2.cloned.1.call-update) | async-done | bytes 6291472 | tf_op jit(solution)/shard_map/all_gather | solution.py:16
  448.6 4.4 convolution_convert_fusion.1
  453.0 0.0 all-reduce.2.cloned.1.call-done
  453.0 1.6 copy.9
Async XLA Ops:
  8.0 1.9 copy-start
  38.8 174.6 %all-to-all-start = ((bf16[64,2,24576]{2,1,0:T(2,128)(2,1)}), bf16[64,2,24576]{2,1,0:T(2,128)(2,1)}, u32[]{:S(2)}, u32[]{:S(2)}) async-start(bf16[64,2,24576]{2,1,0:T(2,128)(2,1)} %reshape.13), calls=%async_computation | async-start | bytes 12582912 | tf_op jit(solution)/shard_map/all_to_all | solution.py:24
  53.9 394.7 %all-gather.2.cloned.1.call-start = ((), (), s32[]{:S(2)}) async-start(), calls=%async_computation.1 | async-start | bytes 6389760 | tf_op jit(solution)/shard_map/all_gather | solution.py:16
  54.7 398.4 %all-reduce.2.cloned.1.call-start = ((), (), s32[]{:S(2)}) async-start(), calls=%async_computation.2 | async-start | bytes 393216 | tf_op jit(solution)/shard_map/psum | solution.py:27
Sparse Core Ops, SparseCore 0:
  56.8 391.7 all-gather.1
Sparse Core Ops, SparseCore 1:
  267.9 78.7 all-reduce.1
where the time goes:
time: 464 us; the launch traced here: 462 us
  waiting for transfers between devices  340 us (73%)
  local copies, waits for them, and re-layouts  66.5 us (14%)
  between operations  15.5 us (3%)
  starting transfers between devices  15.1 us (3%)
  other arithmetic  14.9 us (3%)
  matrix products  9.73 us (2%)
    all_gather x1, waiting for transfers between devices, local(): lax.all_gather(weight, ('node', 'gpu'), axis=0, tiled=True)  181 us
    all_to_all x1, waiting for transfers between devices, local(): lax.all_to_all(stacked, ('node', 'gpu'), split_axis=0, concat_axis=1, til...  159 us
    unnamed x6, local copies, waits for them, and re-layouts  66 us
    all_to_all x1, starting transfers between devices, local(): lax.all_to_all(stacked, ('node', 'gpu'), split_axis=0, concat_axis=1, til...  15.1 us
  transfers between devices with their start and end apart: 3, of which 2 were waited for; matrix products, arithmetic and copies ran while one was open for 13% of the time, Pallas kernels for 0%

commit v1 on v0

v1 whole, which is shorter than its diff:
```python
import jax
import jax.numpy as jnp
from jax import lax
from jax.sharding import Mesh, PartitionSpec as P


def local(tokens, weight, grad_out):
    rows, width = tokens.shape
    shard, cols = weight.shape
    sharers = lax.axis_size(("c", "x"))
    lines = lax.axis_size(("yh", "yl"))
    depth = lax.axis_size("z")
    part = width // sharers
    piece = shard // lines

    blocks = jnp.stack([tokens[:, k * part : (k + 1) * part] for k in range(sharers)])
    blocks = lax.all_to_all(blocks, ("c", "x"), 0, 0)
    blocks = blocks.reshape(sharers * rows, part)

    swap = [(0, 0), (1, 2), (2, 1), (3, 3)]
    mine = lax.ppermute(weight, ("c", "yl"), swap)
    mine = lax.all_gather(mine, "z", axis=0, tiled=True)

    grads = lax.all_gather(grad_out, ("c", "x"), axis=0, tiled=True)

    term = lax.dot_general(
        blocks, grads, (((0,), (0,)), ((), ())), preferred_element_type=jnp.float32
    ).astype(jnp.bfloat16)
    term = term.reshape(depth, lines, piece, cols).transpose(1, 0, 2, 3)
    term = term.reshape(lines * depth, piece, cols)
    term = lax.all_to_all(term, ("yh", "yl", "z"), 0, 0)
    summed = jnp.sum(term, axis=0, dtype=jnp.float32)

    partial = jnp.dot(blocks, mine, preferred_element_type=jnp.float32)
    partial = lax.all_to_all(partial.reshape(sharers, rows, cols), ("c", "x"), 0, 0)
    output = jnp.sum(partial, axis=0).astype(jnp.bfloat16)

    spread = jnp.broadcast_to(summed[None], (lines, piece, cols))
    spread = lax.all_to_all(spread, ("yh", "yl"), 0, 0).reshape(shard, cols)
    other = lax.ppermute(spread, "c", [(0, 1), (1, 0)])
    own = lax.axis_index("c") == lax.axis_index("yl")
    return output, jnp.where(own, spread, other)


def solution(mesh):
    inner = Mesh(mesh.devices.reshape(4, 2, 2, 4, 8), ("yh", "c", "yl", "x", "z"))
    rows = P(("yh", "c", "yl", "x", "z"), None)
    owners = P(("yl", "x", "z"), None)
    return jax.shard_map(
        local,
        mesh=inner,
        in_specs=(rows, owners, rows),
        out_specs=(rows, owners),
        check_vma=False,
    )
```

time: 464 us -> 186 us (0.40)
  the two profiles are of different devices: /device:TPU:24 before, /device:TPU:1 now
where the time goes in v1:
time: 186 us; the launch traced here: 185 us
  blocking collectives  82 us (44%)
  starting transfers between devices  43.8 us (24%)
  waiting for transfers between devices  34.8 us (19%)
  local copies, waits for them, and re-layouts  15.9 us (9%)
  matrix products  5.15 us (3%)
  other arithmetic  2.68 us (1%)
    all_gather x1, blocking collectives, local(): grads = lax.all_gather(grad_out, ('c', 'x'), axis=0, tiled=True)  58.2 us
    all_gather x1, blocking collectives, local(): mine = lax.all_gather(mine, 'z', axis=0, tiled=True)  23.8 us
    ppermute x1, waiting for transfers between devices, local(): mine = lax.ppermute(weight, ('c', 'yl'), swap)  16.3 us
    all_to_all x1, waiting for transfers between devices, local(): lax.all_to_all(partial.reshape(sharers, rows, cols), ('c', 'x'), 0, 0)  13 us
    unnamed x11, local copies, waits for them, and re-layouts  12.5 us
    all_to_all x1, starting transfers between devices, local(): term = lax.all_to_all(term, ('yh', 'yl', 'z'), 0, 0)  11.9 us
    all_to_all x1, starting transfers between devices, local(): lax.all_to_all(partial.reshape(sharers, rows, cols), ('c', 'x'), 0, 0)  10.8 us
    all_to_all x1, starting transfers between devices, local(): blocks = lax.all_to_all(blocks, ('c', 'x'), 0, 0)  10.6 us
  transfers between devices with their start and end apart: 6, of which 3 were waited for; matrix products, arithmetic and copies ran while one was open for 2% of the time, Pallas kernels for 0%

profile of v1, /device:TPU:1, one launch (start us, length us, event | category | flops | bytes accessed | tf_op | source)
XLA Modules:
  0.0 185.1 jit_solution(12249273473090205176)
XLA Ops:
  0.6 1.8 bitcast_dynamic-update-slice_fusion.7
  2.4 1.8 bitcast_dynamic-update-slice_fusion.6
  4.2 1.8 bitcast_dynamic-update-slice_fusion.5
  6.0 1.8 bitcast_dynamic-update-slice_fusion.4
  7.8 1.8 bitcast_dynamic-update-slice_fusion.3
  9.5 1.8 bitcast_dynamic-update-slice_fusion.2
  11.3 1.8 bitcast_dynamic-update-slice_fusion.1
  13.1 1.8 bitcast_dynamic-update-slice_fusion
  14.9 10.6 %all-to-all-start = ((bf16[8,128,1536]{2,1,0:T(8,128)(2,1)}), bf16[8,128,1536]{2,1,0:T(8,128)(2,1)S(1)}, u32[]{:S(2)}, u32[]{:S(2)}) async-start(bf16[8,128,1536]{2,1,0:T(8,128)(2,1)} %bitcast_dynamic-update-slice_fusion), calls=%async_computation | async-start | bytes 6291456 | tf_op jit(solution)/shard_map/all_to_all | solution.py:17
  25.5 58.2 %all_gather.7 = bf16[1024,256]{1,0:T(8,128)(2,1)} all-gather(bf16[128,256]{1,0:T(8,128)(2,1)S(1)} %copy-done), channel_id=1, replica_groups=mesh['yh'=4,'c'=2,'yl'=2,'x'=4,'z'=8] {'c','x'}, dimensions={0}, use_global_device_ids=true | all-gather | bytes 589824 | tf_op jit(solution)/shard_map/all_gather | solution.py:24
  83.7 2.1 %convolution_convert_fusion = bf16[1536,256]{1,0:T(8,128)(2,1)S(1)} fusion(bf16[1024,1536]{1,0:T(8,128)(2,1)S(1)} %bitcast.29, bf16[1024,256]{1,0:T(8,128)(2,1)} %all_gather.7), kind=kOutput, calls=%fused_computation | convolution fusion | flops 805699584 | bytes 4456448 | tf_op jit(solution)/shard_map/dot_general | solution.py:26
  85.8 0.9 copy.5
  86.7 11.9 %all-to-all-start.2 = ((bf16[64,24,256]{2,1,0:T(8,128)(2,1)}), bf16[64,24,256]{2,1,0:T(8,128)(2,1)}, u32[]{:S(2)}, u32[]{:S(2)}) async-start(bf16[64,24,256]{2,1,0:T(8,128)(2,1)} %bitcast.30), calls=%async_computation.2 | async-start | bytes 1572864 | tf_op jit(solution)/shard_map/all_to_all | solution.py:31
  98.6 3.6 %collective-permute-start = (bf16[192,256]{1,0:T(8,128)(2,1)S(1)}, bf16[192,256]{1,0:T(8,128)(2,1)S(1)}, u32[]{:S(2)}, u32[]{:S(2)}) collective-permute-start(bf16[192,256]{1,0:T(8,128)(2,1)S(1)} %copy-done.1), channel_id=1, source_target_pairs={{0,0},{32,64},{64,32},{96,96},{1,1},{33,65},{65,33},{97,97},{2,2},... | collective-permute-start | bytes 294920 | tf_op jit(solution)/shard_map/ppermute | solution.py:21
  102.2 16.3 %collective-permute-done = bf16[192,256]{1,0:T(8,128)(2,1)S(1)} collective-permute-done((bf16[192,256]{1,0:T(8,128)(2,1)S(1)}, bf16[192,256]{1,0:T(8,128)(2,1)S(1)}, u32[]{:S(2)}, u32[]{:S(2)}) %collective-permute-start) | collective-permute-done | bytes 98336 | tf_op jit(solution)/shard_map/ppermute | solution.py:21
  118.5 23.8 %all_gather.6 = bf16[1536,256]{1,0:T(8,128)(2,1)} all-gather(bf16[192,256]{1,0:T(8,128)(2,1)S(1)} %collective-permute-done), channel_id=1, replica_groups=mesh['yh'=4,'c'=2,'yl'=2,'x'=4,'z'=8] {'z'}, dimensions={0}, use_global_device_ids=true | all-gather | bytes 884736 | tf_op jit(solution)/shard_map/all_gather | solution.py:22
  142.3 1.3 convert_reduce_fusion
  144.3 5.0 %all-to-all-start.3 = ((f32[8,24,256]{2,1,0:T(8,128)}), f32[8,24,256]{2,1,0:T(8,128)S(1)}, u32[]{:S(2)}, u32[]{:S(2)}) async-start(f32[8,24,256]{2,1,0:T(8,128)} %broadcast_in_dim.2), calls=%async_computation.3 | async-start | bytes 393216 | tf_op jit(solution)/shard_map/all_to_all | solution.py:39
  149.3 3.1 %fusion = f32[8,128,256]{2,1,0:T(8,128)} fusion(bf16[8,128,1536]{2,1,0:T(8,128)(2,1)S(1)} %all-to-all-done, bf16[1536,256]{1,0:T(8,128)(2,1)} %all_gather.6), kind=kOutput, calls=%fused_computation.2 | convolution fusion | flops 805306368 | bytes 4980736 | tf_op jit(solution)/shard_map/dot_general | solution.py:34
  152.4 5.5 %all-to-all-done.3 = f32[8,24,256]{2,1,0:T(8,128)S(1)} async-done(((f32[8,24,256]{2,1,0:T(8,128)}), f32[8,24,256]{2,1,0:T(8,128)S(1)}, u32[]{:S(2)}, u32[]{:S(2)}) %all-to-all-start.3) | async-done | bytes 196640 | tf_op jit(solution)/shard_map/all_to_all | solution.py:39
  158.0 10.8 %all-to-all-start.1 = ((f32[8,128,256]{2,1,0:T(8,128)}), f32[8,128,256]{2,1,0:T(8,128)S(1)}, u32[]{:S(2)}, u32[]{:S(2)}) async-start(f32[8,128,256]{2,1,0:T(8,128)} %fusion), calls=%async_computation.1 | async-start | bytes 2097152 | tf_op jit(solution)/shard_map/all_to_all | solution.py:35
  168.7 2.0 %collective-permute-start.1 = (f32[192,256]{1,0:T(8,128)S(1)}, f32[192,256]{1,0:T(8,128)S(1)}, u32[]{:S(2)}, u32[]{:S(2)}) collective-permute-start(f32[192,256]{1,0:T(8,128)S(1)} %bitcast.32), channel_id=1, source_target_pairs={{0,64},{64,0},{1,65},{65,1},{2,66},{66,2},{3,67},{67,3},{4,68},{68... | collective-permute-start | bytes 589832 | tf_op jit(solution)/shard_map/ppermute | solution.py:40
  170.7 13.0 %all-to-all-done.1 = f32[8,128,256]{2,1,0:T(8,128)S(1)} async-done(((f32[8,128,256]{2,1,0:T(8,128)}), f32[8,128,256]{2,1,0:T(8,128)S(1)}, u32[]{:S(2)}, u32[]{:S(2)}) %all-to-all-start.1) | async-done | bytes 1048608 | tf_op jit(solution)/shard_map/all_to_all | solution.py:35
  184.4 0.7 broadcast_select_fusion
  (9 shorter events, 1.4 us)
Async XLA Ops:
  14.9 10.6 %copy-start = (bf16[128,256]{1,0:T(8,128)(2,1)S(1)}, bf16[128,256]{1,0:T(8,128)(2,1)}, u32[]{:S(2)}) copy-start(bf16[128,256]{1,0:T(8,128)(2,1)} %param.5) | copy-start | bytes 196612
  14.9 68.8 %all-to-all-start = ((bf16[8,128,1536]{2,1,0:T(8,128)(2,1)}), bf16[8,128,1536]{2,1,0:T(8,128)(2,1)S(1)}, u32[]{:S(2)}, u32[]{:S(2)}) async-start(bf16[8,128,1536]{2,1,0:T(8,128)(2,1)} %bitcast_dynamic-update-slice_fusion), calls=%async_computation | async-start | bytes 6291456 | tf_op jit(solution)/shard_map/all_to_all | solution.py:17
  85.8 12.8 %copy-start.1 = (bf16[192,256]{1,0:T(8,128)(2,1)S(1)}, bf16[192,256]{1,0:T(8,128)(2,1)}, u32[]{:S(2)}) copy-start(bf16[192,256]{1,0:T(8,128)(2,1)} %param.4) | copy-start | bytes 294916
  86.7 55.6 %all-to-all-start.2 = ((bf16[64,24,256]{2,1,0:T(8,128)(2,1)}), bf16[64,24,256]{2,1,0:T(8,128)(2,1)}, u32[]{:S(2)}, u32[]{:S(2)}) async-start(bf16[64,24,256]{2,1,0:T(8,128)(2,1)} %bitcast.30), calls=%async_computation.2 | async-start | bytes 1572864 | tf_op jit(solution)/shard_map/all_to_all | solution.py:31
  98.6 19.9 %collective-permute-start = (bf16[192,256]{1,0:T(8,128)(2,1)S(1)}, bf16[192,256]{1,0:T(8,128)(2,1)S(1)}, u32[]{:S(2)}, u32[]{:S(2)}) collective-permute-start(bf16[192,256]{1,0:T(8,128)(2,1)S(1)} %copy-done.1), channel_id=1, source_target_pairs={{0,0},{32,64},{64,32},{96,96},{1,1},{33,65},{65,33},{97,97},{2,2},... | collective-permute-start | bytes 294920 | tf_op jit(solution)/shard_map/ppermute | solution.py:21
  144.3 13.6 %all-to-all-start.3 = ((f32[8,24,256]{2,1,0:T(8,128)}), f32[8,24,256]{2,1,0:T(8,128)S(1)}, u32[]{:S(2)}, u32[]{:S(2)}) async-start(f32[8,24,256]{2,1,0:T(8,128)} %broadcast_in_dim.2), calls=%async_computation.3 | async-start | bytes 393216 | tf_op jit(solution)/shard_map/all_to_all | solution.py:39
  158.0 25.7 %all-to-all-start.1 = ((f32[8,128,256]{2,1,0:T(8,128)}), f32[8,128,256]{2,1,0:T(8,128)S(1)}, u32[]{:S(2)}, u32[]{:S(2)}) async-start(f32[8,128,256]{2,1,0:T(8,128)} %fusion), calls=%async_computation.1 | async-start | bytes 2097152 | tf_op jit(solution)/shard_map/all_to_all | solution.py:35
  168.7 15.7 %collective-permute-start.1 = (f32[192,256]{1,0:T(8,128)S(1)}, f32[192,256]{1,0:T(8,128)S(1)}, u32[]{:S(2)}, u32[]{:S(2)}) collective-permute-start(f32[192,256]{1,0:T(8,128)S(1)} %bitcast.32), channel_id=1, source_target_pairs={{0,64},{64,0},{1,65},{65,1},{2,66},{66,2},{3,67},{67,3},{4,68},{68... | collective-permute-start | bytes 589832 | tf_op jit(solution)/shard_map/ppermute | solution.py:40

commit v2 on v1

v2 whole, which is shorter than its diff:
```python
import jax
import jax.numpy as jnp
from jax import lax
from jax.experimental import pallas as pl
from jax.experimental.pallas import tpu as pltpu
from jax.sharding import Mesh, PartitionSpec as P

PARAMS = pltpu.CompilerParams(vmem_limit_bytes=32 * 1024 * 1024)


def pack(tokens, grad_out, sharers):
    rows, width = tokens.shape
    cols = grad_out.shape[1]
    part = width // sharers

    def body(t_ref, g_ref, o_ref):
        o_ref[0, :, :part] = t_ref[...]
        o_ref[0, :, part:] = g_ref[...]

    return pl.pallas_call(
        body,
        grid=(sharers,),
        in_specs=[
            pl.BlockSpec((rows, part), lambda k: (0, k)),
            pl.BlockSpec((rows, cols), lambda k: (0, 0)),
        ],
        out_specs=pl.BlockSpec((1, rows, part + cols), lambda k: (k, 0, 0)),
        out_shape=jax.ShapeDtypeStruct((sharers, rows, part + cols), tokens.dtype),
        compiler_params=PARAMS,
    )(tokens, grad_out)


def terms(packed, part, depth, yh, yl):
    sharers, rows, both = packed.shape
    cols = both - part
    shard = part // depth
    high, wide = shard // yh, cols // yl
    step = 2

    def body(t_ref, g_ref, o_ref):
        t = t_ref[...].reshape(sharers * rows, step * shard)
        g = g_ref[...].reshape(sharers * rows, cols)
        term = lax.dot_general(
            t, g, (((0,), (0,)), ((), ())), preferred_element_type=jnp.float32
        )
        for z in range(step):
            for i in range(yh):
                at = z * shard + i * high
                for j in range(yl):
                    o_ref[i, j, z] = term[
                        at : at + high, j * wide : (j + 1) * wide
                    ].astype(o_ref.dtype)

    return pl.pallas_call(
        body,
        grid=(depth // step,),
        in_specs=[
            pl.BlockSpec((sharers, rows, step * shard), lambda k: (0, 0, k)),
            pl.BlockSpec((sharers, rows, cols), lambda k: (0, 0, part // cols)),
        ],
        out_specs=pl.BlockSpec((yh, yl, step, high, wide), lambda k: (0, 0, k, 0, 0)),
        out_shape=jax.ShapeDtypeStruct((yh, yl, depth, high, wide), packed.dtype),
        compiler_params=PARAMS,
    )(packed, packed)


def project(packed, weight):
    sharers, rows, both = packed.shape
    part, cols = weight.shape

    def body(t_ref, w_ref, o_ref):
        o_ref[0] = jnp.dot(t_ref[0], w_ref[...], preferred_element_type=jnp.float32)

    return pl.pallas_call(
        body,
        grid=(sharers,),
        in_specs=[
            pl.BlockSpec((1, rows, part), lambda k: (k, 0, 0)),
            pl.BlockSpec((part, cols), lambda k: (0, 0)),
        ],
        out_specs=pl.BlockSpec((1, rows, cols), lambda k: (k, 0, 0)),
        out_shape=jax.ShapeDtypeStruct((sharers, rows, cols), jnp.float32),
        compiler_params=PARAMS,
    )(packed, weight)


def local(tokens, weight, grad_out):
    rows, width = tokens.shape
    shard, cols = weight.shape
    sharers = lax.axis_size(("c", "x"))
    yh, yl, depth = lax.axis_size("yh"), lax.axis_size("yl"), lax.axis_size("z")
    part = width // sharers

    mine = lax.ppermute(weight, ("c", "yl"), [(0, 0), (1, 2), (2, 1), (3, 3)])
    packed = pack(tokens, grad_out, sharers)
    packed = lax.all_to_all(packed, ("c", "x"), 0, 0)
    mine = jnp.broadcast_to(mine[None], (depth, shard, cols))
    mine = lax.all_to_all(mine, "z", 0, 0).reshape(part, cols)
    packed, mine = lax.optimization_barrier((packed, mine))

    term = terms(packed, part, depth, yh, yl)
    high, wide = term.shape[-2:]
    term = term.reshape(yh * yl * depth, high, wide)
    term = lax.all_to_all(term, ("yh", "yl", "z"), 0, 0)

    partial = project(packed, mine)
    partial = lax.all_to_all(partial, ("c", "x"), 0, 0)
    output = jnp.sum(partial, axis=0).astype(jnp.bfloat16)

    summed = jnp.sum(term, axis=0, dtype=jnp.float32)
    spread = jnp.broadcast_to(summed[None], (yh * yl, high, wide))
    spread = lax.all_to_all(spread, ("yh", "yl"), 0, 0)
    other = lax.ppermute(spread, "c", [(0, 1), (1, 0)])
    own = lax.axis_index("c") == lax.axis_index("yl")
    spread = jnp.where(own, spread, other).reshape(yh, yl, high, wide)
    return output, spread.transpose(0, 2, 1, 3).reshape(shard, cols)


def solution(mesh):
    inner = Mesh(mesh.devices.reshape(4, 2, 2, 4, 8), ("yh", "c", "yl", "x", "z"))
    rows = P(("yh", "c", "yl", "x", "z"), None)
    owners = P(("yl", "x", "z"), None)
    return jax.shard_map(
        local,
        mesh=inner,
        in_specs=(rows, owners, rows),
        out_specs=(rows, owners),
        check_vma=False,
    )
```

time: 186 us -> 157 us (0.84)
  starting transfers between devices: 43.8 us -> 29.5 us
  Pallas kernels: 0 us -> 7.03 us
  local copies, waits for them, and re-layouts: 15.9 us -> 8.96 us
  blocking collectives: 82 us -> 76.6 us
  matrix products: 5.15 us -> 0 us
    all_gather x2 -> x0, blocking collectives: 82 us -> none  [the longest x1 58.2 us: local(): grads = lax.all_gather(grad_out, ('c', 'x'), axis=0, tiled=True)]
    all_to_all x0 -> x2, blocking collectives: none -> 76.6 us  [the longest x1 47.5 us: local(): packed = lax.all_to_all(packed, ('c', 'x'), 0, 0)]
    all_to_all x4 -> x3, starting transfers between devices: 38.2 us -> 22.9 us  [the longest x1 10 us: local(): mine = lax.all_to_all(mine, 'z', 0, 0).reshape(part, cols)]
    ppermute x1, waiting for transfers between devices: 16.3 us -> 2.5 us  [local(): mine = lax.ppermute(weight, ('c', 'yl'), [(0, 0), (1, 2), (2, 1), (3, 3)])]
    all_to_all x4 -> x3, waiting for transfers between devices: 18.5 us -> 30.5 us  [the longest x1 15 us: local(): mine = lax.all_to_all(mine, 'z', 0, 0).reshape(part, cols)]
    pallas_call x0 -> x3, Pallas kernels: none -> 7.03 us  [the longest x1 4.13 us: project(): pl.pallas_call(body, grid=(sharers,), in_specs=[pl.BlockSpec((1, rows, pa...]
    unnamed x11, local copies, waits for them, and re-layouts: 12.5 us -> 7.23 us
    dot_general x2 -> x0, matrix products: 5.15 us -> none  [the longest x1 3.08 us: local(): partial = jnp.dot(blocks, mine, preferred_element_type=jnp.float32)]
  transfers between devices with their start and end apart: 6 -> 5, of which waited for: 3 -> 4; matrix products, arithmetic and copies ran while one was open for 2% -> 0% of each run, Pallas kernels for 0% -> 3%
where the time goes in v2:
time: 157 us
  blocking collectives  76.6 us (49%)
  waiting for transfers between devices  33 us (21%)
  starting transfers between devices  29.5 us (19%)
  local copies, waits for them, and re-layouts  8.96 us (6%)
  Pallas kernels  7.03 us (4%)
    all_to_all x1, blocking collectives, local(): packed = lax.all_to_all(packed, ('c', 'x'), 0, 0)  47.5 us
    all_to_all x1, blocking collectives, local(): term = lax.all_to_all(term, ('yh', 'yl', 'z'), 0, 0)  29.1 us
    all_to_all x1, waiting for transfers between devices, local(): mine = lax.all_to_all(mine, 'z', 0, 0).reshape(part, cols)  15 us
    all_to_all x1, waiting for transfers between devices, local(): partial = lax.all_to_all(partial, ('c', 'x'), 0, 0)  13 us
    all_to_all x1, starting transfers between devices, local(): mine = lax.all_to_all(mine, 'z', 0, 0).reshape(part, cols)  10 us
    unnamed x11, local copies, waits for them, and re-layouts  7.23 us
    all_to_all x1, starting transfers between devices, local(): partial = lax.all_to_all(partial, ('c', 'x'), 0, 0)  6.72 us
    all_to_all x1, starting transfers between devices, local(): spread = lax.all_to_all(spread, ('yh', 'yl'), 0, 0)  6.11 us
  transfers between devices with their start and end apart: 5, of which 4 were waited for; matrix products, arithmetic and copies ran while one was open for 0% of the time, Pallas kernels for 3%

profile of v2, /device:TPU:1, one launch (start us, length us, event | category | flops | bytes accessed | tf_op | source)
XLA Modules:
  0.0 156.7 jit_solution(600219416828049220)
XLA Ops:
  0.6 4.6 %collective-permute-start = (bf16[192,256]{1,0:T(8,128)(2,1)}, bf16[192,256]{1,0:T(8,128)(2,1)S(1)}, u32[]{:S(2)}, u32[]{:S(2)}) collective-permute-start(bf16[192,256]{1,0:T(8,128)(2,1)} %param.4), channel_id=1, source_target_pairs={{0,0},{32,64},{64,32},{96,96},{1,1},{33,65},{65,33},{97,97},{2,2},... | collective-permute-start | bytes 294920 | tf_op jit(solution)/shard_map/ppermute | solution.py:94
  5.2 2.5 %collective-permute-done = bf16[192,256]{1,0:T(8,128)(2,1)S(1)} collective-permute-done((bf16[192,256]{1,0:T(8,128)(2,1)}, bf16[192,256]{1,0:T(8,128)(2,1)S(1)}, u32[]{:S(2)}, u32[]{:S(2)}) %collective-permute-start) | collective-permute-done | bytes 98336 | tf_op jit(solution)/shard_map/ppermute | solution.py:94
  7.7 0.9 broadcast_in_dim.4
  8.7 10.0 %all-to-all-start.1 = ((bf16[8,192,256]{2,1,0:T(8,128)(2,1)}), bf16[8,192,256]{2,1,0:T(8,128)(2,1)S(1)}, u32[]{:S(2)}, u32[]{:S(2)}) async-start(bf16[8,192,256]{2,1,0:T(8,128)(2,1)} %broadcast_in_dim.4), calls=%async_computation.1 | async-start | bytes 1572864 | tf_op jit(solution)/shard_map/all_to_all | solution.py:98
  18.7 1.9 %copy-done.3 = bf16[128,12288]{1,0:T(8,128)(2,1)S(1)} copy-done((bf16[128,12288]{1,0:T(8,128)(2,1)S(1)}, bf16[128,12288]{1,0:T(8,128)(2,1)}, u32[]{:S(2)}) %copy-start.3) | copy-done | bytes 3145752
  20.6 0.8 copy-done.4
  21.4 0.6 shard_map.50
  22.1 1.8 %copy-done.2 = bf16[8,128,1792]{2,1,0:T(8,128)(2,1)} copy-done((bf16[8,128,1792]{2,1,0:T(8,128)(2,1)}, bf16[8,128,1792]{2,1,0:T(8,128)(2,1)S(1)}, u32[]{:S(2)}) %copy-start.2) | copy-done | bytes 3670040
  23.8 15.0 %all-to-all-done.1 = bf16[8,192,256]{2,1,0:T(8,128)(2,1)S(1)} async-done(((bf16[8,192,256]{2,1,0:T(8,128)(2,1)}), bf16[8,192,256]{2,1,0:T(8,128)(2,1)S(1)}, u32[]{:S(2)}, u32[]{:S(2)}) %all-to-all-start.1) | async-done | bytes 786464 | tf_op jit(solution)/shard_map/all_to_all | solution.py:98
  38.8 47.5 %all_to_all.25.t_ref.g_ref = bf16[8,128,1792]{2,1,0:T(8,128)(2,1)S(1)} all-to-all(bf16[8,128,1792]{2,1,0:T(8,128)(2,1)} %copy-done.2), channel_id=1, replica_groups=mesh['yh'=4,'c'=2,'yl'=2,'x'=4,'z'=8] {'c','x'}, dimensions={0} | all-to-all | bytes 7340032 | tf_op jit(solution)/shard_map/all_to_all | solution.py:96
  86.3 2.3 %shard_map.52 = bf16[4,2,8,48,128]{4,3,2,1,0:T(8,128)(2,1)S(1)} custom-call(bf16[8,128,1792]{2,1,0:T(8,128)(2,1)S(1)} %all_to_all.25.t_ref.g_ref, bf16[8,128,1792]{2,1,0:T(8,128)(2,1)S(1)} %all_to_all.25.t_ref.g_ref), custom_call_target="tpu_custom_call" | custom-call | tf_op jit(solution)/shard_map/pallas_call | solution.py:54
  88.6 29.1 %all_to_all.26 = bf16[64,48,128]{2,1,0:T(8,128)(2,1)S(1)} all-to-all(bf16[64,48,128]{2,1,0:T(8,128)(2,1)S(1)} %bitcast.11), channel_id=1, replica_groups=mesh['yh'=4,'c'=2,'yl'=2,'x'=4,'z'=8] {'yh','yl','z'}, dimensions={0} | all-to-all | bytes 1572864 | tf_op jit(solution)/shard_map/all_to_all | solution.py:104
  117.8 0.1 convert_reduce_fusion
  117.9 0.7 broadcast_in_dim.5
  118.6 6.1 %all-to-all-start.4 = ((f32[8,48,128]{2,1,0:T(8,128)}), f32[8,48,128]{2,1,0:T(8,128)S(1)}, u32[]{:S(2)}, u32[]{:S(2)}) async-start(f32[8,48,128]{2,1,0:T(8,128)} %broadcast_in_dim.5), calls=%async_computation.4 | async-start | bytes 393216 | tf_op jit(solution)/shard_map/all_to_all | solution.py:112
  124.7 2.0 %copy-done.1 = bf16[8,128,1792]{2,1,0:T(8,128)(2,1)S(1)} copy-done((bf16[8,128,1792]{2,1,0:T(8,128)(2,1)S(1)}, bf16[8,128,1792]{2,1,0:T(8,128)(2,1)}, u32[]{:S(2)}) %copy-start.1) | copy-done | bytes 3670040
  126.7 4.1 %shard_map.51 = f32[8,128,256]{2,1,0:T(8,128)} custom-call(bf16[8,128,1792]{2,1,0:T(8,128)(2,1)S(1)} %copy-done.1, bf16[1536,256]{1,0:T(8,128)(2,1)S(1)} %bitcast.10), custom_call_target="tpu_custom_call" | custom-call | tf_op jit(solution)/shard_map/pallas_call | solution.py:74
  130.9 2.6 %all-to-all-done.4 = f32[8,48,128]{2,1,0:T(8,128)S(1)} async-done(((f32[8,48,128]{2,1,0:T(8,128)}), f32[8,48,128]{2,1,0:T(8,128)S(1)}, u32[]{:S(2)}, u32[]{:S(2)}) %all-to-all-start.4) | async-done | bytes 196640 | tf_op jit(solution)/shard_map/all_to_all | solution.py:112
  133.4 6.7 %all-to-all-start.2 = ((f32[8,128,256]{2,1,0:T(8,128)}), f32[8,128,256]{2,1,0:T(8,128)S(1)}, u32[]{:S(2)}, u32[]{:S(2)}) async-start(f32[8,128,256]{2,1,0:T(8,128)} %shard_map.51), calls=%async_computation.2 | async-start | bytes 2097152 | tf_op jit(solution)/shard_map/all_to_all | solution.py:107
  140.2 2.0 %collective-permute-start.1 = (f32[8,48,128]{2,1,0:T(8,128)S(1)}, f32[8,48,128]{2,1,0:T(8,128)S(1)}, u32[]{:S(2)}, u32[]{:S(2)}) collective-permute-start(f32[8,48,128]{2,1,0:T(8,128)S(1)} %all-to-all-done.4), channel_id=1, source_target_pairs={{0,64},{64,0},{1,65},{65,1},{2,66},{66,2},{3,67},{67,3},{4,68},{68... | collective-permute-start | bytes 589832 | tf_op jit(solution)/shard_map/ppermute | solution.py:113
  142.2 13.0 %all-to-all-done.2 = f32[8,128,256]{2,1,0:T(8,128)S(1)} async-done(((f32[8,128,256]{2,1,0:T(8,128)}), f32[8,128,256]{2,1,0:T(8,128)S(1)}, u32[]{:S(2)}, u32[]{:S(2)}) %all-to-all-start.2) | async-done | bytes 1048608 | tf_op jit(solution)/shard_map/all_to_all | solution.py:107
  155.2 0.7 reduce_sum.18
  155.9 0.1 copy.5
  156.0 0.7 copy.8
  (8 shorter events, 0.0 us)
Async XLA Ops:
  0.6 7.1 %collective-permute-start = (bf16[192,256]{1,0:T(8,128)(2,1)}, bf16[192,256]{1,0:T(8,128)(2,1)S(1)}, u32[]{:S(2)}, u32[]{:S(2)}) collective-permute-start(bf16[192,256]{1,0:T(8,128)(2,1)} %param.4), channel_id=1, source_target_pairs={{0,0},{32,64},{64,32},{96,96},{1,1},{33,65},{65,33},{97,97},{2,2},... | collective-permute-start | bytes 294920 | tf_op jit(solution)/shard_map/ppermute | solution.py:94
  8.7 30.2 %all-to-all-start.1 = ((bf16[8,192,256]{2,1,0:T(8,128)(2,1)}), bf16[8,192,256]{2,1,0:T(8,128)(2,1)S(1)}, u32[]{:S(2)}, u32[]{:S(2)}) async-start(bf16[8,192,256]{2,1,0:T(8,128)(2,1)} %broadcast_in_dim.4), calls=%async_computation.1 | async-start | bytes 1572864 | tf_op jit(solution)/shard_map/all_to_all | solution.py:98
  18.7 1.9 %copy-start.3 = (bf16[128,12288]{1,0:T(8,128)(2,1)S(1)}, bf16[128,12288]{1,0:T(8,128)(2,1)}, u32[]{:S(2)}) copy-start(bf16[128,12288]{1,0:T(8,128)(2,1)} %t_ref.1) | copy-start | bytes 9437188
  20.6 0.8 copy-start.4
  22.1 1.8 %copy-start.2 = (bf16[8,128,1792]{2,1,0:T(8,128)(2,1)}, bf16[8,128,1792]{2,1,0:T(8,128)(2,1)S(1)}, u32[]{:S(2)}) copy-start(bf16[8,128,1792]{2,1,0:T(8,128)(2,1)S(1)} %shard_map.50) | copy-start | bytes 11010052
  86.3 2.3 %copy-start = (bf16[8,128,1792]{2,1,0:T(8,128)(2,1)}, bf16[8,128,1792]{2,1,0:T(8,128)(2,1)S(1)}, u32[]{:S(2)}) copy-start(bf16[8,128,1792]{2,1,0:T(8,128)(2,1)S(1)} %all_to_all.25.t_ref.g_ref) | copy-start | bytes 11010052
  118.6 14.8 %all-to-all-start.4 = ((f32[8,48,128]{2,1,0:T(8,128)}), f32[8,48,128]{2,1,0:T(8,128)S(1)}, u32[]{:S(2)}, u32[]{:S(2)}) async-start(f32[8,48,128]{2,1,0:T(8,128)} %broadcast_in_dim.5), calls=%async_computation.4 | async-start | bytes 393216 | tf_op jit(solution)/shard_map/all_to_all | solution.py:112
  124.7 2.0 %copy-start.1 = (bf16[8,128,1792]{2,1,0:T(8,128)(2,1)S(1)}, bf16[8,128,1792]{2,1,0:T(8,128)(2,1)}, u32[]{:S(2)}) copy-start(bf16[8,128,1792]{2,1,0:T(8,128)(2,1)} %copy-done) | copy-start | bytes 11010052
  133.4 21.7 %all-to-all-start.2 = ((f32[8,128,256]{2,1,0:T(8,128)}), f32[8,128,256]{2,1,0:T(8,128)S(1)}, u32[]{:S(2)}, u32[]{:S(2)}) async-start(f32[8,128,256]{2,1,0:T(8,128)} %shard_map.51), calls=%async_computation.2 | async-start | bytes 2097152 | tf_op jit(solution)/shard_map/all_to_all | solution.py:107
  140.2 15.7 %collective-permute-start.1 = (f32[8,48,128]{2,1,0:T(8,128)S(1)}, f32[8,48,128]{2,1,0:T(8,128)S(1)}, u32[]{:S(2)}, u32[]{:S(2)}) collective-permute-start(f32[8,48,128]{2,1,0:T(8,128)S(1)} %all-to-all-done.4), channel_id=1, source_target_pairs={{0,64},{64,0},{1,65},{65,1},{2,66},{66,2},{3,67},{67,3},{4,68},{68... | collective-permute-start | bytes 589832 | tf_op jit(solution)/shard_map/ppermute | solution.py:113

commit v3 on v2

v3 whole, which is shorter than its diff:
```python
import jax
import jax.numpy as jnp
from jax import lax
from jax.experimental import pallas as pl
from jax.experimental.pallas import tpu as pltpu
from jax.sharding import Mesh, PartitionSpec as P

PARAMS = pltpu.CompilerParams(vmem_limit_bytes=32 * 1024 * 1024)


def pack(tokens, grad_out, sharers):
    rows, width = tokens.shape
    cols = grad_out.shape[1]
    part = width // sharers

    def body(t_ref, g_ref, o_ref):
        o_ref[0, :, :part] = t_ref[...]
        o_ref[0, :, part:] = g_ref[...]

    return pl.pallas_call(
        body,
        grid=(sharers,),
        in_specs=[
            pl.BlockSpec((rows, part), lambda k: (0, k)),
            pl.BlockSpec((rows, cols), lambda k: (0, 0)),
        ],
        out_specs=pl.BlockSpec((1, rows, part + cols), lambda k: (k, 0, 0)),
        out_shape=jax.ShapeDtypeStruct((sharers, rows, part + cols), tokens.dtype),
        compiler_params=PARAMS,
    )(tokens, grad_out)


def terms(packed, spot, part, depth, yh):
    sharers, rows, both = packed.shape
    cols = both - part
    shard = part // depth
    high, wide = shard // yh, cols // 2
    step = 2
    first = part // wide

    def body(spot_ref, t_ref, own_ref, other_ref, keep_ref, send_ref):
        t = t_ref[...].reshape(sharers * rows, step * shard)
        g = jnp.concatenate([own_ref[...], other_ref[...]], axis=-1)
        term = lax.dot_general(
            t,
            g.reshape(sharers * rows, cols),
            (((0,), (0,)), ((), ())),
            preferred_element_type=jnp.float32,
        )
        for z in range(step):
            for i in range(yh):
                at = z * shard + i * high
                keep_ref[i, z] = term[at : at + high, :wide]
                send_ref[i, z] = term[at : at + high, wide:]

    half = jax.ShapeDtypeStruct((yh, depth, high, wide), jnp.float32)
    half_spec = pl.BlockSpec((yh, step, high, wide), lambda k, spot: (0, k, 0, 0))
    return pl.pallas_call(
        body,
        grid_spec=pltpu.PrefetchScalarGridSpec(
            num_scalar_prefetch=1,
            grid=(depth // step,),
            in_specs=[
                pl.BlockSpec(
                    (sharers, rows, step * shard), lambda k, spot: (0, 0, k)
                ),
                pl.BlockSpec(
                    (sharers, rows, wide), lambda k, spot: (0, 0, first + spot[0])
                ),
                pl.BlockSpec(
                    (sharers, rows, wide), lambda k, spot: (0, 0, first + 1 - spot[0])
                ),
            ],
            out_specs=[half_spec, half_spec],
        ),
        out_shape=[half, half],
        compiler_params=PARAMS,
    )(spot, packed, packed, packed)


def project(packed, weight, spot, away, width):
    rows = packed.shape[1]
    part, cols = weight.shape

    def source(k, spot):
        line = 1 - spot[1] if away else spot[1]
        return line * width + lax.rem(spot[2] + k, width)

    def body(spot_ref, t_ref, w_ref, o_ref):
        o_ref[0] = jnp.dot(t_ref[0], w_ref[...], preferred_element_type=jnp.float32)

    return pl.pallas_call(
        body,
        grid_spec=pltpu.PrefetchScalarGridSpec(
            num_scalar_prefetch=1,
            grid=(width,),
            in_specs=[
                pl.BlockSpec((1, rows, part), lambda k, spot: (source(k, spot), 0, 0)),
                pl.BlockSpec((part, cols), lambda k, spot: (0, 0)),
            ],
            out_specs=pl.BlockSpec((1, rows, cols), lambda k, spot: (k, 0, 0)),
        ),
        out_shape=jax.ShapeDtypeStruct((width, rows, cols), jnp.float32),
        compiler_params=PARAMS,
    )(spot, packed, weight)


def local(tokens, weight, grad_out):
    rows, model = tokens.shape
    shard, cols = weight.shape
    sharers, width = lax.axis_size(("yl", "x")), lax.axis_size("x")
    yh, depth = lax.axis_size("yh"), lax.axis_size("z")
    part = model // sharers
    spot = jnp.stack([lax.axis_index(name) for name in ("c", "yl", "x")])
    spot = spot.astype(jnp.int32)

    packed = pack(tokens, grad_out, sharers)
    packed = lax.all_to_all(packed, ("yl", "x"), 0, 0)
    mine = lax.all_gather(weight, "z", axis=0, tiled=True)
    packed, mine = lax.optimization_barrier((packed, mine))

    keep, send = terms(packed, spot, part, depth, yh)
    high, wide = keep.shape[-2:]
    term = (keep + lax.ppermute(send, "c", [(0, 1), (1, 0)])).astype(jnp.bfloat16)
    term = lax.all_to_all(term.reshape(yh * depth, high, wide), ("yh", "z"), 0, 0)
    summed = jnp.sum(term, axis=0, dtype=jnp.float32)

    away = project(packed, mine, spot, True, width)
    near = project(packed, mine, spot, False, width)
    near = near + lax.ppermute(away, "yl", [(0, 1), (1, 0)])
    output = near[0]
    for d in range(1, width):
        shift = [(i, (i + d) % width) for i in range(width)]
        output = output + lax.ppermute(near[d], "x", shift)

    spread = jnp.broadcast_to(summed[None], (yh * 2, high, wide))
    spread = lax.all_to_all(spread, ("yh", "c"), 0, 0).reshape(yh, 2, high, wide)
    spread = spread.transpose(0, 2, 1, 3).reshape(shard, cols)
    return output.astype(jnp.bfloat16), spread


def solution(mesh):
    inner = Mesh(mesh.devices.reshape(4, 2, 2, 4, 8), ("yh", "c", "yl", "x", "z"))
    rows = P(("yh", "c", "yl", "x", "z"), None)
    owners = P(("yl", "x", "z"), None)
    return jax.shard_map(
        local,
        mesh=inner,
        in_specs=(rows, owners, rows),
        out_specs=(rows, owners),
        check_vma=False,
    )
```

time: 157 us -> 117 us (0.75)
  blocking collectives: 76.6 us -> 29.2 us
  starting transfers between devices: 29.5 us -> 42.1 us
  waiting for transfers between devices: 33 us -> 24.6 us
  Pallas kernels: 7.03 us -> 12 us
  local copies, waits for them, and re-layouts: 8.96 us -> 6.08 us
    all_to_all x2 -> x0, blocking collectives: 76.6 us -> none  [the longest x1 47.5 us: local(): packed = lax.all_to_all(packed, ('c', 'x'), 0, 0)]
    all_gather x0 -> x1, blocking collectives: none -> 29.2 us  [local(): mine = lax.all_gather(weight, 'z', axis=0, tiled=True)]
    ppermute x2 -> x5, starting transfers between devices: 6.59 us -> 15.1 us  [the longest x3 8.68 us: local(): output = output + lax.ppermute(near[d], 'x', shift)]
    all_to_all x3, waiting for transfers between devices: 30.5 us -> 24.6 us  [the longest x1 13.3 us: local(): packed = lax.all_to_all(packed, ('yl', 'x'), 0, 0)]
    pallas_call x2 -> x3, Pallas kernels: 6.42 us -> 11.4 us  [the longest x2 6.91 us: project(): pl.pallas_call(body, grid_spec=pltpu.PrefetchScalarGridSpec(num_scalar_pr...]
    all_to_all x3, starting transfers between devices: 22.9 us -> 27 us  [the longest x1 15.1 us: local(): lax.all_to_all(term.reshape(yh * depth, high, wide), ('yh', 'z'), 0, 0)]
    ppermute x2 -> x5, waiting for transfers between devices: 2.5 us -> 0.01 us  [the longest x3 0.01 us: local(): output = output + lax.ppermute(near[d], 'x', shift)]
    unnamed x11 -> x9, local copies, waits for them, and re-layouts: 7.23 us -> 5.26 us
  transfers between devices with their start and end apart: 5 -> 8, of which waited for: 4 -> 3; matrix products, arithmetic and copies ran while one was open for 0% -> 2% of each run, Pallas kernels for 3% -> 6%
where the time goes in v3:
time: 117 us; the launch traced here: 116 us
  starting transfers between devices  42.1 us (36%)
  blocking collectives  29.2 us (25%)
  waiting for transfers between devices  24.6 us (21%)
  Pallas kernels  12 us (10%)
  local copies, waits for them, and re-layouts  6.08 us (5%)
  other arithmetic  1.72 us (1%)
    all_gather x1, blocking collectives, local(): mine = lax.all_gather(weight, 'z', axis=0, tiled=True)  29.2 us
    all_to_all x1, starting transfers between devices, local(): lax.all_to_all(term.reshape(yh * depth, high, wide), ('yh', 'z'), 0, 0)  15.1 us
    all_to_all x1, waiting for transfers between devices, local(): packed = lax.all_to_all(packed, ('yl', 'x'), 0, 0)  13.3 us
    ppermute x3, starting transfers between devices, local(): output = output + lax.ppermute(near[d], 'x', shift)  8.68 us
    all_to_all x1, waiting for transfers between devices, local(): lax.all_to_all(spread, ('yh', 'c'), 0, 0).reshape(yh, 2, high, wide)  8 us
    pallas_call x2, Pallas kernels, project(): pl.pallas_call(body, grid_spec=pltpu.PrefetchScalarGridSpec(num_scalar_pr...  6.91 us
    all_to_all x1, starting transfers between devices, local(): packed = lax.all_to_all(packed, ('yl', 'x'), 0, 0)  5.99 us
    all_to_all x1, starting transfers between devices, local(): lax.all_to_all(spread, ('yh', 'c'), 0, 0).reshape(yh, 2, high, wide)  5.99 us
  transfers between devices with their start and end apart: 8, of which 3 were waited for; matrix products, arithmetic and copies ran while one was open for 2% of the time, Pallas kernels for 6%

profile of v3, /device:TPU:1, one launch (start us, length us, event | category | flops | bytes accessed | tf_op | source)
XLA Modules:
  0.0 116.5 jit_solution(6520562787570865303)
XLA Ops:
  0.6 1.9 %copy-done.1 = bf16[128,12288]{1,0:T(8,128)(2,1)S(1)} copy-done((bf16[128,12288]{1,0:T(8,128)(2,1)S(1)}, bf16[128,12288]{1,0:T(8,128)(2,1)}, u32[]{:S(2)}) %copy-start.1) | copy-done | bytes 3145752
  2.5 0.8 copy-done.2
  3.4 0.6 shard_map.50
  4.0 1.8 %copy-done = bf16[8,128,1792]{2,1,0:T(8,128)(2,1)} copy-done((bf16[8,128,1792]{2,1,0:T(8,128)(2,1)}, bf16[8,128,1792]{2,1,0:T(8,128)(2,1)S(1)}, u32[]{:S(2)}) %copy-start) | copy-done | bytes 3670040
  5.8 6.0 %all-to-all-start = ((bf16[8,128,1792]{2,1,0:T(8,128)(2,1)}), bf16[8,128,1792]{2,1,0:T(8,128)(2,1)}, u32[]{:S(2)}, u32[]{:S(2)}) async-start(bf16[8,128,1792]{2,1,0:T(8,128)(2,1)} %copy-done), calls=%async_computation | async-start | bytes 7340032 | tf_op jit(solution)/shard_map/all_to_all | solution.py:118
  11.9 29.2 %all_gather.3.w_ref = bf16[1536,256]{1,0:T(8,128)(2,1)S(1)} all-gather(bf16[192,256]{1,0:T(8,128)(2,1)S(1)} %copy-done.3), channel_id=1, replica_groups=mesh['yh'=4,'c'=2,'yl'=2,'x'=4,'z'=8] {'z'}, dimensions={0}, use_global_device_ids=true | all-gather | bytes 884736 | tf_op jit(solution)/shard_map/all_gather | solution.py:119
  41.1 13.3 %all-to-all-done.t_ref.own_ref.other_ref = bf16[8,128,1792]{2,1,0:T(8,128)(2,1)} async-done(((bf16[8,128,1792]{2,1,0:T(8,128)(2,1)}), bf16[8,128,1792]{2,1,0:T(8,128)(2,1)}, u32[]{:S(2)}, u32[]{:S(2)}) %all-to-all-start) | async-done | bytes 3670048 | tf_op jit(solution)/shard_map/all_to_all | solution.py:118
  54.4 4.4 %shard_map.53 = (f32[4,8,48,128]{3,2,1,0:T(8,128)S(1)}, f32[4,8,48,128]{3,2,1,0:T(8,128)S(1)}) custom-call(s32[3]{0:T(128)S(1)} %pad_add_fusion.spot_ref, bf16[8,128,1792]{2,1,0:T(8,128)(2,1)} %all-to-all-done.t_ref.own_ref.other_ref, bf16[8,128,1792]{2,1,0:T(8,128)(2,1)} %all-to-all-done.t_ref.own_ref.other_ref, ...), custom_call_target="tpu_custom_call" | custom-call | tf_op jit(solution)/shard_map/pallas_call | solution.py:58
  58.8 3.3 %collective-permute-start.4 = (f32[4,8,48,128]{3,2,1,0:T(8,128)S(1)}, f32[4,8,48,128]{3,2,1,0:T(8,128)S(1)}, u32[]{:S(2)}, u32[]{:S(2)}) collective-permute-start(f32[4,8,48,128]{3,2,1,0:T(8,128)S(1)} %get-tuple-element.9), channel_id=1, source_target_pairs={{0,64},{64,0},{1,65},{65,1},{2,66},{66,2},{3,67},{67,3},{4,68},{68... | collective-permute-start | bytes 2359304 | tf_op jit(solution)/shard_map/ppermute | solution.py:124
  62.1 3.5 %shard_map.52 = f32[4,128,256]{2,1,0:T(8,128)S(1)} custom-call(s32[3]{0:T(128)S(1)} %pad_add_fusion.spot_ref, bf16[8,128,1792]{2,1,0:T(8,128)(2,1)} %all-to-all-done.t_ref.own_ref.other_ref, bf16[1536,256]{1,0:T(8,128)(2,1)S(1)} %all_gather.3.w_ref), custom_call_target="tpu_custom_call" | custom-call | tf_op jit(solution)/shard_map/pallas_call | solution.py:92
  65.6 3.1 %collective-permute-start = (f32[4,128,256]{2,1,0:T(8,128)S(1)}, f32[4,128,256]{2,1,0:T(8,128)S(1)}, u32[]{:S(2)}, u32[]{:S(2)}) collective-permute-start(f32[4,128,256]{2,1,0:T(8,128)S(1)} %shard_map.52), channel_id=1, source_target_pairs={{0,32},{32,0},{1,33},{33,1},{2,34},{34,2},{3,35},{35,3},{4,36},{36... | collective-permute-start | bytes 1572872 | tf_op jit(solution)/shard_map/ppermute | solution.py:130
  68.7 0.8 add_convert_fusion
  69.6 15.1 %all-to-all-start.1 = ((bf16[32,48,128]{2,1,0:T(8,128)(2,1)}), bf16[32,48,128]{2,1,0:T(8,128)(2,1)S(1)}, u32[]{:S(2)}, u32[]{:S(2)}) async-start(bf16[32,48,128]{2,1,0:T(8,128)(2,1)} %bitcast.7), calls=%async_computation.1 | async-start | bytes 786432 | tf_op jit(solution)/shard_map/all_to_all | solution.py:125
  84.6 3.5 %shard_map.51 = f32[4,128,256]{2,1,0:T(8,128)S(1)} custom-call(s32[3]{0:T(128)S(1)} %pad_add_fusion.spot_ref, bf16[8,128,1792]{2,1,0:T(8,128)(2,1)} %all-to-all-done.t_ref.own_ref.other_ref, bf16[1536,256]{1,0:T(8,128)(2,1)S(1)} %all_gather.3.w_ref), custom_call_target="tpu_custom_call" | custom-call | tf_op jit(solution)/shard_map/pallas_call | solution.py:92
  88.2 2.5 %collective-permute-start.1 = (f32[128,256]{1,0:T(8,128)S(1)}, f32[128,256]{1,0:T(8,128)S(1)}, u32[]{:S(2)}, u32[]{:S(2)}) collective-permute-start(f32[128,256]{1,0:T(8,128)S(1)} %get-tuple-element.10), channel_id=1, source_target_pairs={{0,8},{8,16},{16,24},{24,0},{1,9},{9,17},{17,25},{25,1},{2,10},{10... | collective-permute-start | bytes 393224 | tf_op jit(solution)/shard_map/ppermute | solution.py:134
  90.7 3.7 %collective-permute-start.2 = (f32[128,256]{1,0:T(8,128)S(1)}, f32[128,256]{1,0:T(8,128)S(1)}, u32[]{:S(2)}, u32[]{:S(2)}) collective-permute-start(f32[128,256]{1,0:T(8,128)S(1)} %get-tuple-element.12), channel_id=1, source_target_pairs={{0,16},{8,24},{16,0},{24,8},{1,17},{9,25},{17,1},{25,9},{2,18},{10... | collective-permute-start | bytes 393224 | tf_op jit(solution)/shard_map/ppermute | solution.py:134
  94.4 2.5 %collective-permute-start.3 = (f32[128,256]{1,0:T(8,128)S(1)}, f32[128,256]{1,0:T(8,128)S(1)}, u32[]{:S(2)}, u32[]{:S(2)}) collective-permute-start(f32[128,256]{1,0:T(8,128)S(1)} %get-tuple-element.11), channel_id=1, source_target_pairs={{0,24},{8,0},{16,8},{24,16},{1,25},{9,1},{17,9},{25,17},{2,26},{10... | collective-permute-start | bytes 393224 | tf_op jit(solution)/shard_map/ppermute | solution.py:134
  96.9 3.3 %all-to-all-done.1 = bf16[32,48,128]{2,1,0:T(8,128)(2,1)S(1)} async-done(((bf16[32,48,128]{2,1,0:T(8,128)(2,1)}), bf16[32,48,128]{2,1,0:T(8,128)(2,1)S(1)}, u32[]{:S(2)}, u32[]{:S(2)}) %all-to-all-start.1) | async-done | bytes 393248 | tf_op jit(solution)/shard_map/all_to_all | solution.py:125
  100.3 0.7 broadcast_in_dim.2
  101.0 6.0 %all-to-all-start.2 = ((f32[8,48,128]{2,1,0:T(8,128)}), f32[8,48,128]{2,1,0:T(8,128)S(1)}, u32[]{:S(2)}, u32[]{:S(2)}) async-start(f32[8,48,128]{2,1,0:T(8,128)} %broadcast_in_dim.2), calls=%async_computation.2 | async-start | bytes 393216 | tf_op jit(solution)/shard_map/all_to_all | solution.py:137
  107.0 0.7 fusion.3
  107.7 8.0 %all-to-all-done.2 = f32[8,48,128]{2,1,0:T(8,128)S(1)} async-done(((f32[8,48,128]{2,1,0:T(8,128)}), f32[8,48,128]{2,1,0:T(8,128)S(1)}, u32[]{:S(2)}, u32[]{:S(2)}) %all-to-all-start.2) | async-done | bytes 196640 | tf_op jit(solution)/shard_map/all_to_all | solution.py:137
  115.7 0.1 copy.5
  115.8 0.7 copy.8
  (14 shorter events, 0.3 us)
Async XLA Ops:
  0.6 1.9 %copy-start.1 = (bf16[128,12288]{1,0:T(8,128)(2,1)S(1)}, bf16[128,12288]{1,0:T(8,128)(2,1)}, u32[]{:S(2)}) copy-start(bf16[128,12288]{1,0:T(8,128)(2,1)} %t_ref.1) | copy-start | bytes 9437188
  2.5 0.8 copy-start.2
  4.0 1.9 %copy-start = (bf16[8,128,1792]{2,1,0:T(8,128)(2,1)}, bf16[8,128,1792]{2,1,0:T(8,128)(2,1)S(1)}, u32[]{:S(2)}) copy-start(bf16[8,128,1792]{2,1,0:T(8,128)(2,1)S(1)} %shard_map.50) | copy-start | bytes 11010052
  5.8 6.1 %copy-start.3 = (bf16[192,256]{1,0:T(8,128)(2,1)S(1)}, bf16[192,256]{1,0:T(8,128)(2,1)}, u32[]{:S(2)}) copy-start(bf16[192,256]{1,0:T(8,128)(2,1)} %param.4) | copy-start | bytes 294916
  5.8 48.5 %all-to-all-start = ((bf16[8,128,1792]{2,1,0:T(8,128)(2,1)}), bf16[8,128,1792]{2,1,0:T(8,128)(2,1)}, u32[]{:S(2)}, u32[]{:S(2)}) async-start(bf16[8,128,1792]{2,1,0:T(8,128)(2,1)} %copy-done), calls=%async_computation | async-start | bytes 7340032 | tf_op jit(solution)/shard_map/all_to_all | solution.py:118
  58.8 9.9 %collective-permute-start.4 = (f32[4,8,48,128]{3,2,1,0:T(8,128)S(1)}, f32[4,8,48,128]{3,2,1,0:T(8,128)S(1)}, u32[]{:S(2)}, u32[]{:S(2)}) collective-permute-start(f32[4,8,48,128]{3,2,1,0:T(8,128)S(1)} %get-tuple-element.9), channel_id=1, source_target_pairs={{0,64},{64,0},{1,65},{65,1},{2,66},{66,2},{3,67},{67,3},{4,68},{68... | collective-permute-start | bytes 2359304 | tf_op jit(solution)/shard_map/ppermute | solution.py:124
  65.6 22.5 %collective-permute-start = (f32[4,128,256]{2,1,0:T(8,128)S(1)}, f32[4,128,256]{2,1,0:T(8,128)S(1)}, u32[]{:S(2)}, u32[]{:S(2)}) collective-permute-start(f32[4,128,256]{2,1,0:T(8,128)S(1)} %shard_map.52), channel_id=1, source_target_pairs={{0,32},{32,0},{1,33},{33,1},{2,34},{34,2},{3,35},{35,3},{4,36},{36... | collective-permute-start | bytes 1572872 | tf_op jit(solution)/shard_map/ppermute | solution.py:130
  69.6 30.7 %all-to-all-start.1 = ((bf16[32,48,128]{2,1,0:T(8,128)(2,1)}), bf16[32,48,128]{2,1,0:T(8,128)(2,1)S(1)}, u32[]{:S(2)}, u32[]{:S(2)}) async-start(bf16[32,48,128]{2,1,0:T(8,128)(2,1)} %bitcast.7), calls=%async_computation.1 | async-start | bytes 786432 | tf_op jit(solution)/shard_map/all_to_all | solution.py:125
  88.2 18.8 %collective-permute-start.1 = (f32[128,256]{1,0:T(8,128)S(1)}, f32[128,256]{1,0:T(8,128)S(1)}, u32[]{:S(2)}, u32[]{:S(2)}) collective-permute-start(f32[128,256]{1,0:T(8,128)S(1)} %get-tuple-element.10), channel_id=1, source_target_pairs={{0,8},{8,16},{16,24},{24,0},{1,9},{9,17},{17,25},{25,1},{2,10},{10... | collective-permute-start | bytes 393224 | tf_op jit(solution)/shard_map/ppermute | solution.py:134
  90.7 16.3 %collective-permute-start.2 = (f32[128,256]{1,0:T(8,128)S(1)}, f32[128,256]{1,0:T(8,128)S(1)}, u32[]{:S(2)}, u32[]{:S(2)}) collective-permute-start(f32[128,256]{1,0:T(8,128)S(1)} %get-tuple-element.12), channel_id=1, source_target_pairs={{0,16},{8,24},{16,0},{24,8},{1,17},{9,25},{17,1},{25,9},{2,18},{10... | collective-permute-start | bytes 393224 | tf_op jit(solution)/shard_map/ppermute | solution.py:134
  94.4 12.6 %collective-permute-start.3 = (f32[128,256]{1,0:T(8,128)S(1)}, f32[128,256]{1,0:T(8,128)S(1)}, u32[]{:S(2)}, u32[]{:S(2)}) collective-permute-start(f32[128,256]{1,0:T(8,128)S(1)} %get-tuple-element.11), channel_id=1, source_target_pairs={{0,24},{8,0},{16,8},{24,16},{1,25},{9,1},{17,9},{25,17},{2,26},{10... | collective-permute-start | bytes 393224 | tf_op jit(solution)/shard_map/ppermute | solution.py:134
  101.0 14.7 %all-to-all-start.2 = ((f32[8,48,128]{2,1,0:T(8,128)}), f32[8,48,128]{2,1,0:T(8,128)S(1)}, u32[]{:S(2)}, u32[]{:S(2)}) async-start(f32[8,48,128]{2,1,0:T(8,128)} %broadcast_in_dim.2), calls=%async_computation.2 | async-start | bytes 393216 | tf_op jit(solution)/shard_map/all_to_all | solution.py:137

commit v4 on v3

--- a/solution.py
+++ b/solution.py
@@ -5,7 +5,9 @@
 from jax.experimental.pallas import tpu as pltpu
 from jax.sharding import Mesh, PartitionSpec as P
 
-PARAMS = pltpu.CompilerParams(vmem_limit_bytes=32 * 1024 * 1024)
+PARAMS = pltpu.CompilerParams(vmem_limit_bytes=16 * 1024 * 1024)
+ALONE = pltpu.CompilerParams(vmem_limit_bytes=60 * 1024 * 1024)
+SWAP = [(0, 1), (1, 0)]
 
 
 def pack(tokens, grad_out, sharers):
@@ -26,20 +28,19 @@
         ],
         out_specs=pl.BlockSpec((1, rows, part + cols), lambda k: (k, 0, 0)),
         out_shape=jax.ShapeDtypeStruct((sharers, rows, part + cols), tokens.dtype),
-        compiler_params=PARAMS,
+        compiler_params=ALONE,
     )(tokens, grad_out)
 
 
-def terms(packed, spot, part, depth, yh):
+def terms(packed, spot, part, depth):
     sharers, rows, both = packed.shape
     cols = both - part
-    shard = part // depth
-    high, wide = shard // yh, cols // 2
-    step = 2
+    wide = cols // 2
+    step = 2 * part // depth
     first = part // wide
 
     def body(spot_ref, t_ref, own_ref, other_ref, keep_ref, send_ref):
-        t = t_ref[...].reshape(sharers * rows, step * shard)
+        t = t_ref[...].reshape(sharers * rows, step)
         g = jnp.concatenate([own_ref[...], other_ref[...]], axis=-1)
         term = lax.dot_general(
             t,
@@ -47,23 +48,18 @@
             (((0,), (0,)), ((), ())),
             preferred_element_type=jnp.float32,
         )
-        for z in range(step):
-            for i in range(yh):
-                at = z * shard + i * high
-                keep_ref[i, z] = term[at : at + high, :wide]
-                send_ref[i, z] = term[at : at + high, wide:]
+        keep_ref[...] = term[:, :wide]
+        send_ref[...] = term[:, wide:]
 
-    half = jax.ShapeDtypeStruct((yh, depth, high, wide), jnp.float32)
-    half_spec = pl.BlockSpec((yh, step, high, wide), lambda k, spot: (0, k, 0, 0))
+    half = jax.ShapeDtypeStruct((part, wide), jnp.float32)
+    half_spec = pl.BlockSpec((step, wide), lambda k, spot: (k, 0))
     return pl.pallas_call(
         body,
         grid_spec=pltpu.PrefetchScalarGridSpec(
             num_scalar_prefetch=1,
-            grid=(depth // step,),
+            grid=(part // step,),
             in_specs=[
-                pl.BlockSpec(
-                    (sharers, rows, step * shard), lambda k, spot: (0, 0, k)
-                ),
+                pl.BlockSpec((sharers, rows, step), lambda k, spot: (0, 0, k)),
                 pl.BlockSpec(
                     (sharers, rows, wide), lambda k, spot: (0, 0, first + spot[0])
                 ),
@@ -119,24 +115,29 @@
     mine = lax.all_gather(weight, "z", axis=0, tiled=True)
     packed, mine = lax.optimization_barrier((packed, mine))
 
-    keep, send = terms(packed, spot, part, depth, yh)
-    high, wide = keep.shape[-2:]
-    term = (keep + lax.ppermute(send, "c", [(0, 1), (1, 0)])).astype(jnp.bfloat16)
-    term = lax.all_to_all(term.reshape(yh * depth, high, wide), ("yh", "z"), 0, 0)
+    keep, send = terms(packed, spot, part, depth)
+    term = (keep + lax.ppermute(send, "c", SWAP)).astype(jnp.bfloat16)
+    away = project(packed, mine, spot, True, width)
+    away, _ = lax.optimization_barrier((away, term))
+    away = lax.ppermute(away, "yl", SWAP)
+    term = lax.all_to_all(term.reshape(depth, shard, cols // 2), "z", 0, 0)
     summed = jnp.sum(term, axis=0, dtype=jnp.float32)
 
-    away = project(packed, mine, spot, True, width)
-    near = project(packed, mine, spot, False, width)
-    near = near + lax.ppermute(away, "yl", [(0, 1), (1, 0)])
+    near = project(packed, mine, spot, False, width) + away
+    near, _ = lax.optimization_barrier((near, summed))
     output = near[0]
     for d in range(1, width):
         shift = [(i, (i + d) % width) for i in range(width)]
         output = output + lax.ppermute(near[d], "x", shift)
 
-    spread = jnp.broadcast_to(summed[None], (yh * 2, high, wide))
-    spread = lax.all_to_all(spread, ("yh", "c"), 0, 0).reshape(yh, 2, high, wide)
-    spread = spread.transpose(0, 2, 1, 3).reshape(shard, cols)
-    return output.astype(jnp.bfloat16), spread
+    lines = jnp.broadcast_to(summed[None], (yh, shard, cols // 2))
+    half = jnp.sum(lax.all_to_all(lines, "yh", 0, 0), axis=0)
+    other = lax.ppermute(half, "c", SWAP)
+    first = spot[0] == 0
+    weight_grad = jnp.concatenate(
+        [jnp.where(first, half, other), jnp.where(first, other, half)], axis=1
+    )
+    return output.astype(jnp.bfloat16), weight_grad
 
 
 def solution(mesh):

time: 117 us -> 118 us (level); the launches traced: 116 us -> 116 us
  Pallas kernels: 12 us -> 17.5 us
  local copies, waits for them, and re-layouts: 6.08 us -> 0.81 us
    pallas_call x1, Pallas kernels: 0.61 us -> 6.25 us  [pack(): pl.pallas_call(body, grid=(sharers,), in_specs=[pl.BlockSpec((rows, part)...]
    unnamed x9 -> x2, local copies, waits for them, and re-layouts: 5.26 us -> 0.01 us
    all_to_all x2, starting transfers between devices: 21.1 us -> 16.2 us  [the longest x1 10 us: local(): term = lax.all_to_all(term.reshape(depth, shard, cols // 2), 'z', 0, 0)]
    ppermute x2 -> x3, starting transfers between devices: 6.42 us -> 9.93 us  [the longest x1 3.52 us: local(): other = lax.ppermute(half, 'c', SWAP)]
    all_to_all x2, waiting for transfers between devices: 11.3 us -> 8.59 us  [the longest x1 8.59 us: local(): term = lax.all_to_all(term.reshape(depth, shard, cols // 2), 'z', 0, 0)]
    ppermute x2 -> x3, waiting for transfers between devices: 0.01 us -> 2.12 us  [the longest x1 1.89 us: local(): term = (keep + lax.ppermute(send, 'c', SWAP)).astype(jnp.bfloat16)]
  transfers between devices with their start and end apart: 8 -> 9, of which waited for: 3 -> 4; matrix products, arithmetic and copies ran while one was open for 2% -> 1% of each run, Pallas kernels for 6% -> 6%
where the time goes in v4:
time: 118 us; the launch traced here: 116 us
  starting transfers between devices  41.5 us (35%)
  blocking collectives  29.2 us (25%)
  waiting for transfers between devices  24 us (20%)
  Pallas kernels  17.5 us (15%)
  other arithmetic  2.42 us (2%)
    all_gather x1, blocking collectives, local(): mine = lax.all_gather(weight, 'z', axis=0, tiled=True)  29.2 us
    all_to_all x1, waiting for transfers between devices, local(): packed = lax.all_to_all(packed, ('yl', 'x'), 0, 0)  13.3 us
    all_to_all x1, starting transfers between devices, local(): term = lax.all_to_all(term.reshape(depth, shard, cols // 2), 'z', 0, 0)  10 us
    ppermute x3, starting transfers between devices, local(): output = output + lax.ppermute(near[d], 'x', shift)  9.38 us
    all_to_all x1, waiting for transfers between devices, local(): term = lax.all_to_all(term.reshape(depth, shard, cols // 2), 'z', 0, 0)  8.59 us
    pallas_call x2, Pallas kernels, project(): pl.pallas_call(body, grid_spec=pltpu.PrefetchScalarGridSpec(num_scalar_pr...  6.91 us
    pallas_call x1, Pallas kernels, pack(): pl.pallas_call(body, grid=(sharers,), in_specs=[pl.BlockSpec((rows, part)...  6.25 us
    all_to_all x1, starting transfers between devices, local(): half = jnp.sum(lax.all_to_all(lines, 'yh', 0, 0), axis=0)  6.16 us
  transfers between devices with their start and end apart: 9, of which 4 were waited for; matrix products, arithmetic and copies ran while one was open for 1% of the time, Pallas kernels for 6%

profile of v4, /device:TPU:1, one launch (start us, length us, event | category | flops | bytes accessed | tf_op | source)
XLA Modules:
  0.0 116.2 jit_solution(18275668363496032338)
XLA Ops:
  0.6 6.3 %shard_map.50 = bf16[8,128,1792]{2,1,0:T(8,128)(2,1)} custom-call(bf16[128,12288]{1,0:T(8,128)(2,1)} %t_ref.1, bf16[128,256]{1,0:T(8,128)(2,1)} %g_ref.1), custom_call_target="tpu_custom_call" | custom-call | tf_op jit(solution)/shard_map/pallas_call | solution.py:22
  6.9 6.0 %all-to-all-start = ((bf16[8,128,1792]{2,1,0:T(8,128)(2,1)}), bf16[8,128,1792]{2,1,0:T(8,128)(2,1)}, u32[]{:S(2)}, u32[]{:S(2)}) async-start(bf16[8,128,1792]{2,1,0:T(8,128)(2,1)} %shard_map.50), calls=%async_computation | async-start | bytes 7340032 | tf_op jit(solution)/shard_map/all_to_all | solution.py:114
  12.9 0.1 pad_add_fusion.spot_ref
  13.0 29.2 %all_gather.3.w_ref = bf16[1536,256]{1,0:T(8,128)(2,1)S(1)} all-gather(bf16[192,256]{1,0:T(8,128)(2,1)S(1)} %copy-done), channel_id=1, replica_groups=mesh['yh'=4,'c'=2,'yl'=2,'x'=4,'z'=8] {'z'}, dimensions={0}, use_global_device_ids=true | all-gather | bytes 884736 | tf_op jit(solution)/shard_map/all_gather | solution.py:115
  42.1 13.3 %all-to-all-done.t_ref.own_ref.other_ref = bf16[8,128,1792]{2,1,0:T(8,128)(2,1)} async-done(((bf16[8,128,1792]{2,1,0:T(8,128)(2,1)}), bf16[8,128,1792]{2,1,0:T(8,128)(2,1)}, u32[]{:S(2)}, u32[]{:S(2)}) %all-to-all-start) | async-done | bytes 3670048 | tf_op jit(solution)/shard_map/all_to_all | solution.py:114
  55.4 4.4 %shard_map.53 = (f32[1536,128]{1,0:T(8,128)S(1)}, f32[1536,128]{1,0:T(8,128)S(1)}) custom-call(s32[3]{0:T(128)S(1)} %pad_add_fusion.spot_ref, bf16[8,128,1792]{2,1,0:T(8,128)(2,1)} %all-to-all-done.t_ref.own_ref.other_ref, bf16[8,128,1792]{2,1,0:T(8,128)(2,1)} %all-to-all-done.t_ref.own_ref.other_ref, bf16[8,128,1792]{2,1,0:T(8,128)(2,1)} %all-to-all-done.t_ref.own_ref.other_ref), custom_call_target="tpu_custom_call" | custom-call | tf_op jit(solution)/shard_map/pallas_call | solution.py:56
  59.8 3.3 %collective-permute-start = (f32[1536,128]{1,0:T(8,128)S(1)}, f32[1536,128]{1,0:T(8,128)S(1)}, u32[]{:S(2)}, u32[]{:S(2)}) collective-permute-start(f32[1536,128]{1,0:T(8,128)S(1)} %get-tuple-element.11), channel_id=1, source_target_pairs={{0,64},{64,0},{1,65},{65,1},{2,66},{66,2},{3,67},{67,3},{4,68},{68... | collective-permute-start | bytes 2359304 | tf_op jit(solution)/shard_map/ppermute | solution.py:119
  63.1 1.9 %collective-permute-done = f32[1536,128]{1,0:T(8,128)S(1)} collective-permute-done((f32[1536,128]{1,0:T(8,128)S(1)}, f32[1536,128]{1,0:T(8,128)S(1)}, u32[]{:S(2)}, u32[]{:S(2)}) %collective-permute-start) | collective-permute-done | bytes 786464 | tf_op jit(solution)/shard_map/ppermute | solution.py:119
  65.0 0.8 add_convert_fusion
  65.8 10.0 %all-to-all-start.1 = ((bf16[8,192,128]{2,1,0:T(8,128)(2,1)}), bf16[8,192,128]{2,1,0:T(8,128)(2,1)S(1)}, u32[]{:S(2)}, u32[]{:S(2)}) async-start(bf16[8,192,128]{2,1,0:T(8,128)(2,1)} %bitcast.3), calls=%async_computation.1 | async-start | bytes 786432 | tf_op jit(solution)/shard_map/all_to_all | solution.py:123
  75.9 3.5 %shard_map.52 = f32[4,128,256]{2,1,0:T(8,128)S(1)} custom-call(s32[3]{0:T(128)S(1)} %pad_add_fusion.spot_ref, bf16[8,128,1792]{2,1,0:T(8,128)(2,1)} %all-to-all-done.t_ref.own_ref.other_ref, bf16[1536,256]{1,0:T(8,128)(2,1)S(1)} %all_gather.3.w_ref), custom_call_target="tpu_custom_call" | custom-call | tf_op jit(solution)/shard_map/pallas_call | solution.py:88
  79.3 3.1 %collective-permute-start.1 = (f32[4,128,256]{2,1,0:T(8,128)S(1)}, f32[4,128,256]{2,1,0:T(8,128)S(1)}, u32[]{:S(2)}, u32[]{:S(2)}) collective-permute-start(f32[4,128,256]{2,1,0:T(8,128)S(1)} %shard_map.52), channel_id=1, source_target_pairs={{0,32},{32,0},{1,33},{33,1},{2,34},{34,2},{3,35},{35,3},{4,36},{36... | collective-permute-start | bytes 1572872 | tf_op jit(solution)/shard_map/ppermute | solution.py:122
  82.4 8.6 %all-to-all-done.1 = bf16[8,192,128]{2,1,0:T(8,128)(2,1)S(1)} async-done(((bf16[8,192,128]{2,1,0:T(8,128)(2,1)}), bf16[8,192,128]{2,1,0:T(8,128)(2,1)S(1)}, u32[]{:S(2)}, u32[]{:S(2)}) %all-to-all-start.1) | async-done | bytes 393248 | tf_op jit(solution)/shard_map/all_to_all | solution.py:123
  91.1 0.8 broadcast_in_dim.2
  91.8 6.2 %all-to-all-start.2 = ((f32[4,192,128]{2,1,0:T(8,128)}), f32[4,192,128]{2,1,0:T(8,128)S(1)}, u32[]{:S(2)}, u32[]{:S(2)}) async-start(f32[4,192,128]{2,1,0:T(8,128)} %broadcast_in_dim.2), calls=%async_computation.2 | async-start | bytes 786432 | tf_op jit(solution)/shard_map/all_to_all | solution.py:134
  98.0 3.5 %shard_map.51 = f32[4,128,256]{2,1,0:T(8,128)S(1)} custom-call(s32[3]{0:T(128)S(1)} %pad_add_fusion.spot_ref, bf16[8,128,1792]{2,1,0:T(8,128)(2,1)} %all-to-all-done.t_ref.own_ref.other_ref, bf16[1536,256]{1,0:T(8,128)(2,1)S(1)} %all_gather.3.w_ref), custom_call_target="tpu_custom_call" | custom-call | tf_op jit(solution)/shard_map/pallas_call | solution.py:88
  101.5 0.1 add.16
  101.6 2.5 %collective-permute-start.2 = (f32[128,256]{1,0:T(8,128)S(1)}, f32[128,256]{1,0:T(8,128)S(1)}, u32[]{:S(2)}, u32[]{:S(2)}) collective-permute-start(f32[128,256]{1,0:T(8,128)S(1)} %get-tuple-element.14), channel_id=1, source_target_pairs={{0,8},{8,16},{16,24},{24,0},{1,9},{9,17},{17,25},{25,1},{2,10},{10... | collective-permute-start | bytes 393224 | tf_op jit(solution)/shard_map/ppermute | solution.py:131
  104.1 4.1 %collective-permute-start.3 = (f32[128,256]{1,0:T(8,128)S(1)}, f32[128,256]{1,0:T(8,128)S(1)}, u32[]{:S(2)}, u32[]{:S(2)}) collective-permute-start(f32[128,256]{1,0:T(8,128)S(1)} %get-tuple-element.16), channel_id=1, source_target_pairs={{0,16},{8,24},{16,0},{24,8},{1,17},{9,25},{17,1},{25,9},{2,18},{10... | collective-permute-start | bytes 393224 | tf_op jit(solution)/shard_map/ppermute | solution.py:131
  108.2 2.8 %collective-permute-start.4 = (f32[128,256]{1,0:T(8,128)S(1)}, f32[128,256]{1,0:T(8,128)S(1)}, u32[]{:S(2)}, u32[]{:S(2)}) collective-permute-start(f32[128,256]{1,0:T(8,128)S(1)} %get-tuple-element.15), channel_id=1, source_target_pairs={{0,24},{8,0},{16,8},{24,16},{1,25},{9,1},{17,9},{25,17},{2,26},{10... | collective-permute-start | bytes 393224 | tf_op jit(solution)/shard_map/ppermute | solution.py:131
  111.0 3.5 %collective-permute-start.5 = (f32[192,128]{1,0:T(8,128)S(1)}, f32[192,128]{1,0:T(8,128)S(1)}, u32[]{:S(2)}, u32[]{:S(2)}) collective-permute-start(f32[192,128]{1,0:T(8,128)S(1)} %reduce_sum.19), channel_id=1, source_target_pairs={{0,64},{64,0},{1,65},{65,1},{2,66},{66,2},{3,67},{67,3},{4,68},{68... | collective-permute-start | bytes 294920 | tf_op jit(solution)/shard_map/ppermute | solution.py:135
  114.6 0.7 fusion.2
  115.3 0.2 collective-permute-done.5
  115.5 0.7 pad_maximum_fusion
  (11 shorter events, 0.1 us)
Async XLA Ops:
  6.9 6.1 %copy-start = (bf16[192,256]{1,0:T(8,128)(2,1)S(1)}, bf16[192,256]{1,0:T(8,128)(2,1)}, u32[]{:S(2)}) copy-start(bf16[192,256]{1,0:T(8,128)(2,1)} %param.4) | copy-start | bytes 294916
  6.9 48.5 %all-to-all-start = ((bf16[8,128,1792]{2,1,0:T(8,128)(2,1)}), bf16[8,128,1792]{2,1,0:T(8,128)(2,1)}, u32[]{:S(2)}, u32[]{:S(2)}) async-start(bf16[8,128,1792]{2,1,0:T(8,128)(2,1)} %shard_map.50), calls=%async_computation | async-start | bytes 7340032 | tf_op jit(solution)/shard_map/all_to_all | solution.py:114
  59.8 5.2 %collective-permute-start = (f32[1536,128]{1,0:T(8,128)S(1)}, f32[1536,128]{1,0:T(8,128)S(1)}, u32[]{:S(2)}, u32[]{:S(2)}) collective-permute-start(f32[1536,128]{1,0:T(8,128)S(1)} %get-tuple-element.11), channel_id=1, source_target_pairs={{0,64},{64,0},{1,65},{65,1},{2,66},{66,2},{3,67},{67,3},{4,68},{68... | collective-permute-start | bytes 2359304 | tf_op jit(solution)/shard_map/ppermute | solution.py:119
  65.8 25.2 %all-to-all-start.1 = ((bf16[8,192,128]{2,1,0:T(8,128)(2,1)}), bf16[8,192,128]{2,1,0:T(8,128)(2,1)S(1)}, u32[]{:S(2)}, u32[]{:S(2)}) async-start(bf16[8,192,128]{2,1,0:T(8,128)(2,1)} %bitcast.3), calls=%async_computation.1 | async-start | bytes 786432 | tf_op jit(solution)/shard_map/all_to_all | solution.py:123
  79.3 22.1 %collective-permute-start.1 = (f32[4,128,256]{2,1,0:T(8,128)S(1)}, f32[4,128,256]{2,1,0:T(8,128)S(1)}, u32[]{:S(2)}, u32[]{:S(2)}) collective-permute-start(f32[4,128,256]{2,1,0:T(8,128)S(1)} %shard_map.52), channel_id=1, source_target_pairs={{0,32},{32,0},{1,33},{33,1},{2,34},{34,2},{3,35},{35,3},{4,36},{36... | collective-permute-start | bytes 1572872 | tf_op jit(solution)/shard_map/ppermute | solution.py:122
  91.8 19.2 %all-to-all-start.2 = ((f32[4,192,128]{2,1,0:T(8,128)}), f32[4,192,128]{2,1,0:T(8,128)S(1)}, u32[]{:S(2)}, u32[]{:S(2)}) async-start(f32[4,192,128]{2,1,0:T(8,128)} %broadcast_in_dim.2), calls=%async_computation.2 | async-start | bytes 786432 | tf_op jit(solution)/shard_map/all_to_all | solution.py:134
  101.6 13.0 %collective-permute-start.2 = (f32[128,256]{1,0:T(8,128)S(1)}, f32[128,256]{1,0:T(8,128)S(1)}, u32[]{:S(2)}, u32[]{:S(2)}) collective-permute-start(f32[128,256]{1,0:T(8,128)S(1)} %get-tuple-element.14), channel_id=1, source_target_pairs={{0,8},{8,16},{16,24},{24,0},{1,9},{9,17},{17,25},{25,1},{2,10},{10... | collective-permute-start | bytes 393224 | tf_op jit(solution)/shard_map/ppermute | solution.py:131
  104.1 10.5 %collective-permute-start.3 = (f32[128,256]{1,0:T(8,128)S(1)}, f32[128,256]{1,0:T(8,128)S(1)}, u32[]{:S(2)}, u32[]{:S(2)}) collective-permute-start(f32[128,256]{1,0:T(8,128)S(1)} %get-tuple-element.16), channel_id=1, source_target_pairs={{0,16},{8,24},{16,0},{24,8},{1,17},{9,25},{17,1},{25,9},{2,18},{10... | collective-permute-start | bytes 393224 | tf_op jit(solution)/shard_map/ppermute | solution.py:131
  108.2 6.4 %collective-permute-start.4 = (f32[128,256]{1,0:T(8,128)S(1)}, f32[128,256]{1,0:T(8,128)S(1)}, u32[]{:S(2)}, u32[]{:S(2)}) collective-permute-start(f32[128,256]{1,0:T(8,128)S(1)} %get-tuple-element.15), channel_id=1, source_target_pairs={{0,24},{8,0},{16,8},{24,16},{1,25},{9,1},{17,9},{25,17},{2,26},{10... | collective-permute-start | bytes 393224 | tf_op jit(solution)/shard_map/ppermute | solution.py:131
  111.0 4.5 %collective-permute-start.5 = (f32[192,128]{1,0:T(8,128)S(1)}, f32[192,128]{1,0:T(8,128)S(1)}, u32[]{:S(2)}, u32[]{:S(2)}) collective-permute-start(f32[192,128]{1,0:T(8,128)S(1)} %reduce_sum.19), channel_id=1, source_target_pairs={{0,64},{64,0},{1,65},{65,1},{2,66},{66,2},{3,67},{67,3},{4,68},{68... | collective-permute-start | bytes 294920 | tf_op jit(solution)/shard_map/ppermute | solution.py:135

commit v5 on v4

v5 whole, which is shorter than its diff:
```python
import jax
import jax.numpy as jnp
from jax import lax
from jax.experimental import pallas as pl
from jax.experimental.pallas import tpu as pltpu
from jax.sharding import Mesh, PartitionSpec as P

PARAMS = pltpu.CompilerParams(vmem_limit_bytes=16 * 1024 * 1024)
SWAP = [(0, 1), (1, 0)]


def pack(tokens, grad_out, spot, part):
    rows, width = tokens.shape
    cols = grad_out.shape[1]
    kind = tokens.dtype

    def body(spot_ref, t_ref, g_ref, a_ref, b0_ref, b1_ref, b2_ref, b3_ref, sems):
        copies = []
        for flip, b_ref in enumerate((b0_ref, b1_ref, b2_ref, b3_ref)):
            yl, xl = flip // 2, flip % 2
            ours = (yl * 4 + xl) * part
            theirs = ((spot_ref[1] ^ yl) * 4 + 2 + (spot_ref[2] ^ xl)) * part
            theirs = pl.multiple_of(theirs, 128)
            for source, target in (
                (t_ref.at[:, pl.ds(ours, part)], a_ref.at[flip, :, pl.ds(0, part)]),
                (g_ref, a_ref.at[flip, :, pl.ds(part, cols)]),
                (t_ref.at[:, pl.ds(theirs, part)], b_ref.at[0, :, pl.ds(0, part)]),
                (g_ref, b_ref.at[0, :, pl.ds(part, cols)]),
            ):
                copy = pltpu.make_async_copy(source, target, sems.at[len(copies)])
                copy.start()
                copies.append(copy)
        for copy in copies:
            copy.wait()

    one = jax.ShapeDtypeStruct((1, rows, part + cols), kind)
    return pl.pallas_call(
        body,
        in_specs=[
            pl.BlockSpec(memory_space=pltpu.SMEM),
            pl.BlockSpec(memory_space=pl.ANY),
            pl.BlockSpec(memory_space=pl.ANY),
        ],
        out_specs=[pl.BlockSpec(memory_space=pl.ANY)] * 5,
        out_shape=[jax.ShapeDtypeStruct((4, rows, part + cols), kind)] + [one] * 4,
        scratch_shapes=[pltpu.SemaphoreType.DMA((16,))],
        compiler_params=pltpu.CompilerParams(vmem_limit_bytes=56 * 1024 * 1024),
    )(spot, tokens, grad_out)


def terms(packed, spot, part):
    rows, both = packed[0].shape[1:]
    cols = both - part
    wide = cols // 2
    step = part // 4
    count = len(packed)

    def body(spot_ref, *refs):
        t = [r[...].reshape(-1, step) for r in refs[:count]]
        g = [r[...].reshape(-1, cols) for r in refs[count : 2 * count]]
        t = jnp.concatenate(t, axis=0) if count > 1 else t[0]
        g = jnp.concatenate(g, axis=0) if count > 1 else g[0]
        left, right = g[:, :wide], g[:, wide:]
        first = spot_ref[0] == 0
        g = jnp.concatenate(
            [jnp.where(first, left, right), jnp.where(first, right, left)], axis=1
        )
        term = lax.dot_general(
            t, g, (((0,), (0,)), ((), ())), preferred_element_type=jnp.float32
        )
        keep_ref, send_ref = refs[2 * count :]
        keep_ref[...] = term[:, :wide]
        send_ref[...] = term[:, wide:]

    half = jax.ShapeDtypeStruct((part, wide), jnp.float32)
    half_spec = pl.BlockSpec((step, wide), lambda k, spot: (k, 0))
    return pl.pallas_call(
        body,
        grid_spec=pltpu.PrefetchScalarGridSpec(
            num_scalar_prefetch=1,
            grid=(part // step,),
            in_specs=[
                pl.BlockSpec((len(p), rows, step), lambda k, spot: (0, 0, k))
                for p in packed
            ]
            + [
                pl.BlockSpec((len(p), rows, cols), lambda k, spot: (0, 0, part // cols))
                for p in packed
            ],
            out_specs=[half_spec, half_spec],
        ),
        out_shape=[half, half],
        compiler_params=PARAMS,
    )(spot, *packed, *packed)


def project(packed, weight, spot, part, at):
    rows, cols = packed[0].shape[1], weight.shape[1]
    steps = 3
    step = part // steps
    count = len(packed)

    def body(spot_ref, *refs):
        w_ref, near_ref, away_ref = refs[count:]
        if count == 1:
            own = spot_ref[1] * 2 + spot_ref[2]
            t = [refs[0][own ^ flip] for flip in range(4)]
        else:
            t = [r[0] for r in refs[:count]]
        new = jnp.dot(
            jnp.concatenate(t, axis=0), w_ref[...], preferred_element_type=jnp.float32
        ).reshape(4, rows, cols)
        k = pl.program_id(0)

        @pl.when(k == 0)
        def _():
            near_ref[...] = new[:2]
            away_ref[...] = new[2:]

        @pl.when(k > 0)
        def _():
            near_ref[...] += new[:2]
            away_ref[...] += new[2:]

    half = jax.ShapeDtypeStruct((2, rows, cols), jnp.float32)
    half_spec = pl.BlockSpec((2, rows, cols), lambda k, spot: (0, 0, 0))
    return pl.pallas_call(
        body,
        grid_spec=pltpu.PrefetchScalarGridSpec(
            num_scalar_prefetch=1,
            grid=(steps,),
            in_specs=[
                pl.BlockSpec((len(p), rows, step), lambda k, spot: (0, 0, k))
                for p in packed
            ]
            + [pl.BlockSpec((step, cols), lambda k, spot: (at * steps + k, 0))],
            out_specs=[half_spec, half_spec],
        ),
        out_shape=[half, half],
        compiler_params=PARAMS,
    )(spot, *packed, weight)


def flips(mesh_shape):
    lines, width = mesh_shape

    def partner(i, n):
        return (i + 1) % n if i % 2 else (i - 1) % n

    flip_x = [(x, partner(x, width)) for x in range(width)]
    flip_y = [(y, partner(y, lines)) for y in range(lines)]
    flip_both = [
        (y * width + x, partner(y, lines) * width + partner(x, width))
        for y in range(lines)
        for x in range(width)
    ]
    return flip_x, flip_y, flip_both


def local(tokens, weight, grad_out):
    rows, model = tokens.shape
    shard, cols = weight.shape
    depth, yh = lax.axis_size("z"), lax.axis_size("yh")
    xs, ys = ("xh", "xl"), ("yh", "yl")
    part = shard * depth
    spot = jnp.stack([lax.axis_index(name) for name in ("c", "yl", "xl")])
    spot = spot.astype(jnp.int32)
    flip_x, flip_y, flip_both = flips((lax.axis_size(ys), lax.axis_size(xs)))

    packed, b0, b1, b2, b3 = pack(tokens, grad_out, spot, part)
    packed = lax.all_to_all(packed, ("yl", "xl"), 0, 0)
    b1 = lax.ppermute(b1, xs, flip_x)
    b2 = lax.ppermute(b2, ys, flip_y)
    b3 = lax.ppermute(b3, ys + xs, flip_both)
    mine = lax.all_gather(weight, ("xh", "z"), axis=0, tiled=True)

    halves = []
    for blocks in ([packed], [b0, b1, b2, b3]):
        keep, send = terms(blocks, spot, part)
        halves.append((keep + lax.ppermute(send, "c", SWAP)).astype(jnp.bfloat16))
    term = jnp.stack(halves).reshape(2 * depth, shard, cols // 2)
    term, mine = lax.optimization_barrier((term, mine))

    near_a, away_a = project([packed], mine, spot, part, 0)
    near_b, away_b = project([b0, b1, b2, b3], mine, spot, part, 1)
    away_a, away_b, _ = lax.optimization_barrier((away_a, away_b, term))
    near_a = near_a + lax.ppermute(away_a, "yl", SWAP)
    near_b = near_b + lax.ppermute(away_b, ys, flip_y)
    output = near_a[0] + near_b[0] + lax.ppermute(near_a[1], "xl", SWAP)
    output = output + lax.ppermute(near_b[1], xs, flip_x)

    term = lax.all_to_all(term, ("xh", "z"), 0, 0)
    summed = jnp.sum(term, axis=0, dtype=jnp.float32)
    lines = jnp.broadcast_to(summed[None], (yh, shard, cols // 2))
    half = jnp.sum(lax.all_to_all(lines, "yh", 0, 0), axis=0)
    other = lax.ppermute(half, "c", SWAP)
    first = spot[0] == 0
    weight_grad = jnp.concatenate(
        [jnp.where(first, half, other), jnp.where(first, other, half)], axis=1
    )
    return output.astype(jnp.bfloat16), weight_grad


def solution(mesh):
    inner = Mesh(
        mesh.devices.reshape(4, 2, 2, 2, 2, 8), ("yh", "c", "yl", "xh", "xl", "z")
    )
    rows = P(("yh", "c", "yl", "xh", "xl", "z"), None)
    owners = P(("yl", "xh", "xl", "z"), None)
    return jax.shard_map(
        local,
        mesh=inner,
        in_specs=(rows, owners, rows),
        out_specs=(rows, owners),
        check_vma=False,
    )
```

time: 118 us -> 279 us (2.36)
  Pallas kernels: 17.5 us -> 123 us
  waiting for transfers between devices: 24 us -> 71.7 us
  blocking collectives: 29.2 us -> 0 us
  starting transfers between devices: 41.5 us -> 57.6 us
  between operations: 0.78 us -> 14.3 us
  local copies, waits for them, and re-layouts: 0.81 us -> 5.6 us
  other arithmetic: 2.42 us -> 5.6 us
    pallas_call x1, Pallas kernels: 6.25 us -> 113 us  [pack(): pl.pallas_call(body, in_specs=[pl.BlockSpec(memory_space=pltpu.SMEM), pl....]
    all_gather x0 -> x1, waiting for transfers between devices: none -> 47.8 us  [local(): mine = lax.all_gather(weight, ('xh', 'z'), axis=0, tiled=True)]
    all_gather x1 -> x0, blocking collectives: 29.2 us -> none  [local(): mine = lax.all_gather(weight, 'z', axis=0, tiled=True)]
    all_to_all x2, waiting for transfers between devices: 21.9 us -> 0.01 us  [the longest x1 0.01 us: local(): packed = lax.all_to_all(packed, ('yl', 'xl'), 0, 0)]
    ppermute x5 -> x9, waiting for transfers between devices: 1.9 us -> 20.8 us  [the longest x1 10.7 us: local(): b3 = lax.ppermute(b3, ys + xs, flip_both)]
    ppermute x5 -> x9, starting transfers between devices: 15.8 us -> 33.3 us  [the longest x2 6.72 us: local(): halves.append((keep + lax.ppermute(send, 'c', SWAP)).astype(jnp.bfloat16))]
    all_to_all x2, starting transfers between devices: 16 us -> 9.46 us  [the longest x1 4.99 us: local(): term = lax.all_to_all(term, ('xh', 'z'), 0, 0)]
    ppermute x1, starting transfers between devices: 3.52 us -> 8.45 us  [local(): other = lax.ppermute(half, 'c', SWAP)]
  transfers between devices with their start and end apart: 9 -> 14, of which waited for: 4 -> 7; matrix products, arithmetic and copies ran while one was open for 1% -> 2% of each run, Pallas kernels for 6% -> 4%
where the time goes in v5:
time: 279 us; the launch traced here: 278 us
  Pallas kernels  123 us (44%)
  waiting for transfers between devices  71.7 us (26%)
  starting transfers between devices  57.6 us (21%)
  between operations  14.3 us (5%)
  other arithmetic  5.6 us (2%)
  local copies, waits for them, and re-layouts  5.6 us (2%)
    pallas_call x1, Pallas kernels, pack(): pl.pallas_call(body, in_specs=[pl.BlockSpec(memory_space=pltpu.SMEM), pl....  113 us
    all_gather x1, waiting for transfers between devices, local(): mine = lax.all_gather(weight, ('xh', 'z'), axis=0, tiled=True)  47.8 us
    ppermute x1, waiting for transfers between devices, local(): b3 = lax.ppermute(b3, ys + xs, flip_both)  10.7 us
    ppermute x1, starting transfers between devices, local(): other = lax.ppermute(half, 'c', SWAP)  8.45 us
    ppermute x1, waiting for transfers between devices, local(): b2 = lax.ppermute(b2, ys, flip_y)  6.8 us
    ppermute x2, starting transfers between devices, local(): halves.append((keep + lax.ppermute(send, 'c', SWAP)).astype(jnp.bfloat16))  6.72 us
    all_to_all x1, starting transfers between devices, local(): half = jnp.sum(lax.all_to_all(lines, 'yh', 0, 0), axis=0)  6.45 us
    ppermute x1, starting transfers between devices, local(): b2 = lax.ppermute(b2, ys, flip_y)  5.89 us
  transfers between devices with their start and end apart: 14, of which 7 were waited for; matrix products, arithmetic and copies ran while one was open for 2% of the time, Pallas kernels for 4%

profile of v5, /device:TPU:1, one launch (start us, length us, event | category | flops | bytes accessed | tf_op | source)
XLA Modules:
  0.0 278.1 jit_solution(15118764749267914258)
XLA Ops:
  7.8 113.1 %shard_map.50 = (bf16[4,128,1792]{2,1,0:T(8,128)(2,1)}, bf16[1,128,1792]{2,1,0:T(8,128)(2,1)}, bf16[1,128,1792]{2,1,0:T(8,128)(2,1)}, bf16[1,128,1792]{2,1,0:T(8,128)(2,1)}, bf16[1,128,1792]{2,1,0:T(8,128)(2,1)}) custom-call(s32[3]{0:T(128)} %pad_add_fusion.spot_ref, bf16[128,12288]{1,0:T(8,128)(2,1)} %t_ref.1, bf16[128,256]{1,0:T(8,128)(2,1)} %g_ref.1), custom_call_target="tpu_custom_call" | custom-call | tf_op jit(solution)/shard_map/pallas_call | solution.py:37
  120.9 4.5 %all-to-all-start = ((bf16[4,128,1792]{2,1,0:T(8,128)(2,1)}), bf16[4,128,1792]{2,1,0:T(8,128)(2,1)S(1)}, u32[]{:S(2)}, u32[]{:S(2)}) async-start(bf16[4,128,1792]{2,1,0:T(8,128)(2,1)} %get-tuple-element.19), calls=%async_computation | async-start | bytes 3670016 | tf_op jit(solution)/shard_map/all_to_all | solution.py:171
  126.1 5.0 %collective-permute-start.1 = (bf16[1,128,1792]{2,1,0:T(8,128)(2,1)}, bf16[1,128,1792]{2,1,0:T(8,128)(2,1)S(1)}, u32[]{:S(2)}, u32[]{:S(2)}) collective-permute-start(bf16[1,128,1792]{2,1,0:T(8,128)(2,1)} %get-tuple-element.23), channel_id=1, source_target_pairs={{0,24},{8,16},{16,8},{24,0},{1,25},{9,17},{17,9},{25,1},{2,26},{10... | collective-permute-start | bytes 1376264 | tf_op jit(solution)/shard_map/ppermute | solution.py:172
  131.1 5.9 %collective-permute-start.2 = (bf16[1,128,1792]{2,1,0:T(8,128)(2,1)S(1)}, bf16[1,128,1792]{2,1,0:T(8,128)(2,1)S(1)}, u32[]{:S(2)}, u32[]{:S(2)}) collective-permute-start(bf16[1,128,1792]{2,1,0:T(8,128)(2,1)S(1)} %copy-done.13), channel_id=1, source_target_pairs={{0,416},{32,128},{128,32},{160,256},{256,160},{288,384},{384,288},... | collective-permute-start | bytes 1376264 | tf_op jit(solution)/shard_map/ppermute | solution.py:173
  137.0 1.9 collective-permute-start.3
  138.9 6.8 %collective-permute-done.2.refs_2_.refs_6_ = bf16[1,128,1792]{2,1,0:T(8,128)(2,1)S(1)} collective-permute-done((bf16[1,128,1792]{2,1,0:T(8,128)(2,1)S(1)}, bf16[1,128,1792]{2,1,0:T(8,128)(2,1)S(1)}, u32[]{:S(2)}, u32[]{:S(2)}) %collective-permute-start.2) | collective-permute-done | bytes 458784 | tf_op jit(solution)/shard_map/ppermute | solution.py:173
  145.7 10.7 %collective-permute-done.3.refs_3_.refs_7_ = bf16[1,128,1792]{2,1,0:T(8,128)(2,1)S(1)} collective-permute-done((bf16[1,128,1792]{2,1,0:T(8,128)(2,1)S(1)}, bf16[1,128,1792]{2,1,0:T(8,128)(2,1)S(1)}, u32[]{:S(2)}, u32[]{:S(2)}) %collective-permute-start.3) | collective-permute-done | bytes 458784 | tf_op jit(solution)/shard_map/ppermute | solution.py:174
  156.4 3.4 %shard_map.52 = (f32[1536,128]{1,0:T(8,128)S(1)}, f32[1536,128]{1,0:T(8,128)}) custom-call(s32[3]{0:T(128)S(1)} %copy-done.11, bf16[1,128,1792]{2,1,0:T(8,128)(2,1)S(1)} %copy-done.1, bf16[1,128,1792]{2,1,0:T(8,128)(2,1)S(1)} %collective-permute-done.1.refs_1_.refs_5_, bf16[1,128,1792]{2,1,0:T(8,128)(2,1)S(1)} %collective-permute-done.2.refs_2_.refs_6_, ...), custom_call_target="tpu_custom_call" | custom-call | tf_op jit(solution)/shard_map/pallas_call | solution.py:77
  159.9 4.8 %collective-permute-start.4 = (f32[1536,128]{1,0:T(8,128)}, f32[1536,128]{1,0:T(8,128)}, u32[]{:S(2)}, u32[]{:S(2)}) collective-permute-start(f32[1536,128]{1,0:T(8,128)} %get-tuple-element.27), channel_id=1, source_target_pairs={{0,64},{64,0},{1,65},{65,1},{2,66},{66,2},{3,67},{67,3},{4,68},{68... | collective-permute-start | bytes 2359304 | tf_op jit(solution)/shard_map/ppermute | solution.py:180
  164.7 2.2 shard_map.51
  166.9 1.9 collective-permute-start
  172.2 47.8 %all-gather.2.cloned.1.call-done.refs_1_.refs_4_ = bf16[3072,256]{1,0:T(8,128)(2,1)} async-done(((bf16[192,256]{1,0:T(8,128)(2,1)}), bf16[3072,256]{1,0:T(8,128)(2,1)}) %all-gather.2.cloned.1.call-update) | async-done | bytes 1572880 | tf_op jit(solution)/shard_map/all_gather | solution.py:175
  219.9 5.0 %all-to-all-start.1 = ((bf16[16,192,128]{2,1,0:T(8,128)(2,1)}), bf16[16,192,128]{2,1,0:T(8,128)(2,1)}, u32[]{:S(2)}, u32[]{:S(2)}) async-start(bf16[16,192,128]{2,1,0:T(8,128)(2,1)} %bitcast.20), calls=%async_computation.1 | async-start | bytes 1572864 | tf_op jit(solution)/shard_map/all_to_all | solution.py:192
  229.0 2.1 shard_map.54
  231.1 2.5 shard_map.53
  234.3 4.6 %collective-permute-start.6 = (f32[2,128,256]{2,1,0:T(8,128)S(1)}, f32[2,128,256]{2,1,0:T(8,128)S(1)}, u32[]{:S(2)}, u32[]{:S(2)}) collective-permute-start(f32[2,128,256]{2,1,0:T(8,128)S(1)} %get-tuple-element.35), channel_id=1, source_target_pairs={{0,416},{32,128},{128,32},{160,256},{256,160},{288,384},{384,288},... | collective-permute-start | bytes 786440 | tf_op jit(solution)/shard_map/ppermute | solution.py:188
  238.9 1.9 collective-permute-start.5
  240.8 2.3 collective-permute-done.6
  243.2 1.3 convert_reduce_fusion
  245.2 6.4 %all-to-all-start.2 = ((f32[4,192,128]{2,1,0:T(8,128)}), f32[4,192,128]{2,1,0:T(8,128)S(1)}, u32[]{:S(2)}, u32[]{:S(2)}) async-start(f32[4,192,128]{2,1,0:T(8,128)} %broadcast_in_dim.2), calls=%async_computation.2 | async-start | bytes 786432 | tf_op jit(solution)/shard_map/all_to_all | solution.py:195
  251.7 5.3 %collective-permute-start.8 = (f32[128,256]{1,0:T(8,128)S(1)}, f32[128,256]{1,0:T(8,128)S(1)}, u32[]{:S(2)}, u32[]{:S(2)}) collective-permute-start(f32[128,256]{1,0:T(8,128)S(1)} %slice_bitcast_fusion), channel_id=1, source_target_pairs={{0,24},{8,16},{16,8},{24,0},{1,25},{9,17},{17,9},{25,1},{2,26},{10... | collective-permute-start | bytes 393224 | tf_op jit(solution)/shard_map/ppermute | solution.py:190
  257.1 1.9 collective-permute-start.7
  259.0 2.1 all-to-all-done.2
  261.2 8.4 %collective-permute-start.9 = (f32[192,128]{1,0:T(8,128)S(1)}, f32[192,128]{1,0:T(8,128)S(1)}, u32[]{:S(2)}, u32[]{:S(2)}) collective-permute-start(f32[192,128]{1,0:T(8,128)S(1)} %reduce_sum.19), channel_id=1, source_target_pairs={{0,64},{64,0},{1,65},{65,1},{2,66},{66,2},{3,67},{67,3},{4,68},{68... | collective-permute-start | bytes 294920 | tf_op jit(solution)/shard_map/ppermute | solution.py:196
  (52 shorter events, 11.9 us)
Async XLA Ops:
  120.9 10.2 %copy-start.13 = (bf16[1,128,1792]{2,1,0:T(8,128)(2,1)S(1)}, bf16[1,128,1792]{2,1,0:T(8,128)(2,1)}, u32[]{:S(2)}) copy-start(bf16[1,128,1792]{2,1,0:T(8,128)(2,1)} %get-tuple-element.24) | copy-start | bytes 1376260
  120.9 16.1 %copy-start.12 = (bf16[1,128,1792]{2,1,0:T(8,128)(2,1)S(1)}, bf16[1,128,1792]{2,1,0:T(8,128)(2,1)}, u32[]{:S(2)}) copy-start(bf16[1,128,1792]{2,1,0:T(8,128)(2,1)} %get-tuple-element.25) | copy-start | bytes 1376260
  120.9 35.6 %copy-start.1 = (bf16[1,128,1792]{2,1,0:T(8,128)(2,1)S(1)}, bf16[1,128,1792]{2,1,0:T(8,128)(2,1)}, u32[]{:S(2)}) copy-start(bf16[1,128,1792]{2,1,0:T(8,128)(2,1)} %get-tuple-element.22.refs_0_.refs_4_) | copy-start | bytes 1376260
  120.9 35.5 %copy-start.11 = (s32[3]{0:T(128)S(1)}, s32[3]{0:T(128)}, u32[]{:S(2)}) copy-start(s32[3]{0:T(128)} %pad_add_fusion.spot_ref) | copy-start | bytes 40
  120.9 43.8 %all-to-all-start = ((bf16[4,128,1792]{2,1,0:T(8,128)(2,1)}), bf16[4,128,1792]{2,1,0:T(8,128)(2,1)S(1)}, u32[]{:S(2)}, u32[]{:S(2)}) async-start(bf16[4,128,1792]{2,1,0:T(8,128)(2,1)} %get-tuple-element.19), calls=%async_computation | async-start | bytes 3670016 | tf_op jit(solution)/shard_map/all_to_all | solution.py:171
  125.4 94.6 %all-gather.2.cloned.1.call-start = ((), (), s32[]{:S(2)}) async-start(), calls=%async_computation.3 | async-start | bytes 1671168 | tf_op jit(solution)/shard_map/all_gather | solution.py:175
  126.1 12.8 %collective-permute-start.1 = (bf16[1,128,1792]{2,1,0:T(8,128)(2,1)}, bf16[1,128,1792]{2,1,0:T(8,128)(2,1)S(1)}, u32[]{:S(2)}, u32[]{:S(2)}) collective-permute-start(bf16[1,128,1792]{2,1,0:T(8,128)(2,1)} %get-tuple-element.23), channel_id=1, source_target_pairs={{0,24},{8,16},{16,8},{24,0},{1,25},{9,17},{17,9},{25,1},{2,26},{10... | collective-permute-start | bytes 1376264 | tf_op jit(solution)/shard_map/ppermute | solution.py:172
  131.1 14.7 %collective-permute-start.2 = (bf16[1,128,1792]{2,1,0:T(8,128)(2,1)S(1)}, bf16[1,128,1792]{2,1,0:T(8,128)(2,1)S(1)}, u32[]{:S(2)}, u32[]{:S(2)}) collective-permute-start(bf16[1,128,1792]{2,1,0:T(8,128)(2,1)S(1)} %copy-done.13), channel_id=1, source_target_pairs={{0,416},{32,128},{128,32},{160,256},{256,160},{288,384},{384,288},... | collective-permute-start | bytes 1376264 | tf_op jit(solution)/shard_map/ppermute | solution.py:173
  137.0 19.4 %collective-permute-start.3 = (bf16[1,128,1792]{2,1,0:T(8,128)(2,1)S(1)}, bf16[1,128,1792]{2,1,0:T(8,128)(2,1)S(1)}, u32[]{:S(2)}, u32[]{:S(2)}) collective-permute-start(bf16[1,128,1792]{2,1,0:T(8,128)(2,1)S(1)} %copy-done.12), channel_id=1, source_target_pairs={{0,440},{8,432},{16,424},{24,416},{32,152},{40,144},{48,136},{56,1... | collective-permute-start | bytes 1376264 | tf_op jit(solution)/shard_map/ppermute | solution.py:174
  138.9 20.9 %copy-start.3 = (bf16[1,128,1792]{2,1,0:T(8,128)(2,1)}, bf16[1,128,1792]{2,1,0:T(8,128)(2,1)S(1)}, u32[]{:S(2)}) copy-start(bf16[1,128,1792]{2,1,0:T(8,128)(2,1)S(1)} %collective-permute-done.1.refs_1_.refs_5_) | copy-start | bytes 1376260
  145.7 14.1 %copy-start.5 = (bf16[1,128,1792]{2,1,0:T(8,128)(2,1)}, bf16[1,128,1792]{2,1,0:T(8,128)(2,1)S(1)}, u32[]{:S(2)}) copy-start(bf16[1,128,1792]{2,1,0:T(8,128)(2,1)S(1)} %collective-permute-done.2.refs_2_.refs_6_) | copy-start | bytes 1376260
  156.4 3.5 %copy-start.7 = (bf16[1,128,1792]{2,1,0:T(8,128)(2,1)}, bf16[1,128,1792]{2,1,0:T(8,128)(2,1)S(1)}, u32[]{:S(2)}) copy-start(bf16[1,128,1792]{2,1,0:T(8,128)(2,1)S(1)} %collective-permute-done.3.refs_3_.refs_7_) | copy-start | bytes 1376260
  159.9 9.0 %collective-permute-start.4 = (f32[1536,128]{1,0:T(8,128)}, f32[1536,128]{1,0:T(8,128)}, u32[]{:S(2)}, u32[]{:S(2)}) collective-permute-start(f32[1536,128]{1,0:T(8,128)} %get-tuple-element.27), channel_id=1, source_target_pairs={{0,64},{64,0},{1,65},{65,1},{2,66},{66,2},{3,67},{67,3},{4,68},{68... | collective-permute-start | bytes 2359304 | tf_op jit(solution)/shard_map/ppermute | solution.py:180
  166.9 4.2 %collective-permute-start = (f32[1536,128]{1,0:T(8,128)S(1)}, f32[1536,128]{1,0:T(8,128)S(1)}, u32[]{:S(2)}, u32[]{:S(2)}) collective-permute-start(f32[1536,128]{1,0:T(8,128)S(1)} %get-tuple-element.21), channel_id=1, source_target_pairs={{0,64},{64,0},{1,65},{65,1},{2,66},{66,2},{3,67},{67,3},{4,68},{68... | collective-permute-start | bytes 2359304 | tf_op jit(solution)/shard_map/ppermute | solution.py:180
  219.9 5.0 %copy-start = (bf16[3072,256]{1,0:T(8,128)(2,1)S(1)}, bf16[3072,256]{1,0:T(8,128)(2,1)}, u32[]{:S(2)}) copy-start(bf16[3072,256]{1,0:T(8,128)(2,1)} %all-gather.2.cloned.1.call-done.refs_1_.refs_4_) | copy-start | bytes 4718596
  219.9 23.3 %all-to-all-start.1 = ((bf16[16,192,128]{2,1,0:T(8,128)(2,1)}), bf16[16,192,128]{2,1,0:T(8,128)(2,1)}, u32[]{:S(2)}, u32[]{:S(2)}) async-start(bf16[16,192,128]{2,1,0:T(8,128)(2,1)} %bitcast.20), calls=%async_computation.1 | async-start | bytes 1572864 | tf_op jit(solution)/shard_map/all_to_all | solution.py:192
  224.9 1.0 copy-start.2
  234.3 22.7 %copy-start.10 = (f32[2,128,256]{2,1,0:T(8,128)S(1)}, f32[2,128,256]{2,1,0:T(8,128)}, u32[]{:S(2)}) copy-start(f32[2,128,256]{2,1,0:T(8,128)} %copy-done.9) | copy-start | bytes 786436
  234.3 8.8 %collective-permute-start.6 = (f32[2,128,256]{2,1,0:T(8,128)S(1)}, f32[2,128,256]{2,1,0:T(8,128)S(1)}, u32[]{:S(2)}, u32[]{:S(2)}) collective-permute-start(f32[2,128,256]{2,1,0:T(8,128)S(1)} %get-tuple-element.35), channel_id=1, source_target_pairs={{0,416},{32,128},{128,32},{160,256},{256,160},{288,384},{384,288},... | collective-permute-start | bytes 786440 | tf_op jit(solution)/shard_map/ppermute | solution.py:188
  238.9 18.1 %collective-permute-start.5 = (f32[2,128,256]{2,1,0:T(8,128)}, f32[2,128,256]{2,1,0:T(8,128)S(1)}, u32[]{:S(2)}, u32[]{:S(2)}) collective-permute-start(f32[2,128,256]{2,1,0:T(8,128)} %get-tuple-element.33), channel_id=1, source_target_pairs={{0,32},{32,0},{1,33},{33,1},{2,34},{34,2},{3,35},{35,3},{4,36},{36... | collective-permute-start | bytes 786440 | tf_op jit(solution)/shard_map/ppermute | solution.py:187
  245.2 16.0 %all-to-all-start.2 = ((f32[4,192,128]{2,1,0:T(8,128)}), f32[4,192,128]{2,1,0:T(8,128)S(1)}, u32[]{:S(2)}, u32[]{:S(2)}) async-start(f32[4,192,128]{2,1,0:T(8,128)} %broadcast_in_dim.2), calls=%async_computation.2 | async-start | bytes 786432 | tf_op jit(solution)/shard_map/all_to_all | solution.py:195
  251.7 18.0 %collective-permute-start.8 = (f32[128,256]{1,0:T(8,128)S(1)}, f32[128,256]{1,0:T(8,128)S(1)}, u32[]{:S(2)}, u32[]{:S(2)}) collective-permute-start(f32[128,256]{1,0:T(8,128)S(1)} %slice_bitcast_fusion), channel_id=1, source_target_pairs={{0,24},{8,16},{16,8},{24,0},{1,25},{9,17},{17,9},{25,1},{2,26},{10... | collective-permute-start | bytes 393224 | tf_op jit(solution)/shard_map/ppermute | solution.py:190
  257.1 12.6 %collective-permute-start.7 = (f32[128,256]{1,0:T(8,128)S(1)}, f32[128,256]{1,0:T(8,128)S(1)}, u32[]{:S(2)}, u32[]{:S(2)}) collective-permute-start(f32[128,256]{1,0:T(8,128)S(1)} %slice_bitcast_fusion.1), channel_id=1, source_target_pairs={{0,8},{8,0},{1,9},{9,1},{2,10},{10,2},{3,11},{11,3},{4,12},{12,4},... | collective-permute-start | bytes 393224 | tf_op jit(solution)/shard_map/ppermute | solution.py:189
  261.2 9.4 %collective-permute-start.9 = (f32[192,128]{1,0:T(8,128)S(1)}, f32[192,128]{1,0:T(8,128)S(1)}, u32[]{:S(2)}, u32[]{:S(2)}) collective-permute-start(f32[192,128]{1,0:T(8,128)S(1)} %reduce_sum.19), channel_id=1, source_target_pairs={{0,64},{64,0},{1,65},{65,1},{2,66},{66,2},{3,67},{67,3},{4,68},{68... | collective-permute-start | bytes 294920 | tf_op jit(solution)/shard_map/ppermute | solution.py:196
  (4 other events, 3.8 us)
Sparse Core Ops, SparseCore 0:
  129.4 90.5 all-gather.1

commit v6 on v4

v6 whole, which is shorter than its diff:
```python
import jax
import jax.numpy as jnp
from jax import lax
from jax.experimental import pallas as pl
from jax.experimental.pallas import tpu as pltpu
from jax.sharding import Mesh, PartitionSpec as P

PARAMS = pltpu.CompilerParams(vmem_limit_bytes=24 * 1024 * 1024)
ALONE = pltpu.CompilerParams(vmem_limit_bytes=60 * 1024 * 1024)
SWAP = [(0, 1), (1, 0)]


def pack(tokens, grad_out, sharers):
    rows, width = tokens.shape
    cols = grad_out.shape[1]
    part = width // sharers

    def body(t_ref, g_ref, o_ref, stage, t_sems, g_sems, o_sems):
        loads, stores = [], []
        for k in range(sharers):
            loads.append(
                (
                    pltpu.make_async_copy(
                        t_ref.at[:, pl.ds(k * part, part)],
                        stage.at[k, :, pl.ds(0, part)],
                        t_sems.at[k],
                    ),
                    pltpu.make_async_copy(
                        g_ref, stage.at[k, :, pl.ds(part, cols)], g_sems.at[k]
                    ),
                )
            )
            stores.append(
                pltpu.make_async_copy(stage.at[k], o_ref.at[k], o_sems.at[k])
            )
        for pair in loads:
            for copy in pair:
                copy.start()
        for pair, store in zip(loads, stores):
            for copy in pair:
                copy.wait()
            store.start()
        for store in stores:
            store.wait()

    shape = (sharers, rows, part + cols)
    return pl.pallas_call(
        body,
        in_specs=[pl.BlockSpec(memory_space=pl.ANY)] * 2,
        out_specs=pl.BlockSpec(memory_space=pl.ANY),
        out_shape=jax.ShapeDtypeStruct(shape, tokens.dtype),
        scratch_shapes=[pltpu.VMEM(shape, tokens.dtype)]
        + [pltpu.SemaphoreType.DMA((sharers,))] * 3,
        compiler_params=ALONE,
    )(tokens, grad_out)


def terms(packed, spot, part):
    sharers, rows, both = packed.shape
    cols = both - part
    wide = cols // 2
    step = 2
    steps = sharers // step

    def body(spot_ref, p_ref, keep_ref, send_ref, stage, sems):
        loads = []
        for k in range(steps):
            at = pl.ds(k * step, step)
            loads.append(
                pltpu.make_async_copy(p_ref.at[at], stage.at[at], sems.at[k])
            )
            loads[-1].start()
        first = spot_ref[0] == 0
        for k in range(steps):
            loads[k].wait()
            p = stage[k * step : (k + 1) * step].reshape(step * rows, both)
            left, right = p[:, part : part + wide], p[:, part + wide :]
            g = jnp.concatenate(
                [jnp.where(first, left, right), jnp.where(first, right, left)], axis=1
            )
            term = lax.dot_general(
                p[:, :part],
                g,
                (((0,), (0,)), ((), ())),
                preferred_element_type=jnp.float32,
            )
            if k == 0:
                keep_ref[...] = term[:, :wide]
                send_ref[...] = term[:, wide:]
            else:
                keep_ref[...] += term[:, :wide]
                send_ref[...] += term[:, wide:]

    half = jax.ShapeDtypeStruct((part, wide), jnp.float32)
    return pl.pallas_call(
        body,
        in_specs=[
            pl.BlockSpec(memory_space=pltpu.SMEM),
            pl.BlockSpec(memory_space=pl.ANY),
        ],
        out_specs=[pl.BlockSpec(memory_space=pltpu.VMEM)] * 2,
        out_shape=[half, half],
        scratch_shapes=[
            pltpu.VMEM(packed.shape, packed.dtype),
            pltpu.SemaphoreType.DMA((steps,)),
        ],
        compiler_params=PARAMS,
    )(spot, packed)


def project(packed, weight, spot, away, width):
    rows = packed.shape[1]
    part, cols = weight.shape
    steps = 3
    step = part // steps

    def body(spot_ref, t_ref, w_ref, o_ref):
        t = [t_ref[lax.rem(spot_ref[2] + d, width)] for d in range(width)]
        new = jnp.dot(
            jnp.concatenate(t, axis=0), w_ref[...], preferred_element_type=jnp.float32
        ).reshape(width, rows, cols)
        k = pl.program_id(0)

        @pl.when(k == 0)
        def _():
            o_ref[...] = new

        @pl.when(k > 0)
        def _():
            o_ref[...] += new

    def line(spot):
        return 1 - spot[1] if away else spot[1]

    return pl.pallas_call(
        body,
        grid_spec=pltpu.PrefetchScalarGridSpec(
            num_scalar_prefetch=1,
            grid=(steps,),
            in_specs=[
                pl.BlockSpec(
                    (width, rows, step),
                    lambda k, spot: (line(spot), 0, k),
                ),
                pl.BlockSpec((step, cols), lambda k, spot: (k, 0)),
            ],
            out_specs=pl.BlockSpec((width, rows, cols), lambda k, spot: (0, 0, 0)),
        ),
        out_shape=jax.ShapeDtypeStruct((width, rows, cols), jnp.float32),
        compiler_params=PARAMS,
    )(spot, packed, weight)


def local(tokens, weight, grad_out):
    rows, model = tokens.shape
    shard, cols = weight.shape
    sharers, width = lax.axis_size(("yl", "x")), lax.axis_size("x")
    yh, depth = lax.axis_size("yh"), lax.axis_size("z")
    part = model // sharers
    spot = jnp.stack([lax.axis_index(name) for name in ("c", "yl", "x")])
    spot = spot.astype(jnp.int32)

    packed = pack(tokens, grad_out, sharers)
    packed = lax.all_to_all(packed, ("yl", "x"), 0, 0)
    mine = lax.all_gather(weight, "z", axis=0, tiled=True)
    packed, mine = lax.optimization_barrier((packed, mine))

    keep, send = terms(packed, spot, part)
    term = (keep + lax.ppermute(send, "c", SWAP)).astype(jnp.bfloat16)
    away = project(packed, mine, spot, True, width)
    away, _ = lax.optimization_barrier((away, term))
    away = lax.ppermute(away, "yl", SWAP)
    term = lax.all_to_all(term.reshape(depth, shard, cols // 2), "z", 0, 0)
    summed = jnp.sum(term, axis=0, dtype=jnp.float32)

    near = project(packed, mine, spot, False, width)
    near, summed = lax.optimization_barrier((near, summed))
    near = near + away
    output = near[0]
    for d in range(1, width):
        shift = [(i, (i + d) % width) for i in range(width)]
        output = output + lax.ppermute(near[d], "x", shift)

    lines = jnp.broadcast_to(summed[None], (yh, shard, cols // 2))
    half = jnp.sum(lax.all_to_all(lines, "yh", 0, 0), axis=0)
    other = lax.ppermute(half, "c", SWAP)
    first = spot[0] == 0
    weight_grad = jnp.concatenate(
        [jnp.where(first, half, other), jnp.where(first, other, half)], axis=1
    )
    return output.astype(jnp.bfloat16), weight_grad


def solution(mesh):
    inner = Mesh(mesh.devices.reshape(4, 2, 2, 4, 8), ("yh", "c", "yl", "x", "z"))
    rows = P(("yh", "c", "yl", "x", "z"), None)
    owners = P(("yl", "x", "z"), None)
    return jax.shard_map(
        local,
        mesh=inner,
        in_specs=(rows, owners, rows),
        out_specs=(rows, owners),
        check_vma=False,
    )
```

time: 118 us -> 114 us (0.966)
  Pallas kernels: 17.5 us -> 14.3 us
  waiting for transfers between devices: 24 us -> 21.4 us
  starting transfers between devices: 41.5 us -> 44 us
    all_to_all x1, waiting for transfers between devices: 8.59 us -> 5.37 us  [local(): term = lax.all_to_all(term.reshape(depth, shard, cols // 2), 'z', 0, 0)]
    pallas_call x2, Pallas kernels: 10.6 us -> 7.69 us  [the longest x1 3.85 us: pack(): pl.pallas_call(body, in_specs=[pl.BlockSpec(memory_space=pl.ANY)] * 2, ou...]
    ppermute x1, starting transfers between devices: 3.52 us -> 5.95 us  [local(): other = lax.ppermute(half, 'c', SWAP)]
  transfers between devices with their start and end apart: 9 -> 9, of which waited for: 4 -> 5; matrix products, arithmetic and copies ran while one was open for 1% -> 1% of each run, Pallas kernels for 6% -> 6%
where the time goes in v6:
time: 114 us; the launch traced here: 113 us
  starting transfers between devices  44 us (39%)
  blocking collectives  29.2 us (26%)
  waiting for transfers between devices  21.4 us (19%)
  Pallas kernels  14.3 us (13%)
  other arithmetic  2.42 us (2%)
    all_gather x1, blocking collectives, local(): mine = lax.all_gather(weight, 'z', axis=0, tiled=True)  29.2 us
    all_to_all x1, waiting for transfers between devices, local(): packed = lax.all_to_all(packed, ('yl', 'x'), 0, 0)  13.3 us
    all_to_all x1, starting transfers between devices, local(): term = lax.all_to_all(term.reshape(depth, shard, cols // 2), 'z', 0, 0)  10 us
    ppermute x3, starting transfers between devices, local(): output = output + lax.ppermute(near[d], 'x', shift)  9.38 us
    pallas_call x2, Pallas kernels, project(): pl.pallas_call(body, grid_spec=pltpu.PrefetchScalarGridSpec(num_scalar_pr...  6.65 us
    all_to_all x1, starting transfers between devices, local(): half = jnp.sum(lax.all_to_all(lines, 'yh', 0, 0), axis=0)  6.17 us
    all_to_all x1, starting transfers between devices, local(): packed = lax.all_to_all(packed, ('yl', 'x'), 0, 0)  6.01 us
    ppermute x1, starting transfers between devices, local(): other = lax.ppermute(half, 'c', SWAP)  5.95 us
  transfers between devices with their start and end apart: 9, of which 5 were waited for; matrix products, arithmetic and copies ran while one was open for 1% of the time, Pallas kernels for 6%

profile of v6, /device:TPU:1, one launch (start us, length us, event | category | flops | bytes accessed | tf_op | source)
XLA Modules:
  0.0 112.9 jit_solution(2731364384469559057)
XLA Ops:
  0.6 3.8 %shard_map.50 = bf16[8,128,1792]{2,1,0:T(8,128)(2,1)} custom-call(bf16[128,12288]{1,0:T(8,128)(2,1)} %t_ref.1, bf16[128,256]{1,0:T(8,128)(2,1)} %g_ref.1), custom_call_target="tpu_custom_call" | custom-call | tf_op jit(solution)/shard_map/pallas_call | solution.py:47
  4.5 6.0 %all-to-all-start = ((bf16[8,128,1792]{2,1,0:T(8,128)(2,1)}), bf16[8,128,1792]{2,1,0:T(8,128)(2,1)}, u32[]{:S(2)}, u32[]{:S(2)}) async-start(bf16[8,128,1792]{2,1,0:T(8,128)(2,1)} %shard_map.50), calls=%async_computation | async-start | bytes 7340032 | tf_op jit(solution)/shard_map/all_to_all | solution.py:164
  10.5 0.1 pad_add_fusion.spot_ref
  10.6 29.2 %all_gather.3.w_ref = bf16[1536,256]{1,0:T(8,128)(2,1)S(1)} all-gather(bf16[192,256]{1,0:T(8,128)(2,1)S(1)} %copy-done), channel_id=1, replica_groups=mesh['yh'=4,'c'=2,'yl'=2,'x'=4,'z'=8] {'z'}, dimensions={0}, use_global_device_ids=true | all-gather | bytes 884736 | tf_op jit(solution)/shard_map/all_gather | solution.py:165
  39.8 13.3 %all-to-all-done.t_ref.p_ref = bf16[8,128,1792]{2,1,0:T(8,128)(2,1)} async-done(((bf16[8,128,1792]{2,1,0:T(8,128)(2,1)}), bf16[8,128,1792]{2,1,0:T(8,128)(2,1)}, u32[]{:S(2)}, u32[]{:S(2)}) %all-to-all-start) | async-done | bytes 3670048 | tf_op jit(solution)/shard_map/all_to_all | solution.py:164
  53.0 3.8 %shard_map.52 = (f32[1536,128]{1,0:T(8,128)S(1)}, f32[1536,128]{1,0:T(8,128)S(1)}) custom-call(s32[3]{0:T(128)S(1)} %pad_add_fusion.spot_ref, bf16[8,128,1792]{2,1,0:T(8,128)(2,1)} %all-to-all-done.t_ref.p_ref), custom_call_target="tpu_custom_call" | custom-call | tf_op jit(solution)/shard_map/pallas_call | solution.py:95
  56.9 3.3 %collective-permute-start = (f32[1536,128]{1,0:T(8,128)S(1)}, f32[1536,128]{1,0:T(8,128)S(1)}, u32[]{:S(2)}, u32[]{:S(2)}) collective-permute-start(f32[1536,128]{1,0:T(8,128)S(1)} %get-tuple-element.12), channel_id=1, source_target_pairs={{0,64},{64,0},{1,65},{65,1},{2,66},{66,2},{3,67},{67,3},{4,68},{68... | collective-permute-start | bytes 2359304 | tf_op jit(solution)/shard_map/ppermute | solution.py:169
  60.2 1.9 %collective-permute-done = f32[1536,128]{1,0:T(8,128)S(1)} collective-permute-done((f32[1536,128]{1,0:T(8,128)S(1)}, f32[1536,128]{1,0:T(8,128)S(1)}, u32[]{:S(2)}, u32[]{:S(2)}) %collective-permute-start) | collective-permute-done | bytes 786464 | tf_op jit(solution)/shard_map/ppermute | solution.py:169
  62.1 0.8 add_convert_fusion
  62.9 10.0 %all-to-all-start.1 = ((bf16[8,192,128]{2,1,0:T(8,128)(2,1)}), bf16[8,192,128]{2,1,0:T(8,128)(2,1)S(1)}, u32[]{:S(2)}, u32[]{:S(2)}) async-start(bf16[8,192,128]{2,1,0:T(8,128)(2,1)} %bitcast.3), calls=%async_computation.1 | async-start | bytes 786432 | tf_op jit(solution)/shard_map/all_to_all | solution.py:173
  73.0 3.3 %shard_map.53 = f32[4,128,256]{2,1,0:T(8,128)S(1)} custom-call(s32[3]{0:T(128)S(1)} %pad_add_fusion.spot_ref, bf16[8,128,1792]{2,1,0:T(8,128)(2,1)} %all-to-all-done.t_ref.p_ref, bf16[1536,256]{1,0:T(8,128)(2,1)S(1)} %all_gather.3.w_ref), custom_call_target="tpu_custom_call" | custom-call | tf_op jit(solution)/shard_map/pallas_call | solution.py:135
  76.3 3.1 %collective-permute-start.1 = (f32[4,128,256]{2,1,0:T(8,128)S(1)}, f32[4,128,256]{2,1,0:T(8,128)S(1)}, u32[]{:S(2)}, u32[]{:S(2)}) collective-permute-start(f32[4,128,256]{2,1,0:T(8,128)S(1)} %shard_map.53), channel_id=1, source_target_pairs={{0,32},{32,0},{1,33},{33,1},{2,34},{34,2},{3,35},{35,3},{4,36},{36... | collective-permute-start | bytes 1572872 | tf_op jit(solution)/shard_map/ppermute | solution.py:172
  79.4 3.3 %shard_map.51 = f32[4,128,256]{2,1,0:T(8,128)S(1)} custom-call(s32[3]{0:T(128)S(1)} %pad_add_fusion.spot_ref, bf16[8,128,1792]{2,1,0:T(8,128)(2,1)} %all-to-all-done.t_ref.p_ref, bf16[1536,256]{1,0:T(8,128)(2,1)S(1)} %all_gather.3.w_ref), custom_call_target="tpu_custom_call" | custom-call | tf_op jit(solution)/shard_map/pallas_call | solution.py:135
  82.7 5.4 %all-to-all-done.1 = bf16[8,192,128]{2,1,0:T(8,128)(2,1)S(1)} async-done(((bf16[8,192,128]{2,1,0:T(8,128)(2,1)}), bf16[8,192,128]{2,1,0:T(8,128)(2,1)S(1)}, u32[]{:S(2)}, u32[]{:S(2)}) %all-to-all-start.1) | async-done | bytes 393248 | tf_op jit(solution)/shard_map/all_to_all | solution.py:173
  88.2 0.8 broadcast_in_dim.2
  89.0 6.2 %all-to-all-start.2 = ((f32[4,192,128]{2,1,0:T(8,128)}), f32[4,192,128]{2,1,0:T(8,128)S(1)}, u32[]{:S(2)}, u32[]{:S(2)}) async-start(f32[4,192,128]{2,1,0:T(8,128)} %broadcast_in_dim.2), calls=%async_computation.2 | async-start | bytes 786432 | tf_op jit(solution)/shard_map/all_to_all | solution.py:185
  95.2 2.5 %collective-permute-start.2 = (f32[128,256]{1,0:T(8,128)S(1)}, f32[128,256]{1,0:T(8,128)S(1)}, u32[]{:S(2)}, u32[]{:S(2)}) collective-permute-start(f32[128,256]{1,0:T(8,128)S(1)} %get-tuple-element.16), channel_id=1, source_target_pairs={{0,8},{8,16},{16,24},{24,0},{1,9},{9,17},{17,25},{25,1},{2,10},{10... | collective-permute-start | bytes 393224 | tf_op jit(solution)/shard_map/ppermute | solution.py:182
  97.7 4.1 %collective-permute-start.3 = (f32[128,256]{1,0:T(8,128)S(1)}, f32[128,256]{1,0:T(8,128)S(1)}, u32[]{:S(2)}, u32[]{:S(2)}) collective-permute-start(f32[128,256]{1,0:T(8,128)S(1)} %get-tuple-element.18), channel_id=1, source_target_pairs={{0,16},{8,24},{16,0},{24,8},{1,17},{9,25},{17,1},{25,9},{2,18},{10... | collective-permute-start | bytes 393224 | tf_op jit(solution)/shard_map/ppermute | solution.py:182
  101.9 2.7 %collective-permute-start.4 = (f32[128,256]{1,0:T(8,128)S(1)}, f32[128,256]{1,0:T(8,128)S(1)}, u32[]{:S(2)}, u32[]{:S(2)}) collective-permute-start(f32[128,256]{1,0:T(8,128)S(1)} %get-tuple-element.17), channel_id=1, source_target_pairs={{0,24},{8,0},{16,8},{24,16},{1,25},{9,1},{17,9},{25,17},{2,26},{10... | collective-permute-start | bytes 393224 | tf_op jit(solution)/shard_map/ppermute | solution.py:182
  104.6 0.6 all-to-all-done.2
  105.3 6.0 %collective-permute-start.5 = (f32[192,128]{1,0:T(8,128)S(1)}, f32[192,128]{1,0:T(8,128)S(1)}, u32[]{:S(2)}, u32[]{:S(2)}) collective-permute-start(f32[192,128]{1,0:T(8,128)S(1)} %reduce_sum.19), channel_id=1, source_target_pairs={{0,64},{64,0},{1,65},{65,1},{2,66},{66,2},{3,67},{67,3},{4,68},{68... | collective-permute-start | bytes 294920 | tf_op jit(solution)/shard_map/ppermute | solution.py:186
  111.3 0.7 fusion.3
  111.9 0.2 collective-permute-done.5
  112.2 0.7 pad_maximum_fusion
  (11 shorter events, 0.2 us)
Async XLA Ops:
  4.5 6.1 %copy-start = (bf16[192,256]{1,0:T(8,128)(2,1)S(1)}, bf16[192,256]{1,0:T(8,128)(2,1)}, u32[]{:S(2)}) copy-start(bf16[192,256]{1,0:T(8,128)(2,1)} %param.4) | copy-start | bytes 294916
  4.5 48.5 %all-to-all-start = ((bf16[8,128,1792]{2,1,0:T(8,128)(2,1)}), bf16[8,128,1792]{2,1,0:T(8,128)(2,1)}, u32[]{:S(2)}, u32[]{:S(2)}) async-start(bf16[8,128,1792]{2,1,0:T(8,128)(2,1)} %shard_map.50), calls=%async_computation | async-start | bytes 7340032 | tf_op jit(solution)/shard_map/all_to_all | solution.py:164
  56.9 5.2 %collective-permute-start = (f32[1536,128]{1,0:T(8,128)S(1)}, f32[1536,128]{1,0:T(8,128)S(1)}, u32[]{:S(2)}, u32[]{:S(2)}) collective-permute-start(f32[1536,128]{1,0:T(8,128)S(1)} %get-tuple-element.12), channel_id=1, source_target_pairs={{0,64},{64,0},{1,65},{65,1},{2,66},{66,2},{3,67},{67,3},{4,68},{68... | collective-permute-start | bytes 2359304 | tf_op jit(solution)/shard_map/ppermute | solution.py:169
  62.9 25.2 %all-to-all-start.1 = ((bf16[8,192,128]{2,1,0:T(8,128)(2,1)}), bf16[8,192,128]{2,1,0:T(8,128)(2,1)S(1)}, u32[]{:S(2)}, u32[]{:S(2)}) async-start(bf16[8,192,128]{2,1,0:T(8,128)(2,1)} %bitcast.3), calls=%async_computation.1 | async-start | bytes 786432 | tf_op jit(solution)/shard_map/all_to_all | solution.py:173
  76.3 18.8 %collective-permute-start.1 = (f32[4,128,256]{2,1,0:T(8,128)S(1)}, f32[4,128,256]{2,1,0:T(8,128)S(1)}, u32[]{:S(2)}, u32[]{:S(2)}) collective-permute-start(f32[4,128,256]{2,1,0:T(8,128)S(1)} %shard_map.53), channel_id=1, source_target_pairs={{0,32},{32,0},{1,33},{33,1},{2,34},{34,2},{3,35},{35,3},{4,36},{36... | collective-permute-start | bytes 1572872 | tf_op jit(solution)/shard_map/ppermute | solution.py:172
  89.0 16.3 %all-to-all-start.2 = ((f32[4,192,128]{2,1,0:T(8,128)}), f32[4,192,128]{2,1,0:T(8,128)S(1)}, u32[]{:S(2)}, u32[]{:S(2)}) async-start(f32[4,192,128]{2,1,0:T(8,128)} %broadcast_in_dim.2), calls=%async_computation.2 | async-start | bytes 786432 | tf_op jit(solution)/shard_map/all_to_all | solution.py:185
  95.2 16.0 %collective-permute-start.2 = (f32[128,256]{1,0:T(8,128)S(1)}, f32[128,256]{1,0:T(8,128)S(1)}, u32[]{:S(2)}, u32[]{:S(2)}) collective-permute-start(f32[128,256]{1,0:T(8,128)S(1)} %get-tuple-element.16), channel_id=1, source_target_pairs={{0,8},{8,16},{16,24},{24,0},{1,9},{9,17},{17,25},{25,1},{2,10},{10... | collective-permute-start | bytes 393224 | tf_op jit(solution)/shard_map/ppermute | solution.py:182
  97.7 13.5 %collective-permute-start.3 = (f32[128,256]{1,0:T(8,128)S(1)}, f32[128,256]{1,0:T(8,128)S(1)}, u32[]{:S(2)}, u32[]{:S(2)}) collective-permute-start(f32[128,256]{1,0:T(8,128)S(1)} %get-tuple-element.18), channel_id=1, source_target_pairs={{0,16},{8,24},{16,0},{24,8},{1,17},{9,25},{17,1},{25,9},{2,18},{10... | collective-permute-start | bytes 393224 | tf_op jit(solution)/shard_map/ppermute | solution.py:182
  101.9 9.4 %collective-permute-start.4 = (f32[128,256]{1,0:T(8,128)S(1)}, f32[128,256]{1,0:T(8,128)S(1)}, u32[]{:S(2)}, u32[]{:S(2)}) collective-permute-start(f32[128,256]{1,0:T(8,128)S(1)} %get-tuple-element.17), channel_id=1, source_target_pairs={{0,24},{8,0},{16,8},{24,16},{1,25},{9,1},{17,9},{25,17},{2,26},{10... | collective-permute-start | bytes 393224 | tf_op jit(solution)/shard_map/ppermute | solution.py:182
  105.3 6.9 %collective-permute-start.5 = (f32[192,128]{1,0:T(8,128)S(1)}, f32[192,128]{1,0:T(8,128)S(1)}, u32[]{:S(2)}, u32[]{:S(2)}) collective-permute-start(f32[192,128]{1,0:T(8,128)S(1)} %reduce_sum.19), channel_id=1, source_target_pairs={{0,64},{64,0},{1,65},{65,1},{2,66},{66,2},{3,67},{67,3},{4,68},{68... | collective-permute-start | bytes 294920 | tf_op jit(solution)/shard_map/ppermute | solution.py:186

commit v7 on v0

v7 whole, which is shorter than its diff:
```python
import jax
import jax.numpy as jnp
from jax import lax
from jax.experimental import pallas as pl
from jax.experimental.pallas import tpu as pltpu
from jax.sharding import Mesh, PartitionSpec as P

PARAMS = pltpu.CompilerParams(vmem_limit_bytes=24 * 1024 * 1024)
ALONE = pltpu.CompilerParams(vmem_limit_bytes=60 * 1024 * 1024)
SWAP = [(0, 1), (1, 0)]
CHIP = ("yh", "c", "yl", "xh", "xl")


def pack(tokens, grad_out, spot, shard):
    rows, width = tokens.shape
    cols = grad_out.shape[1]
    quads = 4
    node = width // 8
    part = width // 8
    half = shard // 2

    def body(spot_ref, t_ref, g_ref, keep_ref, send_ref, held, stage, t_sems, g_sems, o_sems):
        loads, sides = [], []
        for k in range(8):
            at = pl.ds(k * node, node)
            copy = pltpu.make_async_copy(t_ref.at[:, at], held.at[:, at], t_sems.at[k])
            copy.start()
            loads.append(copy)
        for side in range(2):
            for quad in range(quads):
                copy = pltpu.make_async_copy(
                    g_ref,
                    stage.at[side, quad, :, pl.ds(part, cols)],
                    g_sems.at[side, quad],
                )
                copy.start()
                sides.append(copy)
        for copy in sides:
            copy.wait()
        stores = []
        for quad in range(quads):
            for xh in range(2):
                k = (quad // 2) * 4 + xh * 2 + quad % 2
                loads[k].wait()
                t = held[:, k * node : (k + 1) * node]
                for side in range(2):
                    pieces = [
                        t[:, at + side * half : at + side * half + half]
                        for at in range(0, node, shard)
                    ]
                    stage[side, quad, :, xh * node // 2 : (xh + 1) * node // 2] = (
                        jnp.concatenate(pieces, axis=1)
                    )
            for n, ref in enumerate((keep_ref, send_ref)):
                copy = pltpu.make_async_copy(
                    stage.at[spot_ref[0] ^ n, quad], ref.at[quad], o_sems.at[n, quad]
                )
                copy.start()
                stores.append(copy)
        for copy in stores:
            copy.wait()

    shape = (quads, rows, part + cols)
    out = jax.ShapeDtypeStruct(shape, tokens.dtype)
    return pl.pallas_call(
        body,
        in_specs=[pl.BlockSpec(memory_space=pltpu.SMEM)]
        + [pl.BlockSpec(memory_space=pl.ANY)] * 2,
        out_specs=[pl.BlockSpec(memory_space=pl.ANY)] * 2,
        out_shape=[out, out],
        scratch_shapes=[
            pltpu.VMEM(tokens.shape, tokens.dtype),
            pltpu.VMEM((2,) + shape, tokens.dtype),
            pltpu.SemaphoreType.DMA((8,)),
            pltpu.SemaphoreType.DMA((2, quads)),
            pltpu.SemaphoreType.DMA((2, quads)),
        ],
        compiler_params=ALONE,
    )(spot, tokens, grad_out)


def terms(packed, part):
    quads, cores, rows, both = packed.shape
    cols = both - part

    def body(p_ref, o_ref, stage, total, sems):
        loads = []
        for k in range(quads):
            loads.append(
                pltpu.make_async_copy(p_ref.at[k], stage.at[k], sems.at[k])
            )
            loads[-1].start()
        for k in range(quads):
            loads[k].wait()
            p = stage[k].reshape(cores * rows, both)
            term = lax.dot_general(
                p[:, :part],
                p[:, part:],
                (((0,), (0,)), ((), ())),
                preferred_element_type=jnp.float32,
            )
            if k == 0:
                total[...] = term
            elif k < quads - 1:
                total[...] += term
            else:
                o_ref[...] = (total[...] + term).astype(o_ref.dtype)

    return pl.pallas_call(
        body,
        in_specs=[pl.BlockSpec(memory_space=pl.ANY)],
        out_specs=pl.BlockSpec(memory_space=pltpu.VMEM),
        out_shape=jax.ShapeDtypeStruct((part, cols), packed.dtype),
        scratch_shapes=[
            pltpu.VMEM(packed.shape, packed.dtype),
            pltpu.VMEM((part, cols), jnp.float32),
            pltpu.SemaphoreType.DMA((quads,)),
        ],
        compiler_params=PARAMS,
    )(packed)


def project(packed, weight, spot):
    quads, cores, rows, _ = packed.shape
    part, cols = weight.shape
    steps = 3
    step = part // steps

    def body(spot_ref, t_ref, w_ref, near_ref, away_ref):
        own = spot_ref[1] * 2 + spot_ref[2]
        t = [t_ref[own ^ flip].reshape(cores * rows, step) for flip in range(quads)]
        new = jnp.dot(
            jnp.concatenate(t, axis=0), w_ref[...], preferred_element_type=jnp.float32
        ).reshape(quads, cores, rows, cols)
        k = pl.program_id(0)

        @pl.when(k == 0)
        def _():
            near_ref[...] = new[:2]
            away_ref[...] = new[2:]

        @pl.when(k > 0)
        def _():
            near_ref[...] += new[:2]
            away_ref[...] += new[2:]

    shape = (2, cores, rows, cols)
    half = jax.ShapeDtypeStruct(shape, jnp.float32)
    half_spec = pl.BlockSpec(shape, lambda k, spot: (0, 0, 0, 0))
    return pl.pallas_call(
        body,
        grid_spec=pltpu.PrefetchScalarGridSpec(
            num_scalar_prefetch=1,
            grid=(steps,),
            in_specs=[
                pl.BlockSpec((quads, cores, rows, step), lambda k, spot: (0, 0, 0, k)),
                pl.BlockSpec((step, cols), lambda k, spot: (k, 0)),
            ],
            out_specs=[half_spec, half_spec],
        ),
        out_shape=[half, half],
        compiler_params=PARAMS,
    )(spot, packed, weight)


def partners(sizes):
    yh, cores, yl, xh, xl = sizes
    lines, width = yh * yl, xh * xl

    def place(y, c, x):
        return ((((y // yl) * cores + c) * yl + y % yl) * xh + x // xl) * xl + x % xl

    def other(i, n, c):
        if c == 0:
            return i ^ 1
        return (i + 1) % n if i % 2 else (i - 1) % n

    flip_x, flip_y, squares = [], [], []
    for y in range(lines):
        for c in range(cores):
            for x in range(width):
                flip_x.append((place(y, c, x), place(y, c, other(x, width, c))))
                flip_y.append((place(y, c, x), place(other(y, lines, c), c, x)))
                if y % 2 == 0 and x % 2 == 0:
                    ys, xs = (y, other(y, lines, c)), (x, other(x, width, c))
                    squares.append([place(a, c, b) for a in ys for b in xs])
    return squares, flip_x, flip_y


def local(tokens, weight, grad_out):
    rows, _ = tokens.shape
    shard, cols = weight.shape
    half = shard // 2
    squares, flip_x, flip_y = partners([lax.axis_size(name) for name in CHIP])
    spot = jnp.stack([lax.axis_index(name) for name in ("c", "yl", "xl")])
    spot = spot.astype(jnp.int32)

    keep, send = pack(tokens, grad_out, spot, shard)
    packed = jnp.stack([keep, lax.ppermute(send, "c", SWAP)], axis=1)
    packed = lax.all_to_all(packed, CHIP, 0, 0, axis_index_groups=squares)
    mine = lax.dynamic_slice(weight, (spot[0] * half, 0), (half, cols))
    mine = lax.all_gather(mine, ("xh", "z"), axis=0, tiled=True)
    part = mine.shape[0]
    packed, mine = lax.optimization_barrier((packed, mine))

    term = terms(packed, part).reshape(part // half, half, cols)
    near, away = project(packed, mine, spot)
    away = lax.ppermute(away, CHIP, flip_y)
    term = lax.all_to_all(term, ("xh", "z"), 0, 0)
    summed = jnp.sum(term, axis=0, dtype=jnp.float32)
    near = near + away
    near = near[0] + lax.ppermute(near[1], CHIP, flip_x)
    output = near[0] + lax.ppermute(near[1], "c", SWAP)

    lines = jnp.broadcast_to(summed[None], (lax.axis_size("yh"), half, cols))
    mid = jnp.sum(lax.all_to_all(lines, "yh", 0, 0), axis=0)
    other = lax.ppermute(mid, "c", SWAP)
    first = spot[0] == 0
    weight_grad = jnp.concatenate(
        [jnp.where(first, mid, other), jnp.where(first, other, mid)], axis=0
    )
    return output.astype(jnp.bfloat16), weight_grad


def solution(mesh):
    inner = Mesh(
        mesh.devices.reshape(4, 2, 2, 2, 2, 8), ("yh", "c", "yl", "xh", "xl", "z")
    )
    rows = P(("yh", "c", "yl", "xh", "xl", "z"), None)
    owners = P(("yl", "xh", "xl", "z"), None)
    return jax.shard_map(
        local,
        mesh=inner,
        in_specs=(rows, owners, rows),
        out_specs=(rows, owners),
        check_vma=False,
    )
```

time: 464 us -> 125 us (0.27)
  the two profiles are of different devices: /device:TPU:24 before, /device:TPU:1 now
where the time goes in v7:
time: 125 us; the launch traced here: 124 us
  starting transfers between devices  48.1 us (38%)
  blocking collectives  41.4 us (33%)
  Pallas kernels  13.7 us (11%)
  waiting for transfers between devices  13.4 us (11%)
  other arithmetic  5.8 us (5%)
    all_gather x1, blocking collectives, local(): mine = lax.all_gather(mine, ('xh', 'z'), axis=0, tiled=True)  41.4 us
    ppermute x1, starting transfers between devices, local(): packed = jnp.stack([keep, lax.ppermute(send, 'c', SWAP)], axis=1)  8.79 us
    ppermute x1, starting transfers between devices, local(): other = lax.ppermute(mid, 'c', SWAP)  8 us
    ppermute x1, waiting for transfers between devices, local(): away = lax.ppermute(away, CHIP, flip_y)  7.06 us
    ppermute x1, starting transfers between devices, local(): output = near[0] + lax.ppermute(near[1], 'c', SWAP)  6.98 us
    ppermute x1, starting transfers between devices, local(): near = near[0] + lax.ppermute(near[1], CHIP, flip_x)  6.11 us
    all_to_all x1, starting transfers between devices, local(): mid = jnp.sum(lax.all_to_all(lines, 'yh', 0, 0), axis=0)  5.49 us
    pallas_call x1, Pallas kernels, pack(): pl.pallas_call(body, in_specs=[pl.BlockSpec(memory_space=pltpu.SMEM)] + [...  5.44 us
  transfers between devices with their start and end apart: 8, of which 4 were waited for; matrix products, arithmetic and copies ran while one was open for 1% of the time, Pallas kernels for 3%

profile of v7, /device:TPU:1, one launch (start us, length us, event | category | flops | bytes accessed | tf_op | source)
XLA Modules:
  0.0 124.0 jit_solution(10510305434009570460)
XLA Ops:
  0.6 0.0 copy-start
  0.7 0.6 pad_add_fusion.spot_ref
  1.2 5.4 %shard_map.50 = (bf16[4,128,1792]{2,1,0:T(8,128)(2,1)}, bf16[4,128,1792]{2,1,0:T(8,128)(2,1)}) custom-call(s32[3]{0:T(128)} %pad_add_fusion.spot_ref, bf16[128,12288]{1,0:T(8,128)(2,1)} %t_ref.1, bf16[128,256]{1,0:T(8,128)(2,1)} %g_ref.1), custom_call_target="tpu_custom_call" | custom-call | tf_op jit(solution)/shard_map/pallas_call | solution.py:65
  6.7 8.8 %collective-permute-start = (bf16[4,128,1792]{2,1,0:T(8,128)(2,1)}, bf16[4,128,1792]{2,1,0:T(8,128)(2,1)S(1)}, u32[]{:S(2)}, u32[]{:S(2)}) collective-permute-start(bf16[4,128,1792]{2,1,0:T(8,128)(2,1)} %get-tuple-element.9), channel_id=1, source_target_pairs={{0,64},{64,0},{1,65},{65,1},{2,66},{66,2},{3,67},{67,3},{4,68},{68... | collective-permute-start | bytes 5505032 | tf_op jit(solution)/shard_map/ppermute | solution.py:199
  15.4 3.6 %collective-permute-done = bf16[4,128,1792]{2,1,0:T(8,128)(2,1)S(1)} collective-permute-done((bf16[4,128,1792]{2,1,0:T(8,128)(2,1)}, bf16[4,128,1792]{2,1,0:T(8,128)(2,1)S(1)}, u32[]{:S(2)}, u32[]{:S(2)}) %collective-permute-start) | collective-permute-done | bytes 1835040 | tf_op jit(solution)/shard_map/ppermute | solution.py:199
  19.0 3.7 %pad_maximum_fusion = bf16[4,2,128,1792]{3,2,1,0:T(8,128)(2,1)} fusion(bf16[4,1,128,1792]{3,2,1,0:T(8,128)(2,1)S(1)} %bitcast.21, bf16[4,1,128,1792]{3,2,1,0:T(8,128)(2,1)} %bitcast.20), kind=kLoop, calls=%fused_computation | loop fusion | flops 1835008 | bytes 7340032 | tf_op jit(solution)/shard_map/stack | solution.py:199
  22.7 4.7 %all-to-all-start = ((bf16[4,2,128,1792]{3,2,1,0:T(8,128)(2,1)}), bf16[4,2,128,1792]{3,2,1,0:T(8,128)(2,1)}, u32[]{:S(2)}, u32[]{:S(2)}) async-start(bf16[4,2,128,1792]{3,2,1,0:T(8,128)(2,1)} %pad_maximum_fusion), calls=%async_computation | async-start | bytes 7340032 | tf_op jit(solution)/shard_map/all_to_all | solution.py:200
  27.5 41.4 %all_gather.3.w_ref = bf16[1536,256]{1,0:T(8,128)(2,1)S(1)} all-gather(bf16[96,256]{1,0:T(8,128)(2,1)S(1)} %constant_dynamic-slice_fusion), channel_id=1, replica_groups=mesh['yh'=4,'c'=2,'yl'=2,'xh'=2,'xl'=2,'z'=8] {'xh','z'}, dimensions={0}, use_global_device_ids=true | all-gather | bytes 835584 | tf_op jit(solution)/shard_map/all_gather | solution.py:202
  68.9 4.2 %shard_map.52 = bf16[1536,256]{1,0:T(8,128)(2,1)} custom-call(bf16[4,2,128,1792]{3,2,1,0:T(8,128)(2,1)} %all-to-all-done.t_ref.p_ref), custom_call_target="tpu_custom_call" | custom-call | tf_op jit(solution)/shard_map/pallas_call | solution.py:109
  73.1 3.6 %all-to-all-start.1 = ((bf16[16,96,256]{2,1,0:T(8,128)(2,1)}), bf16[16,96,256]{2,1,0:T(8,128)(2,1)S(1)}, u32[]{:S(2)}, u32[]{:S(2)}) async-start(bf16[16,96,256]{2,1,0:T(8,128)(2,1)} %bitcast.9), calls=%async_computation.1 | async-start | bytes 1572864 | tf_op jit(solution)/shard_map/all_to_all | solution.py:209
  76.7 4.1 %shard_map.51 = (f32[2,2,128,256]{3,2,1,0:T(8,128)S(1)}, f32[2,2,128,256]{3,2,1,0:T(8,128)S(1)}) custom-call(s32[3]{0:T(128)S(1)} %copy-done.1, bf16[4,2,128,1792]{3,2,1,0:T(8,128)(2,1)} %all-to-all-done.t_ref.p_ref, bf16[1536,256]{1,0:T(8,128)(2,1)S(1)} %all_gather.3.w_ref), custom_call_target="tpu_custom_call" | custom-call | tf_op jit(solution)/shard_map/pallas_call | solution.py:150
  80.8 4.4 %collective-permute-start.1 = (f32[2,2,128,256]{3,2,1,0:T(8,128)S(1)}, f32[2,2,128,256]{3,2,1,0:T(8,128)S(1)}, u32[]{:S(2)}, u32[]{:S(2)}) collective-permute-start(f32[2,2,128,256]{3,2,1,0:T(8,128)S(1)} %get-tuple-element.13), channel_id=1, source_target_pairs={{0,32},{8,40},{16,48},{24,56},{64,480},{72,488},{80,496},{88,504},... | collective-permute-start | bytes 1572872 | tf_op jit(solution)/shard_map/ppermute | solution.py:208
  85.1 7.1 %collective-permute-done.1 = f32[2,2,128,256]{3,2,1,0:T(8,128)S(1)} collective-permute-done((f32[2,2,128,256]{3,2,1,0:T(8,128)S(1)}, f32[2,2,128,256]{3,2,1,0:T(8,128)S(1)}, u32[]{:S(2)}, u32[]{:S(2)}) %collective-permute-start.1) | collective-permute-done | bytes 524320 | tf_op jit(solution)/shard_map/ppermute | solution.py:208
  92.2 0.1 add.13
  92.3 6.1 %collective-permute-start.2 = (f32[2,128,256]{2,1,0:T(8,128)S(1)}, f32[2,128,256]{2,1,0:T(8,128)S(1)}, u32[]{:S(2)}, u32[]{:S(2)}) collective-permute-start(f32[2,128,256]{2,1,0:T(8,128)S(1)} %slice_bitcast_fusion), channel_id=1, source_target_pairs={{0,8},{8,0},{16,24},{24,16},{64,88},{72,80},{80,72},{88,64},{32,40... | collective-permute-start | bytes 786440 | tf_op jit(solution)/shard_map/ppermute | solution.py:212
  98.4 0.1 convert_reduce_fusion
  98.5 0.8 broadcast_in_dim.2
  99.3 5.5 %all-to-all-start.2 = ((f32[4,96,256]{2,1,0:T(8,128)}), f32[4,96,256]{2,1,0:T(8,128)S(1)}, u32[]{:S(2)}, u32[]{:S(2)}) async-start(f32[4,96,256]{2,1,0:T(8,128)} %broadcast_in_dim.2), calls=%async_computation.2 | async-start | bytes 786432 | tf_op jit(solution)/shard_map/all_to_all | solution.py:216
  104.9 7.0 %collective-permute-start.3 = (f32[128,256]{1,0:T(8,128)S(1)}, f32[128,256]{1,0:T(8,128)S(1)}, u32[]{:S(2)}, u32[]{:S(2)}) collective-permute-start(f32[128,256]{1,0:T(8,128)S(1)} %slice_bitcast_fusion.2), channel_id=1, source_target_pairs={{0,64},{64,0},{1,65},{65,1},{2,66},{66,2},{3,67},{67,3},{4,68},{68... | collective-permute-start | bytes 393224 | tf_op jit(solution)/shard_map/ppermute | solution.py:213
  111.9 2.5 %all-to-all-done.2 = f32[4,96,256]{2,1,0:T(8,128)S(1)} async-done(((f32[4,96,256]{2,1,0:T(8,128)}), f32[4,96,256]{2,1,0:T(8,128)S(1)}, u32[]{:S(2)}, u32[]{:S(2)}) %all-to-all-start.2) | async-done | bytes 393248 | tf_op jit(solution)/shard_map/all_to_all | solution.py:216
  114.3 8.0 %collective-permute-start.4 = (f32[96,256]{1,0:T(8,128)S(1)}, f32[96,256]{1,0:T(8,128)S(1)}, u32[]{:S(2)}, u32[]{:S(2)}) collective-permute-start(f32[96,256]{1,0:T(8,128)S(1)} %reduce_sum.19), channel_id=1, source_target_pairs={{0,64},{64,0},{1,65},{65,1},{2,66},{66,2},{3,67},{67,3},{4,68},{68... | collective-permute-start | bytes 294920 | tf_op jit(solution)/shard_map/ppermute | solution.py:217
  122.4 0.6 fusion.2
  123.0 0.3 collective-permute-done.4
  123.3 0.7 pad_maximum_fusion.1
  (13 shorter events, 0.1 us)
Async XLA Ops:
  0.6 26.8 %copy-start = (bf16[192,256]{1,0:T(8,128)(2,1)S(1)}, bf16[192,256]{1,0:T(8,128)(2,1)}, u32[]{:S(2)}) copy-start(bf16[192,256]{1,0:T(8,128)(2,1)} %param.4) | copy-start | bytes 294916
  6.7 12.4 %collective-permute-start = (bf16[4,128,1792]{2,1,0:T(8,128)(2,1)}, bf16[4,128,1792]{2,1,0:T(8,128)(2,1)S(1)}, u32[]{:S(2)}, u32[]{:S(2)}) collective-permute-start(bf16[4,128,1792]{2,1,0:T(8,128)(2,1)} %get-tuple-element.9), channel_id=1, source_target_pairs={{0,64},{64,0},{1,65},{65,1},{2,66},{66,2},{3,67},{67,3},{4,68},{68... | collective-permute-start | bytes 5505032 | tf_op jit(solution)/shard_map/ppermute | solution.py:199
  22.7 46.2 %all-to-all-start = ((bf16[4,2,128,1792]{3,2,1,0:T(8,128)(2,1)}), bf16[4,2,128,1792]{3,2,1,0:T(8,128)(2,1)}, u32[]{:S(2)}, u32[]{:S(2)}) async-start(bf16[4,2,128,1792]{3,2,1,0:T(8,128)(2,1)} %pad_maximum_fusion), calls=%async_computation | async-start | bytes 7340032 | tf_op jit(solution)/shard_map/all_to_all | solution.py:200
  68.9 7.8 %copy-start.1 = (s32[3]{0:T(128)S(1)}, s32[3]{0:T(128)}, u32[]{:S(2)}) copy-start(s32[3]{0:T(128)} %pad_add_fusion.spot_ref) | copy-start | bytes 40
  73.1 25.4 %all-to-all-start.1 = ((bf16[16,96,256]{2,1,0:T(8,128)(2,1)}), bf16[16,96,256]{2,1,0:T(8,128)(2,1)S(1)}, u32[]{:S(2)}, u32[]{:S(2)}) async-start(bf16[16,96,256]{2,1,0:T(8,128)(2,1)} %bitcast.9), calls=%async_computation.1 | async-start | bytes 1572864 | tf_op jit(solution)/shard_map/all_to_all | solution.py:209
  80.8 11.4 %collective-permute-start.1 = (f32[2,2,128,256]{3,2,1,0:T(8,128)S(1)}, f32[2,2,128,256]{3,2,1,0:T(8,128)S(1)}, u32[]{:S(2)}, u32[]{:S(2)}) collective-permute-start(f32[2,2,128,256]{3,2,1,0:T(8,128)S(1)} %get-tuple-element.13), channel_id=1, source_target_pairs={{0,32},{8,40},{16,48},{24,56},{64,480},{72,488},{80,496},{88,504},... | collective-permute-start | bytes 1572872 | tf_op jit(solution)/shard_map/ppermute | solution.py:208
  92.3 12.5 %collective-permute-start.2 = (f32[2,128,256]{2,1,0:T(8,128)S(1)}, f32[2,128,256]{2,1,0:T(8,128)S(1)}, u32[]{:S(2)}, u32[]{:S(2)}) collective-permute-start(f32[2,128,256]{2,1,0:T(8,128)S(1)} %slice_bitcast_fusion), channel_id=1, source_target_pairs={{0,8},{8,0},{16,24},{24,16},{64,88},{72,80},{80,72},{88,64},{32,40... | collective-permute-start | bytes 786440 | tf_op jit(solution)/shard_map/ppermute | solution.py:212
  99.3 15.0 %all-to-all-start.2 = ((f32[4,96,256]{2,1,0:T(8,128)}), f32[4,96,256]{2,1,0:T(8,128)S(1)}, u32[]{:S(2)}, u32[]{:S(2)}) async-start(f32[4,96,256]{2,1,0:T(8,128)} %broadcast_in_dim.2), calls=%async_computation.2 | async-start | bytes 786432 | tf_op jit(solution)/shard_map/all_to_all | solution.py:216
  104.9 17.5 %collective-permute-start.3 = (f32[128,256]{1,0:T(8,128)S(1)}, f32[128,256]{1,0:T(8,128)S(1)}, u32[]{:S(2)}, u32[]{:S(2)}) collective-permute-start(f32[128,256]{1,0:T(8,128)S(1)} %slice_bitcast_fusion.2), channel_id=1, source_target_pairs={{0,64},{64,0},{1,65},{65,1},{2,66},{66,2},{3,67},{67,3},{4,68},{68... | collective-permute-start | bytes 393224 | tf_op jit(solution)/shard_map/ppermute | solution.py:213
  114.3 8.9 %collective-permute-start.4 = (f32[96,256]{1,0:T(8,128)S(1)}, f32[96,256]{1,0:T(8,128)S(1)}, u32[]{:S(2)}, u32[]{:S(2)}) collective-permute-start(f32[96,256]{1,0:T(8,128)S(1)} %reduce_sum.19), channel_id=1, source_target_pairs={{0,64},{64,0},{1,65},{65,1},{2,66},{66,2},{3,67},{67,3},{4,68},{68... | collective-permute-start | bytes 294920 | tf_op jit(solution)/shard_map/ppermute | solution.py:217

commit v8 on v7

--- a/solution.py
+++ b/solution.py
@@ -11,7 +11,7 @@
 CHIP = ("yh", "c", "yl", "xh", "xl")
 
 
-def pack(tokens, grad_out, spot, shard):
+def pack(tokens, grad_out, spot, shard, away, after=()):
     rows, width = tokens.shape
     cols = grad_out.shape[1]
     quads = 4
@@ -19,64 +19,93 @@
     part = width // 8
     half = shard // 2
 
-    def body(spot_ref, t_ref, g_ref, keep_ref, send_ref, held, stage, t_sems, g_sems, o_sems):
+    def body(spot_ref, t_ref, g_ref, *refs):
+        o_ref, held, stage, t_sems, g_sems, o_sems = refs[len(after) :]
         loads, sides = [], []
-        for k in range(8):
-            at = pl.ds(k * node, node)
-            copy = pltpu.make_async_copy(t_ref.at[:, at], held.at[:, at], t_sems.at[k])
+        order = [(quad, xh) for quad in range(quads) for xh in range(2)]
+        for n, (quad, xh) in enumerate(order):
+            at = pl.ds(((quad // 2) * 4 + xh * 2 + quad % 2) * node, node)
+            copy = pltpu.make_async_copy(t_ref.at[:, at], held.at[n], t_sems.at[n])
             copy.start()
             loads.append(copy)
-        for side in range(2):
-            for quad in range(quads):
-                copy = pltpu.make_async_copy(
-                    g_ref,
-                    stage.at[side, quad, :, pl.ds(part, cols)],
-                    g_sems.at[side, quad],
+        for quad in range(quads):
+            copy = pltpu.make_async_copy(
+                g_ref, stage.at[quad, :, pl.ds(part, cols)], g_sems.at[quad]
+            )
+            copy.start()
+            sides.append(copy)
+        family = spot_ref[0] ^ 1 if away else spot_ref[0]
+
+        def squeeze(quad, side):
+            for xh in range(2):
+                t = held[quad * 2 + xh]
+                pieces = [
+                    t[:, at + side * half : at + side * half + half]
+                    for at in range(0, node, shard)
+                ]
+                stage[quad, :, xh * node // 2 : (xh + 1) * node // 2] = (
+                    jnp.concatenate(pieces, axis=1)
                 )
-                copy.start()
-                sides.append(copy)
-        for copy in sides:
-            copy.wait()
+
         stores = []
         for quad in range(quads):
-            for xh in range(2):
-                k = (quad // 2) * 4 + xh * 2 + quad % 2
-                loads[k].wait()
-                t = held[:, k * node : (k + 1) * node]
-                for side in range(2):
-                    pieces = [
-                        t[:, at + side * half : at + side * half + half]
-                        for at in range(0, node, shard)
-                    ]
-                    stage[side, quad, :, xh * node // 2 : (xh + 1) * node // 2] = (
-                        jnp.concatenate(pieces, axis=1)
-                    )
-            for n, ref in enumerate((keep_ref, send_ref)):
-                copy = pltpu.make_async_copy(
-                    stage.at[spot_ref[0] ^ n, quad], ref.at[quad], o_sems.at[n, quad]
-                )
-                copy.start()
-                stores.append(copy)
+            loads[2 * quad].wait()
+            loads[2 * quad + 1].wait()
+            sides[quad].wait()
+            for side in range(2):
+                pl.when(family == side)(lambda quad=quad, side=side: squeeze(quad, side))
+            target = o_ref.at[quad] if away else o_ref.at[quad, 0]
+            copy = pltpu.make_async_copy(stage.at[quad], target, o_sems.at[quad])
+            copy.start()
+            stores.append(copy)
         for copy in stores:
             copy.wait()
 
     shape = (quads, rows, part + cols)
-    out = jax.ShapeDtypeStruct(shape, tokens.dtype)
+    whole = shape if away else (quads, 2, rows, part + cols)
     return pl.pallas_call(
         body,
         in_specs=[pl.BlockSpec(memory_space=pltpu.SMEM)]
-        + [pl.BlockSpec(memory_space=pl.ANY)] * 2,
-        out_specs=[pl.BlockSpec(memory_space=pl.ANY)] * 2,
-        out_shape=[out, out],
+        + [pl.BlockSpec(memory_space=pl.ANY)] * (2 + len(after)),
+        out_specs=pl.BlockSpec(memory_space=pl.ANY),
+        out_shape=jax.ShapeDtypeStruct(whole, tokens.dtype),
         scratch_shapes=[
-            pltpu.VMEM(tokens.shape, tokens.dtype),
-            pltpu.VMEM((2,) + shape, tokens.dtype),
+            pltpu.VMEM((8, rows, node), tokens.dtype),
+            pltpu.VMEM(shape, tokens.dtype),
             pltpu.SemaphoreType.DMA((8,)),
-            pltpu.SemaphoreType.DMA((2, quads)),
-            pltpu.SemaphoreType.DMA((2, quads)),
+            pltpu.SemaphoreType.DMA((quads,)),
+            pltpu.SemaphoreType.DMA((quads,)),
         ],
         compiler_params=ALONE,
-    )(spot, tokens, grad_out)
+    )(spot, tokens, grad_out, *after)
+
+
+def insert(packed, received, after):
+    quads = packed.shape[0]
+
+    def body(p_ref, r_ref, after_ref, o_ref, sems):
+        copies = [
+            pltpu.make_async_copy(r_ref.at[q], o_ref.at[q, 1], sems.at[q])
+            for q in range(quads)
+        ]
+        for copy in copies:
+            copy.start()
+        for copy in copies:
+            copy.wait()
+
+    return pl.pallas_call(
+        body,
+        in_specs=[
+            pl.BlockSpec(memory_space=pltpu.HBM),
+            pl.BlockSpec(memory_space=pltpu.VMEM),
+            pl.BlockSpec(memory_space=pl.ANY),
+        ],
+        out_specs=pl.BlockSpec(memory_space=pltpu.HBM),
+        out_shape=jax.ShapeDtypeStruct(packed.shape, packed.dtype),
+        scratch_shapes=[pltpu.SemaphoreType.DMA((quads,))],
+        input_output_aliases={0: 0},
+        compiler_params=pltpu.CompilerParams(vmem_limit_bytes=57 * 1024 * 1024),
+    )(packed, received, after)
 
 
 def terms(packed, part):
@@ -122,15 +151,16 @@
 
 def project(packed, weight, spot):
     quads, cores, rows, _ = packed.shape
-    part, cols = weight.shape
-    steps = 3
-    step = part // steps
+    depth, steps, _, half, cols = weight.shape
+    step = depth * half
 
     def body(spot_ref, t_ref, w_ref, near_ref, away_ref):
         own = spot_ref[1] * 2 + spot_ref[2]
         t = [t_ref[own ^ flip].reshape(cores * rows, step) for flip in range(quads)]
         new = jnp.dot(
-            jnp.concatenate(t, axis=0), w_ref[...], preferred_element_type=jnp.float32
+            jnp.concatenate(t, axis=0),
+            w_ref[...].reshape(step, cols),
+            preferred_element_type=jnp.float32,
         ).reshape(quads, cores, rows, cols)
         k = pl.program_id(0)
 
@@ -145,8 +175,8 @@
             away_ref[...] += new[2:]
 
     shape = (2, cores, rows, cols)
-    half = jax.ShapeDtypeStruct(shape, jnp.float32)
-    half_spec = pl.BlockSpec(shape, lambda k, spot: (0, 0, 0, 0))
+    out = jax.ShapeDtypeStruct(shape, jnp.float32)
+    out_spec = pl.BlockSpec(shape, lambda k, spot: (0, 0, 0, 0))
     return pl.pallas_call(
         body,
         grid_spec=pltpu.PrefetchScalarGridSpec(
@@ -154,11 +184,14 @@
             grid=(steps,),
             in_specs=[
                 pl.BlockSpec((quads, cores, rows, step), lambda k, spot: (0, 0, 0, k)),
-                pl.BlockSpec((step, cols), lambda k, spot: (k, 0)),
+                pl.BlockSpec(
+                    (depth, 1, 1, half, cols),
+                    lambda k, spot: (0, k ^ spot[3], spot[0], 0, 0),
+                ),
             ],
-            out_specs=[half_spec, half_spec],
+            out_specs=[out_spec, out_spec],
         ),
-        out_shape=[half, half],
+        out_shape=[out, out],
         compiler_params=PARAMS,
     )(spot, packed, weight)
 
@@ -192,29 +225,34 @@
     shard, cols = weight.shape
     half = shard // 2
     squares, flip_x, flip_y = partners([lax.axis_size(name) for name in CHIP])
-    spot = jnp.stack([lax.axis_index(name) for name in ("c", "yl", "xl")])
+    spot = jnp.stack([lax.axis_index(name) for name in ("c", "yl", "xl", "xh")])
     spot = spot.astype(jnp.int32)
 
-    keep, send = pack(tokens, grad_out, spot, shard)
-    packed = jnp.stack([keep, lax.ppermute(send, "c", SWAP)], axis=1)
+    mine = jnp.stack([weight, lax.ppermute(weight, "xh", SWAP)])
+    send = pack(tokens, grad_out, spot, shard, True)
+    packed = pack(tokens, grad_out, spot, shard, False, (send,))
+    packed = insert(packed, lax.ppermute(send, "c", SWAP), mine)
     packed = lax.all_to_all(packed, CHIP, 0, 0, axis_index_groups=squares)
-    mine = lax.dynamic_slice(weight, (spot[0] * half, 0), (half, cols))
-    mine = lax.all_gather(mine, ("xh", "z"), axis=0, tiled=True)
-    part = mine.shape[0]
-    packed, mine = lax.optimization_barrier((packed, mine))
+    part = packed.shape[-1] - cols
+
+    mine = lax.all_gather(mine, "z", axis=0)
+    mine = mine.reshape(mine.shape[:2] + (2, half, cols))
 
     term = terms(packed, part).reshape(part // half, half, cols)
+    term, mine = lax.optimization_barrier((term, mine))
     near, away = project(packed, mine, spot)
     away = lax.ppermute(away, CHIP, flip_y)
     term = lax.all_to_all(term, ("xh", "z"), 0, 0)
     summed = jnp.sum(term, axis=0, dtype=jnp.float32)
+    near, _ = lax.optimization_barrier((near, summed))
     near = near + away
     near = near[0] + lax.ppermute(near[1], CHIP, flip_x)
-    output = near[0] + lax.ppermute(near[1], "c", SWAP)
 
     lines = jnp.broadcast_to(summed[None], (lax.axis_size("yh"), half, cols))
     mid = jnp.sum(lax.all_to_all(lines, "yh", 0, 0), axis=0)
     other = lax.ppermute(mid, "c", SWAP)
+    near, _ = lax.optimization_barrier((near, mid))
+    output = near[0] + lax.ppermute(near[1], "c", SWAP)
     first = spot[0] == 0
     weight_grad = jnp.concatenate(
         [jnp.where(first, mid, other), jnp.where(first, other, mid)], axis=0

time: 125 us -> 142 us (1.14)
  blocking collectives: 41.4 us -> 0 us
  waiting for transfers between devices: 13.4 us -> 54.1 us
  between operations: 0.81 us -> 14.2 us
  Pallas kernels: 13.7 us -> 18.6 us
  other arithmetic: 5.8 us -> 2.91 us
  local copies, waits for them, and re-layouts: 0.83 us -> 3.49 us
    all_gather x1 -> x0, blocking collectives: 41.4 us -> none  [local(): mine = lax.all_gather(mine, ('xh', 'z'), axis=0, tiled=True)]
    all_to_all x1, waiting for transfers between devices: 0.01 us -> 23.1 us  [local(): packed = lax.all_to_all(packed, CHIP, 0, 0, axis_index_groups=squares)]
    all_gather x0 -> x1, waiting for transfers between devices: none -> 14.4 us  [local(): mine = lax.all_gather(mine, 'z', axis=0)]
    ppermute x1, waiting for transfers between devices: 7.06 us -> 0.01 us  [local(): away = lax.ppermute(away, CHIP, flip_y)]
    all_to_all x1, waiting for transfers between devices: 0.01 us -> 6.83 us  [local(): term = lax.all_to_all(term, ('xh', 'z'), 0, 0)]
    ppermute x1, waiting for transfers between devices: 0.01 us -> 6.33 us  [local(): near = near[0] + lax.ppermute(near[1], CHIP, flip_x)]
    ppermute x1, starting transfers between devices: 6.98 us -> 1.92 us  [local(): output = near[0] + lax.ppermute(near[1], 'c', SWAP)]
    ppermute x1, starting transfers between devices: 6.11 us -> 1.98 us  [local(): near = near[0] + lax.ppermute(near[1], CHIP, flip_x)]
  transfers between devices with their start and end apart: 8 -> 10, of which waited for: 4 -> 7; matrix products, arithmetic and copies ran while one was open for 1% -> 2% of each run, Pallas kernels for 3% -> 8%
where the time goes in v8:
time: 142 us; the launch traced here: 141 us
  waiting for transfers between devices  54.1 us (38%)
  starting transfers between devices  47.9 us (34%)
  Pallas kernels  18.6 us (13%)
  between operations  14.2 us (10%)
  local copies, waits for them, and re-layouts  3.49 us (2%)
  other arithmetic  2.91 us (2%)
    all_to_all x1, waiting for transfers between devices, local(): packed = lax.all_to_all(packed, CHIP, 0, 0, axis_index_groups=squares)  23.1 us
    all_gather x1, waiting for transfers between devices, local(): mine = lax.all_gather(mine, 'z', axis=0)  14.4 us
    ppermute x1, starting transfers between devices, local(): other = lax.ppermute(mid, 'c', SWAP)  11.3 us
    ppermute x1, starting transfers between devices, local(): packed = insert(packed, lax.ppermute(send, 'c', SWAP), mine)  8.79 us
    pallas_call x2, Pallas kernels, pack(): pl.pallas_call(body, in_specs=[pl.BlockSpec(memory_space=pltpu.SMEM)] + [...  8.28 us
    all_to_all x1, waiting for transfers between devices, local(): term = lax.all_to_all(term, ('xh', 'z'), 0, 0)  6.83 us
    all_to_all x1, starting transfers between devices, local(): mid = jnp.sum(lax.all_to_all(lines, 'yh', 0, 0), axis=0)  6.46 us
    all_to_all x1, starting transfers between devices, local(): term = lax.all_to_all(term, ('xh', 'z'), 0, 0)  6.34 us
  transfers between devices with their start and end apart: 10, of which 7 were waited for; matrix products, arithmetic and copies ran while one was open for 2% of the time, Pallas kernels for 8%

profile of v8, /device:TPU:1, one launch (start us, length us, event | category | flops | bytes accessed | tf_op | source)
XLA Modules:
  0.0 141.2 jit_solution(12983525780178896224)
XLA Ops:
  7.8 4.1 %shard_map.50.refs_0_ = bf16[4,128,1792]{2,1,0:T(8,128)(2,1)} custom-call(s32[4]{0:T(128)} %pad_add_fusion.spot_ref, bf16[128,12288]{1,0:T(8,128)(2,1)} %t_ref.3, bf16[128,256]{1,0:T(8,128)(2,1)} %g_ref.3), custom_call_target="tpu_custom_call" | custom-call | tf_op jit(solution)/shard_map/pallas_call | solution.py:66
  12.0 8.8 %collective-permute-start = (bf16[4,128,1792]{2,1,0:T(8,128)(2,1)}, bf16[4,128,1792]{2,1,0:T(8,128)(2,1)S(1)}, u32[]{:S(2)}, u32[]{:S(2)}) collective-permute-start(bf16[4,128,1792]{2,1,0:T(8,128)(2,1)} %shard_map.50.refs_0_), channel_id=1, source_target_pairs={{0,64},{64,0},{1,65},{65,1},{2,66},{66,2},{3,67},{67,3},{4,68},{68... | collective-permute-start | bytes 5505032 | tf_op jit(solution)/shard_map/ppermute | solution.py:234
  20.8 1.9 %collective-permute-start.1 = (bf16[192,256]{1,0:T(8,128)(2,1)S(1)}, bf16[192,256]{1,0:T(8,128)(2,1)S(1)}, u32[]{:S(2)}, u32[]{:S(2)}) collective-permute-start(bf16[192,256]{1,0:T(8,128)(2,1)S(1)} %copy-done.3), channel_id=1, source_target_pairs={{0,16},{16,0},{1,17},{17,1},{2,18},{18,2},{3,19},{19,3},{4,20},{20... | collective-permute-start | bytes 294920 | tf_op jit(solution)/shard_map/ppermute | solution.py:231
  22.7 4.1 %shard_map.51.p_ref = bf16[4,2,128,1792]{3,2,1,0:T(8,128)(2,1)} custom-call(s32[4]{0:T(128)} %pad_add_fusion.spot_ref, bf16[128,12288]{1,0:T(8,128)(2,1)} %t_ref.3, bf16[128,256]{1,0:T(8,128)(2,1)} %g_ref.3, bf16[4,128,1792]{2,1,0:T(8,128)(2,1)} %shard_map.50.refs_0_), custom_call_target="tpu_custom_call" | custom-call | tf_op jit(solution)/shard_map/pallas_call | solution.py:66
  26.8 1.7 %collective-permute-done.1 = bf16[192,256]{1,0:T(8,128)(2,1)S(1)} collective-permute-done((bf16[192,256]{1,0:T(8,128)(2,1)S(1)}, bf16[192,256]{1,0:T(8,128)(2,1)S(1)}, u32[]{:S(2)}, u32[]{:S(2)}) %collective-permute-start.1) | collective-permute-done | bytes 98336 | tf_op jit(solution)/shard_map/ppermute | solution.py:231
  28.6 0.7 pad_maximum_fusion.after_ref
  29.3 1.3 copy-done.2
  30.5 2.8 %shard_map.52 = bf16[4,2,128,1792]{3,2,1,0:T(8,128)(2,1)} custom-call(bf16[4,2,128,1792]{3,2,1,0:T(8,128)(2,1)} %shard_map.51.p_ref, bf16[4,128,1792]{2,1,0:T(8,128)(2,1)} %copy-done.2, bf16[2,192,256]{2,1,0:T(8,128)(2,1)} %pad_maximum_fusion.after_ref), custom_call_target="tpu_custom_call", output_to_operand_aliasing={{}: (0, {})} | custom-call | tf_op jit(solution)/shard_map/pallas_call | solution.py:96
  33.3 4.8 %all-to-all-start = ((bf16[4,2,128,1792]{3,2,1,0:T(8,128)(2,1)}), bf16[4,2,128,1792]{3,2,1,0:T(8,128)(2,1)}, u32[]{:S(2)}, u32[]{:S(2)}) async-start(bf16[4,2,128,1792]{3,2,1,0:T(8,128)(2,1)} %shard_map.52), calls=%async_computation | async-start | bytes 7340032 | tf_op jit(solution)/shard_map/all_to_all | solution.py:235
  38.9 23.1 %all-to-all-done.p_ref.t_ref = bf16[4,2,128,1792]{3,2,1,0:T(8,128)(2,1)} async-done(((bf16[4,2,128,1792]{3,2,1,0:T(8,128)(2,1)}), bf16[4,2,128,1792]{3,2,1,0:T(8,128)(2,1)}, u32[]{:S(2)}, u32[]{:S(2)}) %all-to-all-start) | async-done | bytes 3670048 | tf_op jit(solution)/shard_map/all_to_all | solution.py:235
  62.0 4.2 %shard_map.53 = bf16[1536,256]{1,0:T(8,128)(2,1)} custom-call(bf16[4,2,128,1792]{3,2,1,0:T(8,128)(2,1)} %all-to-all-done.p_ref.t_ref), custom_call_target="tpu_custom_call" | custom-call | tf_op jit(solution)/shard_map/pallas_call | solution.py:138
  66.2 14.4 %all-gather.3.cloned.1.call-done = bf16[16,192,256]{2,1,0:T(8,128)(2,1)} async-done(((bf16[2,192,256]{2,1,0:T(8,128)(2,1)}), bf16[16,192,256]{2,1,0:T(8,128)(2,1)}) %all-gather.3.cloned.1.call-update) | async-done | bytes 1572880 | tf_op jit(solution)/shard_map/all_gather | solution.py:238
  80.6 6.3 %all-to-all-start.1 = ((bf16[16,96,256]{2,1,0:T(8,128)(2,1)}), bf16[16,96,256]{2,1,0:T(8,128)(2,1)S(1)}, u32[]{:S(2)}, u32[]{:S(2)}) async-start(bf16[16,96,256]{2,1,0:T(8,128)(2,1)} %bitcast.6), calls=%async_computation.1 | async-start | bytes 1572864 | tf_op jit(solution)/shard_map/all_to_all | solution.py:245
  87.0 1.4 copy-done
  88.4 3.3 %shard_map.54 = (f32[2,2,128,256]{3,2,1,0:T(8,128)S(1)}, f32[2,2,128,256]{3,2,1,0:T(8,128)S(1)}) custom-call(s32[4]{0:T(128)S(1)} %copy-done.1, bf16[4,2,128,1792]{3,2,1,0:T(8,128)(2,1)} %all-to-all-done.p_ref.t_ref, bf16[8,2,2,96,256]{4,3,2,1,0:T(8,128)(2,1)S(1)} %bitcast.20), custom_call_target="tpu_custom_call" | custom-call | tf_op jit(solution)/shard_map/pallas_call | solution.py:180
  91.7 4.5 %collective-permute-start.2 = (f32[2,2,128,256]{3,2,1,0:T(8,128)S(1)}, f32[2,2,128,256]{3,2,1,0:T(8,128)S(1)}, u32[]{:S(2)}, u32[]{:S(2)}) collective-permute-start(f32[2,2,128,256]{3,2,1,0:T(8,128)S(1)} %get-tuple-element.12), channel_id=1, source_target_pairs={{0,32},{8,40},{16,48},{24,56},{64,480},{72,488},{80,496},{88,504},... | collective-permute-start | bytes 1572872 | tf_op jit(solution)/shard_map/ppermute | solution.py:244
  96.2 6.8 %all-to-all-done.1 = bf16[16,96,256]{2,1,0:T(8,128)(2,1)S(1)} async-done(((bf16[16,96,256]{2,1,0:T(8,128)(2,1)}), bf16[16,96,256]{2,1,0:T(8,128)(2,1)S(1)}, u32[]{:S(2)}, u32[]{:S(2)}) %all-to-all-start.1) | async-done | bytes 786464 | tf_op jit(solution)/shard_map/all_to_all | solution.py:245
  103.1 0.8 broadcast_in_dim.2
  103.9 6.5 %all-to-all-start.2 = ((f32[4,96,256]{2,1,0:T(8,128)}), f32[4,96,256]{2,1,0:T(8,128)S(1)}, u32[]{:S(2)}, u32[]{:S(2)}) async-start(f32[4,96,256]{2,1,0:T(8,128)} %broadcast_in_dim.2), calls=%async_computation.2 | async-start | bytes 786432 | tf_op jit(solution)/shard_map/all_to_all | solution.py:252
  110.4 2.0 %collective-permute-start.3 = (f32[2,128,256]{2,1,0:T(8,128)S(1)}, f32[2,128,256]{2,1,0:T(8,128)S(1)}, u32[]{:S(2)}, u32[]{:S(2)}) collective-permute-start(f32[2,128,256]{2,1,0:T(8,128)S(1)} %slice_bitcast_fusion), channel_id=1, source_target_pairs={{0,8},{8,0},{16,24},{24,16},{64,88},{72,80},{80,72},{88,64},{32,40... | collective-permute-start | bytes 786440 | tf_op jit(solution)/shard_map/ppermute | solution.py:249
  112.4 6.3 %collective-permute-done.3 = f32[2,128,256]{2,1,0:T(8,128)S(1)} collective-permute-done((f32[2,128,256]{2,1,0:T(8,128)S(1)}, f32[2,128,256]{2,1,0:T(8,128)S(1)}, u32[]{:S(2)}, u32[]{:S(2)}) %collective-permute-start.3) | collective-permute-done | bytes 262176 | tf_op jit(solution)/shard_map/ppermute | solution.py:249
  119.2 11.3 %collective-permute-start.5 = (f32[96,256]{1,0:T(8,128)S(1)}, f32[96,256]{1,0:T(8,128)S(1)}, u32[]{:S(2)}, u32[]{:S(2)}) collective-permute-start(f32[96,256]{1,0:T(8,128)S(1)} %reduce_sum.19), channel_id=1, source_target_pairs={{0,64},{64,0},{1,65},{65,1},{2,66},{66,2},{3,67},{67,3},{4,68},{68... | collective-permute-start | bytes 294920 | tf_op jit(solution)/shard_map/ppermute | solution.py:253
  130.5 1.9 %collective-permute-start.4 = (f32[128,256]{1,0:T(8,128)S(1)}, f32[128,256]{1,0:T(8,128)S(1)}, u32[]{:S(2)}, u32[]{:S(2)}) collective-permute-start(f32[128,256]{1,0:T(8,128)S(1)} %slice_bitcast_fusion.2), channel_id=1, source_target_pairs={{0,64},{64,0},{1,65},{65,1},{2,66},{66,2},{3,67},{67,3},{4,68},{68... | collective-permute-start | bytes 393224 | tf_op jit(solution)/shard_map/ppermute | solution.py:255
  132.5 0.7 pad_maximum_fusion.1
  (22 shorter events, 3.2 us)
Async XLA Ops:
  7.2 13.6 %copy-start.3 = (bf16[192,256]{1,0:T(8,128)(2,1)S(1)}, bf16[192,256]{1,0:T(8,128)(2,1)}, u32[]{:S(2)}) copy-start(bf16[192,256]{1,0:T(8,128)(2,1)} %param.4) | copy-start | bytes 294916
  12.0 17.3 %collective-permute-start = (bf16[4,128,1792]{2,1,0:T(8,128)(2,1)}, bf16[4,128,1792]{2,1,0:T(8,128)(2,1)S(1)}, u32[]{:S(2)}, u32[]{:S(2)}) collective-permute-start(bf16[4,128,1792]{2,1,0:T(8,128)(2,1)} %shard_map.50.refs_0_), channel_id=1, source_target_pairs={{0,64},{64,0},{1,65},{65,1},{2,66},{66,2},{3,67},{67,3},{4,68},{68... | collective-permute-start | bytes 5505032 | tf_op jit(solution)/shard_map/ppermute | solution.py:234
  20.8 7.8 %collective-permute-start.1 = (bf16[192,256]{1,0:T(8,128)(2,1)S(1)}, bf16[192,256]{1,0:T(8,128)(2,1)S(1)}, u32[]{:S(2)}, u32[]{:S(2)}) collective-permute-start(bf16[192,256]{1,0:T(8,128)(2,1)S(1)} %copy-done.3), channel_id=1, source_target_pairs={{0,16},{16,0},{1,17},{17,1},{2,18},{18,2},{3,19},{19,3},{4,20},{20... | collective-permute-start | bytes 294920 | tf_op jit(solution)/shard_map/ppermute | solution.py:231
  29.3 1.3 copy-start.2
  33.3 28.6 %all-to-all-start = ((bf16[4,2,128,1792]{3,2,1,0:T(8,128)(2,1)}), bf16[4,2,128,1792]{3,2,1,0:T(8,128)(2,1)}, u32[]{:S(2)}, u32[]{:S(2)}) async-start(bf16[4,2,128,1792]{3,2,1,0:T(8,128)(2,1)} %shard_map.52), calls=%async_computation | async-start | bytes 7340032 | tf_op jit(solution)/shard_map/all_to_all | solution.py:235
  38.1 48.8 %copy-start.1 = (s32[4]{0:T(128)S(1)}, s32[4]{0:T(128)}, u32[]{:S(2)}) copy-start(s32[4]{0:T(128)} %pad_add_fusion.spot_ref) | copy-start | bytes 52
  38.1 42.5 %all-gather.3.cloned.1.call-start = ((), (), s32[]{:S(2)}) async-start(), calls=%async_computation.3 | async-start | bytes 1769472 | tf_op jit(solution)/shard_map/all_gather | solution.py:238
  80.6 22.4 %all-to-all-start.1 = ((bf16[16,96,256]{2,1,0:T(8,128)(2,1)}), bf16[16,96,256]{2,1,0:T(8,128)(2,1)S(1)}, u32[]{:S(2)}, u32[]{:S(2)}) async-start(bf16[16,96,256]{2,1,0:T(8,128)(2,1)} %bitcast.6), calls=%async_computation.1 | async-start | bytes 1572864 | tf_op jit(solution)/shard_map/all_to_all | solution.py:245
  87.0 1.4 copy-start
  91.7 18.6 %collective-permute-start.2 = (f32[2,2,128,256]{3,2,1,0:T(8,128)S(1)}, f32[2,2,128,256]{3,2,1,0:T(8,128)S(1)}, u32[]{:S(2)}, u32[]{:S(2)}) collective-permute-start(f32[2,2,128,256]{3,2,1,0:T(8,128)S(1)} %get-tuple-element.12), channel_id=1, source_target_pairs={{0,32},{8,40},{16,48},{24,56},{64,480},{72,488},{80,496},{88,504},... | collective-permute-start | bytes 1572872 | tf_op jit(solution)/shard_map/ppermute | solution.py:244
  103.9 15.3 %all-to-all-start.2 = ((f32[4,96,256]{2,1,0:T(8,128)}), f32[4,96,256]{2,1,0:T(8,128)S(1)}, u32[]{:S(2)}, u32[]{:S(2)}) async-start(f32[4,96,256]{2,1,0:T(8,128)} %broadcast_in_dim.2), calls=%async_computation.2 | async-start | bytes 786432 | tf_op jit(solution)/shard_map/all_to_all | solution.py:252
  110.4 8.3 %collective-permute-start.3 = (f32[2,128,256]{2,1,0:T(8,128)S(1)}, f32[2,128,256]{2,1,0:T(8,128)S(1)}, u32[]{:S(2)}, u32[]{:S(2)}) collective-permute-start(f32[2,128,256]{2,1,0:T(8,128)S(1)} %slice_bitcast_fusion), channel_id=1, source_target_pairs={{0,8},{8,0},{16,24},{24,16},{64,88},{72,80},{80,72},{88,64},{32,40... | collective-permute-start | bytes 786440 | tf_op jit(solution)/shard_map/ppermute | solution.py:249
  119.2 13.2 %collective-permute-start.5 = (f32[96,256]{1,0:T(8,128)S(1)}, f32[96,256]{1,0:T(8,128)S(1)}, u32[]{:S(2)}, u32[]{:S(2)}) collective-permute-start(f32[96,256]{1,0:T(8,128)S(1)} %reduce_sum.19), channel_id=1, source_target_pairs={{0,64},{64,0},{1,65},{65,1},{2,66},{66,2},{3,67},{67,3},{4,68},{68... | collective-permute-start | bytes 294920 | tf_op jit(solution)/shard_map/ppermute | solution.py:253
  130.5 3.2 %collective-permute-start.4 = (f32[128,256]{1,0:T(8,128)S(1)}, f32[128,256]{1,0:T(8,128)S(1)}, u32[]{:S(2)}, u32[]{:S(2)}) collective-permute-start(f32[128,256]{1,0:T(8,128)S(1)} %slice_bitcast_fusion.2), channel_id=1, source_target_pairs={{0,64},{64,0},{1,65},{65,1},{2,66},{66,2},{3,67},{67,3},{4,68},{68... | collective-permute-start | bytes 393224 | tf_op jit(solution)/shard_map/ppermute | solution.py:255
Sparse Core Ops, SparseCore 0:
  41.6 38.9 all-gather.2

commit v9 on v6

v9 whole, which is shorter than its diff:
```python
import jax
import jax.numpy as jnp
from jax import lax
from jax.experimental import pallas as pl
from jax.experimental.pallas import tpu as pltpu
from jax.sharding import Mesh, PartitionSpec as P

PARAMS = pltpu.CompilerParams(vmem_limit_bytes=32 * 1024 * 1024)
ALONE = pltpu.CompilerParams(vmem_limit_bytes=60 * 1024 * 1024)
SWAP = [(0, 1), (1, 0)]
CHIP = ("yh", "c", "yl", "xh", "xl")


def pack(tokens, grad_out):
    rows, width = tokens.shape
    cols = grad_out.shape[1]
    quads, node = 4, width // 8

    def body(t_ref, g_ref, o_ref, stage, t_sems, g_sems, o_sems):
        loads, stores = [], []
        for quad in range(quads):
            group = []
            for xh in range(2):
                at = ((quad // 2) * 4 + xh * 2 + quad % 2) * node
                group.append(
                    pltpu.make_async_copy(
                        t_ref.at[:, pl.ds(at, node)],
                        stage.at[quad, :, pl.ds(xh * node, node)],
                        t_sems.at[quad, xh],
                    )
                )
            group.append(
                pltpu.make_async_copy(
                    g_ref, stage.at[quad, :, pl.ds(2 * node, cols)], g_sems.at[quad]
                )
            )
            loads.append(group)
            stores.append(
                pltpu.make_async_copy(stage.at[quad], o_ref.at[quad], o_sems.at[quad])
            )
        for group in loads:
            for copy in group:
                copy.start()
        for group, store in zip(loads, stores):
            for copy in group:
                copy.wait()
            store.start()
        for store in stores:
            store.wait()

    shape = (quads, rows, 2 * node + cols)
    return pl.pallas_call(
        body,
        in_specs=[pl.BlockSpec(memory_space=pl.ANY)] * 2,
        out_specs=pl.BlockSpec(memory_space=pl.ANY),
        out_shape=jax.ShapeDtypeStruct(shape, tokens.dtype),
        scratch_shapes=[
            pltpu.VMEM(shape, tokens.dtype),
            pltpu.SemaphoreType.DMA((quads, 2)),
            pltpu.SemaphoreType.DMA((quads,)),
            pltpu.SemaphoreType.DMA((quads,)),
        ],
        compiler_params=ALONE,
    )(tokens, grad_out)


def terms(packed, spot, part):
    sharers, rows, both = packed.shape
    cols = both - part
    wide = cols // 2
    step = 2
    steps = sharers // step

    def body(spot_ref, p_ref, keep_ref, send_ref, stage, sems):
        loads = []
        for k in range(steps):
            at = pl.ds(k * step, step)
            loads.append(
                pltpu.make_async_copy(p_ref.at[at], stage.at[at], sems.at[k])
            )
            loads[-1].start()
        first = spot_ref[0] == 0
        for k in range(steps):
            loads[k].wait()
            p = stage[k * step : (k + 1) * step].reshape(step * rows, both)
            left, right = p[:, part : part + wide], p[:, part + wide :]
            g = jnp.concatenate(
                [jnp.where(first, left, right), jnp.where(first, right, left)], axis=1
            )
            term = lax.dot_general(
                p[:, :part],
                g,
                (((0,), (0,)), ((), ())),
                preferred_element_type=jnp.float32,
            )
            if k == 0:
                keep_ref[...] = term[:, :wide]
                send_ref[...] = term[:, wide:]
            else:
                keep_ref[...] += term[:, :wide]
                send_ref[...] += term[:, wide:]

    half = jax.ShapeDtypeStruct((part, wide), jnp.float32)
    return pl.pallas_call(
        body,
        in_specs=[
            pl.BlockSpec(memory_space=pltpu.SMEM),
            pl.BlockSpec(memory_space=pl.ANY),
        ],
        out_specs=[pl.BlockSpec(memory_space=pltpu.VMEM)] * 2,
        out_shape=[half, half],
        scratch_shapes=[
            pltpu.VMEM(packed.shape, packed.dtype),
            pltpu.SemaphoreType.DMA((steps,)),
        ],
        compiler_params=PARAMS,
    )(spot, packed)


def project(packed, mine, other, spot):
    quads, rows, both = packed.shape
    depth, xhs, shard, wide = mine.shape
    part, cols = depth * xhs * shard, 2 * wide

    def body(spot_ref, p_ref, m_ref, r_ref, near_ref, away_ref, stage, whole, sems):
        core, yl, xl, xh, z = (spot_ref[i] for i in range(5))
        loads = []
        for flip in range(quads):
            loads.append(
                pltpu.make_async_copy(
                    p_ref.at[(yl * 2 + xl) ^ flip], stage.at[flip], sems.at[flip]
                )
            )
            loads[-1].start()
        for back in range(depth):
            at_z = lax.rem(z + depth - back, depth)
            for slot in range(xhs):
                left = jnp.where(core == 0, m_ref[back, slot], r_ref[back, slot])
                right = jnp.where(core == 0, r_ref[back, slot], m_ref[back, slot])
                whole[xh ^ slot, at_z] = jnp.concatenate([left, right], axis=1)
        for load in loads:
            load.wait()
        t = stage[...].reshape(quads * rows, both)[:, :part]
        new = jnp.dot(
            t, whole[...].reshape(part, cols), preferred_element_type=jnp.float32
        ).reshape(quads, rows, cols)
        near_ref[...] = new[:2]
        away_ref[...] = new[2:]

    out = jax.ShapeDtypeStruct((2, rows, cols), jnp.float32)
    return pl.pallas_call(
        body,
        in_specs=[
            pl.BlockSpec(memory_space=pltpu.SMEM),
            pl.BlockSpec(memory_space=pl.ANY),
            pl.BlockSpec(memory_space=pltpu.VMEM),
            pl.BlockSpec(memory_space=pltpu.VMEM),
        ],
        out_specs=[pl.BlockSpec(memory_space=pltpu.VMEM)] * 2,
        out_shape=[out, out],
        scratch_shapes=[
            pltpu.VMEM(packed.shape, packed.dtype),
            pltpu.VMEM((xhs, depth, shard, cols), mine.dtype),
            pltpu.SemaphoreType.DMA((quads,)),
        ],
        compiler_params=PARAMS,
    )(spot, packed, mine, other)


def partners(sizes):
    yh, cores, yl, xh, xl = sizes
    lines, width = yh * yl, xh * xl

    def place(y, c, x):
        return ((((y // yl) * cores + c) * yl + y % yl) * xh + x // xl) * xl + x % xl

    def other(i, n, c):
        if c == 0:
            return i ^ 1
        return (i + 1) % n if i % 2 else (i - 1) % n

    flip_x, flip_y, squares = [], [], []
    for y in range(lines):
        for c in range(cores):
            for x in range(width):
                flip_x.append((place(y, c, x), place(y, c, other(x, width, c))))
                flip_y.append((place(y, c, x), place(other(y, lines, c), c, x)))
                if y % 2 == 0 and x % 2 == 0:
                    ys, xs = (y, other(y, lines, c)), (x, other(x, width, c))
                    squares.append([place(a, c, b) for a in ys for b in xs])
    return squares, flip_x, flip_y


def local(tokens, weight, grad_out):
    shard, cols = weight.shape
    wide = cols // 2
    depth = lax.axis_size("z")
    squares, flip_x, flip_y = partners([lax.axis_size(name) for name in CHIP])
    spot = jnp.stack([lax.axis_index(name) for name in ("c", "yl", "xl", "xh", "z")])
    spot = spot.astype(jnp.int32)

    mine = jnp.where(spot[0] == 0, weight[:, :wide], weight[:, wide:])
    mine = jnp.stack([mine, lax.ppermute(mine, "xh", SWAP)])
    packed = pack(tokens, grad_out)
    packed = lax.all_to_all(packed, CHIP, 0, 0, axis_index_groups=squares)
    part = packed.shape[-1] - cols
    gathered = [mine]
    for back in range(1, depth):
        shift = [(i, (i + back) % depth) for i in range(depth)]
        gathered.append(lax.ppermute(mine, "z", shift))
    packed, *gathered = lax.optimization_barrier((packed, *gathered))

    keep, send = terms(packed, spot, part)
    term = (keep + lax.ppermute(send, "c", SWAP)).astype(jnp.bfloat16)
    mine = jnp.stack(gathered)
    mine, _ = lax.optimization_barrier((mine, send))
    other = lax.ppermute(mine, "c", SWAP)
    term = lax.all_to_all(term.reshape(-1, shard, wide), ("xh", "z"), 0, 0)
    summed = jnp.sum(term, axis=0, dtype=jnp.float32)

    near, away = project(packed, mine, other, spot)
    away = lax.ppermute(away, CHIP, flip_y)
    near, _ = lax.optimization_barrier((near, summed))
    near = near + away
    output = near[0] + lax.ppermute(near[1], CHIP, flip_x)

    lines = jnp.broadcast_to(summed[None], (lax.axis_size("yh"), shard, wide))
    half = jnp.sum(lax.all_to_all(lines, "yh", 0, 0), axis=0)
    other = lax.ppermute(half, "c", SWAP)
    first = spot[0] == 0
    weight_grad = jnp.concatenate(
        [jnp.where(first, half, other), jnp.where(first, other, half)], axis=1
    )
    return output.astype(jnp.bfloat16), weight_grad


def solution(mesh):
    inner = Mesh(
        mesh.devices.reshape(4, 2, 2, 2, 2, 8), ("yh", "c", "yl", "xh", "xl", "z")
    )
    rows = P(("yh", "c", "yl", "xh", "xl", "z"), None)
    owners = P(("yl", "xh", "xl", "z"), None)
    return jax.shard_map(
        local,
        mesh=inner,
        in_specs=(rows, owners, rows),
        out_specs=(rows, owners),
        check_vma=False,
    )
```

time: 114 us -> 139 us (1.22)
  starting transfers between devices: 44 us -> 83 us
  blocking collectives: 29.2 us -> 0 us
  local copies, waits for them, and re-layouts: 0.81 us -> 12.8 us
  waiting for transfers between devices: 21.4 us -> 27.6 us
  Pallas kernels: 14.3 us -> 10.3 us
    ppermute x4 -> x11, starting transfers between devices: 12.5 us -> 44.1 us  [the longest x7 30.4 us: local(): gathered.append(lax.ppermute(mine, 'z', shift))]
    all_gather x1 -> x0, blocking collectives: 29.2 us -> none  [local(): mine = lax.all_gather(weight, 'z', axis=0, tiled=True)]
    ppermute x4 -> x11, waiting for transfers between devices: 0.01 us -> 20.6 us  [the longest x1 11.7 us: local(): mine = jnp.stack([mine, lax.ppermute(mine, 'xh', SWAP)])]
    all_to_all x2, waiting for transfers between devices: 18.7 us -> 1.04 us  [the longest x1 1.03 us: local(): term = lax.all_to_all(term.reshape(-1, shard, wide), ('xh', 'z'), 0, 0)]
    unnamed x2 -> x19, local copies, waits for them, and re-layouts: 0.01 us -> 11.2 us
    ppermute x1, starting transfers between devices: 3.32 us -> 8.84 us  [local(): term = (keep + lax.ppermute(send, 'c', SWAP)).astype(jnp.bfloat16)]
    all_to_all x1, waiting for transfers between devices: 0.62 us -> 5.64 us  [local(): half = jnp.sum(lax.all_to_all(lines, 'yh', 0, 0), axis=0)]
    pallas_call x2 -> x1, Pallas kernels: 6.65 us -> 3.6 us  [project(): pl.pallas_call(body, in_specs=[pl.BlockSpec(memory_space=pltpu.SMEM), pl....]
  transfers between devices with their start and end apart: 9 -> 16, of which waited for: 5 -> 7; matrix products, arithmetic and copies ran while one was open for 1% -> 10% of each run, Pallas kernels for 6% -> 3%
where the time goes in v9:
time: 139 us; the launch traced here: 138 us
  starting transfers between devices  83 us (60%)
  waiting for transfers between devices  27.6 us (20%)
  local copies, waits for them, and re-layouts  12.8 us (9%)
  Pallas kernels  10.3 us (7%)
  other arithmetic  3.75 us (3%)
    ppermute x7, starting transfers between devices, local(): gathered.append(lax.ppermute(mine, 'z', shift))  30.4 us
    ppermute x1, waiting for transfers between devices, local(): mine = jnp.stack([mine, lax.ppermute(mine, 'xh', SWAP)])  11.7 us
    unnamed x19, local copies, waits for them, and re-layouts  11.2 us
    ppermute x1, starting transfers between devices, local(): term = (keep + lax.ppermute(send, 'c', SWAP)).astype(jnp.bfloat16)  8.84 us
    ppermute x1, starting transfers between devices, local(): other = lax.ppermute(half, 'c', SWAP)  8.62 us
    all_to_all x1, starting transfers between devices, local(): packed = lax.all_to_all(packed, CHIP, 0, 0, axis_index_groups=squares)  7.63 us
    all_to_all x1, starting transfers between devices, local(): term = lax.all_to_all(term.reshape(-1, shard, wide), ('xh', 'z'), 0, 0)  7.06 us
    all_to_all x1, starting transfers between devices, local(): half = jnp.sum(lax.all_to_all(lines, 'yh', 0, 0), axis=0)  6.75 us
  transfers between devices with their start and end apart: 16, of which 7 were waited for; matrix products, arithmetic and copies ran while one was open for 10% of the time, Pallas kernels for 3%

profile of v9, /device:TPU:1, one launch (start us, length us, event | category | flops | bytes accessed | tf_op | source)
XLA Modules:
  0.0 138.2 jit_solution(98829839886165862)
XLA Ops:
  0.6 3.6 %shard_map.50 = bf16[4,128,3328]{2,1,0:T(8,128)(2,1)} custom-call(bf16[128,12288]{1,0:T(8,128)(2,1)} %t_ref.1, bf16[128,256]{1,0:T(8,128)(2,1)} %g_ref.1), custom_call_target="tpu_custom_call" | custom-call | tf_op jit(solution)/shard_map/pallas_call | solution.py:52
  4.2 7.6 %all-to-all-start = ((bf16[4,128,3328]{2,1,0:T(8,128)(2,1)}), bf16[4,128,3328]{2,1,0:T(8,128)(2,1)S(1)}, u32[]{:S(2)}, u32[]{:S(2)}) async-start(bf16[4,128,3328]{2,1,0:T(8,128)(2,1)} %shard_map.50), calls=%async_computation | async-start | bytes 6815744 | tf_op jit(solution)/shard_map/all_to_all | solution.py:205
  11.8 2.5 %collective-permute-start = (bf16[192,128]{1,0:T(8,128)(2,1)S(1)}, bf16[192,128]{1,0:T(8,128)(2,1)S(1)}, u32[]{:S(2)}, u32[]{:S(2)}) collective-permute-start(bf16[192,128]{1,0:T(8,128)(2,1)S(1)} %slice_select_fusion), channel_id=1, source_target_pairs={{0,16},{16,0},{1,17},{17,1},{2,18},{18,2},{3,19},{19,3},{4,20},{20... | collective-permute-start | bytes 147464 | tf_op jit(solution)/shard_map/ppermute | solution.py:203
  14.3 11.7 %collective-permute-done = bf16[192,128]{1,0:T(8,128)(2,1)S(1)} collective-permute-done((bf16[192,128]{1,0:T(8,128)(2,1)S(1)}, bf16[192,128]{1,0:T(8,128)(2,1)S(1)}, u32[]{:S(2)}, u32[]{:S(2)}) %collective-permute-start) | collective-permute-done | bytes 49184 | tf_op jit(solution)/shard_map/ppermute | solution.py:203
  26.0 10.7 %collective-permute-start.7 = (bf16[2,192,128]{2,1,0:T(8,128)(2,1)S(1)}, bf16[2,192,128]{2,1,0:T(8,128)(2,1)S(1)}, u32[]{:S(2)}, u32[]{:S(2)}) collective-permute-start(bf16[2,192,128]{2,1,0:T(8,128)(2,1)S(1)} %pad_maximum_fusion.1), channel_id=1, source_target_pairs={{0,7},{1,0},{2,1},{3,2},{4,3},{5,4},{6,5},{7,6},{8,15},{9,8},{10,9... | collective-permute-start | bytes 294920 | tf_op jit(solution)/shard_map/ppermute | solution.py:210
  36.7 2.2 %collective-permute-start.6 = (bf16[2,192,128]{2,1,0:T(8,128)(2,1)S(1)}, bf16[2,192,128]{2,1,0:T(8,128)(2,1)S(1)}, u32[]{:S(2)}, u32[]{:S(2)}) collective-permute-start(bf16[2,192,128]{2,1,0:T(8,128)(2,1)S(1)} %pad_maximum_fusion.1), channel_id=1, source_target_pairs={{0,6},{1,7},{2,0},{3,1},{4,2},{5,3},{6,4},{7,5},{8,14},{9,15},{10,... | collective-permute-start | bytes 294920 | tf_op jit(solution)/shard_map/ppermute | solution.py:210
  38.9 1.9 %collective-permute-start.5 = (bf16[2,192,128]{2,1,0:T(8,128)(2,1)S(1)}, bf16[2,192,128]{2,1,0:T(8,128)(2,1)}, u32[]{:S(2)}, u32[]{:S(2)}) collective-permute-start(bf16[2,192,128]{2,1,0:T(8,128)(2,1)S(1)} %pad_maximum_fusion.1), channel_id=1, source_target_pairs={{0,5},{1,6},{2,7},{3,0},{4,1},{5,2},{6,3},{7,4},{8,13},{9,14},{10,... | collective-permute-start | bytes 294920 | tf_op jit(solution)/shard_map/ppermute | solution.py:210
  40.8 7.3 %collective-permute-start.4 = (bf16[2,192,128]{2,1,0:T(8,128)(2,1)S(1)}, bf16[2,192,128]{2,1,0:T(8,128)(2,1)}, u32[]{:S(2)}, u32[]{:S(2)}) collective-permute-start(bf16[2,192,128]{2,1,0:T(8,128)(2,1)S(1)} %pad_maximum_fusion.1), channel_id=1, source_target_pairs={{0,4},{1,5},{2,6},{3,7},{4,0},{5,1},{6,2},{7,3},{8,12},{9,13},{10,... | collective-permute-start | bytes 294920 | tf_op jit(solution)/shard_map/ppermute | solution.py:210
  48.1 1.9 %collective-permute-start.3 = (bf16[2,192,128]{2,1,0:T(8,128)(2,1)S(1)}, bf16[2,192,128]{2,1,0:T(8,128)(2,1)}, u32[]{:S(2)}, u32[]{:S(2)}) collective-permute-start(bf16[2,192,128]{2,1,0:T(8,128)(2,1)S(1)} %pad_maximum_fusion.1), channel_id=1, source_target_pairs={{0,3},{1,4},{2,5},{3,6},{4,7},{5,0},{6,1},{7,2},{8,11},{9,12},{10,... | collective-permute-start | bytes 294920 | tf_op jit(solution)/shard_map/ppermute | solution.py:210
  50.1 3.1 %collective-permute-start.2 = (bf16[2,192,128]{2,1,0:T(8,128)(2,1)S(1)}, bf16[2,192,128]{2,1,0:T(8,128)(2,1)}, u32[]{:S(2)}, u32[]{:S(2)}) collective-permute-start(bf16[2,192,128]{2,1,0:T(8,128)(2,1)S(1)} %pad_maximum_fusion.1), channel_id=1, source_target_pairs={{0,2},{1,3},{2,4},{3,5},{4,6},{5,7},{6,0},{7,1},{8,10},{9,11},{10,... | collective-permute-start | bytes 294920 | tf_op jit(solution)/shard_map/ppermute | solution.py:210
  53.8 3.3 %collective-permute-start.1 = (bf16[2,192,128]{2,1,0:T(8,128)(2,1)S(1)}, bf16[2,192,128]{2,1,0:T(8,128)(2,1)}, u32[]{:S(2)}, u32[]{:S(2)}) collective-permute-start(bf16[2,192,128]{2,1,0:T(8,128)(2,1)S(1)} %pad_maximum_fusion.1), channel_id=1, source_target_pairs={{0,1},{1,2},{2,3},{3,4},{4,5},{5,6},{6,7},{7,0},{8,9},{9,10},{10,1... | collective-permute-start | bytes 294920 | tf_op jit(solution)/shard_map/ppermute | solution.py:210
  57.3 2.9 %collective-permute-done.2 = bf16[2,192,128]{2,1,0:T(8,128)(2,1)} collective-permute-done((bf16[2,192,128]{2,1,0:T(8,128)(2,1)S(1)}, bf16[2,192,128]{2,1,0:T(8,128)(2,1)}, u32[]{:S(2)}, u32[]{:S(2)}) %collective-permute-start.2) | collective-permute-done | bytes 98336 | tf_op jit(solution)/shard_map/ppermute | solution.py:210
  60.2 3.8 %collective-permute-done.1 = bf16[2,192,128]{2,1,0:T(8,128)(2,1)} collective-permute-done((bf16[2,192,128]{2,1,0:T(8,128)(2,1)S(1)}, bf16[2,192,128]{2,1,0:T(8,128)(2,1)}, u32[]{:S(2)}, u32[]{:S(2)}) %collective-permute-start.1) | collective-permute-done | bytes 98336 | tf_op jit(solution)/shard_map/ppermute | solution.py:210
  64.0 3.1 %shard_map.51 = (f32[3072,128]{1,0:T(8,128)S(1)}, f32[3072,128]{1,0:T(8,128)S(1)}) custom-call(s32[5]{0:T(128)S(1)} %stack.59.spot_ref, bf16[4,128,3328]{2,1,0:T(8,128)(2,1)S(1)} %all-to-all-done.p_ref), custom_call_target="tpu_custom_call" | custom-call | tf_op jit(solution)/shard_map/pallas_call | solution.py:104
  67.1 8.8 %collective-permute-start.9 = (f32[3072,128]{1,0:T(8,128)S(1)}, f32[3072,128]{1,0:T(8,128)S(1)}, u32[]{:S(2)}, u32[]{:S(2)}) collective-permute-start(f32[3072,128]{1,0:T(8,128)S(1)} %get-tuple-element.26), channel_id=1, source_target_pairs={{0,64},{64,0},{1,65},{65,1},{2,66},{66,2},{3,67},{67,3},{4,68},{68... | collective-permute-start | bytes 4718600 | tf_op jit(solution)/shard_map/ppermute | solution.py:214
  82.3 7.1 %all-to-all-start.1 = ((bf16[16,192,128]{2,1,0:T(8,128)(2,1)}), bf16[16,192,128]{2,1,0:T(8,128)(2,1)}, u32[]{:S(2)}, u32[]{:S(2)}) async-start(bf16[16,192,128]{2,1,0:T(8,128)(2,1)} %bitcast.33), calls=%async_computation.1 | async-start | bytes 1572864 | tf_op jit(solution)/shard_map/all_to_all | solution.py:218
  94.6 2.2 %collective-permute-start.8 = (bf16[8,2,192,128]{3,2,1,0:T(8,128)(2,1)}, bf16[8,2,192,128]{3,2,1,0:T(8,128)(2,1)S(1)}, u32[]{:S(2)}, u32[]{:S(2)}) collective-permute-start(bf16[8,2,192,128]{3,2,1,0:T(8,128)(2,1)} %bitcast_dynamic-update-slice_fusion.m_ref), channel_id=1, source_target_pairs={{0,64},{64,0},{1,65},{65,1},{2,66},{66,2},{3,67},{67,3},{4,68},{68... | collective-permute-start | bytes 2359304 | tf_op jit(solution)/shard_map/ppermute | solution.py:217
  96.8 2.2 %collective-permute-done.8.r_ref = bf16[8,2,192,128]{3,2,1,0:T(8,128)(2,1)S(1)} collective-permute-done((bf16[8,2,192,128]{3,2,1,0:T(8,128)(2,1)}, bf16[8,2,192,128]{3,2,1,0:T(8,128)(2,1)S(1)}, u32[]{:S(2)}, u32[]{:S(2)}) %collective-permute-start.8) | collective-permute-done | bytes 786464 | tf_op jit(solution)/shard_map/ppermute | solution.py:217
  99.0 3.6 %shard_map.52 = (f32[2,128,256]{2,1,0:T(8,128)S(1)}, f32[2,128,256]{2,1,0:T(8,128)}) custom-call(s32[5]{0:T(128)S(1)} %stack.59.spot_ref, bf16[4,128,3328]{2,1,0:T(8,128)(2,1)S(1)} %all-to-all-done.p_ref, bf16[8,2,192,128]{3,2,1,0:T(8,128)(2,1)} %bitcast_dynamic-update-slice_fusion.m_ref, bf16[8,2,192,128]{3,2,1,0:T(8,128)(2,1)S(1)} %collective-permute-done.8.r_ref), custom_call_target="tpu_custom_call" | custom-call | tf_op jit(solution)/shard_map/pallas_call | solution.py:151
  103.3 6.0 %collective-permute-start.10 = (f32[2,128,256]{2,1,0:T(8,128)}, f32[2,128,256]{2,1,0:T(8,128)S(1)}, u32[]{:S(2)}, u32[]{:S(2)}) collective-permute-start(f32[2,128,256]{2,1,0:T(8,128)} %get-tuple-element.31), channel_id=1, source_target_pairs={{0,32},{8,40},{16,48},{24,56},{64,480},{72,488},{80,496},{88,504},... | collective-permute-start | bytes 786440 | tf_op jit(solution)/shard_map/ppermute | solution.py:222
  112.4 6.7 %all-to-all-start.2 = ((f32[4,192,128]{2,1,0:T(8,128)}), f32[4,192,128]{2,1,0:T(8,128)S(1)}, u32[]{:S(2)}, u32[]{:S(2)}) async-start(f32[4,192,128]{2,1,0:T(8,128)} %broadcast_in_dim.2), calls=%async_computation.2 | async-start | bytes 786432 | tf_op jit(solution)/shard_map/all_to_all | solution.py:228
  119.2 3.0 %collective-permute-start.11 = (f32[128,256]{1,0:T(8,128)S(1)}, f32[128,256]{1,0:T(8,128)S(1)}, u32[]{:S(2)}, u32[]{:S(2)}) collective-permute-start(f32[128,256]{1,0:T(8,128)S(1)} %slice_bitcast_fusion), channel_id=1, source_target_pairs={{0,8},{8,0},{16,24},{24,16},{64,88},{72,80},{80,72},{88,64},{32,40... | collective-permute-start | bytes 393224 | tf_op jit(solution)/shard_map/ppermute | solution.py:225
  122.3 5.6 %all-to-all-done.2 = f32[4,192,128]{2,1,0:T(8,128)S(1)} async-done(((f32[4,192,128]{2,1,0:T(8,128)}), f32[4,192,128]{2,1,0:T(8,128)S(1)}, u32[]{:S(2)}, u32[]{:S(2)}) %all-to-all-start.2) | async-done | bytes 393248 | tf_op jit(solution)/shard_map/all_to_all | solution.py:228
  127.9 8.6 %collective-permute-start.12 = (f32[192,128]{1,0:T(8,128)S(1)}, f32[192,128]{1,0:T(8,128)S(1)}, u32[]{:S(2)}, u32[]{:S(2)}) collective-permute-start(f32[192,128]{1,0:T(8,128)S(1)} %reduce_sum.19), channel_id=1, source_target_pairs={{0,64},{64,0},{1,65},{65,1},{2,66},{66,2},{3,67},{67,3},{4,68},{68... | collective-permute-start | bytes 294920 | tf_op jit(solution)/shard_map/ppermute | solution.py:229
  (44 shorter events, 17.8 us)
Async XLA Ops:
  4.2 7.6 %copy-start.2 = (bf16[192,256]{1,0:T(8,128)(2,1)S(1)}, bf16[192,256]{1,0:T(8,128)(2,1)}, u32[]{:S(2)}) copy-start(bf16[192,256]{1,0:T(8,128)(2,1)} %param.4) | copy-start | bytes 294916
  4.2 59.8 %all-to-all-start = ((bf16[4,128,3328]{2,1,0:T(8,128)(2,1)}), bf16[4,128,3328]{2,1,0:T(8,128)(2,1)S(1)}, u32[]{:S(2)}, u32[]{:S(2)}) async-start(bf16[4,128,3328]{2,1,0:T(8,128)(2,1)} %shard_map.50), calls=%async_computation | async-start | bytes 6815744 | tf_op jit(solution)/shard_map/all_to_all | solution.py:205
  11.8 14.2 %collective-permute-start = (bf16[192,128]{1,0:T(8,128)(2,1)S(1)}, bf16[192,128]{1,0:T(8,128)(2,1)S(1)}, u32[]{:S(2)}, u32[]{:S(2)}) collective-permute-start(bf16[192,128]{1,0:T(8,128)(2,1)S(1)} %slice_select_fusion), channel_id=1, source_target_pairs={{0,16},{16,0},{1,17},{17,1},{2,18},{18,2},{3,19},{19,3},{4,20},{20... | collective-permute-start | bytes 147464 | tf_op jit(solution)/shard_map/ppermute | solution.py:203
  26.0 24.0 %collective-permute-start.7 = (bf16[2,192,128]{2,1,0:T(8,128)(2,1)S(1)}, bf16[2,192,128]{2,1,0:T(8,128)(2,1)S(1)}, u32[]{:S(2)}, u32[]{:S(2)}) collective-permute-start(bf16[2,192,128]{2,1,0:T(8,128)(2,1)S(1)} %pad_maximum_fusion.1), channel_id=1, source_target_pairs={{0,7},{1,0},{2,1},{3,2},{4,3},{5,4},{6,5},{7,6},{8,15},{9,8},{10,9... | collective-permute-start | bytes 294920 | tf_op jit(solution)/shard_map/ppermute | solution.py:210
  36.7 16.5 %collective-permute-start.6 = (bf16[2,192,128]{2,1,0:T(8,128)(2,1)S(1)}, bf16[2,192,128]{2,1,0:T(8,128)(2,1)S(1)}, u32[]{:S(2)}, u32[]{:S(2)}) collective-permute-start(bf16[2,192,128]{2,1,0:T(8,128)(2,1)S(1)} %pad_maximum_fusion.1), channel_id=1, source_target_pairs={{0,6},{1,7},{2,0},{3,1},{4,2},{5,3},{6,4},{7,5},{8,14},{9,15},{10,... | collective-permute-start | bytes 294920 | tf_op jit(solution)/shard_map/ppermute | solution.py:210
  38.9 18.4 %collective-permute-start.5 = (bf16[2,192,128]{2,1,0:T(8,128)(2,1)S(1)}, bf16[2,192,128]{2,1,0:T(8,128)(2,1)}, u32[]{:S(2)}, u32[]{:S(2)}) collective-permute-start(bf16[2,192,128]{2,1,0:T(8,128)(2,1)S(1)} %pad_maximum_fusion.1), channel_id=1, source_target_pairs={{0,5},{1,6},{2,7},{3,0},{4,1},{5,2},{6,3},{7,4},{8,13},{9,14},{10,... | collective-permute-start | bytes 294920 | tf_op jit(solution)/shard_map/ppermute | solution.py:210
  40.8 16.4 %collective-permute-start.4 = (bf16[2,192,128]{2,1,0:T(8,128)(2,1)S(1)}, bf16[2,192,128]{2,1,0:T(8,128)(2,1)}, u32[]{:S(2)}, u32[]{:S(2)}) collective-permute-start(bf16[2,192,128]{2,1,0:T(8,128)(2,1)S(1)} %pad_maximum_fusion.1), channel_id=1, source_target_pairs={{0,4},{1,5},{2,6},{3,7},{4,0},{5,1},{6,2},{7,3},{8,12},{9,13},{10,... | collective-permute-start | bytes 294920 | tf_op jit(solution)/shard_map/ppermute | solution.py:210
  48.1 9.2 %collective-permute-start.3 = (bf16[2,192,128]{2,1,0:T(8,128)(2,1)S(1)}, bf16[2,192,128]{2,1,0:T(8,128)(2,1)}, u32[]{:S(2)}, u32[]{:S(2)}) collective-permute-start(bf16[2,192,128]{2,1,0:T(8,128)(2,1)S(1)} %pad_maximum_fusion.1), channel_id=1, source_target_pairs={{0,3},{1,4},{2,5},{3,6},{4,7},{5,0},{6,1},{7,2},{8,11},{9,12},{10,... | collective-permute-start | bytes 294920 | tf_op jit(solution)/shard_map/ppermute | solution.py:210
  50.0 3.1 %copy-start.3 = (bf16[2,192,128]{2,1,0:T(8,128)(2,1)}, bf16[2,192,128]{2,1,0:T(8,128)(2,1)S(1)}, u32[]{:S(2)}) copy-start(bf16[2,192,128]{2,1,0:T(8,128)(2,1)S(1)} %collective-permute-done.7) | copy-start | bytes 294916
  50.1 10.1 %collective-permute-start.2 = (bf16[2,192,128]{2,1,0:T(8,128)(2,1)S(1)}, bf16[2,192,128]{2,1,0:T(8,128)(2,1)}, u32[]{:S(2)}, u32[]{:S(2)}) collective-permute-start(bf16[2,192,128]{2,1,0:T(8,128)(2,1)S(1)} %pad_maximum_fusion.1), channel_id=1, source_target_pairs={{0,2},{1,3},{2,4},{3,5},{4,6},{5,7},{6,0},{7,1},{8,10},{9,11},{10,... | collective-permute-start | bytes 294920 | tf_op jit(solution)/shard_map/ppermute | solution.py:210
  53.2 0.6 copy-start.5
  53.8 10.2 %collective-permute-start.1 = (bf16[2,192,128]{2,1,0:T(8,128)(2,1)S(1)}, bf16[2,192,128]{2,1,0:T(8,128)(2,1)}, u32[]{:S(2)}, u32[]{:S(2)}) collective-permute-start(bf16[2,192,128]{2,1,0:T(8,128)(2,1)S(1)} %pad_maximum_fusion.1), channel_id=1, source_target_pairs={{0,1},{1,2},{2,3},{3,4},{4,5},{5,6},{6,7},{7,0},{8,9},{9,10},{10,1... | collective-permute-start | bytes 294920 | tf_op jit(solution)/shard_map/ppermute | solution.py:210
  67.1 14.1 %collective-permute-start.9 = (f32[3072,128]{1,0:T(8,128)S(1)}, f32[3072,128]{1,0:T(8,128)S(1)}, u32[]{:S(2)}, u32[]{:S(2)}) collective-permute-start(f32[3072,128]{1,0:T(8,128)S(1)} %get-tuple-element.26), channel_id=1, source_target_pairs={{0,64},{64,0},{1,65},{65,1},{2,66},{66,2},{3,67},{67,3},{4,68},{68... | collective-permute-start | bytes 4718600 | tf_op jit(solution)/shard_map/ppermute | solution.py:214
  82.3 11.7 %copy-start.4 = (bf16[2,192,128]{2,1,0:T(8,128)(2,1)S(1)}, bf16[2,192,128]{2,1,0:T(8,128)(2,1)}, u32[]{:S(2)}) copy-start(bf16[2,192,128]{2,1,0:T(8,128)(2,1)} %copy-done.3) | copy-start | bytes 294916
  82.3 28.1 %all-to-all-start.1 = ((bf16[16,192,128]{2,1,0:T(8,128)(2,1)}), bf16[16,192,128]{2,1,0:T(8,128)(2,1)}, u32[]{:S(2)}, u32[]{:S(2)}) async-start(bf16[16,192,128]{2,1,0:T(8,128)(2,1)} %bitcast.33), calls=%async_computation.1 | async-start | bytes 1572864 | tf_op jit(solution)/shard_map/all_to_all | solution.py:218
  94.6 4.4 %collective-permute-start.8 = (bf16[8,2,192,128]{3,2,1,0:T(8,128)(2,1)}, bf16[8,2,192,128]{3,2,1,0:T(8,128)(2,1)S(1)}, u32[]{:S(2)}, u32[]{:S(2)}) collective-permute-start(bf16[8,2,192,128]{3,2,1,0:T(8,128)(2,1)} %bitcast_dynamic-update-slice_fusion.m_ref), channel_id=1, source_target_pairs={{0,64},{64,0},{1,65},{65,1},{2,66},{66,2},{3,67},{67,3},{4,68},{68... | collective-permute-start | bytes 2359304 | tf_op jit(solution)/shard_map/ppermute | solution.py:217
  102.6 0.7 copy-start
  103.3 15.8 %copy-start.1 = (f32[2,128,256]{2,1,0:T(8,128)S(1)}, f32[2,128,256]{2,1,0:T(8,128)}, u32[]{:S(2)}) copy-start(f32[2,128,256]{2,1,0:T(8,128)} %copy-done) | copy-start | bytes 786436
  103.3 15.8 %collective-permute-start.10 = (f32[2,128,256]{2,1,0:T(8,128)}, f32[2,128,256]{2,1,0:T(8,128)S(1)}, u32[]{:S(2)}, u32[]{:S(2)}) collective-permute-start(f32[2,128,256]{2,1,0:T(8,128)} %get-tuple-element.31), channel_id=1, source_target_pairs={{0,32},{8,40},{16,48},{24,56},{64,480},{72,488},{80,496},{88,504},... | collective-permute-start | bytes 786440 | tf_op jit(solution)/shard_map/ppermute | solution.py:222
  112.4 15.5 %all-to-all-start.2 = ((f32[4,192,128]{2,1,0:T(8,128)}), f32[4,192,128]{2,1,0:T(8,128)S(1)}, u32[]{:S(2)}, u32[]{:S(2)}) async-start(f32[4,192,128]{2,1,0:T(8,128)} %broadcast_in_dim.2), calls=%async_computation.2 | async-start | bytes 786432 | tf_op jit(solution)/shard_map/all_to_all | solution.py:228
  119.2 17.3 %collective-permute-start.11 = (f32[128,256]{1,0:T(8,128)S(1)}, f32[128,256]{1,0:T(8,128)S(1)}, u32[]{:S(2)}, u32[]{:S(2)}) collective-permute-start(f32[128,256]{1,0:T(8,128)S(1)} %slice_bitcast_fusion), channel_id=1, source_target_pairs={{0,8},{8,0},{16,24},{24,16},{64,88},{72,80},{80,72},{88,64},{32,40... | collective-permute-start | bytes 393224 | tf_op jit(solution)/shard_map/ppermute | solution.py:225
  127.9 9.6 %collective-permute-start.12 = (f32[192,128]{1,0:T(8,128)S(1)}, f32[192,128]{1,0:T(8,128)S(1)}, u32[]{:S(2)}, u32[]{:S(2)}) collective-permute-start(f32[192,128]{1,0:T(8,128)S(1)} %reduce_sum.19), channel_id=1, source_target_pairs={{0,64},{64,0},{1,65},{65,1},{2,66},{66,2},{3,67},{67,3},{4,68},{68... | collective-permute-start | bytes 294920 | tf_op jit(solution)/shard_map/ppermute | solution.py:229

commit v10 on v9

--- a/solution.py
+++ b/solution.py
@@ -117,9 +117,33 @@
     )(spot, packed)
 
 
+def join(parts):
+    count = len(parts)
+
+    def body(*refs):
+        o_ref, sems = refs[count:]
+        copies = [
+            pltpu.make_async_copy(refs[n], o_ref.at[n], sems.at[n]) for n in range(count)
+        ]
+        for copy in copies:
+            copy.start()
+        for copy in copies:
+            copy.wait()
+
+    return pl.pallas_call(
+        body,
+        in_specs=[pl.BlockSpec(memory_space=pl.ANY)] * count,
+        out_specs=pl.BlockSpec(memory_space=pltpu.VMEM),
+        out_shape=jax.ShapeDtypeStruct((count,) + parts[0].shape, parts[0].dtype),
+        scratch_shapes=[pltpu.SemaphoreType.DMA((count,))],
+        compiler_params=PARAMS,
+    )(*parts)
+
+
 def project(packed, mine, other, spot):
     quads, rows, both = packed.shape
-    depth, xhs, shard, wide = mine.shape
+    pairs, zs, xhs, shard, wide = mine.shape
+    depth = pairs * zs
     part, cols = depth * xhs * shard, 2 * wide
 
     def body(spot_ref, p_ref, m_ref, r_ref, near_ref, away_ref, stage, whole, sems):
@@ -132,12 +156,16 @@
                 )
             )
             loads[-1].start()
-        for back in range(depth):
-            at_z = lax.rem(z + depth - back, depth)
-            for slot in range(xhs):
-                left = jnp.where(core == 0, m_ref[back, slot], r_ref[back, slot])
-                right = jnp.where(core == 0, r_ref[back, slot], m_ref[back, slot])
-                whole[xh ^ slot, at_z] = jnp.concatenate([left, right], axis=1)
+        for back in range(pairs):
+            at_z = lax.rem(z + depth - zs * back, depth)
+            for slot in range(zs):
+                for side in range(xhs):
+                    ours, theirs = m_ref[back, slot, side], r_ref[back, slot, side]
+                    left = jnp.where(core == 0, ours, theirs)
+                    right = jnp.where(core == 0, theirs, ours)
+                    whole[xh ^ side, at_z ^ slot] = jnp.concatenate(
+                        [left, right], axis=1
+                    )
         for load in loads:
             load.wait()
         t = stage[...].reshape(quads * rows, both)[:, :part]
@@ -153,14 +181,13 @@
         in_specs=[
             pl.BlockSpec(memory_space=pltpu.SMEM),
             pl.BlockSpec(memory_space=pl.ANY),
-            pl.BlockSpec(memory_space=pltpu.VMEM),
-            pl.BlockSpec(memory_space=pltpu.VMEM),
-        ],
+        ]
+        + [pl.BlockSpec(memory_space=pltpu.VMEM)] * 2,
         out_specs=[pl.BlockSpec(memory_space=pltpu.VMEM)] * 2,
         out_shape=[out, out],
         scratch_shapes=[
             pltpu.VMEM(packed.shape, packed.dtype),
-            pltpu.VMEM((xhs, depth, shard, cols), mine.dtype),
+            pltpu.VMEM((xhs, depth, shard, cols), packed.dtype),
             pltpu.SemaphoreType.DMA((quads,)),
         ],
         compiler_params=PARAMS,
@@ -200,19 +227,22 @@
     spot = spot.astype(jnp.int32)
 
     mine = jnp.where(spot[0] == 0, weight[:, :wide], weight[:, wide:])
+    pair = [(i, i ^ 1) for i in range(depth)]
     mine = jnp.stack([mine, lax.ppermute(mine, "xh", SWAP)])
     packed = pack(tokens, grad_out)
+    packed, mine = lax.optimization_barrier((packed, mine))
     packed = lax.all_to_all(packed, CHIP, 0, 0, axis_index_groups=squares)
     part = packed.shape[-1] - cols
+    mine = jnp.stack([mine, lax.ppermute(mine, "z", pair)])
     gathered = [mine]
-    for back in range(1, depth):
+    for back in range(2, depth, 2):
         shift = [(i, (i + back) % depth) for i in range(depth)]
         gathered.append(lax.ppermute(mine, "z", shift))
     packed, *gathered = lax.optimization_barrier((packed, *gathered))
 
     keep, send = terms(packed, spot, part)
     term = (keep + lax.ppermute(send, "c", SWAP)).astype(jnp.bfloat16)
-    mine = jnp.stack(gathered)
+    mine = join(gathered)
     mine, _ = lax.optimization_barrier((mine, send))
     other = lax.ppermute(mine, "c", SWAP)
     term = lax.all_to_all(term.reshape(-1, shard, wide), ("xh", "z"), 0, 0)

time: 139 us -> 119 us (0.86)
  starting transfers between devices: 83 us -> 68.8 us
  local copies, waits for them, and re-layouts: 12.8 us -> 1.59 us
  other arithmetic: 3.75 us -> 6.11 us
  waiting for transfers between devices: 27.6 us -> 29.2 us
    ppermute x7 -> x3, starting transfers between devices: 30.4 us -> 17.4 us  [local(): gathered.append(lax.ppermute(mine, 'z', shift))]
    ppermute x1, waiting for transfers between devices: 11.7 us -> 0.01 us  [local(): mine = jnp.stack([mine, lax.ppermute(mine, 'xh', SWAP)])]
    unnamed x19 -> x4, local copies, waits for them, and re-layouts: 11.2 us -> 0.72 us
    all_to_all x1, waiting for transfers between devices: 1.03 us -> 7.29 us  [local(): term = lax.all_to_all(term.reshape(-1, shard, wide), ('xh', 'z'), 0, 0)]
    ppermute x1, starting transfers between devices: 8.84 us -> 2.84 us  [local(): term = (keep + lax.ppermute(send, 'c', SWAP)).astype(jnp.bfloat16)]
    ppermute x7 -> x3, waiting for transfers between devices: 6.74 us -> 10.9 us  [local(): gathered.append(lax.ppermute(mine, 'z', shift))]
    ppermute x0 -> x1, starting transfers between devices: none -> 3.99 us  [local(): mine = jnp.stack([mine, lax.ppermute(mine, 'z', pair)])]
    all_to_all x1, starting transfers between devices: 7.06 us -> 10.6 us  [local(): term = lax.all_to_all(term.reshape(-1, shard, wide), ('xh', 'z'), 0, 0)]
  transfers between devices with their start and end apart: 16 -> 13, of which waited for: 7 -> 7; matrix products, arithmetic and copies ran while one was open for 10% -> 4% of each run, Pallas kernels for 3% -> 7%
where the time goes in v10:
time: 119 us; the launch traced here: 117 us
  starting transfers between devices  68.8 us (58%)
  waiting for transfers between devices  29.2 us (25%)
  Pallas kernels  10.9 us (9%)
  other arithmetic  6.11 us (5%)
  local copies, waits for them, and re-layouts  1.59 us (1%)
    ppermute x3, starting transfers between devices, local(): gathered.append(lax.ppermute(mine, 'z', shift))  17.4 us
    ppermute x3, waiting for transfers between devices, local(): gathered.append(lax.ppermute(mine, 'z', shift))  10.9 us
    all_to_all x1, starting transfers between devices, local(): term = lax.all_to_all(term.reshape(-1, shard, wide), ('xh', 'z'), 0, 0)  10.6 us
    ppermute x1, starting transfers between devices, local(): other = lax.ppermute(half, 'c', SWAP)  7.8 us
    all_to_all x1, waiting for transfers between devices, local(): term = lax.all_to_all(term.reshape(-1, shard, wide), ('xh', 'z'), 0, 0)  7.29 us
    ppermute x1, starting transfers between devices, local(): mine = jnp.stack([mine, lax.ppermute(mine, 'xh', SWAP)])  5.47 us
    all_to_all x1, starting transfers between devices, local(): packed = lax.all_to_all(packed, CHIP, 0, 0, axis_index_groups=squares)  5.05 us
    ppermute x1, starting transfers between devices, local(): output = near[0] + lax.ppermute(near[1], CHIP, flip_x)  4.84 us
  transfers between devices with their start and end apart: 13, of which 7 were waited for; matrix products, arithmetic and copies ran while one was open for 4% of the time, Pallas kernels for 7%

profile of v10, /device:TPU:1, one launch (start us, length us, event | category | flops | bytes accessed | tf_op | source)
XLA Modules:
  0.0 117.4 jit_solution(5217002754320195804)
XLA Ops:
  1.5 5.5 %collective-permute-start = (bf16[192,128]{1,0:T(8,128)(2,1)S(1)}, bf16[192,128]{1,0:T(8,128)(2,1)S(1)}, u32[]{:S(2)}, u32[]{:S(2)}) collective-permute-start(bf16[192,128]{1,0:T(8,128)(2,1)S(1)} %slice_select_fusion), channel_id=1, source_target_pairs={{0,16},{16,0},{1,17},{17,1},{2,18},{18,2},{3,19},{19,3},{4,20},{20... | collective-permute-start | bytes 147464 | tf_op jit(solution)/shard_map/ppermute | solution.py:231
  7.8 3.6 %shard_map.50 = bf16[4,128,3328]{2,1,0:T(8,128)(2,1)} custom-call(bf16[128,12288]{1,0:T(8,128)(2,1)} %t_ref.1, bf16[128,256]{1,0:T(8,128)(2,1)} %g_ref.1), custom_call_target="tpu_custom_call" | custom-call | tf_op jit(solution)/shard_map/pallas_call | solution.py:52
  11.4 5.0 %all-to-all-start = ((bf16[4,128,3328]{2,1,0:T(8,128)(2,1)}), bf16[4,128,3328]{2,1,0:T(8,128)(2,1)S(1)}, u32[]{:S(2)}, u32[]{:S(2)}) async-start(bf16[4,128,3328]{2,1,0:T(8,128)(2,1)} %shard_map.50), calls=%async_computation | async-start | bytes 6815744 | tf_op jit(solution)/shard_map/all_to_all | solution.py:234
  16.4 4.0 %collective-permute-start.1 = (bf16[2,192,128]{2,1,0:T(8,128)(2,1)S(1)}, bf16[2,192,128]{2,1,0:T(8,128)(2,1)S(1)}, u32[]{:S(2)}, u32[]{:S(2)}) collective-permute-start(bf16[2,192,128]{2,1,0:T(8,128)(2,1)S(1)} %pad_maximum_fusion.2), channel_id=1, source_target_pairs={{0,1},{1,0},{2,3},{3,2},{4,5},{5,4},{6,7},{7,6},{8,9},{9,8},{10,11... | collective-permute-start | bytes 294920 | tf_op jit(solution)/shard_map/ppermute | solution.py:236
  20.4 2.0 %collective-permute-done.1 = bf16[2,192,128]{2,1,0:T(8,128)(2,1)S(1)} collective-permute-done((bf16[2,192,128]{2,1,0:T(8,128)(2,1)S(1)}, bf16[2,192,128]{2,1,0:T(8,128)(2,1)S(1)}, u32[]{:S(2)}, u32[]{:S(2)}) %collective-permute-start.1) | collective-permute-done | bytes 98336 | tf_op jit(solution)/shard_map/ppermute | solution.py:236
  23.1 11.2 %collective-permute-start.4 = (bf16[2,2,192,128]{3,2,1,0:T(8,128)(2,1)}, bf16[2,2,192,128]{3,2,1,0:T(8,128)(2,1)}, u32[]{:S(2)}, u32[]{:S(2)}) collective-permute-start(bf16[2,2,192,128]{3,2,1,0:T(8,128)(2,1)} %pad_maximum_fusion.refs_0_), channel_id=1, source_target_pairs={{0,6},{1,7},{2,0},{3,1},{4,2},{5,3},{6,4},{7,5},{8,14},{9,15},{10,... | collective-permute-start | bytes 589832 | tf_op jit(solution)/shard_map/ppermute | solution.py:240
  34.3 1.9 %collective-permute-start.3 = (bf16[2,2,192,128]{3,2,1,0:T(8,128)(2,1)}, bf16[2,2,192,128]{3,2,1,0:T(8,128)(2,1)}, u32[]{:S(2)}, u32[]{:S(2)}) collective-permute-start(bf16[2,2,192,128]{3,2,1,0:T(8,128)(2,1)} %pad_maximum_fusion.refs_0_), channel_id=1, source_target_pairs={{0,4},{1,5},{2,6},{3,7},{4,0},{5,1},{6,2},{7,3},{8,12},{9,13},{10,... | collective-permute-start | bytes 589832 | tf_op jit(solution)/shard_map/ppermute | solution.py:240
  36.3 4.2 %collective-permute-start.2 = (bf16[2,2,192,128]{3,2,1,0:T(8,128)(2,1)}, bf16[2,2,192,128]{3,2,1,0:T(8,128)(2,1)}, u32[]{:S(2)}, u32[]{:S(2)}) collective-permute-start(bf16[2,2,192,128]{3,2,1,0:T(8,128)(2,1)} %pad_maximum_fusion.refs_0_), channel_id=1, source_target_pairs={{0,2},{1,3},{2,4},{3,5},{4,6},{5,7},{6,0},{7,1},{8,10},{9,11},{10,... | collective-permute-start | bytes 589832 | tf_op jit(solution)/shard_map/ppermute | solution.py:240
  40.6 10.8 %collective-permute-done.3.refs_2_ = bf16[2,2,192,128]{3,2,1,0:T(8,128)(2,1)} collective-permute-done((bf16[2,2,192,128]{3,2,1,0:T(8,128)(2,1)}, bf16[2,2,192,128]{3,2,1,0:T(8,128)(2,1)}, u32[]{:S(2)}, u32[]{:S(2)}) %collective-permute-start.3) | collective-permute-done | bytes 196640 | tf_op jit(solution)/shard_map/ppermute | solution.py:240
  51.5 3.1 %shard_map.52 = (f32[3072,128]{1,0:T(8,128)S(1)}, f32[3072,128]{1,0:T(8,128)S(1)}) custom-call(s32[5]{0:T(128)S(1)} %stack.41.spot_ref, bf16[4,128,3328]{2,1,0:T(8,128)(2,1)S(1)} %all-to-all-done.p_ref), custom_call_target="tpu_custom_call" | custom-call | tf_op jit(solution)/shard_map/pallas_call | solution.py:104
  54.6 2.8 %collective-permute-start.6 = (f32[3072,128]{1,0:T(8,128)S(1)}, f32[3072,128]{1,0:T(8,128)S(1)}, u32[]{:S(2)}, u32[]{:S(2)}) collective-permute-start(f32[3072,128]{1,0:T(8,128)S(1)} %get-tuple-element.22), channel_id=1, source_target_pairs={{0,64},{64,0},{1,65},{65,1},{2,66},{66,2},{3,67},{67,3},{4,68},{68... | collective-permute-start | bytes 4718600 | tf_op jit(solution)/shard_map/ppermute | solution.py:244
  57.4 3.0 %collective-permute-done.6 = f32[3072,128]{1,0:T(8,128)S(1)} collective-permute-done((f32[3072,128]{1,0:T(8,128)S(1)}, f32[3072,128]{1,0:T(8,128)S(1)}, u32[]{:S(2)}, u32[]{:S(2)}) %collective-permute-start.6) | collective-permute-done | bytes 1572896 | tf_op jit(solution)/shard_map/ppermute | solution.py:244
  61.5 10.6 %all-to-all-start.1 = ((bf16[16,192,128]{2,1,0:T(8,128)(2,1)}), bf16[16,192,128]{2,1,0:T(8,128)(2,1)}, u32[]{:S(2)}, u32[]{:S(2)}) async-start(bf16[16,192,128]{2,1,0:T(8,128)(2,1)} %bitcast.19), calls=%async_computation.1 | async-start | bytes 1572864 | tf_op jit(solution)/shard_map/all_to_all | solution.py:248
  72.2 1.3 %shard_map.51.m_ref = bf16[4,2,2,192,128]{4,3,2,1,0:T(8,128)(2,1)S(1)} custom-call(bf16[2,2,192,128]{3,2,1,0:T(8,128)(2,1)} %pad_maximum_fusion.refs_0_, bf16[2,2,192,128]{3,2,1,0:T(8,128)(2,1)} %collective-permute-done.2.refs_1_, bf16[2,2,192,128]{3,2,1,0:T(8,128)(2,1)} %collective-permute-done.3.refs_2_, ...), custom_call_target="tpu_custom_call" | custom-call | tf_op jit(solution)/shard_map/pallas_call | solution.py:133
  73.4 2.6 %collective-permute-start.5 = (bf16[4,2,2,192,128]{4,3,2,1,0:T(8,128)(2,1)S(1)}, bf16[4,2,2,192,128]{4,3,2,1,0:T(8,128)(2,1)S(1)}, u32[]{:S(2)}, u32[]{:S(2)}) collective-permute-start(bf16[4,2,2,192,128]{4,3,2,1,0:T(8,128)(2,1)S(1)} %shard_map.51.m_ref), channel_id=1, source_target_pairs={{0,64},{64,0},{1,65},{65,1},{2,66},{66,2},{3,67},{67,3},{4,68},{68... | collective-permute-start | bytes 2359304 | tf_op jit(solution)/shard_map/ppermute | solution.py:247
  76.0 1.9 %collective-permute-done.5.r_ref = bf16[4,2,2,192,128]{4,3,2,1,0:T(8,128)(2,1)S(1)} collective-permute-done((bf16[4,2,2,192,128]{4,3,2,1,0:T(8,128)(2,1)S(1)}, bf16[4,2,2,192,128]{4,3,2,1,0:T(8,128)(2,1)S(1)}, u32[]{:S(2)}, u32[]{:S(2)}) %collective-permute-start.5) | collective-permute-done | bytes 786464 | tf_op jit(solution)/shard_map/ppermute | solution.py:247
  77.9 3.0 %shard_map.53 = (f32[2,128,256]{2,1,0:T(8,128)S(1)}, f32[2,128,256]{2,1,0:T(8,128)}) custom-call(s32[5]{0:T(128)S(1)} %stack.41.spot_ref, bf16[4,128,3328]{2,1,0:T(8,128)(2,1)S(1)} %all-to-all-done.p_ref, bf16[4,2,2,192,128]{4,3,2,1,0:T(8,128)(2,1)S(1)} %shard_map.51.m_ref, bf16[4,2,2,192,128]{4,3,2,1,0:T(8,128)(2,1)S(1)} %collective-permute-done.5.r_ref), custom_call_target="tpu_custom_call" | custom-call | tf_op jit(solution)/shard_map/pallas_call | solution.py:179
  81.6 4.2 %collective-permute-start.7 = (f32[2,128,256]{2,1,0:T(8,128)}, f32[2,128,256]{2,1,0:T(8,128)S(1)}, u32[]{:S(2)}, u32[]{:S(2)}) collective-permute-start(f32[2,128,256]{2,1,0:T(8,128)} %get-tuple-element.27), channel_id=1, source_target_pairs={{0,32},{8,40},{16,48},{24,56},{64,480},{72,488},{80,496},{88,504},... | collective-permute-start | bytes 786440 | tf_op jit(solution)/shard_map/ppermute | solution.py:252
  85.8 7.3 %all-to-all-done.1 = bf16[16,192,128]{2,1,0:T(8,128)(2,1)} async-done(((bf16[16,192,128]{2,1,0:T(8,128)(2,1)}), bf16[16,192,128]{2,1,0:T(8,128)(2,1)}, u32[]{:S(2)}, u32[]{:S(2)}) %all-to-all-start.1) | async-done | bytes 786464 | tf_op jit(solution)/shard_map/all_to_all | solution.py:248
  93.1 1.2 %convert_reduce_fusion = f32[192,128]{1,0:T(8,128)S(1)} fusion(bf16[16,192,128]{2,1,0:T(8,128)(2,1)} %all-to-all-done.1), kind=kLoop, calls=%fused_computation | loop fusion | flops 761856 | bytes 884736 | tf_op jit(solution)/shard_map/reduce_sum | solution.py:249
  95.1 4.1 %all-to-all-start.2 = ((f32[4,192,128]{2,1,0:T(8,128)}), f32[4,192,128]{2,1,0:T(8,128)S(1)}, u32[]{:S(2)}, u32[]{:S(2)}) async-start(f32[4,192,128]{2,1,0:T(8,128)} %broadcast_in_dim.2), calls=%async_computation.2 | async-start | bytes 786432 | tf_op jit(solution)/shard_map/all_to_all | solution.py:258
  99.3 4.8 %collective-permute-start.8 = (f32[128,256]{1,0:T(8,128)S(1)}, f32[128,256]{1,0:T(8,128)S(1)}, u32[]{:S(2)}, u32[]{:S(2)}) collective-permute-start(f32[128,256]{1,0:T(8,128)S(1)} %slice_bitcast_fusion), channel_id=1, source_target_pairs={{0,8},{8,0},{16,24},{24,16},{64,88},{72,80},{80,72},{88,64},{32,40... | collective-permute-start | bytes 393224 | tf_op jit(solution)/shard_map/ppermute | solution.py:255
  104.1 3.9 %all-to-all-done.2 = f32[4,192,128]{2,1,0:T(8,128)S(1)} async-done(((f32[4,192,128]{2,1,0:T(8,128)}), f32[4,192,128]{2,1,0:T(8,128)S(1)}, u32[]{:S(2)}, u32[]{:S(2)}) %all-to-all-start.2) | async-done | bytes 393248 | tf_op jit(solution)/shard_map/all_to_all | solution.py:258
  108.0 7.8 %collective-permute-start.9 = (f32[192,128]{1,0:T(8,128)S(1)}, f32[192,128]{1,0:T(8,128)S(1)}, u32[]{:S(2)}, u32[]{:S(2)}) collective-permute-start(f32[192,128]{1,0:T(8,128)S(1)} %reduce_sum.19), channel_id=1, source_target_pairs={{0,64},{64,0},{1,65},{65,1},{2,66},{66,2},{3,67},{67,3},{4,68},{68... | collective-permute-start | bytes 294920 | tf_op jit(solution)/shard_map/ppermute | solution.py:259
  (24 shorter events, 6.7 us)
Async XLA Ops:
  1.5 9.9 %collective-permute-start = (bf16[192,128]{1,0:T(8,128)(2,1)S(1)}, bf16[192,128]{1,0:T(8,128)(2,1)S(1)}, u32[]{:S(2)}, u32[]{:S(2)}) collective-permute-start(bf16[192,128]{1,0:T(8,128)(2,1)S(1)} %slice_select_fusion), channel_id=1, source_target_pairs={{0,16},{16,0},{1,17},{17,1},{2,18},{18,2},{3,19},{19,3},{4,20},{20... | collective-permute-start | bytes 147464 | tf_op jit(solution)/shard_map/ppermute | solution.py:231
  11.4 40.1 %all-to-all-start = ((bf16[4,128,3328]{2,1,0:T(8,128)(2,1)}), bf16[4,128,3328]{2,1,0:T(8,128)(2,1)S(1)}, u32[]{:S(2)}, u32[]{:S(2)}) async-start(bf16[4,128,3328]{2,1,0:T(8,128)(2,1)} %shard_map.50), calls=%async_computation | async-start | bytes 6815744 | tf_op jit(solution)/shard_map/all_to_all | solution.py:234
  16.4 6.0 %collective-permute-start.1 = (bf16[2,192,128]{2,1,0:T(8,128)(2,1)S(1)}, bf16[2,192,128]{2,1,0:T(8,128)(2,1)S(1)}, u32[]{:S(2)}, u32[]{:S(2)}) collective-permute-start(bf16[2,192,128]{2,1,0:T(8,128)(2,1)S(1)} %pad_maximum_fusion.2), channel_id=1, source_target_pairs={{0,1},{1,0},{2,3},{3,2},{4,5},{5,4},{6,7},{7,6},{8,9},{9,8},{10,11... | collective-permute-start | bytes 294920 | tf_op jit(solution)/shard_map/ppermute | solution.py:236
  23.1 17.5 %collective-permute-start.4 = (bf16[2,2,192,128]{3,2,1,0:T(8,128)(2,1)}, bf16[2,2,192,128]{3,2,1,0:T(8,128)(2,1)}, u32[]{:S(2)}, u32[]{:S(2)}) collective-permute-start(bf16[2,2,192,128]{3,2,1,0:T(8,128)(2,1)} %pad_maximum_fusion.refs_0_), channel_id=1, source_target_pairs={{0,6},{1,7},{2,0},{3,1},{4,2},{5,3},{6,4},{7,5},{8,14},{9,15},{10,... | collective-permute-start | bytes 589832 | tf_op jit(solution)/shard_map/ppermute | solution.py:240
  34.3 17.1 %collective-permute-start.3 = (bf16[2,2,192,128]{3,2,1,0:T(8,128)(2,1)}, bf16[2,2,192,128]{3,2,1,0:T(8,128)(2,1)}, u32[]{:S(2)}, u32[]{:S(2)}) collective-permute-start(bf16[2,2,192,128]{3,2,1,0:T(8,128)(2,1)} %pad_maximum_fusion.refs_0_), channel_id=1, source_target_pairs={{0,4},{1,5},{2,6},{3,7},{4,0},{5,1},{6,2},{7,3},{8,12},{9,13},{10,... | collective-permute-start | bytes 589832 | tf_op jit(solution)/shard_map/ppermute | solution.py:240
  36.3 15.2 %collective-permute-start.2 = (bf16[2,2,192,128]{3,2,1,0:T(8,128)(2,1)}, bf16[2,2,192,128]{3,2,1,0:T(8,128)(2,1)}, u32[]{:S(2)}, u32[]{:S(2)}) collective-permute-start(bf16[2,2,192,128]{3,2,1,0:T(8,128)(2,1)} %pad_maximum_fusion.refs_0_), channel_id=1, source_target_pairs={{0,2},{1,3},{2,4},{3,5},{4,6},{5,7},{6,0},{7,1},{8,10},{9,11},{10,... | collective-permute-start | bytes 589832 | tf_op jit(solution)/shard_map/ppermute | solution.py:240
  54.6 5.9 %collective-permute-start.6 = (f32[3072,128]{1,0:T(8,128)S(1)}, f32[3072,128]{1,0:T(8,128)S(1)}, u32[]{:S(2)}, u32[]{:S(2)}) collective-permute-start(f32[3072,128]{1,0:T(8,128)S(1)} %get-tuple-element.22), channel_id=1, source_target_pairs={{0,64},{64,0},{1,65},{65,1},{2,66},{66,2},{3,67},{67,3},{4,68},{68... | collective-permute-start | bytes 4718600 | tf_op jit(solution)/shard_map/ppermute | solution.py:244
  61.5 31.6 %all-to-all-start.1 = ((bf16[16,192,128]{2,1,0:T(8,128)(2,1)}), bf16[16,192,128]{2,1,0:T(8,128)(2,1)}, u32[]{:S(2)}, u32[]{:S(2)}) async-start(bf16[16,192,128]{2,1,0:T(8,128)(2,1)} %bitcast.19), calls=%async_computation.1 | async-start | bytes 1572864 | tf_op jit(solution)/shard_map/all_to_all | solution.py:248
  73.4 4.5 %collective-permute-start.5 = (bf16[4,2,2,192,128]{4,3,2,1,0:T(8,128)(2,1)S(1)}, bf16[4,2,2,192,128]{4,3,2,1,0:T(8,128)(2,1)S(1)}, u32[]{:S(2)}, u32[]{:S(2)}) collective-permute-start(bf16[4,2,2,192,128]{4,3,2,1,0:T(8,128)(2,1)S(1)} %shard_map.51.m_ref), channel_id=1, source_target_pairs={{0,64},{64,0},{1,65},{65,1},{2,66},{66,2},{3,67},{67,3},{4,68},{68... | collective-permute-start | bytes 2359304 | tf_op jit(solution)/shard_map/ppermute | solution.py:247
  80.9 0.7 copy-start
  81.6 17.6 %copy-start.1 = (f32[2,128,256]{2,1,0:T(8,128)S(1)}, f32[2,128,256]{2,1,0:T(8,128)}, u32[]{:S(2)}) copy-start(f32[2,128,256]{2,1,0:T(8,128)} %copy-done) | copy-start | bytes 786436
  81.6 17.6 %collective-permute-start.7 = (f32[2,128,256]{2,1,0:T(8,128)}, f32[2,128,256]{2,1,0:T(8,128)S(1)}, u32[]{:S(2)}, u32[]{:S(2)}) collective-permute-start(f32[2,128,256]{2,1,0:T(8,128)} %get-tuple-element.27), channel_id=1, source_target_pairs={{0,32},{8,40},{16,48},{24,56},{64,480},{72,488},{80,496},{88,504},... | collective-permute-start | bytes 786440 | tf_op jit(solution)/shard_map/ppermute | solution.py:252
  95.1 12.8 %all-to-all-start.2 = ((f32[4,192,128]{2,1,0:T(8,128)}), f32[4,192,128]{2,1,0:T(8,128)S(1)}, u32[]{:S(2)}, u32[]{:S(2)}) async-start(f32[4,192,128]{2,1,0:T(8,128)} %broadcast_in_dim.2), calls=%async_computation.2 | async-start | bytes 786432 | tf_op jit(solution)/shard_map/all_to_all | solution.py:258
  99.3 16.5 %collective-permute-start.8 = (f32[128,256]{1,0:T(8,128)S(1)}, f32[128,256]{1,0:T(8,128)S(1)}, u32[]{:S(2)}, u32[]{:S(2)}) collective-permute-start(f32[128,256]{1,0:T(8,128)S(1)} %slice_bitcast_fusion), channel_id=1, source_target_pairs={{0,8},{8,0},{16,24},{24,16},{64,88},{72,80},{80,72},{88,64},{32,40... | collective-permute-start | bytes 393224 | tf_op jit(solution)/shard_map/ppermute | solution.py:255
  108.0 8.7 %collective-permute-start.9 = (f32[192,128]{1,0:T(8,128)S(1)}, f32[192,128]{1,0:T(8,128)S(1)}, u32[]{:S(2)}, u32[]{:S(2)}) collective-permute-start(f32[192,128]{1,0:T(8,128)S(1)} %reduce_sum.19), channel_id=1, source_target_pairs={{0,64},{64,0},{1,65},{65,1},{2,66},{66,2},{3,67},{67,3},{4,68},{68... | collective-permute-start | bytes 294920 | tf_op jit(solution)/shard_map/ppermute | solution.py:259

commit v11 on v9

--- a/solution.py
+++ b/solution.py
@@ -123,7 +123,7 @@
     part, cols = depth * xhs * shard, 2 * wide
 
     def body(spot_ref, p_ref, m_ref, r_ref, near_ref, away_ref, stage, whole, sems):
-        core, yl, xl, xh, z = (spot_ref[i] for i in range(5))
+        core, yl, xl, xh = (spot_ref[i] for i in range(4))
         loads = []
         for flip in range(quads):
             loads.append(
@@ -132,12 +132,12 @@
                 )
             )
             loads[-1].start()
-        for back in range(depth):
-            at_z = lax.rem(z + depth - back, depth)
-            for slot in range(xhs):
-                left = jnp.where(core == 0, m_ref[back, slot], r_ref[back, slot])
-                right = jnp.where(core == 0, r_ref[back, slot], m_ref[back, slot])
-                whole[xh ^ slot, at_z] = jnp.concatenate([left, right], axis=1)
+        for z in range(depth):
+            for side in range(xhs):
+                ours, theirs = m_ref[z, side], r_ref[z, side]
+                left = jnp.where(core == 0, ours, theirs)
+                right = jnp.where(core == 0, theirs, ours)
+                whole[xh ^ side, z] = jnp.concatenate([left, right], axis=1)
         for load in loads:
             load.wait()
         t = stage[...].reshape(quads * rows, both)[:, :part]
@@ -153,14 +153,13 @@
         in_specs=[
             pl.BlockSpec(memory_space=pltpu.SMEM),
             pl.BlockSpec(memory_space=pl.ANY),
-            pl.BlockSpec(memory_space=pltpu.VMEM),
-            pl.BlockSpec(memory_space=pltpu.VMEM),
-        ],
+        ]
+        + [pl.BlockSpec(memory_space=pltpu.VMEM)] * 2,
         out_specs=[pl.BlockSpec(memory_space=pltpu.VMEM)] * 2,
         out_shape=[out, out],
         scratch_shapes=[
             pltpu.VMEM(packed.shape, packed.dtype),
-            pltpu.VMEM((xhs, depth, shard, cols), mine.dtype),
+            pltpu.VMEM((xhs, depth, shard, cols), packed.dtype),
             pltpu.SemaphoreType.DMA((quads,)),
         ],
         compiler_params=PARAMS,
@@ -194,25 +193,22 @@
 def local(tokens, weight, grad_out):
     shard, cols = weight.shape
     wide = cols // 2
-    depth = lax.axis_size("z")
     squares, flip_x, flip_y = partners([lax.axis_size(name) for name in CHIP])
-    spot = jnp.stack([lax.axis_index(name) for name in ("c", "yl", "xl", "xh", "z")])
+    spot = jnp.stack([lax.axis_index(name) for name in ("c", "yl", "xl", "xh")])
     spot = spot.astype(jnp.int32)
 
-    mine = jnp.where(spot[0] == 0, weight[:, :wide], weight[:, wide:])
-    mine = jnp.stack([mine, lax.ppermute(mine, "xh", SWAP)])
+    other = lax.ppermute(weight, "xh", SWAP)
     packed = pack(tokens, grad_out)
+    packed, other = lax.optimization_barrier((packed, other))
     packed = lax.all_to_all(packed, CHIP, 0, 0, axis_index_groups=squares)
     part = packed.shape[-1] - cols
-    gathered = [mine]
-    for back in range(1, depth):
-        shift = [(i, (i + back) % depth) for i in range(depth)]
-        gathered.append(lax.ppermute(mine, "z", shift))
-    packed, *gathered = lax.optimization_barrier((packed, *gathered))
+    mine = jnp.stack([weight, other])
+    mine = jnp.where(spot[0] == 0, mine[..., :wide], mine[..., wide:])
+    mine = lax.all_gather(mine, "z", axis=0)
+    packed, mine = lax.optimization_barrier((packed, mine))
 
     keep, send = terms(packed, spot, part)
     term = (keep + lax.ppermute(send, "c", SWAP)).astype(jnp.bfloat16)
-    mine = jnp.stack(gathered)
     mine, _ = lax.optimization_barrier((mine, send))
     other = lax.ppermute(mine, "c", SWAP)
     term = lax.all_to_all(term.reshape(-1, shard, wide), ("xh", "z"), 0, 0)

time: 139 us -> 115 us (0.83)
  starting transfers between devices: 83 us -> 48.8 us
  blocking collectives: 0 us -> 29.6 us
  local copies, waits for them, and re-layouts: 12.8 us -> 2.64 us
  waiting for transfers between devices: 27.6 us -> 17.9 us
    all_gather x0 -> x1, blocking collectives: none -> 29.6 us  [local(): mine = lax.all_gather(mine, 'z', axis=0)]
    ppermute x8 -> x1, starting transfers between devices: 32.8 us -> 5.48 us  [local(): other = lax.ppermute(weight, 'xh', SWAP)]
    ppermute x8 -> x1, waiting for transfers between devices: 18.4 us -> 0.01 us  [local(): other = lax.ppermute(weight, 'xh', SWAP)]
    unnamed x19 -> x8, local copies, waits for them, and re-layouts: 11.2 us -> 1.86 us
    all_to_all x1, waiting for transfers between devices: 1.03 us -> 5.03 us  [local(): term = lax.all_to_all(term.reshape(-1, shard, wide), ('xh', 'z'), 0, 0)]
    ppermute x1, waiting for transfers between devices: 0.01 us -> 3.01 us  [local(): term = (keep + lax.ppermute(send, 'c', SWAP)).astype(jnp.bfloat16)]
    ppermute x1, starting transfers between devices: 8.84 us -> 6.09 us  [local(): term = (keep + lax.ppermute(send, 'c', SWAP)).astype(jnp.bfloat16)]
    all_to_all x1, starting transfers between devices: 7.63 us -> 5.58 us  [local(): packed = lax.all_to_all(packed, CHIP, 0, 0, axis_index_groups=squares)]
  transfers between devices with their start and end apart: 16 -> 9, of which waited for: 7 -> 5; matrix products, arithmetic and copies ran while one was open for 10% -> 3% of each run, Pallas kernels for 3% -> 6%
where the time goes in v11:
time: 115 us; the launch traced here: 114 us
  starting transfers between devices  48.8 us (42%)
  blocking collectives  29.6 us (26%)
  waiting for transfers between devices  17.9 us (16%)
  Pallas kernels  9.66 us (8%)
  other arithmetic  4.66 us (4%)
  local copies, waits for them, and re-layouts  2.64 us (2%)
    all_gather x1, blocking collectives, local(): mine = lax.all_gather(mine, 'z', axis=0)  29.6 us
    all_to_all x1, waiting for transfers between devices, local(): half = jnp.sum(lax.all_to_all(lines, 'yh', 0, 0), axis=0)  7.48 us
    ppermute x1, starting transfers between devices, local(): other = lax.ppermute(half, 'c', SWAP)  7.48 us
    all_to_all x1, starting transfers between devices, local(): half = jnp.sum(lax.all_to_all(lines, 'yh', 0, 0), axis=0)  7.13 us
    ppermute x1, starting transfers between devices, local(): away = lax.ppermute(away, CHIP, flip_y)  6.38 us
    ppermute x1, starting transfers between devices, local(): term = (keep + lax.ppermute(send, 'c', SWAP)).astype(jnp.bfloat16)  6.09 us
    all_to_all x1, starting transfers between devices, local(): term = lax.all_to_all(term.reshape(-1, shard, wide), ('xh', 'z'), 0, 0)  5.9 us
    all_to_all x1, starting transfers between devices, local(): packed = lax.all_to_all(packed, CHIP, 0, 0, axis_index_groups=squares)  5.58 us
  transfers between devices with their start and end apart: 9, of which 5 were waited for; matrix products, arithmetic and copies ran while one was open for 3% of the time, Pallas kernels for 6%

profile of v11, /device:TPU:1, one launch (start us, length us, event | category | flops | bytes accessed | tf_op | source)
XLA Modules:
  0.0 114.0 jit_solution(16732694039983564940)
XLA Ops:
  0.6 5.5 %collective-permute-start = (bf16[192,256]{1,0:T(8,128)(2,1)}, bf16[192,256]{1,0:T(8,128)(2,1)}, u32[]{:S(2)}, u32[]{:S(2)}) collective-permute-start(bf16[192,256]{1,0:T(8,128)(2,1)} %param.4), channel_id=1, source_target_pairs={{0,16},{16,0},{1,17},{17,1},{2,18},{18,2},{3,19},{19,3},{4,20},{20... | collective-permute-start | bytes 294920 | tf_op jit(solution)/shard_map/ppermute | solution.py:200
  6.1 3.6 %shard_map.50 = bf16[4,128,3328]{2,1,0:T(8,128)(2,1)} custom-call(bf16[128,12288]{1,0:T(8,128)(2,1)} %t_ref.1, bf16[128,256]{1,0:T(8,128)(2,1)} %g_ref.1), custom_call_target="tpu_custom_call" | custom-call | tf_op jit(solution)/shard_map/pallas_call | solution.py:52
  9.7 5.6 %all-to-all-start = ((bf16[4,128,3328]{2,1,0:T(8,128)(2,1)}), bf16[4,128,3328]{2,1,0:T(8,128)(2,1)S(1)}, u32[]{:S(2)}, u32[]{:S(2)}) async-start(bf16[4,128,3328]{2,1,0:T(8,128)(2,1)} %shard_map.50), calls=%async_computation | async-start | bytes 6815744 | tf_op jit(solution)/shard_map/all_to_all | solution.py:203
  15.4 0.9 fusion.3
  16.2 29.6 %all-gather = bf16[16,192,128]{2,1,0:T(8,128)(2,1)} all-gather(bf16[2,192,128]{2,1,0:T(8,128)(2,1)S(1)} %fusion.3), channel_id=2, replica_groups=mesh['yh'=4,'c'=2,'yl'=2,'xh'=2,'xl'=2,'z'=8] {'z'}, dimensions={0}, use_global_device_ids=true | all-gather | bytes 884736 | tf_op jit(solution)/shard_map/all_gather | solution.py:207
  45.8 3.1 %shard_map.51 = (f32[3072,128]{1,0:T(8,128)S(1)}, f32[3072,128]{1,0:T(8,128)S(1)}) custom-call(s32[4]{0:T(128)S(1)} %pad_add_fusion.spot_ref, bf16[4,128,3328]{2,1,0:T(8,128)(2,1)S(1)} %all-to-all-done.p_ref), custom_call_target="tpu_custom_call" | custom-call | tf_op jit(solution)/shard_map/pallas_call | solution.py:104
  48.9 6.1 %collective-permute-start.2 = (f32[3072,128]{1,0:T(8,128)S(1)}, f32[3072,128]{1,0:T(8,128)S(1)}, u32[]{:S(2)}, u32[]{:S(2)}) collective-permute-start(f32[3072,128]{1,0:T(8,128)S(1)} %get-tuple-element.16), channel_id=1, source_target_pairs={{0,64},{64,0},{1,65},{65,1},{2,66},{66,2},{3,67},{67,3},{4,68},{68... | collective-permute-start | bytes 4718600 | tf_op jit(solution)/shard_map/ppermute | solution.py:211
  55.0 3.0 %collective-permute-done.2 = f32[3072,128]{1,0:T(8,128)S(1)} collective-permute-done((f32[3072,128]{1,0:T(8,128)S(1)}, f32[3072,128]{1,0:T(8,128)S(1)}, u32[]{:S(2)}, u32[]{:S(2)}) %collective-permute-start.2) | collective-permute-done | bytes 1572896 | tf_op jit(solution)/shard_map/ppermute | solution.py:211
  58.0 1.1 add_convert_fusion
  59.1 5.9 %all-to-all-start.1 = ((bf16[16,192,128]{2,1,0:T(8,128)(2,1)}), bf16[16,192,128]{2,1,0:T(8,128)(2,1)}, u32[]{:S(2)}, u32[]{:S(2)}) async-start(bf16[16,192,128]{2,1,0:T(8,128)(2,1)} %bitcast.18), calls=%async_computation.1 | async-start | bytes 1572864 | tf_op jit(solution)/shard_map/all_to_all | solution.py:214
  65.0 2.6 %collective-permute-start.1 = (bf16[8,2,192,128]{3,2,1,0:T(8,128)(2,1)}, bf16[8,2,192,128]{3,2,1,0:T(8,128)(2,1)S(1)}, u32[]{:S(2)}, u32[]{:S(2)}) collective-permute-start(bf16[8,2,192,128]{3,2,1,0:T(8,128)(2,1)} %bitcast.16), channel_id=1, source_target_pairs={{0,64},{64,0},{1,65},{65,1},{2,66},{66,2},{3,67},{67,3},{4,68},{68... | collective-permute-start | bytes 2359304 | tf_op jit(solution)/shard_map/ppermute | solution.py:213
  67.6 2.1 %collective-permute-done.1.r_ref = bf16[8,2,192,128]{3,2,1,0:T(8,128)(2,1)S(1)} collective-permute-done((bf16[8,2,192,128]{3,2,1,0:T(8,128)(2,1)}, bf16[8,2,192,128]{3,2,1,0:T(8,128)(2,1)S(1)}, u32[]{:S(2)}, u32[]{:S(2)}) %collective-permute-start.1) | collective-permute-done | bytes 786464 | tf_op jit(solution)/shard_map/ppermute | solution.py:213
  69.7 1.1 copy-done
  70.8 3.0 %shard_map.52 = (f32[2,128,256]{2,1,0:T(8,128)S(1)}, f32[2,128,256]{2,1,0:T(8,128)}) custom-call(s32[4]{0:T(128)S(1)} %pad_add_fusion.spot_ref, bf16[4,128,3328]{2,1,0:T(8,128)(2,1)S(1)} %all-to-all-done.p_ref, bf16[8,2,192,128]{3,2,1,0:T(8,128)(2,1)S(1)} %bitcast.17, bf16[8,2,192,128]{3,2,1,0:T(8,128)(2,1)S(1)} %collective-permute-done.1.r_ref), custom_call_target="tpu_custom_call" | custom-call | tf_op jit(solution)/shard_map/pallas_call | solution.py:151
  73.8 0.7 copy-done.1
  74.5 6.4 %collective-permute-start.3 = (f32[2,128,256]{2,1,0:T(8,128)}, f32[2,128,256]{2,1,0:T(8,128)S(1)}, u32[]{:S(2)}, u32[]{:S(2)}) collective-permute-start(f32[2,128,256]{2,1,0:T(8,128)} %get-tuple-element.21), channel_id=1, source_target_pairs={{0,32},{8,40},{16,48},{24,56},{64,480},{72,488},{80,496},{88,504},... | collective-permute-start | bytes 786440 | tf_op jit(solution)/shard_map/ppermute | solution.py:218
  80.9 5.0 %all-to-all-done.1 = bf16[16,192,128]{2,1,0:T(8,128)(2,1)} async-done(((bf16[16,192,128]{2,1,0:T(8,128)(2,1)}), bf16[16,192,128]{2,1,0:T(8,128)(2,1)}, u32[]{:S(2)}, u32[]{:S(2)}) %all-to-all-start.1) | async-done | bytes 786464 | tf_op jit(solution)/shard_map/all_to_all | solution.py:214
  86.0 1.2 %convert_reduce_fusion = f32[192,128]{1,0:T(8,128)S(1)} fusion(bf16[16,192,128]{2,1,0:T(8,128)(2,1)} %all-to-all-done.1), kind=kLoop, calls=%fused_computation | loop fusion | flops 761856 | bytes 884736 | tf_op jit(solution)/shard_map/reduce_sum | solution.py:215
  87.2 0.8 broadcast_in_dim.2
  88.0 7.1 %all-to-all-start.2 = ((f32[4,192,128]{2,1,0:T(8,128)}), f32[4,192,128]{2,1,0:T(8,128)S(1)}, u32[]{:S(2)}, u32[]{:S(2)}) async-start(f32[4,192,128]{2,1,0:T(8,128)} %broadcast_in_dim.2), calls=%async_computation.2 | async-start | bytes 786432 | tf_op jit(solution)/shard_map/all_to_all | solution.py:224
  95.2 2.2 %collective-permute-start.4 = (f32[128,256]{1,0:T(8,128)S(1)}, f32[128,256]{1,0:T(8,128)S(1)}, u32[]{:S(2)}, u32[]{:S(2)}) collective-permute-start(f32[128,256]{1,0:T(8,128)S(1)} %slice_bitcast_fusion), channel_id=1, source_target_pairs={{0,8},{8,0},{16,24},{24,16},{64,88},{72,80},{80,72},{88,64},{32,40... | collective-permute-start | bytes 393224 | tf_op jit(solution)/shard_map/ppermute | solution.py:221
  97.4 7.5 %all-to-all-done.2 = f32[4,192,128]{2,1,0:T(8,128)S(1)} async-done(((f32[4,192,128]{2,1,0:T(8,128)}), f32[4,192,128]{2,1,0:T(8,128)S(1)}, u32[]{:S(2)}, u32[]{:S(2)}) %all-to-all-start.2) | async-done | bytes 393248 | tf_op jit(solution)/shard_map/all_to_all | solution.py:224
  104.9 7.5 %collective-permute-start.5 = (f32[192,128]{1,0:T(8,128)S(1)}, f32[192,128]{1,0:T(8,128)S(1)}, u32[]{:S(2)}, u32[]{:S(2)}) collective-permute-start(f32[192,128]{1,0:T(8,128)S(1)} %reduce_sum.19), channel_id=1, source_target_pairs={{0,64},{64,0},{1,65},{65,1},{2,66},{66,2},{3,67},{67,3},{4,68},{68... | collective-permute-start | bytes 294920 | tf_op jit(solution)/shard_map/ppermute | solution.py:225
  113.4 0.7 pad_maximum_fusion
  (17 shorter events, 1.1 us)
Async XLA Ops:
  0.6 9.1 %collective-permute-start = (bf16[192,256]{1,0:T(8,128)(2,1)}, bf16[192,256]{1,0:T(8,128)(2,1)}, u32[]{:S(2)}, u32[]{:S(2)}) collective-permute-start(bf16[192,256]{1,0:T(8,128)(2,1)} %param.4), channel_id=1, source_target_pairs={{0,16},{16,0},{1,17},{17,1},{2,18},{18,2},{3,19},{19,3},{4,20},{20... | collective-permute-start | bytes 294920 | tf_op jit(solution)/shard_map/ppermute | solution.py:200
  9.7 5.7 %copy-start.3 = (bf16[192,256]{1,0:T(8,128)(2,1)S(1)}, bf16[192,256]{1,0:T(8,128)(2,1)}, u32[]{:S(2)}) copy-start(bf16[192,256]{1,0:T(8,128)(2,1)} %param.4) | copy-start | bytes 294916
  9.7 36.1 %all-to-all-start = ((bf16[4,128,3328]{2,1,0:T(8,128)(2,1)}), bf16[4,128,3328]{2,1,0:T(8,128)(2,1)S(1)}, u32[]{:S(2)}, u32[]{:S(2)}) async-start(bf16[4,128,3328]{2,1,0:T(8,128)(2,1)} %shard_map.50), calls=%async_computation | async-start | bytes 6815744 | tf_op jit(solution)/shard_map/all_to_all | solution.py:203
  48.9 9.1 %collective-permute-start.2 = (f32[3072,128]{1,0:T(8,128)S(1)}, f32[3072,128]{1,0:T(8,128)S(1)}, u32[]{:S(2)}, u32[]{:S(2)}) collective-permute-start(f32[3072,128]{1,0:T(8,128)S(1)} %get-tuple-element.16), channel_id=1, source_target_pairs={{0,64},{64,0},{1,65},{65,1},{2,66},{66,2},{3,67},{67,3},{4,68},{68... | collective-permute-start | bytes 4718600 | tf_op jit(solution)/shard_map/ppermute | solution.py:211
  59.1 26.9 %all-to-all-start.1 = ((bf16[16,192,128]{2,1,0:T(8,128)(2,1)}), bf16[16,192,128]{2,1,0:T(8,128)(2,1)}, u32[]{:S(2)}, u32[]{:S(2)}) async-start(bf16[16,192,128]{2,1,0:T(8,128)(2,1)} %bitcast.18), calls=%async_computation.1 | async-start | bytes 1572864 | tf_op jit(solution)/shard_map/all_to_all | solution.py:214
  65.0 4.7 %collective-permute-start.1 = (bf16[8,2,192,128]{3,2,1,0:T(8,128)(2,1)}, bf16[8,2,192,128]{3,2,1,0:T(8,128)(2,1)S(1)}, u32[]{:S(2)}, u32[]{:S(2)}) collective-permute-start(bf16[8,2,192,128]{3,2,1,0:T(8,128)(2,1)} %bitcast.16), channel_id=1, source_target_pairs={{0,64},{64,0},{1,65},{65,1},{2,66},{66,2},{3,67},{67,3},{4,68},{68... | collective-permute-start | bytes 2359304 | tf_op jit(solution)/shard_map/ppermute | solution.py:213
  69.7 1.1 copy-start
  73.8 0.7 copy-start.1
  74.5 20.6 %copy-start.2 = (f32[2,128,256]{2,1,0:T(8,128)S(1)}, f32[2,128,256]{2,1,0:T(8,128)}, u32[]{:S(2)}) copy-start(f32[2,128,256]{2,1,0:T(8,128)} %copy-done.1) | copy-start | bytes 786436
  74.5 20.6 %collective-permute-start.3 = (f32[2,128,256]{2,1,0:T(8,128)}, f32[2,128,256]{2,1,0:T(8,128)S(1)}, u32[]{:S(2)}, u32[]{:S(2)}) collective-permute-start(f32[2,128,256]{2,1,0:T(8,128)} %get-tuple-element.21), channel_id=1, source_target_pairs={{0,32},{8,40},{16,48},{24,56},{64,480},{72,488},{80,496},{88,504},... | collective-permute-start | bytes 786440 | tf_op jit(solution)/shard_map/ppermute | solution.py:218
  88.0 16.9 %all-to-all-start.2 = ((f32[4,192,128]{2,1,0:T(8,128)}), f32[4,192,128]{2,1,0:T(8,128)S(1)}, u32[]{:S(2)}, u32[]{:S(2)}) async-start(f32[4,192,128]{2,1,0:T(8,128)} %broadcast_in_dim.2), calls=%async_computation.2 | async-start | bytes 786432 | tf_op jit(solution)/shard_map/all_to_all | solution.py:224
  95.2 17.2 %collective-permute-start.4 = (f32[128,256]{1,0:T(8,128)S(1)}, f32[128,256]{1,0:T(8,128)S(1)}, u32[]{:S(2)}, u32[]{:S(2)}) collective-permute-start(f32[128,256]{1,0:T(8,128)S(1)} %slice_bitcast_fusion), channel_id=1, source_target_pairs={{0,8},{8,0},{16,24},{24,16},{64,88},{72,80},{80,72},{88,64},{32,40... | collective-permute-start | bytes 393224 | tf_op jit(solution)/shard_map/ppermute | solution.py:221
  104.9 8.4 %collective-permute-start.5 = (f32[192,128]{1,0:T(8,128)S(1)}, f32[192,128]{1,0:T(8,128)S(1)}, u32[]{:S(2)}, u32[]{:S(2)}) collective-permute-start(f32[192,128]{1,0:T(8,128)S(1)} %reduce_sum.19), channel_id=1, source_target_pairs={{0,64},{64,0},{1,65},{65,1},{2,66},{66,2},{3,67},{67,3},{4,68},{68... | collective-permute-start | bytes 294920 | tf_op jit(solution)/shard_map/ppermute | solution.py:225

commit v12 on v11

v12 whole, which is shorter than its diff:
```python
import jax
import jax.numpy as jnp
from jax import lax
from jax.experimental import pallas as pl
from jax.experimental.pallas import tpu as pltpu
from jax.sharding import Mesh, PartitionSpec as P

PARAMS = pltpu.CompilerParams(vmem_limit_bytes=32 * 1024 * 1024)
ALONE = pltpu.CompilerParams(vmem_limit_bytes=60 * 1024 * 1024)
SWAP = [(0, 1), (1, 0)]
CHIP = ("yh", "c", "yl", "xh", "xl", "zh", "zl")


def pack(tokens, grad_out, shard):
    rows, width = tokens.shape
    cols = grad_out.shape[1]
    node = width // 8
    part = width // 8

    def body(t_ref, g_ref, o_ref, held, stage, t_sems, g_sems, o_sems):
        loads, sides, stores = [], [], []
        for quad in range(4):
            for xh in range(2):
                at = ((quad // 2) * 4 + xh * 2 + quad % 2) * node
                copy = pltpu.make_async_copy(
                    t_ref.at[:, pl.ds(at, node)],
                    held.at[quad * 2 + xh],
                    t_sems.at[quad * 2 + xh],
                )
                copy.start()
                loads.append(copy)
        for o in range(8):
            copy = pltpu.make_async_copy(
                g_ref, stage.at[o, :, pl.ds(part, cols)], g_sems.at[o]
            )
            copy.start()
            sides.append(copy)
        for quad in range(4):
            for xh in range(2):
                loads[quad * 2 + xh].wait()
                t = held[quad * 2 + xh]
                for zl in range(2):
                    pieces = [
                        t[:, at : at + shard]
                        for at in range(zl * shard, node, 2 * shard)
                    ]
                    stage[quad * 2 + zl, :, xh * node // 2 : (xh + 1) * node // 2] = (
                        jnp.concatenate(pieces, axis=1)
                    )
            for zl in range(2):
                o = quad * 2 + zl
                sides[o].wait()
                copy = pltpu.make_async_copy(stage.at[o], o_ref.at[o], o_sems.at[o])
                copy.start()
                stores.append(copy)
        for copy in stores:
            copy.wait()

    shape = (8, rows, part + cols)
    return pl.pallas_call(
        body,
        in_specs=[pl.BlockSpec(memory_space=pl.ANY)] * 2,
        out_specs=pl.BlockSpec(memory_space=pl.ANY),
        out_shape=jax.ShapeDtypeStruct(shape, tokens.dtype),
        scratch_shapes=[
            pltpu.VMEM((8, rows, node), tokens.dtype),
            pltpu.VMEM(shape, tokens.dtype),
        ]
        + [pltpu.SemaphoreType.DMA((8,))] * 3,
        compiler_params=ALONE,
    )(tokens, grad_out)


def terms(packed, spot, part):
    sharers, rows, both = packed.shape
    cols = both - part
    wide = cols // 2
    step = 2
    steps = sharers // step

    def body(spot_ref, p_ref, keep_ref, send_ref, stage, sems):
        loads = []
        for k in range(steps):
            at = pl.ds(k * step, step)
            loads.append(
                pltpu.make_async_copy(p_ref.at[at], stage.at[at], sems.at[k])
            )
            loads[-1].start()
        first = spot_ref[0] == 0
        for k in range(steps):
            loads[k].wait()
            p = stage[k * step : (k + 1) * step].reshape(step * rows, both)
            left, right = p[:, part : part + wide], p[:, part + wide :]
            g = jnp.concatenate(
                [jnp.where(first, left, right), jnp.where(first, right, left)], axis=1
            )
            term = lax.dot_general(
                p[:, :part],
                g,
                (((0,), (0,)), ((), ())),
                preferred_element_type=jnp.float32,
            )
            if k == 0:
                keep_ref[...] = term[:, :wide]
                send_ref[...] = term[:, wide:]
            else:
                keep_ref[...] += term[:, :wide]
                send_ref[...] += term[:, wide:]

    half = jax.ShapeDtypeStruct((part, wide), jnp.float32)
    return pl.pallas_call(
        body,
        in_specs=[
            pl.BlockSpec(memory_space=pltpu.SMEM),
            pl.BlockSpec(memory_space=pl.ANY),
        ],
        out_specs=[pl.BlockSpec(memory_space=pltpu.VMEM)] * 2,
        out_shape=[half, half],
        scratch_shapes=[
            pltpu.VMEM(packed.shape, packed.dtype),
            pltpu.SemaphoreType.DMA((steps,)),
        ],
        compiler_params=PARAMS,
    )(spot, packed)


def project(packed, mine, other, spot):
    sharers, rows, both = packed.shape
    depth, xhs, shard, wide = mine.shape
    part, cols = depth * xhs * shard, 2 * wide

    def body(spot_ref, p_ref, m_ref, r_ref, near_ref, away_ref, stage, whole, sems):
        core, yl, xl, zl, xh = (spot_ref[i] for i in range(5))
        own = (yl * 2 + xl) * 2 + zl
        loads = []
        for flip in range(sharers):
            loads.append(
                pltpu.make_async_copy(
                    p_ref.at[own ^ flip], stage.at[flip], sems.at[flip]
                )
            )
            loads[-1].start()
        for z in range(depth):
            for side in range(xhs):
                ours, theirs = m_ref[z, side], r_ref[z, side]
                left = jnp.where(core == 0, ours, theirs)
                right = jnp.where(core == 0, theirs, ours)
                whole[xh ^ side, z] = jnp.concatenate([left, right], axis=1)
        for load in loads:
            load.wait()
        t = stage[...].reshape(sharers * rows, both)[:, :part]
        new = jnp.dot(
            t, whole[...].reshape(part, cols), preferred_element_type=jnp.float32
        ).reshape(sharers, rows, cols)
        near_ref[...] = new[: sharers // 2]
        away_ref[...] = new[sharers // 2 :]

    out = jax.ShapeDtypeStruct((sharers // 2, rows, cols), jnp.float32)
    return pl.pallas_call(
        body,
        in_specs=[
            pl.BlockSpec(memory_space=pltpu.SMEM),
            pl.BlockSpec(memory_space=pl.ANY),
        ]
        + [pl.BlockSpec(memory_space=pltpu.VMEM)] * 2,
        out_specs=[pl.BlockSpec(memory_space=pltpu.VMEM)] * 2,
        out_shape=[out, out],
        scratch_shapes=[
            pltpu.VMEM(packed.shape, packed.dtype),
            pltpu.VMEM((xhs, depth, shard, cols), packed.dtype),
            pltpu.SemaphoreType.DMA((sharers,)),
        ],
        compiler_params=PARAMS,
    )(spot, packed, mine, other)


def partners(sizes):
    yh, cores, yl, xh, xl, zh, zl = sizes
    rings = (yh * yl, xh * xl, zh * zl)

    def place(c, y, x, z):
        at = ((y // yl) * cores + c) * yl + y % yl
        return (at * xh * xl + x) * zh * zl + z

    def other(i, n, c):
        if c == 0:
            return i ^ 1
        return (i + 1) % n if i % 2 else (i - 1) % n

    flips, cubes = ([], [], []), []
    for c in range(cores):
        for y in range(rings[0]):
            for x in range(rings[1]):
                for z in range(rings[2]):
                    here = (y, x, z)
                    there = [other(i, n, c) for i, n in zip(here, rings)]
                    for axis in range(3):
                        to = list(here)
                        to[axis] = there[axis]
                        flips[axis].append((place(c, *here), place(c, *to)))
                    if all(i % 2 == 0 for i in here):
                        pairs = list(zip(here, there))
                        cubes.append(
                            [
                                place(c, a, b, d)
                                for a in pairs[0]
                                for b in pairs[1]
                                for d in pairs[2]
                            ]
                        )
    return cubes, *flips


def local(tokens, weight, grad_out):
    shard, cols = weight.shape
    wide = cols // 2
    cubes, flip_y, flip_x, flip_z = partners([lax.axis_size(name) for name in CHIP])
    spot = jnp.stack([lax.axis_index(name) for name in ("c", "yl", "xl", "zl", "xh")])
    spot = spot.astype(jnp.int32)

    other = lax.ppermute(weight, "xh", SWAP)
    packed = pack(tokens, grad_out, shard)
    packed, other = lax.optimization_barrier((packed, other))
    packed = lax.all_to_all(packed, CHIP, 0, 0, axis_index_groups=cubes)
    part = packed.shape[-1] - cols
    mine = jnp.stack([weight, other])
    mine = jnp.where(spot[0] == 0, mine[..., :wide], mine[..., wide:])
    mine = lax.all_gather(mine, "zh", axis=0)
    packed, mine = lax.optimization_barrier((packed, mine))

    keep, send = terms(packed, spot, part)
    term = (keep + lax.ppermute(send, "c", SWAP)).astype(jnp.bfloat16)
    mine, _ = lax.optimization_barrier((mine, send))
    other = lax.ppermute(mine, "c", SWAP)
    term = lax.all_to_all(term.reshape(-1, shard, wide), ("xh", "zh"), 0, 0)
    summed = jnp.sum(term, axis=0, dtype=jnp.float32)

    near, away = project(packed, mine, other, spot)
    away = lax.ppermute(away, CHIP, flip_y)
    near, _ = lax.optimization_barrier((near, summed))
    near = near + away
    near = near[:2] + lax.ppermute(near[2:], CHIP, flip_x)

    lines = jnp.broadcast_to(summed[None], (lax.axis_size("yh"), shard, wide))
    half = jnp.sum(lax.all_to_all(lines, "yh", 0, 0), axis=0)
    other = lax.ppermute(half, "c", SWAP)
    near, _ = lax.optimization_barrier((near, half))
    output = near[0] + lax.ppermute(near[1], CHIP, flip_z)
    first = spot[0] == 0
    weight_grad = jnp.concatenate(
        [jnp.where(first, half, other), jnp.where(first, other, half)], axis=1
    )
    return output.astype(jnp.bfloat16), weight_grad


def solution(mesh):
    inner = Mesh(mesh.devices.reshape(4, 2, 2, 2, 2, 4, 2), CHIP)
    rows = P(CHIP, None)
    owners = P(("yl", "xh", "xl", "zh", "zl"), None)
    return jax.shard_map(
        local,
        mesh=inner,
        in_specs=(rows, owners, rows),
        out_specs=(rows, owners),
        check_vma=False,
    )
```

time: 115 us -> 117 us (1.017)
  starting transfers between devices: 48.8 us -> 57.2 us
  waiting for transfers between devices: 17.9 us -> 12.6 us
  other arithmetic: 4.66 us -> 2.39 us
  local copies, waits for them, and re-layouts: 2.64 us -> 0.89 us
  Pallas kernels: 9.66 us -> 11.3 us
  blocking collectives: 29.6 us -> 30.9 us
    ppermute x1 -> x2, waiting for transfers between devices: 0.01 us -> 8.31 us  [the longest x1 6.69 us: local(): near = near[:2] + lax.ppermute(near[2:], CHIP, flip_x)]
    all_to_all x2, starting transfers between devices: 11.5 us -> 19 us  [the longest x1 13.6 us: local(): packed = lax.all_to_all(packed, CHIP, 0, 0, axis_index_groups=cubes)]
    all_to_all x1, waiting for transfers between devices: 7.48 us -> 1.24 us  [local(): half = jnp.sum(lax.all_to_all(lines, 'yh', 0, 0), axis=0)]
    ppermute x1 -> x2, starting transfers between devices: 2.23 us -> 7.56 us  [the longest x1 5.64 us: local(): output = near[0] + lax.ppermute(near[1], CHIP, flip_z)]
    ppermute x1, starting transfers between devices: 7.48 us -> 4.33 us  [local(): other = lax.ppermute(half, 'c', SWAP)]
    ppermute x1, waiting for transfers between devices: 3.01 us -> 0.01 us  [local(): term = (keep + lax.ppermute(send, 'c', SWAP)).astype(jnp.bfloat16)]
    ppermute x1, starting transfers between devices: 6.09 us -> 3.95 us  [local(): term = (keep + lax.ppermute(send, 'c', SWAP)).astype(jnp.bfloat16)]
    ppermute x1, waiting for transfers between devices: 2.1 us -> 0.01 us  [local(): other = lax.ppermute(mine, 'c', SWAP)]
  transfers between devices with their start and end apart: 9 -> 10, of which waited for: 5 -> 4; matrix products, arithmetic and copies ran while one was open for 3% -> 2% of each run, Pallas kernels for 6% -> 6%
where the time goes in v12:
time: 117 us; the launch traced here: 116 us
  starting transfers between devices  57.2 us (49%)
  blocking collectives  30.9 us (26%)
  waiting for transfers between devices  12.6 us (11%)
  Pallas kernels  11.3 us (10%)
  other arithmetic  2.39 us (2%)
    all_gather x1, blocking collectives, local(): mine = lax.all_gather(mine, 'zh', axis=0)  30.9 us
    all_to_all x1, starting transfers between devices, local(): packed = lax.all_to_all(packed, CHIP, 0, 0, axis_index_groups=cubes)  13.6 us
    all_to_all x1, starting transfers between devices, local(): half = jnp.sum(lax.all_to_all(lines, 'yh', 0, 0), axis=0)  7.92 us
    ppermute x1, starting transfers between devices, local(): away = lax.ppermute(away, CHIP, flip_y)  7.04 us
    ppermute x1, waiting for transfers between devices, local(): near = near[:2] + lax.ppermute(near[2:], CHIP, flip_x)  6.69 us
    ppermute x1, starting transfers between devices, local(): output = near[0] + lax.ppermute(near[1], CHIP, flip_z)  5.64 us
    ppermute x1, starting transfers between devices, local(): other = lax.ppermute(weight, 'xh', SWAP)  5.48 us
    all_to_all x1, starting transfers between devices, local(): term = lax.all_to_all(term.reshape(-1, shard, wide), ('xh', 'zh'), 0, 0)  5.37 us
  transfers between devices with their start and end apart: 10, of which 4 were waited for; matrix products, arithmetic and copies ran while one was open for 2% of the time, Pallas kernels for 6%

profile of v12, /device:TPU:1, one launch (start us, length us, event | category | flops | bytes accessed | tf_op | source)
XLA Modules:
  0.0 116.1 jit_solution(9985929375889347759)
XLA Ops:
  0.6 5.5 %collective-permute-start = (bf16[192,256]{1,0:T(8,128)(2,1)}, bf16[192,256]{1,0:T(8,128)(2,1)S(1)}, u32[]{:S(2)}, u32[]{:S(2)}) collective-permute-start(bf16[192,256]{1,0:T(8,128)(2,1)} %param.4), channel_id=1, source_target_pairs={{0,16},{16,0},{1,17},{17,1},{2,18},{18,2},{3,19},{19,3},{4,20},{20... | collective-permute-start | bytes 294920 | tf_op jit(solution)/shard_map/ppermute | solution.py:221
  6.1 3.9 %shard_map.50 = bf16[8,128,1792]{2,1,0:T(8,128)(2,1)} custom-call(bf16[128,12288]{1,0:T(8,128)(2,1)} %t_ref.1, bf16[128,256]{1,0:T(8,128)(2,1)} %g_ref.1), custom_call_target="tpu_custom_call" | custom-call | tf_op jit(solution)/shard_map/pallas_call | solution.py:60
  10.0 13.6 %all-to-all-start = ((bf16[8,128,1792]{2,1,0:T(8,128)(2,1)}), bf16[8,128,1792]{2,1,0:T(8,128)(2,1)}, u32[]{:S(2)}, u32[]{:S(2)}) async-start(bf16[8,128,1792]{2,1,0:T(8,128)(2,1)} %shard_map.50), calls=%async_computation | async-start | bytes 7340032 | tf_op jit(solution)/shard_map/all_to_all | solution.py:224
  23.7 0.1 stack.32.spot_ref
  23.8 30.9 %all-gather = bf16[8,192,128]{2,1,0:T(8,128)(2,1)S(1)} all-gather(bf16[2,192,128]{2,1,0:T(8,128)(2,1)S(1)} %fusion.2), channel_id=2, replica_groups=mesh['yh'=4,'c'=2,'yl'=2,'xh'=2,'xl'=2,'zh'=4,'zl'=2] {'zh'}, dimensions={0}, use_global_device_ids=true | all-gather | bytes 491520 | tf_op jit(solution)/shard_map/all_gather | solution.py:228
  54.7 3.8 %shard_map.51 = (f32[1536,128]{1,0:T(8,128)S(1)}, f32[1536,128]{1,0:T(8,128)S(1)}) custom-call(s32[5]{0:T(128)S(1)} %stack.32.spot_ref, bf16[8,128,1792]{2,1,0:T(8,128)(2,1)} %all-to-all-done.p_ref), custom_call_target="tpu_custom_call" | custom-call | tf_op jit(solution)/shard_map/pallas_call | solution.py:111
  58.5 3.9 %collective-permute-start.2 = (f32[1536,128]{1,0:T(8,128)S(1)}, f32[1536,128]{1,0:T(8,128)S(1)}, u32[]{:S(2)}, u32[]{:S(2)}) collective-permute-start(f32[1536,128]{1,0:T(8,128)S(1)} %get-tuple-element.17), channel_id=1, source_target_pairs={{0,64},{64,0},{1,65},{65,1},{2,66},{66,2},{3,67},{67,3},{4,68},{68... | collective-permute-start | bytes 2359304 | tf_op jit(solution)/shard_map/ppermute | solution.py:232
  62.5 1.9 %collective-permute-start.1 = (bf16[4,2,192,128]{3,2,1,0:T(8,128)(2,1)S(1)}, bf16[4,2,192,128]{3,2,1,0:T(8,128)(2,1)S(1)}, u32[]{:S(2)}, u32[]{:S(2)}) collective-permute-start(bf16[4,2,192,128]{3,2,1,0:T(8,128)(2,1)S(1)} %bitcast.15), channel_id=1, source_target_pairs={{0,64},{64,0},{1,65},{65,1},{2,66},{66,2},{3,67},{67,3},{4,68},{68... | collective-permute-start | bytes 1179656 | tf_op jit(solution)/shard_map/ppermute | solution.py:234
  64.4 0.8 add_convert_fusion
  65.2 5.4 %all-to-all-start.1 = ((bf16[8,192,128]{2,1,0:T(8,128)(2,1)}), bf16[8,192,128]{2,1,0:T(8,128)(2,1)S(1)}, u32[]{:S(2)}, u32[]{:S(2)}) async-start(bf16[8,192,128]{2,1,0:T(8,128)(2,1)} %bitcast.8), calls=%async_computation.1 | async-start | bytes 786432 | tf_op jit(solution)/shard_map/all_to_all | solution.py:235
  70.6 3.6 %shard_map.52 = (f32[4,128,256]{2,1,0:T(8,128)S(1)}, f32[4,128,256]{2,1,0:T(8,128)S(1)}) custom-call(s32[5]{0:T(128)S(1)} %stack.32.spot_ref, bf16[8,128,1792]{2,1,0:T(8,128)(2,1)} %all-to-all-done.p_ref, bf16[4,2,192,128]{3,2,1,0:T(8,128)(2,1)S(1)} %bitcast.16, bf16[4,2,192,128]{3,2,1,0:T(8,128)(2,1)S(1)} %collective-permute-done.1.r_ref), custom_call_target="tpu_custom_call" | custom-call | tf_op jit(solution)/shard_map/pallas_call | solution.py:159
  74.2 7.0 %collective-permute-start.3 = (f32[4,128,256]{2,1,0:T(8,128)S(1)}, f32[4,128,256]{2,1,0:T(8,128)S(1)}, u32[]{:S(2)}, u32[]{:S(2)}) collective-permute-start(f32[4,128,256]{2,1,0:T(8,128)S(1)} %get-tuple-element.22), channel_id=1, source_target_pairs={{0,32},{1,33},{2,34},{3,35},{4,36},{5,37},{6,38},{7,39},{8,40},{9,... | collective-permute-start | bytes 1572872 | tf_op jit(solution)/shard_map/ppermute | solution.py:239
  81.3 3.1 %all-to-all-done.1 = bf16[8,192,128]{2,1,0:T(8,128)(2,1)S(1)} async-done(((bf16[8,192,128]{2,1,0:T(8,128)(2,1)}), bf16[8,192,128]{2,1,0:T(8,128)(2,1)S(1)}, u32[]{:S(2)}, u32[]{:S(2)}) %all-to-all-start.1) | async-done | bytes 393248 | tf_op jit(solution)/shard_map/all_to_all | solution.py:235
  84.4 0.8 broadcast_in_dim.2
  85.1 7.9 %all-to-all-start.2 = ((f32[4,192,128]{2,1,0:T(8,128)}), f32[4,192,128]{2,1,0:T(8,128)S(1)}, u32[]{:S(2)}, u32[]{:S(2)}) async-start(f32[4,192,128]{2,1,0:T(8,128)} %broadcast_in_dim.2), calls=%async_computation.2 | async-start | bytes 786432 | tf_op jit(solution)/shard_map/all_to_all | solution.py:245
  93.1 0.1 add.13
  93.2 1.9 %collective-permute-start.4 = (f32[2,128,256]{2,1,0:T(8,128)S(1)}, f32[2,128,256]{2,1,0:T(8,128)S(1)}, u32[]{:S(2)}, u32[]{:S(2)}) collective-permute-start(f32[2,128,256]{2,1,0:T(8,128)S(1)} %slice.27), channel_id=1, source_target_pairs={{0,8},{1,9},{2,10},{3,11},{4,12},{5,13},{6,14},{7,15},{8,0},{9,1},... | collective-permute-start | bytes 786440 | tf_op jit(solution)/shard_map/ppermute | solution.py:242
  95.1 6.7 %collective-permute-done.4 = f32[2,128,256]{2,1,0:T(8,128)S(1)} collective-permute-done((f32[2,128,256]{2,1,0:T(8,128)S(1)}, f32[2,128,256]{2,1,0:T(8,128)S(1)}, u32[]{:S(2)}, u32[]{:S(2)}) %collective-permute-start.4) | collective-permute-done | bytes 262176 | tf_op jit(solution)/shard_map/ppermute | solution.py:242
  101.8 1.2 %all-to-all-done.2 = f32[4,192,128]{2,1,0:T(8,128)S(1)} async-done(((f32[4,192,128]{2,1,0:T(8,128)}), f32[4,192,128]{2,1,0:T(8,128)S(1)}, u32[]{:S(2)}, u32[]{:S(2)}) %all-to-all-start.2) | async-done | bytes 393248 | tf_op jit(solution)/shard_map/all_to_all | solution.py:245
  103.1 4.3 %collective-permute-start.6 = (f32[192,128]{1,0:T(8,128)S(1)}, f32[192,128]{1,0:T(8,128)S(1)}, u32[]{:S(2)}, u32[]{:S(2)}) collective-permute-start(f32[192,128]{1,0:T(8,128)S(1)} %reduce_sum.19), channel_id=1, source_target_pairs={{0,64},{64,0},{1,65},{65,1},{2,66},{66,2},{3,67},{67,3},{4,68},{68... | collective-permute-start | bytes 294920 | tf_op jit(solution)/shard_map/ppermute | solution.py:246
  107.4 5.6 %collective-permute-start.5 = (f32[128,256]{1,0:T(8,128)S(1)}, f32[128,256]{1,0:T(8,128)S(1)}, u32[]{:S(2)}, u32[]{:S(2)}) collective-permute-start(f32[128,256]{1,0:T(8,128)S(1)} %slice_bitcast_fusion), channel_id=1, source_target_pairs={{0,1},{1,0},{2,3},{3,2},{4,5},{5,4},{6,7},{7,6},{8,9},{9,8},{10,11... | collective-permute-start | bytes 393224 | tf_op jit(solution)/shard_map/ppermute | solution.py:248
  113.1 0.7 pad_maximum_fusion
  113.8 1.6 %collective-permute-done.5 = f32[128,256]{1,0:T(8,128)S(1)} collective-permute-done((f32[128,256]{1,0:T(8,128)S(1)}, f32[128,256]{1,0:T(8,128)S(1)}, u32[]{:S(2)}, u32[]{:S(2)}) %collective-permute-start.5) | collective-permute-done | bytes 131104 | tf_op jit(solution)/shard_map/ppermute | solution.py:248
  115.4 0.6 fusion
  (15 shorter events, 0.2 us)
Async XLA Ops:
  0.6 9.4 %collective-permute-start = (bf16[192,256]{1,0:T(8,128)(2,1)}, bf16[192,256]{1,0:T(8,128)(2,1)S(1)}, u32[]{:S(2)}, u32[]{:S(2)}) collective-permute-start(bf16[192,256]{1,0:T(8,128)(2,1)} %param.4), channel_id=1, source_target_pairs={{0,16},{16,0},{1,17},{17,1},{2,18},{18,2},{3,19},{19,3},{4,20},{20... | collective-permute-start | bytes 294920 | tf_op jit(solution)/shard_map/ppermute | solution.py:221
  10.0 13.7 %copy-start = (bf16[192,256]{1,0:T(8,128)(2,1)S(1)}, bf16[192,256]{1,0:T(8,128)(2,1)}, u32[]{:S(2)}) copy-start(bf16[192,256]{1,0:T(8,128)(2,1)} %param.4) | copy-start | bytes 294916
  10.0 44.6 %all-to-all-start = ((bf16[8,128,1792]{2,1,0:T(8,128)(2,1)}), bf16[8,128,1792]{2,1,0:T(8,128)(2,1)}, u32[]{:S(2)}, u32[]{:S(2)}) async-start(bf16[8,128,1792]{2,1,0:T(8,128)(2,1)} %shard_map.50), calls=%async_computation | async-start | bytes 7340032 | tf_op jit(solution)/shard_map/all_to_all | solution.py:224
  58.5 5.9 %collective-permute-start.2 = (f32[1536,128]{1,0:T(8,128)S(1)}, f32[1536,128]{1,0:T(8,128)S(1)}, u32[]{:S(2)}, u32[]{:S(2)}) collective-permute-start(f32[1536,128]{1,0:T(8,128)S(1)} %get-tuple-element.17), channel_id=1, source_target_pairs={{0,64},{64,0},{1,65},{65,1},{2,66},{66,2},{3,67},{67,3},{4,68},{68... | collective-permute-start | bytes 2359304 | tf_op jit(solution)/shard_map/ppermute | solution.py:232
  62.5 8.1 %collective-permute-start.1 = (bf16[4,2,192,128]{3,2,1,0:T(8,128)(2,1)S(1)}, bf16[4,2,192,128]{3,2,1,0:T(8,128)(2,1)S(1)}, u32[]{:S(2)}, u32[]{:S(2)}) collective-permute-start(bf16[4,2,192,128]{3,2,1,0:T(8,128)(2,1)S(1)} %bitcast.15), channel_id=1, source_target_pairs={{0,64},{64,0},{1,65},{65,1},{2,66},{66,2},{3,67},{67,3},{4,68},{68... | collective-permute-start | bytes 1179656 | tf_op jit(solution)/shard_map/ppermute | solution.py:234
  65.2 19.1 %all-to-all-start.1 = ((bf16[8,192,128]{2,1,0:T(8,128)(2,1)}), bf16[8,192,128]{2,1,0:T(8,128)(2,1)S(1)}, u32[]{:S(2)}, u32[]{:S(2)}) async-start(bf16[8,192,128]{2,1,0:T(8,128)(2,1)} %bitcast.8), calls=%async_computation.1 | async-start | bytes 786432 | tf_op jit(solution)/shard_map/all_to_all | solution.py:235
  74.2 18.8 %collective-permute-start.3 = (f32[4,128,256]{2,1,0:T(8,128)S(1)}, f32[4,128,256]{2,1,0:T(8,128)S(1)}, u32[]{:S(2)}, u32[]{:S(2)}) collective-permute-start(f32[4,128,256]{2,1,0:T(8,128)S(1)} %get-tuple-element.22), channel_id=1, source_target_pairs={{0,32},{1,33},{2,34},{3,35},{4,36},{5,37},{6,38},{7,39},{8,40},{9,... | collective-permute-start | bytes 1572872 | tf_op jit(solution)/shard_map/ppermute | solution.py:239
  85.1 17.9 %all-to-all-start.2 = ((f32[4,192,128]{2,1,0:T(8,128)}), f32[4,192,128]{2,1,0:T(8,128)S(1)}, u32[]{:S(2)}, u32[]{:S(2)}) async-start(f32[4,192,128]{2,1,0:T(8,128)} %broadcast_in_dim.2), calls=%async_computation.2 | async-start | bytes 786432 | tf_op jit(solution)/shard_map/all_to_all | solution.py:245
  93.2 8.6 %collective-permute-start.4 = (f32[2,128,256]{2,1,0:T(8,128)S(1)}, f32[2,128,256]{2,1,0:T(8,128)S(1)}, u32[]{:S(2)}, u32[]{:S(2)}) collective-permute-start(f32[2,128,256]{2,1,0:T(8,128)S(1)} %slice.27), channel_id=1, source_target_pairs={{0,8},{1,9},{2,10},{3,11},{4,12},{5,13},{6,14},{7,15},{8,0},{9,1},... | collective-permute-start | bytes 786440 | tf_op jit(solution)/shard_map/ppermute | solution.py:242
  103.1 10.0 %collective-permute-start.6 = (f32[192,128]{1,0:T(8,128)S(1)}, f32[192,128]{1,0:T(8,128)S(1)}, u32[]{:S(2)}, u32[]{:S(2)}) collective-permute-start(f32[192,128]{1,0:T(8,128)S(1)} %reduce_sum.19), channel_id=1, source_target_pairs={{0,64},{64,0},{1,65},{65,1},{2,66},{66,2},{3,67},{67,3},{4,68},{68... | collective-permute-start | bytes 294920 | tf_op jit(solution)/shard_map/ppermute | solution.py:246
  107.4 8.0 %collective-permute-start.5 = (f32[128,256]{1,0:T(8,128)S(1)}, f32[128,256]{1,0:T(8,128)S(1)}, u32[]{:S(2)}, u32[]{:S(2)}) collective-permute-start(f32[128,256]{1,0:T(8,128)S(1)} %slice_bitcast_fusion), channel_id=1, source_target_pairs={{0,1},{1,0},{2,3},{3,2},{4,5},{5,4},{6,7},{7,6},{8,9},{9,8},{10,11... | collective-permute-start | bytes 393224 | tf_op jit(solution)/shard_map/ppermute | solution.py:248

commit v13 on v12

--- a/solution.py
+++ b/solution.py
@@ -124,13 +124,36 @@
     )(spot, packed)
 
 
+def join(parts):
+    count = len(parts)
+
+    def body(*refs):
+        o_ref, sems = refs[count:]
+        copies = [
+            pltpu.make_async_copy(refs[n], o_ref.at[n], sems.at[n]) for n in range(count)
+        ]
+        for copy in copies:
+            copy.start()
+        for copy in copies:
+            copy.wait()
+
+    return pl.pallas_call(
+        body,
+        in_specs=[pl.BlockSpec(memory_space=pl.ANY)] * count,
+        out_specs=pl.BlockSpec(memory_space=pltpu.VMEM),
+        out_shape=jax.ShapeDtypeStruct((count,) + parts[0].shape, parts[0].dtype),
+        scratch_shapes=[pltpu.SemaphoreType.DMA((count,))],
+        compiler_params=PARAMS,
+    )(*parts)
+
+
 def project(packed, mine, other, spot):
     sharers, rows, both = packed.shape
     depth, xhs, shard, wide = mine.shape
     part, cols = depth * xhs * shard, 2 * wide
 
     def body(spot_ref, p_ref, m_ref, r_ref, near_ref, away_ref, stage, whole, sems):
-        core, yl, xl, zl, xh = (spot_ref[i] for i in range(5))
+        core, yl, xl, zl, xh, zh = (spot_ref[i] for i in range(6))
         own = (yl * 2 + xl) * 2 + zl
         loads = []
         for flip in range(sharers):
@@ -140,12 +163,13 @@
                 )
             )
             loads[-1].start()
-        for z in range(depth):
+        for back in range(depth):
+            at_z = lax.rem(zh + depth - back, depth)
             for side in range(xhs):
-                ours, theirs = m_ref[z, side], r_ref[z, side]
+                ours, theirs = m_ref[back, side], r_ref[back, side]
                 left = jnp.where(core == 0, ours, theirs)
                 right = jnp.where(core == 0, theirs, ours)
-                whole[xh ^ side, z] = jnp.concatenate([left, right], axis=1)
+                whole[xh ^ side, at_z] = jnp.concatenate([left, right], axis=1)
         for load in loads:
             load.wait()
         t = stage[...].reshape(sharers * rows, both)[:, :part]
@@ -215,7 +239,8 @@
     shard, cols = weight.shape
     wide = cols // 2
     cubes, flip_y, flip_x, flip_z = partners([lax.axis_size(name) for name in CHIP])
-    spot = jnp.stack([lax.axis_index(name) for name in ("c", "yl", "xl", "zl", "xh")])
+    here = ("c", "yl", "xl", "zl", "xh", "zh")
+    spot = jnp.stack([lax.axis_index(name) for name in here])
     spot = spot.astype(jnp.int32)
 
     other = lax.ppermute(weight, "xh", SWAP)
@@ -225,12 +250,16 @@
     part = packed.shape[-1] - cols
     mine = jnp.stack([weight, other])
     mine = jnp.where(spot[0] == 0, mine[..., :wide], mine[..., wide:])
-    mine = lax.all_gather(mine, "zh", axis=0)
-    packed, mine = lax.optimization_barrier((packed, mine))
+    depth = lax.axis_size("zh")
+    gathered = [mine]
+    for back in range(1, depth):
+        shift = [(i, (i + back) % depth) for i in range(depth)]
+        gathered.append(lax.ppermute(mine, "zh", shift))
+    packed, *gathered = lax.optimization_barrier((packed, *gathered))
 
     keep, send = terms(packed, spot, part)
     term = (keep + lax.ppermute(send, "c", SWAP)).astype(jnp.bfloat16)
-    mine, _ = lax.optimization_barrier((mine, send))
+    mine, _ = lax.optimization_barrier((join(gathered), send))
     other = lax.ppermute(mine, "c", SWAP)
     term = lax.all_to_all(term.reshape(-1, shard, wide), ("xh", "zh"), 0, 0)
     summed = jnp.sum(term, axis=0, dtype=jnp.float32)
@@ -242,9 +271,10 @@
     near = near[:2] + lax.ppermute(near[2:], CHIP, flip_x)
 
     lines = jnp.broadcast_to(summed[None], (lax.axis_size("yh"), shard, wide))
-    half = jnp.sum(lax.all_to_all(lines, "yh", 0, 0), axis=0)
+    lines = lax.all_to_all(lines, "yh", 0, 0)
+    near, lines = lax.optimization_barrier((near, lines))
+    half = jnp.sum(lines, axis=0)
     other = lax.ppermute(half, "c", SWAP)
-    near, _ = lax.optimization_barrier((near, half))
     output = near[0] + lax.ppermute(near[1], CHIP, flip_z)
     first = spot[0] == 0
     weight_grad = jnp.concatenate(

time: 117 us -> 114 us (0.974)
  blocking collectives: 30.9 us -> 0 us
  waiting for transfers between devices: 12.6 us -> 41.5 us
  starting transfers between devices: 57.2 us -> 55.6 us
    all_gather x1 -> x0, blocking collectives: 30.9 us -> none  [local(): mine = lax.all_gather(mine, 'zh', axis=0)]
    ppermute x0 -> x3, waiting for transfers between devices: none -> 20.3 us  [local(): gathered.append(lax.ppermute(mine, 'zh', shift))]
    ppermute x0 -> x3, starting transfers between devices: none -> 8.34 us  [local(): gathered.append(lax.ppermute(mine, 'zh', shift))]
    all_to_all x1, waiting for transfers between devices: 3.05 us -> 7.74 us  [local(): term = lax.all_to_all(term.reshape(-1, shard, wide), ('xh', 'zh'), 0, 0)]
    all_to_all x1, starting transfers between devices: 7.92 us -> 3.46 us  [local(): lines = lax.all_to_all(lines, 'yh', 0, 0)]
    all_to_all x1, waiting for transfers between devices: 0.01 us -> 3.9 us  [local(): packed = lax.all_to_all(packed, CHIP, 0, 0, axis_index_groups=cubes)]
    ppermute x1, starting transfers between devices: 7.04 us -> 4.03 us  [local(): away = lax.ppermute(away, CHIP, flip_y)]
    ppermute x1, starting transfers between devices: 3.95 us -> 1.92 us  [local(): term = (keep + lax.ppermute(send, 'c', SWAP)).astype(jnp.bfloat16)]
  transfers between devices with their start and end apart: 10 -> 13, of which waited for: 4 -> 6; matrix products, arithmetic and copies ran while one was open for 2% -> 2% of each run, Pallas kernels for 6% -> 7%
where the time goes in v13:
time: 114 us; the launch traced here: 113 us
  starting transfers between devices  55.6 us (49%)
  waiting for transfers between devices  41.5 us (36%)
  Pallas kernels  11.9 us (10%)
  other arithmetic  2.4 us (2%)
    ppermute x3, waiting for transfers between devices, local(): gathered.append(lax.ppermute(mine, 'zh', shift))  20.3 us
    all_to_all x1, starting transfers between devices, local(): packed = lax.all_to_all(packed, CHIP, 0, 0, axis_index_groups=cubes)  13.6 us
    ppermute x3, starting transfers between devices, local(): gathered.append(lax.ppermute(mine, 'zh', shift))  8.34 us
    all_to_all x1, waiting for transfers between devices, local(): term = lax.all_to_all(term.reshape(-1, shard, wide), ('xh', 'zh'), 0, 0)  7.74 us
    ppermute x1, waiting for transfers between devices, local(): near = near[:2] + lax.ppermute(near[2:], CHIP, flip_x)  6.6 us
    ppermute x1, starting transfers between devices, local(): output = near[0] + lax.ppermute(near[1], CHIP, flip_z)  5.54 us
    ppermute x1, starting transfers between devices, local(): other = lax.ppermute(weight, 'xh', SWAP)  5.48 us
    ppermute x1, starting transfers between devices, local(): other = lax.ppermute(half, 'c', SWAP)  5.29 us
  transfers between devices with their start and end apart: 13, of which 6 were waited for; matrix products, arithmetic and copies ran while one was open for 2% of the time, Pallas kernels for 7%

profile of v13, /device:TPU:1, one launch (start us, length us, event | category | flops | bytes accessed | tf_op | source)
XLA Modules:
  0.0 113.1 jit_solution(11536893360030099792)
XLA Ops:
  0.6 5.5 %collective-permute-start = (bf16[192,256]{1,0:T(8,128)(2,1)}, bf16[192,256]{1,0:T(8,128)(2,1)S(1)}, u32[]{:S(2)}, u32[]{:S(2)}) collective-permute-start(bf16[192,256]{1,0:T(8,128)(2,1)} %param.4), channel_id=1, source_target_pairs={{0,16},{16,0},{1,17},{17,1},{2,18},{18,2},{3,19},{19,3},{4,20},{20... | collective-permute-start | bytes 294920 | tf_op jit(solution)/shard_map/ppermute | solution.py:246
  6.1 3.9 %shard_map.50 = bf16[8,128,1792]{2,1,0:T(8,128)(2,1)} custom-call(bf16[128,12288]{1,0:T(8,128)(2,1)} %t_ref.1, bf16[128,256]{1,0:T(8,128)(2,1)} %g_ref.1), custom_call_target="tpu_custom_call" | custom-call | tf_op jit(solution)/shard_map/pallas_call | solution.py:60
  10.1 13.6 %all-to-all-start = ((bf16[8,128,1792]{2,1,0:T(8,128)(2,1)}), bf16[8,128,1792]{2,1,0:T(8,128)(2,1)}, u32[]{:S(2)}, u32[]{:S(2)}) async-start(bf16[8,128,1792]{2,1,0:T(8,128)(2,1)} %shard_map.50), calls=%async_computation | async-start | bytes 7340032 | tf_op jit(solution)/shard_map/all_to_all | solution.py:249
  23.7 2.2 %collective-permute-start.3 = (bf16[2,192,128]{2,1,0:T(8,128)(2,1)S(1)}, bf16[2,192,128]{2,1,0:T(8,128)(2,1)S(1)}, u32[]{:S(2)}, u32[]{:S(2)}) collective-permute-start(bf16[2,192,128]{2,1,0:T(8,128)(2,1)S(1)} %fusion.2.refs_0_), channel_id=1, source_target_pairs={{0,6},{2,0},{4,2},{6,4},{1,7},{3,1},{5,3},{7,5},{8,14},{10,8},{12,... | collective-permute-start | bytes 294920 | tf_op jit(solution)/shard_map/ppermute | solution.py:257
  25.9 1.9 %collective-permute-start.2 = (bf16[2,192,128]{2,1,0:T(8,128)(2,1)S(1)}, bf16[2,192,128]{2,1,0:T(8,128)(2,1)S(1)}, u32[]{:S(2)}, u32[]{:S(2)}) collective-permute-start(bf16[2,192,128]{2,1,0:T(8,128)(2,1)S(1)} %fusion.2.refs_0_), channel_id=1, source_target_pairs={{0,4},{2,6},{4,0},{6,2},{1,5},{3,7},{5,1},{7,3},{8,12},{10,14},{12... | collective-permute-start | bytes 294920 | tf_op jit(solution)/shard_map/ppermute | solution.py:257
  27.8 4.2 %collective-permute-start.1 = (bf16[2,192,128]{2,1,0:T(8,128)(2,1)S(1)}, bf16[2,192,128]{2,1,0:T(8,128)(2,1)S(1)}, u32[]{:S(2)}, u32[]{:S(2)}) collective-permute-start(bf16[2,192,128]{2,1,0:T(8,128)(2,1)S(1)} %fusion.2.refs_0_), channel_id=1, source_target_pairs={{0,2},{2,4},{4,6},{6,0},{1,3},{3,5},{5,7},{7,1},{8,10},{10,12},{12... | collective-permute-start | bytes 294920 | tf_op jit(solution)/shard_map/ppermute | solution.py:257
  32.2 20.3 %collective-permute-done.3.refs_3_ = bf16[2,192,128]{2,1,0:T(8,128)(2,1)S(1)} collective-permute-done((bf16[2,192,128]{2,1,0:T(8,128)(2,1)S(1)}, bf16[2,192,128]{2,1,0:T(8,128)(2,1)S(1)}, u32[]{:S(2)}, u32[]{:S(2)}) %collective-permute-start.3) | collective-permute-done | bytes 98336 | tf_op jit(solution)/shard_map/ppermute | solution.py:257
  52.5 3.9 %all-to-all-done.p_ref = bf16[8,128,1792]{2,1,0:T(8,128)(2,1)} async-done(((bf16[8,128,1792]{2,1,0:T(8,128)(2,1)}), bf16[8,128,1792]{2,1,0:T(8,128)(2,1)}, u32[]{:S(2)}, u32[]{:S(2)}) %all-to-all-start) | async-done | bytes 3670048 | tf_op jit(solution)/shard_map/all_to_all | solution.py:249
  56.4 3.8 %shard_map.52 = (f32[1536,128]{1,0:T(8,128)S(1)}, f32[1536,128]{1,0:T(8,128)S(1)}) custom-call(s32[6]{0:T(128)S(1)} %stack.36.spot_ref, bf16[8,128,1792]{2,1,0:T(8,128)(2,1)} %all-to-all-done.p_ref), custom_call_target="tpu_custom_call" | custom-call | tf_op jit(solution)/shard_map/pallas_call | solution.py:111
  60.3 1.9 %collective-permute-start.5 = (f32[1536,128]{1,0:T(8,128)S(1)}, f32[1536,128]{1,0:T(8,128)S(1)}, u32[]{:S(2)}, u32[]{:S(2)}) collective-permute-start(f32[1536,128]{1,0:T(8,128)S(1)} %get-tuple-element.24), channel_id=1, source_target_pairs={{0,64},{64,0},{1,65},{65,1},{2,66},{66,2},{3,67},{67,3},{4,68},{68... | collective-permute-start | bytes 2359304 | tf_op jit(solution)/shard_map/ppermute | solution.py:261
  62.8 2.4 %collective-permute-start.4 = (bf16[4,2,192,128]{3,2,1,0:T(8,128)(2,1)S(1)}, bf16[4,2,192,128]{3,2,1,0:T(8,128)(2,1)S(1)}, u32[]{:S(2)}, u32[]{:S(2)}) collective-permute-start(bf16[4,2,192,128]{3,2,1,0:T(8,128)(2,1)S(1)} %shard_map.51.m_ref), channel_id=1, source_target_pairs={{0,64},{64,0},{1,65},{65,1},{2,66},{66,2},{3,67},{67,3},{4,68},{68... | collective-permute-start | bytes 1179656 | tf_op jit(solution)/shard_map/ppermute | solution.py:263
  65.2 0.8 add_convert_fusion
  66.0 3.5 %all-to-all-start.1 = ((bf16[8,192,128]{2,1,0:T(8,128)(2,1)}), bf16[8,192,128]{2,1,0:T(8,128)(2,1)S(1)}, u32[]{:S(2)}, u32[]{:S(2)}) async-start(bf16[8,192,128]{2,1,0:T(8,128)(2,1)} %bitcast.8), calls=%async_computation.1 | async-start | bytes 786432 | tf_op jit(solution)/shard_map/all_to_all | solution.py:264
  69.5 3.6 %shard_map.53 = (f32[4,128,256]{2,1,0:T(8,128)S(1)}, f32[4,128,256]{2,1,0:T(8,128)S(1)}) custom-call(s32[6]{0:T(128)S(1)} %stack.36.spot_ref, bf16[8,128,1792]{2,1,0:T(8,128)(2,1)} %all-to-all-done.p_ref, bf16[4,2,192,128]{3,2,1,0:T(8,128)(2,1)S(1)} %shard_map.51.m_ref, bf16[4,2,192,128]{3,2,1,0:T(8,128)(2,1)S(1)} %collective-permute-done.4.r_ref), custom_call_target="tpu_custom_call" | custom-call | tf_op jit(solution)/shard_map/pallas_call | solution.py:183
  73.1 4.0 %collective-permute-start.6 = (f32[4,128,256]{2,1,0:T(8,128)S(1)}, f32[4,128,256]{2,1,0:T(8,128)S(1)}, u32[]{:S(2)}, u32[]{:S(2)}) collective-permute-start(f32[4,128,256]{2,1,0:T(8,128)S(1)} %get-tuple-element.29), channel_id=1, source_target_pairs={{0,32},{1,33},{2,34},{3,35},{4,36},{5,37},{6,38},{7,39},{8,40},{9,... | collective-permute-start | bytes 1572872 | tf_op jit(solution)/shard_map/ppermute | solution.py:268
  77.1 7.7 %all-to-all-done.1 = bf16[8,192,128]{2,1,0:T(8,128)(2,1)S(1)} async-done(((bf16[8,192,128]{2,1,0:T(8,128)(2,1)}), bf16[8,192,128]{2,1,0:T(8,128)(2,1)S(1)}, u32[]{:S(2)}, u32[]{:S(2)}) %all-to-all-start.1) | async-done | bytes 393248 | tf_op jit(solution)/shard_map/all_to_all | solution.py:264
  84.9 0.8 broadcast_in_dim.2
  85.7 3.5 %all-to-all-start.2 = ((f32[4,192,128]{2,1,0:T(8,128)}), f32[4,192,128]{2,1,0:T(8,128)S(1)}, u32[]{:S(2)}, u32[]{:S(2)}) async-start(f32[4,192,128]{2,1,0:T(8,128)} %broadcast_in_dim.2), calls=%async_computation.2 | async-start | bytes 786432 | tf_op jit(solution)/shard_map/all_to_all | solution.py:274
  89.3 2.0 %collective-permute-start.7 = (f32[2,128,256]{2,1,0:T(8,128)S(1)}, f32[2,128,256]{2,1,0:T(8,128)S(1)}, u32[]{:S(2)}, u32[]{:S(2)}) collective-permute-start(f32[2,128,256]{2,1,0:T(8,128)S(1)} %slice.27), channel_id=1, source_target_pairs={{0,8},{1,9},{2,10},{3,11},{4,12},{5,13},{6,14},{7,15},{8,0},{9,1},... | collective-permute-start | bytes 786440 | tf_op jit(solution)/shard_map/ppermute | solution.py:271
  91.3 6.6 %collective-permute-done.7 = f32[2,128,256]{2,1,0:T(8,128)S(1)} collective-permute-done((f32[2,128,256]{2,1,0:T(8,128)S(1)}, f32[2,128,256]{2,1,0:T(8,128)S(1)}, u32[]{:S(2)}, u32[]{:S(2)}) %collective-permute-start.7) | collective-permute-done | bytes 262176 | tf_op jit(solution)/shard_map/ppermute | solution.py:271
  97.9 1.2 %all-to-all-done.2 = f32[4,192,128]{2,1,0:T(8,128)S(1)} async-done(((f32[4,192,128]{2,1,0:T(8,128)}), f32[4,192,128]{2,1,0:T(8,128)S(1)}, u32[]{:S(2)}, u32[]{:S(2)}) %all-to-all-start.2) | async-done | bytes 393248 | tf_op jit(solution)/shard_map/all_to_all | solution.py:274
  99.2 5.3 %collective-permute-start.9 = (f32[192,128]{1,0:T(8,128)S(1)}, f32[192,128]{1,0:T(8,128)S(1)}, u32[]{:S(2)}, u32[]{:S(2)}) collective-permute-start(f32[192,128]{1,0:T(8,128)S(1)} %reduce_sum.19), channel_id=1, source_target_pairs={{0,64},{64,0},{1,65},{65,1},{2,66},{66,2},{3,67},{67,3},{4,68},{68... | collective-permute-start | bytes 294920 | tf_op jit(solution)/shard_map/ppermute | solution.py:277
  104.5 5.5 %collective-permute-start.8 = (f32[128,256]{1,0:T(8,128)S(1)}, f32[128,256]{1,0:T(8,128)S(1)}, u32[]{:S(2)}, u32[]{:S(2)}) collective-permute-start(f32[128,256]{1,0:T(8,128)S(1)} %slice_bitcast_fusion), channel_id=1, source_target_pairs={{0,1},{1,0},{2,3},{3,2},{4,5},{5,4},{6,7},{7,6},{8,9},{9,8},{10,11... | collective-permute-start | bytes 393224 | tf_op jit(solution)/shard_map/ppermute | solution.py:278
  110.8 1.6 %collective-permute-done.8 = f32[128,256]{1,0:T(8,128)S(1)} collective-permute-done((f32[128,256]{1,0:T(8,128)S(1)}, f32[128,256]{1,0:T(8,128)S(1)}, u32[]{:S(2)}, u32[]{:S(2)}) %collective-permute-start.8) | collective-permute-done | bytes 131104 | tf_op jit(solution)/shard_map/ppermute | solution.py:278
  (21 shorter events, 2.3 us)
Async XLA Ops:
  0.6 9.4 %collective-permute-start = (bf16[192,256]{1,0:T(8,128)(2,1)}, bf16[192,256]{1,0:T(8,128)(2,1)S(1)}, u32[]{:S(2)}, u32[]{:S(2)}) collective-permute-start(bf16[192,256]{1,0:T(8,128)(2,1)} %param.4), channel_id=1, source_target_pairs={{0,16},{16,0},{1,17},{17,1},{2,18},{18,2},{3,19},{19,3},{4,20},{20... | collective-permute-start | bytes 294920 | tf_op jit(solution)/shard_map/ppermute | solution.py:246
  10.0 13.6 %copy-start = (bf16[192,256]{1,0:T(8,128)(2,1)S(1)}, bf16[192,256]{1,0:T(8,128)(2,1)}, u32[]{:S(2)}) copy-start(bf16[192,256]{1,0:T(8,128)(2,1)} %param.4) | copy-start | bytes 294916
  10.1 46.4 %all-to-all-start = ((bf16[8,128,1792]{2,1,0:T(8,128)(2,1)}), bf16[8,128,1792]{2,1,0:T(8,128)(2,1)}, u32[]{:S(2)}, u32[]{:S(2)}) async-start(bf16[8,128,1792]{2,1,0:T(8,128)(2,1)} %shard_map.50), calls=%async_computation | async-start | bytes 7340032 | tf_op jit(solution)/shard_map/all_to_all | solution.py:249
  23.7 28.8 %collective-permute-start.3 = (bf16[2,192,128]{2,1,0:T(8,128)(2,1)S(1)}, bf16[2,192,128]{2,1,0:T(8,128)(2,1)S(1)}, u32[]{:S(2)}, u32[]{:S(2)}) collective-permute-start(bf16[2,192,128]{2,1,0:T(8,128)(2,1)S(1)} %fusion.2.refs_0_), channel_id=1, source_target_pairs={{0,6},{2,0},{4,2},{6,4},{1,7},{3,1},{5,3},{7,5},{8,14},{10,8},{12,... | collective-permute-start | bytes 294920 | tf_op jit(solution)/shard_map/ppermute | solution.py:257
  25.9 26.6 %collective-permute-start.2 = (bf16[2,192,128]{2,1,0:T(8,128)(2,1)S(1)}, bf16[2,192,128]{2,1,0:T(8,128)(2,1)S(1)}, u32[]{:S(2)}, u32[]{:S(2)}) collective-permute-start(bf16[2,192,128]{2,1,0:T(8,128)(2,1)S(1)} %fusion.2.refs_0_), channel_id=1, source_target_pairs={{0,4},{2,6},{4,0},{6,2},{1,5},{3,7},{5,1},{7,3},{8,12},{10,14},{12... | collective-permute-start | bytes 294920 | tf_op jit(solution)/shard_map/ppermute | solution.py:257
  27.8 24.7 %collective-permute-start.1 = (bf16[2,192,128]{2,1,0:T(8,128)(2,1)S(1)}, bf16[2,192,128]{2,1,0:T(8,128)(2,1)S(1)}, u32[]{:S(2)}, u32[]{:S(2)}) collective-permute-start(bf16[2,192,128]{2,1,0:T(8,128)(2,1)S(1)} %fusion.2.refs_0_), channel_id=1, source_target_pairs={{0,2},{2,4},{4,6},{6,0},{1,3},{3,5},{5,7},{7,1},{8,10},{10,12},{12... | collective-permute-start | bytes 294920 | tf_op jit(solution)/shard_map/ppermute | solution.py:257
  60.3 4.9 %collective-permute-start.5 = (f32[1536,128]{1,0:T(8,128)S(1)}, f32[1536,128]{1,0:T(8,128)S(1)}, u32[]{:S(2)}, u32[]{:S(2)}) collective-permute-start(f32[1536,128]{1,0:T(8,128)S(1)} %get-tuple-element.24), channel_id=1, source_target_pairs={{0,64},{64,0},{1,65},{65,1},{2,66},{66,2},{3,67},{67,3},{4,68},{68... | collective-permute-start | bytes 2359304 | tf_op jit(solution)/shard_map/ppermute | solution.py:261
  62.8 6.7 %collective-permute-start.4 = (bf16[4,2,192,128]{3,2,1,0:T(8,128)(2,1)S(1)}, bf16[4,2,192,128]{3,2,1,0:T(8,128)(2,1)S(1)}, u32[]{:S(2)}, u32[]{:S(2)}) collective-permute-start(bf16[4,2,192,128]{3,2,1,0:T(8,128)(2,1)S(1)} %shard_map.51.m_ref), channel_id=1, source_target_pairs={{0,64},{64,0},{1,65},{65,1},{2,66},{66,2},{3,67},{67,3},{4,68},{68... | collective-permute-start | bytes 1179656 | tf_op jit(solution)/shard_map/ppermute | solution.py:263
  66.0 18.9 %all-to-all-start.1 = ((bf16[8,192,128]{2,1,0:T(8,128)(2,1)}), bf16[8,192,128]{2,1,0:T(8,128)(2,1)S(1)}, u32[]{:S(2)}, u32[]{:S(2)}) async-start(bf16[8,192,128]{2,1,0:T(8,128)(2,1)} %bitcast.8), calls=%async_computation.1 | async-start | bytes 786432 | tf_op jit(solution)/shard_map/all_to_all | solution.py:264
  73.1 16.1 %collective-permute-start.6 = (f32[4,128,256]{2,1,0:T(8,128)S(1)}, f32[4,128,256]{2,1,0:T(8,128)S(1)}, u32[]{:S(2)}, u32[]{:S(2)}) collective-permute-start(f32[4,128,256]{2,1,0:T(8,128)S(1)} %get-tuple-element.29), channel_id=1, source_target_pairs={{0,32},{1,33},{2,34},{3,35},{4,36},{5,37},{6,38},{7,39},{8,40},{9,... | collective-permute-start | bytes 1572872 | tf_op jit(solution)/shard_map/ppermute | solution.py:268
  85.7 13.5 %all-to-all-start.2 = ((f32[4,192,128]{2,1,0:T(8,128)}), f32[4,192,128]{2,1,0:T(8,128)S(1)}, u32[]{:S(2)}, u32[]{:S(2)}) async-start(f32[4,192,128]{2,1,0:T(8,128)} %broadcast_in_dim.2), calls=%async_computation.2 | async-start | bytes 786432 | tf_op jit(solution)/shard_map/all_to_all | solution.py:274
  89.3 8.6 %collective-permute-start.7 = (f32[2,128,256]{2,1,0:T(8,128)S(1)}, f32[2,128,256]{2,1,0:T(8,128)S(1)}, u32[]{:S(2)}, u32[]{:S(2)}) collective-permute-start(f32[2,128,256]{2,1,0:T(8,128)S(1)} %slice.27), channel_id=1, source_target_pairs={{0,8},{1,9},{2,10},{3,11},{4,12},{5,13},{6,14},{7,15},{8,0},{9,1},... | collective-permute-start | bytes 786440 | tf_op jit(solution)/shard_map/ppermute | solution.py:271
  99.2 10.9 %collective-permute-start.9 = (f32[192,128]{1,0:T(8,128)S(1)}, f32[192,128]{1,0:T(8,128)S(1)}, u32[]{:S(2)}, u32[]{:S(2)}) collective-permute-start(f32[192,128]{1,0:T(8,128)S(1)} %reduce_sum.19), channel_id=1, source_target_pairs={{0,64},{64,0},{1,65},{65,1},{2,66},{66,2},{3,67},{67,3},{4,68},{68... | collective-permute-start | bytes 294920 | tf_op jit(solution)/shard_map/ppermute | solution.py:277
  104.5 7.9 %collective-permute-start.8 = (f32[128,256]{1,0:T(8,128)S(1)}, f32[128,256]{1,0:T(8,128)S(1)}, u32[]{:S(2)}, u32[]{:S(2)}) collective-permute-start(f32[128,256]{1,0:T(8,128)S(1)} %slice_bitcast_fusion), channel_id=1, source_target_pairs={{0,1},{1,0},{2,3},{3,2},{4,5},{5,4},{6,7},{7,6},{8,9},{9,8},{10,11... | collective-permute-start | bytes 393224 | tf_op jit(solution)/shard_map/ppermute | solution.py:278

commit v14 on v13

--- a/solution.py
+++ b/solution.py
@@ -211,17 +211,17 @@
             return i ^ 1
         return (i + 1) % n if i % 2 else (i - 1) % n
 
-    flips, cubes = ([], [], []), []
+    moves = ((1, 0, 0), (0, 0, 1), (0, 1, 0), (0, 1, 1))
+    flips, cubes = [[] for _ in moves], []
     for c in range(cores):
         for y in range(rings[0]):
             for x in range(rings[1]):
                 for z in range(rings[2]):
                     here = (y, x, z)
                     there = [other(i, n, c) for i, n in zip(here, rings)]
-                    for axis in range(3):
-                        to = list(here)
-                        to[axis] = there[axis]
-                        flips[axis].append((place(c, *here), place(c, *to)))
+                    for move, flip in zip(moves, flips):
+                        to = [b if m else a for a, b, m in zip(here, there, move)]
+                        flip.append((place(c, *here), place(c, *to)))
                     if all(i % 2 == 0 for i in here):
                         pairs = list(zip(here, there))
                         cubes.append(
@@ -232,13 +232,13 @@
                                 for d in pairs[2]
                             ]
                         )
-    return cubes, *flips
+    return cubes, flips[0], flips[1:]
 
 
 def local(tokens, weight, grad_out):
     shard, cols = weight.shape
     wide = cols // 2
-    cubes, flip_y, flip_x, flip_z = partners([lax.axis_size(name) for name in CHIP])
+    cubes, flip_y, flips = partners([lax.axis_size(name) for name in CHIP])
     here = ("c", "yl", "xl", "zl", "xh", "zh")
     spot = jnp.stack([lax.axis_index(name) for name in here])
     spot = spot.astype(jnp.int32)
@@ -268,14 +268,13 @@
     away = lax.ppermute(away, CHIP, flip_y)
     near, _ = lax.optimization_barrier((near, summed))
     near = near + away
-    near = near[:2] + lax.ppermute(near[2:], CHIP, flip_x)
+    output = near[0]
+    for n, flip in enumerate(flips):
+        output = output + lax.ppermute(near[n + 1], CHIP, flip)
 
     lines = jnp.broadcast_to(summed[None], (lax.axis_size("yh"), shard, wide))
-    lines = lax.all_to_all(lines, "yh", 0, 0)
-    near, lines = lax.optimization_barrier((near, lines))
-    half = jnp.sum(lines, axis=0)
+    half = jnp.sum(lax.all_to_all(lines, "yh", 0, 0), axis=0)
     other = lax.ppermute(half, "c", SWAP)
-    output = near[0] + lax.ppermute(near[1], CHIP, flip_z)
     first = spot[0] == 0
     weight_grad = jnp.concatenate(
         [jnp.where(first, half, other), jnp.where(first, other, half)], axis=1

time: 114 us -> 114 us (level)
  starting transfers between devices: 55.6 us -> 63.3 us
  waiting for transfers between devices: 41.5 us -> 33.9 us
    ppermute x2 -> x3, starting transfers between devices: 7.55 us -> 18.6 us  [local(): output = output + lax.ppermute(near[n + 1], CHIP, flip)]
    ppermute x2 -> x3, waiting for transfers between devices: 8.21 us -> 3.01 us  [local(): output = output + lax.ppermute(near[n + 1], CHIP, flip)]
    all_to_all x1, waiting for transfers between devices: 7.74 us -> 2.86 us  [local(): term = lax.all_to_all(term.reshape(-1, shard, wide), ('xh', 'zh'), 0, 0)]
    ppermute x1, starting transfers between devices: 5.29 us -> 1.92 us  [local(): other = lax.ppermute(half, 'c', SWAP)]
    ppermute x1, waiting for transfers between devices: 0.01 us -> 2.25 us  [local(): term = (keep + lax.ppermute(send, 'c', SWAP)).astype(jnp.bfloat16)]
    ppermute x1, waiting for transfers between devices: 0.01 us -> 1.56 us  [local(): other = lax.ppermute(mine, 'c', SWAP)]
    all_to_all x1, waiting for transfers between devices: 1.25 us -> 0.01 us  [local(): half = jnp.sum(lax.all_to_all(lines, 'yh', 0, 0), axis=0)]
  transfers between devices with their start and end apart: 13 -> 14, of which waited for: 6 -> 6; matrix products, arithmetic and copies ran while one was open for 2% -> 2% of each run, Pallas kernels for 7% -> 7%
where the time goes in v14:
time: 114 us; the launch traced here: 113 us
  starting transfers between devices  63.3 us (56%)
  waiting for transfers between devices  33.9 us (30%)
  Pallas kernels  11.9 us (10%)
  other arithmetic  2.38 us (2%)
    ppermute x3, waiting for transfers between devices, local(): gathered.append(lax.ppermute(mine, 'zh', shift))  20.3 us
    ppermute x3, starting transfers between devices, local(): output = output + lax.ppermute(near[n + 1], CHIP, flip)  18.6 us
    all_to_all x1, starting transfers between devices, local(): packed = lax.all_to_all(packed, CHIP, 0, 0, axis_index_groups=cubes)  13.6 us
    ppermute x3, starting transfers between devices, local(): gathered.append(lax.ppermute(mine, 'zh', shift))  8.34 us
    ppermute x1, starting transfers between devices, local(): other = lax.ppermute(weight, 'xh', SWAP)  5.48 us
    ppermute x1, starting transfers between devices, local(): away = lax.ppermute(away, CHIP, flip_y)  4.44 us
    all_to_all x1, waiting for transfers between devices, local(): packed = lax.all_to_all(packed, CHIP, 0, 0, axis_index_groups=cubes)  3.9 us
    pallas_call x1, Pallas kernels, pack(): pl.pallas_call(body, in_specs=[pl.BlockSpec(memory_space=pl.ANY)] * 2, ou...  3.89 us
  transfers between devices with their start and end apart: 14, of which 6 were waited for; matrix products, arithmetic and copies ran while one was open for 2% of the time, Pallas kernels for 7%

profile of v14, /device:TPU:1, one launch (start us, length us, event | category | flops | bytes accessed | tf_op | source)
XLA Modules:
  0.0 113.3 jit_solution(1789308579793532002)
XLA Ops:
  0.6 5.5 %collective-permute-start = (bf16[192,256]{1,0:T(8,128)(2,1)}, bf16[192,256]{1,0:T(8,128)(2,1)S(1)}, u32[]{:S(2)}, u32[]{:S(2)}) collective-permute-start(bf16[192,256]{1,0:T(8,128)(2,1)} %param.4), channel_id=1, source_target_pairs={{0,16},{16,0},{1,17},{17,1},{2,18},{18,2},{3,19},{19,3},{4,20},{20... | collective-permute-start | bytes 294920 | tf_op jit(solution)/shard_map/ppermute | solution.py:246
  6.1 3.9 %shard_map.50 = bf16[8,128,1792]{2,1,0:T(8,128)(2,1)} custom-call(bf16[128,12288]{1,0:T(8,128)(2,1)} %t_ref.1, bf16[128,256]{1,0:T(8,128)(2,1)} %g_ref.1), custom_call_target="tpu_custom_call" | custom-call | tf_op jit(solution)/shard_map/pallas_call | solution.py:60
  10.0 13.6 %all-to-all-start = ((bf16[8,128,1792]{2,1,0:T(8,128)(2,1)}), bf16[8,128,1792]{2,1,0:T(8,128)(2,1)}, u32[]{:S(2)}, u32[]{:S(2)}) async-start(bf16[8,128,1792]{2,1,0:T(8,128)(2,1)} %shard_map.50), calls=%async_computation | async-start | bytes 7340032 | tf_op jit(solution)/shard_map/all_to_all | solution.py:249
  23.7 2.2 %collective-permute-start.3 = (bf16[2,192,128]{2,1,0:T(8,128)(2,1)S(1)}, bf16[2,192,128]{2,1,0:T(8,128)(2,1)S(1)}, u32[]{:S(2)}, u32[]{:S(2)}) collective-permute-start(bf16[2,192,128]{2,1,0:T(8,128)(2,1)S(1)} %fusion.5.refs_0_), channel_id=1, source_target_pairs={{0,6},{2,0},{4,2},{6,4},{1,7},{3,1},{5,3},{7,5},{8,14},{10,8},{12,... | collective-permute-start | bytes 294920 | tf_op jit(solution)/shard_map/ppermute | solution.py:257
  25.9 1.9 %collective-permute-start.2 = (bf16[2,192,128]{2,1,0:T(8,128)(2,1)S(1)}, bf16[2,192,128]{2,1,0:T(8,128)(2,1)S(1)}, u32[]{:S(2)}, u32[]{:S(2)}) collective-permute-start(bf16[2,192,128]{2,1,0:T(8,128)(2,1)S(1)} %fusion.5.refs_0_), channel_id=1, source_target_pairs={{0,4},{2,6},{4,0},{6,2},{1,5},{3,7},{5,1},{7,3},{8,12},{10,14},{12... | collective-permute-start | bytes 294920 | tf_op jit(solution)/shard_map/ppermute | solution.py:257
  27.8 4.2 %collective-permute-start.1 = (bf16[2,192,128]{2,1,0:T(8,128)(2,1)S(1)}, bf16[2,192,128]{2,1,0:T(8,128)(2,1)S(1)}, u32[]{:S(2)}, u32[]{:S(2)}) collective-permute-start(bf16[2,192,128]{2,1,0:T(8,128)(2,1)S(1)} %fusion.5.refs_0_), channel_id=1, source_target_pairs={{0,2},{2,4},{4,6},{6,0},{1,3},{3,5},{5,7},{7,1},{8,10},{10,12},{12... | collective-permute-start | bytes 294920 | tf_op jit(solution)/shard_map/ppermute | solution.py:257
  32.2 20.3 %collective-permute-done.3.refs_3_ = bf16[2,192,128]{2,1,0:T(8,128)(2,1)S(1)} collective-permute-done((bf16[2,192,128]{2,1,0:T(8,128)(2,1)S(1)}, bf16[2,192,128]{2,1,0:T(8,128)(2,1)S(1)}, u32[]{:S(2)}, u32[]{:S(2)}) %collective-permute-start.3) | collective-permute-done | bytes 98336 | tf_op jit(solution)/shard_map/ppermute | solution.py:257
  52.5 3.9 %all-to-all-done.p_ref = bf16[8,128,1792]{2,1,0:T(8,128)(2,1)} async-done(((bf16[8,128,1792]{2,1,0:T(8,128)(2,1)}), bf16[8,128,1792]{2,1,0:T(8,128)(2,1)}, u32[]{:S(2)}, u32[]{:S(2)}) %all-to-all-start) | async-done | bytes 3670048 | tf_op jit(solution)/shard_map/all_to_all | solution.py:249
  56.4 3.8 %shard_map.52 = (f32[1536,128]{1,0:T(8,128)S(1)}, f32[1536,128]{1,0:T(8,128)S(1)}) custom-call(s32[6]{0:T(128)S(1)} %stack.36.spot_ref, bf16[8,128,1792]{2,1,0:T(8,128)(2,1)} %all-to-all-done.p_ref), custom_call_target="tpu_custom_call" | custom-call | tf_op jit(solution)/shard_map/pallas_call | solution.py:111
  60.3 1.9 %collective-permute-start.5 = (f32[1536,128]{1,0:T(8,128)S(1)}, f32[1536,128]{1,0:T(8,128)S(1)}, u32[]{:S(2)}, u32[]{:S(2)}) collective-permute-start(f32[1536,128]{1,0:T(8,128)S(1)} %get-tuple-element.22), channel_id=1, source_target_pairs={{0,64},{64,0},{1,65},{65,1},{2,66},{66,2},{3,67},{67,3},{4,68},{68... | collective-permute-start | bytes 2359304 | tf_op jit(solution)/shard_map/ppermute | solution.py:261
  62.2 2.3 %collective-permute-done.5 = f32[1536,128]{1,0:T(8,128)S(1)} collective-permute-done((f32[1536,128]{1,0:T(8,128)S(1)}, f32[1536,128]{1,0:T(8,128)S(1)}, u32[]{:S(2)}, u32[]{:S(2)}) %collective-permute-start.5) | collective-permute-done | bytes 786464 | tf_op jit(solution)/shard_map/ppermute | solution.py:261
  64.5 0.8 add_convert_fusion
  65.3 3.5 %all-to-all-start.1 = ((bf16[8,192,128]{2,1,0:T(8,128)(2,1)}), bf16[8,192,128]{2,1,0:T(8,128)(2,1)S(1)}, u32[]{:S(2)}, u32[]{:S(2)}) async-start(bf16[8,192,128]{2,1,0:T(8,128)(2,1)} %bitcast.8), calls=%async_computation.1 | async-start | bytes 786432 | tf_op jit(solution)/shard_map/all_to_all | solution.py:264
  69.3 2.0 %collective-permute-start.4 = (bf16[4,2,192,128]{3,2,1,0:T(8,128)(2,1)S(1)}, bf16[4,2,192,128]{3,2,1,0:T(8,128)(2,1)S(1)}, u32[]{:S(2)}, u32[]{:S(2)}) collective-permute-start(bf16[4,2,192,128]{3,2,1,0:T(8,128)(2,1)S(1)} %shard_map.51.m_ref), channel_id=1, source_target_pairs={{0,64},{64,0},{1,65},{65,1},{2,66},{66,2},{3,67},{67,3},{4,68},{68... | collective-permute-start | bytes 1179656 | tf_op jit(solution)/shard_map/ppermute | solution.py:263
  71.3 1.6 %collective-permute-done.4.r_ref = bf16[4,2,192,128]{3,2,1,0:T(8,128)(2,1)S(1)} collective-permute-done((bf16[4,2,192,128]{3,2,1,0:T(8,128)(2,1)S(1)}, bf16[4,2,192,128]{3,2,1,0:T(8,128)(2,1)S(1)}, u32[]{:S(2)}, u32[]{:S(2)}) %collective-permute-start.4) | collective-permute-done | bytes 393248 | tf_op jit(solution)/shard_map/ppermute | solution.py:263
  72.9 3.6 %shard_map.53 = (f32[4,128,256]{2,1,0:T(8,128)S(1)}, f32[4,128,256]{2,1,0:T(8,128)S(1)}) custom-call(s32[6]{0:T(128)S(1)} %stack.36.spot_ref, bf16[8,128,1792]{2,1,0:T(8,128)(2,1)} %all-to-all-done.p_ref, bf16[4,2,192,128]{3,2,1,0:T(8,128)(2,1)S(1)} %shard_map.51.m_ref, bf16[4,2,192,128]{3,2,1,0:T(8,128)(2,1)S(1)} %collective-permute-done.4.r_ref), custom_call_target="tpu_custom_call" | custom-call | tf_op jit(solution)/shard_map/pallas_call | solution.py:183
  76.5 4.4 %collective-permute-start.6 = (f32[4,128,256]{2,1,0:T(8,128)S(1)}, f32[4,128,256]{2,1,0:T(8,128)S(1)}, u32[]{:S(2)}, u32[]{:S(2)}) collective-permute-start(f32[4,128,256]{2,1,0:T(8,128)S(1)} %get-tuple-element.27), channel_id=1, source_target_pairs={{0,32},{1,33},{2,34},{3,35},{4,36},{5,37},{6,38},{7,39},{8,40},{9,... | collective-permute-start | bytes 1572872 | tf_op jit(solution)/shard_map/ppermute | solution.py:268
  81.0 2.9 %all-to-all-done.1 = bf16[8,192,128]{2,1,0:T(8,128)(2,1)S(1)} async-done(((bf16[8,192,128]{2,1,0:T(8,128)(2,1)}), bf16[8,192,128]{2,1,0:T(8,128)(2,1)S(1)}, u32[]{:S(2)}, u32[]{:S(2)}) %all-to-all-start.1) | async-done | bytes 393248 | tf_op jit(solution)/shard_map/all_to_all | solution.py:264
  84.7 3.5 %all-to-all-start.2 = ((f32[4,192,128]{2,1,0:T(8,128)}), f32[4,192,128]{2,1,0:T(8,128)S(1)}, u32[]{:S(2)}, u32[]{:S(2)}) async-start(f32[4,192,128]{2,1,0:T(8,128)} %broadcast_in_dim.2), calls=%async_computation.2 | async-start | bytes 786432 | tf_op jit(solution)/shard_map/all_to_all | solution.py:276
  88.3 6.8 %collective-permute-start.7 = (f32[128,256]{1,0:T(8,128)S(1)}, f32[128,256]{1,0:T(8,128)S(1)}, u32[]{:S(2)}, u32[]{:S(2)}) collective-permute-start(f32[128,256]{1,0:T(8,128)S(1)} %get-tuple-element.28), channel_id=1, source_target_pairs={{0,1},{1,0},{2,3},{3,2},{4,5},{5,4},{6,7},{7,6},{8,9},{9,8},{10,11... | collective-permute-start | bytes 393224 | tf_op jit(solution)/shard_map/ppermute | solution.py:273
  95.1 9.9 %collective-permute-start.9 = (f32[128,256]{1,0:T(8,128)S(1)}, f32[128,256]{1,0:T(8,128)S(1)}, u32[]{:S(2)}, u32[]{:S(2)}) collective-permute-start(f32[128,256]{1,0:T(8,128)S(1)} %get-tuple-element.29), channel_id=1, source_target_pairs={{0,9},{1,8},{2,11},{3,10},{4,13},{5,12},{6,15},{7,14},{8,1},{9,0},... | collective-permute-start | bytes 393224 | tf_op jit(solution)/shard_map/ppermute | solution.py:273
  105.0 1.9 %collective-permute-start.8 = (f32[128,256]{1,0:T(8,128)S(1)}, f32[128,256]{1,0:T(8,128)S(1)}, u32[]{:S(2)}, u32[]{:S(2)}) collective-permute-start(f32[128,256]{1,0:T(8,128)S(1)} %get-tuple-element.30), channel_id=1, source_target_pairs={{0,8},{1,9},{2,10},{3,11},{4,12},{5,13},{6,14},{7,15},{8,0},{9,1},... | collective-permute-start | bytes 393224 | tf_op jit(solution)/shard_map/ppermute | solution.py:273
  106.9 1.9 %collective-permute-start.10 = (f32[192,128]{1,0:T(8,128)S(1)}, f32[192,128]{1,0:T(8,128)S(1)}, u32[]{:S(2)}, u32[]{:S(2)}) collective-permute-start(f32[192,128]{1,0:T(8,128)S(1)} %reduce_sum.19), channel_id=1, source_target_pairs={{0,64},{64,0},{1,65},{65,1},{2,66},{66,2},{3,67},{67,3},{4,68},{68... | collective-permute-start | bytes 294920 | tf_op jit(solution)/shard_map/ppermute | solution.py:277
  108.9 3.0 %collective-permute-done.8 = f32[128,256]{1,0:T(8,128)S(1)} collective-permute-done((f32[128,256]{1,0:T(8,128)S(1)}, f32[128,256]{1,0:T(8,128)S(1)}, u32[]{:S(2)}, u32[]{:S(2)}) %collective-permute-start.8) | collective-permute-done | bytes 131104 | tf_op jit(solution)/shard_map/ppermute | solution.py:273
  (21 shorter events, 3.0 us)
Async XLA Ops:
  0.6 9.4 %collective-permute-start = (bf16[192,256]{1,0:T(8,128)(2,1)}, bf16[192,256]{1,0:T(8,128)(2,1)S(1)}, u32[]{:S(2)}, u32[]{:S(2)}) collective-permute-start(bf16[192,256]{1,0:T(8,128)(2,1)} %param.4), channel_id=1, source_target_pairs={{0,16},{16,0},{1,17},{17,1},{2,18},{18,2},{3,19},{19,3},{4,20},{20... | collective-permute-start | bytes 294920 | tf_op jit(solution)/shard_map/ppermute | solution.py:246
  10.0 13.7 %copy-start = (bf16[192,256]{1,0:T(8,128)(2,1)S(1)}, bf16[192,256]{1,0:T(8,128)(2,1)}, u32[]{:S(2)}) copy-start(bf16[192,256]{1,0:T(8,128)(2,1)} %param.4) | copy-start | bytes 294916
  10.0 46.4 %all-to-all-start = ((bf16[8,128,1792]{2,1,0:T(8,128)(2,1)}), bf16[8,128,1792]{2,1,0:T(8,128)(2,1)}, u32[]{:S(2)}, u32[]{:S(2)}) async-start(bf16[8,128,1792]{2,1,0:T(8,128)(2,1)} %shard_map.50), calls=%async_computation | async-start | bytes 7340032 | tf_op jit(solution)/shard_map/all_to_all | solution.py:249
  23.7 28.8 %collective-permute-start.3 = (bf16[2,192,128]{2,1,0:T(8,128)(2,1)S(1)}, bf16[2,192,128]{2,1,0:T(8,128)(2,1)S(1)}, u32[]{:S(2)}, u32[]{:S(2)}) collective-permute-start(bf16[2,192,128]{2,1,0:T(8,128)(2,1)S(1)} %fusion.5.refs_0_), channel_id=1, source_target_pairs={{0,6},{2,0},{4,2},{6,4},{1,7},{3,1},{5,3},{7,5},{8,14},{10,8},{12,... | collective-permute-start | bytes 294920 | tf_op jit(solution)/shard_map/ppermute | solution.py:257
  25.9 26.6 %collective-permute-start.2 = (bf16[2,192,128]{2,1,0:T(8,128)(2,1)S(1)}, bf16[2,192,128]{2,1,0:T(8,128)(2,1)S(1)}, u32[]{:S(2)}, u32[]{:S(2)}) collective-permute-start(bf16[2,192,128]{2,1,0:T(8,128)(2,1)S(1)} %fusion.5.refs_0_), channel_id=1, source_target_pairs={{0,4},{2,6},{4,0},{6,2},{1,5},{3,7},{5,1},{7,3},{8,12},{10,14},{12... | collective-permute-start | bytes 294920 | tf_op jit(solution)/shard_map/ppermute | solution.py:257
  27.8 24.7 %collective-permute-start.1 = (bf16[2,192,128]{2,1,0:T(8,128)(2,1)S(1)}, bf16[2,192,128]{2,1,0:T(8,128)(2,1)S(1)}, u32[]{:S(2)}, u32[]{:S(2)}) collective-permute-start(bf16[2,192,128]{2,1,0:T(8,128)(2,1)S(1)} %fusion.5.refs_0_), channel_id=1, source_target_pairs={{0,2},{2,4},{4,6},{6,0},{1,3},{3,5},{5,7},{7,1},{8,10},{10,12},{12... | collective-permute-start | bytes 294920 | tf_op jit(solution)/shard_map/ppermute | solution.py:257
  60.3 4.2 %collective-permute-start.5 = (f32[1536,128]{1,0:T(8,128)S(1)}, f32[1536,128]{1,0:T(8,128)S(1)}, u32[]{:S(2)}, u32[]{:S(2)}) collective-permute-start(f32[1536,128]{1,0:T(8,128)S(1)} %get-tuple-element.22), channel_id=1, source_target_pairs={{0,64},{64,0},{1,65},{65,1},{2,66},{66,2},{3,67},{67,3},{4,68},{68... | collective-permute-start | bytes 2359304 | tf_op jit(solution)/shard_map/ppermute | solution.py:261
  65.3 18.5 %all-to-all-start.1 = ((bf16[8,192,128]{2,1,0:T(8,128)(2,1)}), bf16[8,192,128]{2,1,0:T(8,128)(2,1)S(1)}, u32[]{:S(2)}, u32[]{:S(2)}) async-start(bf16[8,192,128]{2,1,0:T(8,128)(2,1)} %bitcast.8), calls=%async_computation.1 | async-start | bytes 786432 | tf_op jit(solution)/shard_map/all_to_all | solution.py:264
  69.3 3.6 %collective-permute-start.4 = (bf16[4,2,192,128]{3,2,1,0:T(8,128)(2,1)S(1)}, bf16[4,2,192,128]{3,2,1,0:T(8,128)(2,1)S(1)}, u32[]{:S(2)}, u32[]{:S(2)}) collective-permute-start(bf16[4,2,192,128]{3,2,1,0:T(8,128)(2,1)S(1)} %shard_map.51.m_ref), channel_id=1, source_target_pairs={{0,64},{64,0},{1,65},{65,1},{2,66},{66,2},{3,67},{67,3},{4,68},{68... | collective-permute-start | bytes 1179656 | tf_op jit(solution)/shard_map/ppermute | solution.py:263
  76.5 11.6 %collective-permute-start.6 = (f32[4,128,256]{2,1,0:T(8,128)S(1)}, f32[4,128,256]{2,1,0:T(8,128)S(1)}, u32[]{:S(2)}, u32[]{:S(2)}) collective-permute-start(f32[4,128,256]{2,1,0:T(8,128)S(1)} %get-tuple-element.27), channel_id=1, source_target_pairs={{0,32},{1,33},{2,34},{3,35},{4,36},{5,37},{6,38},{7,39},{8,40},{9,... | collective-permute-start | bytes 1572872 | tf_op jit(solution)/shard_map/ppermute | solution.py:268
  84.7 22.2 %all-to-all-start.2 = ((f32[4,192,128]{2,1,0:T(8,128)}), f32[4,192,128]{2,1,0:T(8,128)S(1)}, u32[]{:S(2)}, u32[]{:S(2)}) async-start(f32[4,192,128]{2,1,0:T(8,128)} %broadcast_in_dim.2), calls=%async_computation.2 | async-start | bytes 786432 | tf_op jit(solution)/shard_map/all_to_all | solution.py:276
  88.3 20.6 %collective-permute-start.7 = (f32[128,256]{1,0:T(8,128)S(1)}, f32[128,256]{1,0:T(8,128)S(1)}, u32[]{:S(2)}, u32[]{:S(2)}) collective-permute-start(f32[128,256]{1,0:T(8,128)S(1)} %get-tuple-element.28), channel_id=1, source_target_pairs={{0,1},{1,0},{2,3},{3,2},{4,5},{5,4},{6,7},{7,6},{8,9},{9,8},{10,11... | collective-permute-start | bytes 393224 | tf_op jit(solution)/shard_map/ppermute | solution.py:273
  95.1 13.8 %collective-permute-start.9 = (f32[128,256]{1,0:T(8,128)S(1)}, f32[128,256]{1,0:T(8,128)S(1)}, u32[]{:S(2)}, u32[]{:S(2)}) collective-permute-start(f32[128,256]{1,0:T(8,128)S(1)} %get-tuple-element.29), channel_id=1, source_target_pairs={{0,9},{1,8},{2,11},{3,10},{4,13},{5,12},{6,15},{7,14},{8,1},{9,0},... | collective-permute-start | bytes 393224 | tf_op jit(solution)/shard_map/ppermute | solution.py:273
  105.0 6.9 %collective-permute-start.8 = (f32[128,256]{1,0:T(8,128)S(1)}, f32[128,256]{1,0:T(8,128)S(1)}, u32[]{:S(2)}, u32[]{:S(2)}) collective-permute-start(f32[128,256]{1,0:T(8,128)S(1)} %get-tuple-element.30), channel_id=1, source_target_pairs={{0,8},{1,9},{2,10},{3,11},{4,12},{5,13},{6,14},{7,15},{8,0},{9,1},... | collective-permute-start | bytes 393224 | tf_op jit(solution)/shard_map/ppermute | solution.py:273
  106.9 5.6 %collective-permute-start.10 = (f32[192,128]{1,0:T(8,128)S(1)}, f32[192,128]{1,0:T(8,128)S(1)}, u32[]{:S(2)}, u32[]{:S(2)}) collective-permute-start(f32[192,128]{1,0:T(8,128)S(1)} %reduce_sum.19), channel_id=1, source_target_pairs={{0,64},{64,0},{1,65},{65,1},{2,66},{66,2},{3,67},{67,3},{4,68},{68... | collective-permute-start | bytes 294920 | tf_op jit(solution)/shard_map/ppermute | solution.py:277

commit v15 on v14

--- a/solution.py
+++ b/solution.py
@@ -149,11 +149,11 @@
 
 def project(packed, mine, other, spot):
     sharers, rows, both = packed.shape
-    depth, xhs, shard, wide = mine.shape
-    part, cols = depth * xhs * shard, 2 * wide
+    depth, shard, cols = mine.shape
+    part = 2 * depth * shard
 
     def body(spot_ref, p_ref, m_ref, r_ref, near_ref, away_ref, stage, whole, sems):
-        core, yl, xl, zl, xh, zh = (spot_ref[i] for i in range(6))
+        core, yl, xl, zl, zh = (spot_ref[i] for i in range(5))
         own = (yl * 2 + xl) * 2 + zl
         loads = []
         for flip in range(sharers):
@@ -165,11 +165,8 @@
             loads[-1].start()
         for back in range(depth):
             at_z = lax.rem(zh + depth - back, depth)
-            for side in range(xhs):
-                ours, theirs = m_ref[back, side], r_ref[back, side]
-                left = jnp.where(core == 0, ours, theirs)
-                right = jnp.where(core == 0, theirs, ours)
-                whole[xh ^ side, at_z] = jnp.concatenate([left, right], axis=1)
+            whole[core, at_z] = m_ref[back]
+            whole[1 - core, at_z] = r_ref[back]
         for load in loads:
             load.wait()
         t = stage[...].reshape(sharers * rows, both)[:, :part]
@@ -191,7 +188,7 @@
         out_shape=[out, out],
         scratch_shapes=[
             pltpu.VMEM(packed.shape, packed.dtype),
-            pltpu.VMEM((xhs, depth, shard, cols), packed.dtype),
+            pltpu.VMEM((2, depth, shard, cols), packed.dtype),
             pltpu.SemaphoreType.DMA((sharers,)),
         ],
         compiler_params=PARAMS,
@@ -239,22 +236,26 @@
     shard, cols = weight.shape
     wide = cols // 2
     cubes, flip_y, flips = partners([lax.axis_size(name) for name in CHIP])
-    here = ("c", "yl", "xl", "zl", "xh", "zh")
+    here = ("c", "yl", "xl", "zl", "zh")
     spot = jnp.stack([lax.axis_index(name) for name in here])
     spot = spot.astype(jnp.int32)
 
-    other = lax.ppermute(weight, "xh", SWAP)
     packed = pack(tokens, grad_out, shard)
-    packed, other = lax.optimization_barrier((packed, other))
     packed = lax.all_to_all(packed, CHIP, 0, 0, axis_index_groups=cubes)
     part = packed.shape[-1] - cols
-    mine = jnp.stack([weight, other])
-    mine = jnp.where(spot[0] == 0, mine[..., :wide], mine[..., wide:])
     depth = lax.axis_size("zh")
-    gathered = [mine]
-    for back in range(1, depth):
-        shift = [(i, (i + back) % depth) for i in range(depth)]
-        gathered.append(lax.ppermute(mine, "zh", shift))
+    gathered = []
+    for back in range(depth):
+        shift = [
+            (
+                (c * 2 + x) * depth + z,
+                (x * 2 + (x ^ c)) * depth + (z + back) % depth,
+            )
+            for c in range(2)
+            for x in range(2)
+            for z in range(depth)
+        ]
+        gathered.append(lax.ppermute(weight, ("c", "xh", "zh"), shift))
     packed, *gathered = lax.optimization_barrier((packed, *gathered))
 
     keep, send = terms(packed, spot, part)

time: 114 us -> 113 us (level)
  the two profiles are of different devices: /device:TPU:1 before, /device:TPU:57 now
where the time goes in v15:
time: 113 us; the launch traced here: 112 us
  starting transfers between devices  65.7 us (58%)
  waiting for transfers between devices  30.5 us (27%)
  Pallas kernels  11.9 us (11%)
  other arithmetic  2.34 us (2%)
    ppermute x4, starting transfers between devices, local(): gathered.append(lax.ppermute(weight, ('c', 'xh', 'zh'), shift))  17 us
    ppermute x3, starting transfers between devices, local(): output = output + lax.ppermute(near[n + 1], CHIP, flip)  16.1 us
    all_to_all x1, starting transfers between devices, local(): packed = lax.all_to_all(packed, CHIP, 0, 0, axis_index_groups=cubes)  14.8 us
    ppermute x4, waiting for transfers between devices, local(): gathered.append(lax.ppermute(weight, ('c', 'xh', 'zh'), shift))  12.6 us
    all_to_all x1, waiting for transfers between devices, local(): term = lax.all_to_all(term.reshape(-1, shard, wide), ('xh', 'zh'), 0, 0)  5.62 us
    ppermute x3, waiting for transfers between devices, local(): output = output + lax.ppermute(near[n + 1], CHIP, flip)  5.11 us
    all_to_all x1, starting transfers between devices, local(): half = jnp.sum(lax.all_to_all(lines, 'yh', 0, 0), axis=0)  4.84 us
    all_to_all x1, starting transfers between devices, local(): term = lax.all_to_all(term.reshape(-1, shard, wide), ('xh', 'zh'), 0, 0)  4.56 us
  transfers between devices with their start and end apart: 14, of which 7 were waited for; matrix products, arithmetic and copies ran while one was open for 2% of the time, Pallas kernels for 4%

profile of v15, /device:TPU:57, one launch (start us, length us, event | category | flops | bytes accessed | tf_op | source)
XLA Modules:
  0.0 112.1 jit_solution(13360491832664963960)
XLA Ops:
  0.6 3.9 %shard_map.50 = bf16[8,128,1792]{2,1,0:T(8,128)(2,1)} custom-call(bf16[128,12288]{1,0:T(8,128)(2,1)} %t_ref.1, bf16[128,256]{1,0:T(8,128)(2,1)} %g_ref.1), custom_call_target="tpu_custom_call" | custom-call | tf_op jit(solution)/shard_map/pallas_call | solution.py:60
  4.5 14.8 %all-to-all-start = ((bf16[8,128,1792]{2,1,0:T(8,128)(2,1)}), bf16[8,128,1792]{2,1,0:T(8,128)(2,1)}, u32[]{:S(2)}, u32[]{:S(2)}) async-start(bf16[8,128,1792]{2,1,0:T(8,128)(2,1)} %shard_map.50), calls=%async_computation | async-start | bytes 7340032 | tf_op jit(solution)/shard_map/all_to_all | solution.py:244
  19.3 1.9 %collective-permute-start = (bf16[192,256]{1,0:T(8,128)(2,1)S(1)}, bf16[192,256]{1,0:T(8,128)(2,1)S(1)}, u32[]{:S(2)}, u32[]{:S(2)}) collective-permute-start(bf16[192,256]{1,0:T(8,128)(2,1)S(1)} %copy-done), channel_id=1, source_target_pairs={{0,0},{2,2},{4,4},{6,6},{16,80},{18,82},{20,84},{22,86},{64,16},{6... | collective-permute-start | bytes 294920 | tf_op jit(solution)/shard_map/ppermute | solution.py:258
  21.2 1.9 %collective-permute-start.1 = (bf16[192,256]{1,0:T(8,128)(2,1)S(1)}, bf16[192,256]{1,0:T(8,128)(2,1)S(1)}, u32[]{:S(2)}, u32[]{:S(2)}) collective-permute-start(bf16[192,256]{1,0:T(8,128)(2,1)S(1)} %copy-done), channel_id=1, source_target_pairs={{0,2},{2,4},{4,6},{6,0},{16,82},{18,84},{20,86},{22,80},{64,18},{6... | collective-permute-start | bytes 294920 | tf_op jit(solution)/shard_map/ppermute | solution.py:258
  23.2 7.2 %collective-permute-start.2 = (bf16[192,256]{1,0:T(8,128)(2,1)S(1)}, bf16[192,256]{1,0:T(8,128)(2,1)S(1)}, u32[]{:S(2)}, u32[]{:S(2)}) collective-permute-start(bf16[192,256]{1,0:T(8,128)(2,1)S(1)} %copy-done), channel_id=1, source_target_pairs={{0,4},{2,6},{4,0},{6,2},{16,84},{18,86},{20,80},{22,82},{64,20},{6... | collective-permute-start | bytes 294920 | tf_op jit(solution)/shard_map/ppermute | solution.py:258
  30.4 6.0 %collective-permute-start.3 = (bf16[192,256]{1,0:T(8,128)(2,1)S(1)}, bf16[192,256]{1,0:T(8,128)(2,1)S(1)}, u32[]{:S(2)}, u32[]{:S(2)}) collective-permute-start(bf16[192,256]{1,0:T(8,128)(2,1)S(1)} %copy-done), channel_id=1, source_target_pairs={{0,6},{2,0},{4,2},{6,4},{16,86},{18,80},{20,82},{22,84},{64,22},{6... | collective-permute-start | bytes 294920 | tf_op jit(solution)/shard_map/ppermute | solution.py:258
  36.5 7.7 %collective-permute-done.2.refs_2_ = bf16[192,256]{1,0:T(8,128)(2,1)S(1)} collective-permute-done((bf16[192,256]{1,0:T(8,128)(2,1)S(1)}, bf16[192,256]{1,0:T(8,128)(2,1)S(1)}, u32[]{:S(2)}, u32[]{:S(2)}) %collective-permute-start.2) | collective-permute-done | bytes 98336 | tf_op jit(solution)/shard_map/ppermute | solution.py:258
  44.1 5.0 %collective-permute-done.3.refs_3_ = bf16[192,256]{1,0:T(8,128)(2,1)S(1)} collective-permute-done((bf16[192,256]{1,0:T(8,128)(2,1)S(1)}, bf16[192,256]{1,0:T(8,128)(2,1)S(1)}, u32[]{:S(2)}, u32[]{:S(2)}) %collective-permute-start.3) | collective-permute-done | bytes 98336 | tf_op jit(solution)/shard_map/ppermute | solution.py:258
  49.1 3.6 %all-to-all-done.p_ref = bf16[8,128,1792]{2,1,0:T(8,128)(2,1)} async-done(((bf16[8,128,1792]{2,1,0:T(8,128)(2,1)}), bf16[8,128,1792]{2,1,0:T(8,128)(2,1)}, u32[]{:S(2)}, u32[]{:S(2)}) %all-to-all-start) | async-done | bytes 3670048 | tf_op jit(solution)/shard_map/all_to_all | solution.py:244
  52.7 3.8 %shard_map.52 = (f32[1536,128]{1,0:T(8,128)S(1)}, f32[1536,128]{1,0:T(8,128)S(1)}) custom-call(s32[5]{0:T(128)S(1)} %stack.23.spot_ref, bf16[8,128,1792]{2,1,0:T(8,128)(2,1)} %all-to-all-done.p_ref), custom_call_target="tpu_custom_call" | custom-call | tf_op jit(solution)/shard_map/pallas_call | solution.py:111
  56.5 1.9 %collective-permute-start.5 = (f32[1536,128]{1,0:T(8,128)S(1)}, f32[1536,128]{1,0:T(8,128)S(1)}, u32[]{:S(2)}, u32[]{:S(2)}) collective-permute-start(f32[1536,128]{1,0:T(8,128)S(1)} %get-tuple-element.18), channel_id=1, source_target_pairs={{0,64},{64,0},{1,65},{65,1},{2,66},{66,2},{3,67},{67,3},{4,68},{68... | collective-permute-start | bytes 2359304 | tf_op jit(solution)/shard_map/ppermute | solution.py:262
  58.5 2.3 %collective-permute-done.5 = f32[1536,128]{1,0:T(8,128)S(1)} collective-permute-done((f32[1536,128]{1,0:T(8,128)S(1)}, f32[1536,128]{1,0:T(8,128)S(1)}, u32[]{:S(2)}, u32[]{:S(2)}) %collective-permute-start.5) | collective-permute-done | bytes 786464 | tf_op jit(solution)/shard_map/ppermute | solution.py:262
  61.5 4.6 %all-to-all-start.1 = ((bf16[8,192,128]{2,1,0:T(8,128)(2,1)}), bf16[8,192,128]{2,1,0:T(8,128)(2,1)S(1)}, u32[]{:S(2)}, u32[]{:S(2)}) async-start(bf16[8,192,128]{2,1,0:T(8,128)(2,1)} %bitcast.5), calls=%async_computation.1 | async-start | bytes 786432 | tf_op jit(solution)/shard_map/all_to_all | solution.py:265
  66.6 2.6 %collective-permute-start.4 = (bf16[4,192,256]{2,1,0:T(8,128)(2,1)S(1)}, bf16[4,192,256]{2,1,0:T(8,128)(2,1)S(1)}, u32[]{:S(2)}, u32[]{:S(2)}) collective-permute-start(bf16[4,192,256]{2,1,0:T(8,128)(2,1)S(1)} %shard_map.51.m_ref), channel_id=1, source_target_pairs={{0,64},{64,0},{1,65},{65,1},{2,66},{66,2},{3,67},{67,3},{4,68},{68... | collective-permute-start | bytes 1179656 | tf_op jit(solution)/shard_map/ppermute | solution.py:264
  69.2 1.3 %collective-permute-done.4.r_ref = bf16[4,192,256]{2,1,0:T(8,128)(2,1)S(1)} collective-permute-done((bf16[4,192,256]{2,1,0:T(8,128)(2,1)S(1)}, bf16[4,192,256]{2,1,0:T(8,128)(2,1)S(1)}, u32[]{:S(2)}, u32[]{:S(2)}) %collective-permute-start.4) | collective-permute-done | bytes 393248 | tf_op jit(solution)/shard_map/ppermute | solution.py:264
  70.5 3.6 %shard_map.53 = (f32[4,128,256]{2,1,0:T(8,128)S(1)}, f32[4,128,256]{2,1,0:T(8,128)S(1)}) custom-call(s32[5]{0:T(128)S(1)} %stack.23.spot_ref, bf16[8,128,1792]{2,1,0:T(8,128)(2,1)} %all-to-all-done.p_ref, bf16[4,192,256]{2,1,0:T(8,128)(2,1)S(1)} %shard_map.51.m_ref, bf16[4,192,256]{2,1,0:T(8,128)(2,1)S(1)} %collective-permute-done.4.r_ref), custom_call_target="tpu_custom_call" | custom-call | tf_op jit(solution)/shard_map/pallas_call | solution.py:180
  74.1 1.9 %collective-permute-start.6 = (f32[4,128,256]{2,1,0:T(8,128)S(1)}, f32[4,128,256]{2,1,0:T(8,128)S(1)}, u32[]{:S(2)}, u32[]{:S(2)}) collective-permute-start(f32[4,128,256]{2,1,0:T(8,128)S(1)} %get-tuple-element.23), channel_id=1, source_target_pairs={{0,32},{1,33},{2,34},{3,35},{4,36},{5,37},{6,38},{7,39},{8,40},{9,... | collective-permute-start | bytes 1572872 | tf_op jit(solution)/shard_map/ppermute | solution.py:269
  76.1 5.6 %all-to-all-done.1 = bf16[8,192,128]{2,1,0:T(8,128)(2,1)S(1)} async-done(((bf16[8,192,128]{2,1,0:T(8,128)(2,1)}), bf16[8,192,128]{2,1,0:T(8,128)(2,1)S(1)}, u32[]{:S(2)}, u32[]{:S(2)}) %all-to-all-start.1) | async-done | bytes 393248 | tf_op jit(solution)/shard_map/all_to_all | solution.py:265
  82.5 4.8 %all-to-all-start.2 = ((f32[4,192,128]{2,1,0:T(8,128)}), f32[4,192,128]{2,1,0:T(8,128)S(1)}, u32[]{:S(2)}, u32[]{:S(2)}) async-start(f32[4,192,128]{2,1,0:T(8,128)} %broadcast_in_dim.2), calls=%async_computation.2 | async-start | bytes 786432 | tf_op jit(solution)/shard_map/all_to_all | solution.py:277
  87.5 8.6 %collective-permute-start.7 = (f32[128,256]{1,0:T(8,128)S(1)}, f32[128,256]{1,0:T(8,128)S(1)}, u32[]{:S(2)}, u32[]{:S(2)}) collective-permute-start(f32[128,256]{1,0:T(8,128)S(1)} %get-tuple-element.24), channel_id=1, source_target_pairs={{0,1},{1,0},{2,3},{3,2},{4,5},{5,4},{6,7},{7,6},{8,9},{9,8},{10,11... | collective-permute-start | bytes 393224 | tf_op jit(solution)/shard_map/ppermute | solution.py:274
  96.1 5.6 %collective-permute-start.8 = (f32[128,256]{1,0:T(8,128)S(1)}, f32[128,256]{1,0:T(8,128)S(1)}, u32[]{:S(2)}, u32[]{:S(2)}) collective-permute-start(f32[128,256]{1,0:T(8,128)S(1)} %get-tuple-element.26), channel_id=1, source_target_pairs={{0,8},{1,9},{2,10},{3,11},{4,12},{5,13},{6,14},{7,15},{8,0},{9,1},... | collective-permute-start | bytes 393224 | tf_op jit(solution)/shard_map/ppermute | solution.py:274
  101.7 1.9 %collective-permute-start.9 = (f32[128,256]{1,0:T(8,128)S(1)}, f32[128,256]{1,0:T(8,128)S(1)}, u32[]{:S(2)}, u32[]{:S(2)}) collective-permute-start(f32[128,256]{1,0:T(8,128)S(1)} %get-tuple-element.25), channel_id=1, source_target_pairs={{0,9},{1,8},{2,11},{3,10},{4,13},{5,12},{6,15},{7,14},{8,1},{9,0},... | collective-permute-start | bytes 393224 | tf_op jit(solution)/shard_map/ppermute | solution.py:274
  103.7 1.9 %collective-permute-start.10 = (f32[192,128]{1,0:T(8,128)S(1)}, f32[192,128]{1,0:T(8,128)S(1)}, u32[]{:S(2)}, u32[]{:S(2)}) collective-permute-start(f32[192,128]{1,0:T(8,128)S(1)} %reduce_sum.19), channel_id=1, source_target_pairs={{0,64},{64,0},{1,65},{65,1},{2,66},{66,2},{3,67},{67,3},{4,68},{68... | collective-permute-start | bytes 294920 | tf_op jit(solution)/shard_map/ppermute | solution.py:278
  105.6 5.1 %collective-permute-done.9 = f32[128,256]{1,0:T(8,128)S(1)} collective-permute-done((f32[128,256]{1,0:T(8,128)S(1)}, f32[128,256]{1,0:T(8,128)S(1)}, u32[]{:S(2)}, u32[]{:S(2)}) %collective-permute-start.9) | collective-permute-done | bytes 131104 | tf_op jit(solution)/shard_map/ppermute | solution.py:274
  (20 shorter events, 3.8 us)
Async XLA Ops:
  4.5 14.8 %copy-start = (bf16[192,256]{1,0:T(8,128)(2,1)S(1)}, bf16[192,256]{1,0:T(8,128)(2,1)}, u32[]{:S(2)}) copy-start(bf16[192,256]{1,0:T(8,128)(2,1)} %param.4) | copy-start | bytes 294916
  4.5 48.1 %all-to-all-start = ((bf16[8,128,1792]{2,1,0:T(8,128)(2,1)}), bf16[8,128,1792]{2,1,0:T(8,128)(2,1)}, u32[]{:S(2)}, u32[]{:S(2)}) async-start(bf16[8,128,1792]{2,1,0:T(8,128)(2,1)} %shard_map.50), calls=%async_computation | async-start | bytes 7340032 | tf_op jit(solution)/shard_map/all_to_all | solution.py:244
  19.3 17.2 %collective-permute-start = (bf16[192,256]{1,0:T(8,128)(2,1)S(1)}, bf16[192,256]{1,0:T(8,128)(2,1)S(1)}, u32[]{:S(2)}, u32[]{:S(2)}) collective-permute-start(bf16[192,256]{1,0:T(8,128)(2,1)S(1)} %copy-done), channel_id=1, source_target_pairs={{0,0},{2,2},{4,4},{6,6},{16,80},{18,82},{20,84},{22,86},{64,16},{6... | collective-permute-start | bytes 294920 | tf_op jit(solution)/shard_map/ppermute | solution.py:258
  21.2 15.3 %collective-permute-start.1 = (bf16[192,256]{1,0:T(8,128)(2,1)S(1)}, bf16[192,256]{1,0:T(8,128)(2,1)S(1)}, u32[]{:S(2)}, u32[]{:S(2)}) collective-permute-start(bf16[192,256]{1,0:T(8,128)(2,1)S(1)} %copy-done), channel_id=1, source_target_pairs={{0,2},{2,4},{4,6},{6,0},{16,82},{18,84},{20,86},{22,80},{64,18},{6... | collective-permute-start | bytes 294920 | tf_op jit(solution)/shard_map/ppermute | solution.py:258
  23.2 21.0 %collective-permute-start.2 = (bf16[192,256]{1,0:T(8,128)(2,1)S(1)}, bf16[192,256]{1,0:T(8,128)(2,1)S(1)}, u32[]{:S(2)}, u32[]{:S(2)}) collective-permute-start(bf16[192,256]{1,0:T(8,128)(2,1)S(1)} %copy-done), channel_id=1, source_target_pairs={{0,4},{2,6},{4,0},{6,2},{16,84},{18,86},{20,80},{22,82},{64,20},{6... | collective-permute-start | bytes 294920 | tf_op jit(solution)/shard_map/ppermute | solution.py:258
  30.4 18.7 %collective-permute-start.3 = (bf16[192,256]{1,0:T(8,128)(2,1)S(1)}, bf16[192,256]{1,0:T(8,128)(2,1)S(1)}, u32[]{:S(2)}, u32[]{:S(2)}) collective-permute-start(bf16[192,256]{1,0:T(8,128)(2,1)S(1)} %copy-done), channel_id=1, source_target_pairs={{0,6},{2,0},{4,2},{6,4},{16,86},{18,80},{20,82},{22,84},{64,22},{6... | collective-permute-start | bytes 294920 | tf_op jit(solution)/shard_map/ppermute | solution.py:258
  56.5 4.2 %collective-permute-start.5 = (f32[1536,128]{1,0:T(8,128)S(1)}, f32[1536,128]{1,0:T(8,128)S(1)}, u32[]{:S(2)}, u32[]{:S(2)}) collective-permute-start(f32[1536,128]{1,0:T(8,128)S(1)} %get-tuple-element.18), channel_id=1, source_target_pairs={{0,64},{64,0},{1,65},{65,1},{2,66},{66,2},{3,67},{67,3},{4,68},{68... | collective-permute-start | bytes 2359304 | tf_op jit(solution)/shard_map/ppermute | solution.py:262
  61.5 20.2 %all-to-all-start.1 = ((bf16[8,192,128]{2,1,0:T(8,128)(2,1)}), bf16[8,192,128]{2,1,0:T(8,128)(2,1)S(1)}, u32[]{:S(2)}, u32[]{:S(2)}) async-start(bf16[8,192,128]{2,1,0:T(8,128)(2,1)} %bitcast.5), calls=%async_computation.1 | async-start | bytes 786432 | tf_op jit(solution)/shard_map/all_to_all | solution.py:265
  66.6 3.9 %collective-permute-start.4 = (bf16[4,192,256]{2,1,0:T(8,128)(2,1)S(1)}, bf16[4,192,256]{2,1,0:T(8,128)(2,1)S(1)}, u32[]{:S(2)}, u32[]{:S(2)}) collective-permute-start(bf16[4,192,256]{2,1,0:T(8,128)(2,1)S(1)} %shard_map.51.m_ref), channel_id=1, source_target_pairs={{0,64},{64,0},{1,65},{65,1},{2,66},{66,2},{3,67},{67,3},{4,68},{68... | collective-permute-start | bytes 1179656 | tf_op jit(solution)/shard_map/ppermute | solution.py:264
  74.1 13.2 %collective-permute-start.6 = (f32[4,128,256]{2,1,0:T(8,128)S(1)}, f32[4,128,256]{2,1,0:T(8,128)S(1)}, u32[]{:S(2)}, u32[]{:S(2)}) collective-permute-start(f32[4,128,256]{2,1,0:T(8,128)S(1)} %get-tuple-element.23), channel_id=1, source_target_pairs={{0,32},{1,33},{2,34},{3,35},{4,36},{5,37},{6,38},{7,39},{8,40},{9,... | collective-permute-start | bytes 1572872 | tf_op jit(solution)/shard_map/ppermute | solution.py:269
  82.5 21.1 %all-to-all-start.2 = ((f32[4,192,128]{2,1,0:T(8,128)}), f32[4,192,128]{2,1,0:T(8,128)S(1)}, u32[]{:S(2)}, u32[]{:S(2)}) async-start(f32[4,192,128]{2,1,0:T(8,128)} %broadcast_in_dim.2), calls=%async_computation.2 | async-start | bytes 786432 | tf_op jit(solution)/shard_map/all_to_all | solution.py:277
  87.5 18.1 %collective-permute-start.7 = (f32[128,256]{1,0:T(8,128)S(1)}, f32[128,256]{1,0:T(8,128)S(1)}, u32[]{:S(2)}, u32[]{:S(2)}) collective-permute-start(f32[128,256]{1,0:T(8,128)S(1)} %get-tuple-element.24), channel_id=1, source_target_pairs={{0,1},{1,0},{2,3},{3,2},{4,5},{5,4},{6,7},{7,6},{8,9},{9,8},{10,11... | collective-permute-start | bytes 393224 | tf_op jit(solution)/shard_map/ppermute | solution.py:274
  96.1 9.5 %collective-permute-start.8 = (f32[128,256]{1,0:T(8,128)S(1)}, f32[128,256]{1,0:T(8,128)S(1)}, u32[]{:S(2)}, u32[]{:S(2)}) collective-permute-start(f32[128,256]{1,0:T(8,128)S(1)} %get-tuple-element.26), channel_id=1, source_target_pairs={{0,8},{1,9},{2,10},{3,11},{4,12},{5,13},{6,14},{7,15},{8,0},{9,1},... | collective-permute-start | bytes 393224 | tf_op jit(solution)/shard_map/ppermute | solution.py:274
  101.7 9.0 %collective-permute-start.9 = (f32[128,256]{1,0:T(8,128)S(1)}, f32[128,256]{1,0:T(8,128)S(1)}, u32[]{:S(2)}, u32[]{:S(2)}) collective-permute-start(f32[128,256]{1,0:T(8,128)S(1)} %get-tuple-element.25), channel_id=1, source_target_pairs={{0,9},{1,8},{2,11},{3,10},{4,13},{5,12},{6,15},{7,14},{8,1},{9,0},... | collective-permute-start | bytes 393224 | tf_op jit(solution)/shard_map/ppermute | solution.py:274
  103.7 7.7 %collective-permute-start.10 = (f32[192,128]{1,0:T(8,128)S(1)}, f32[192,128]{1,0:T(8,128)S(1)}, u32[]{:S(2)}, u32[]{:S(2)}) collective-permute-start(f32[192,128]{1,0:T(8,128)S(1)} %reduce_sum.19), channel_id=1, source_target_pairs={{0,64},{64,0},{1,65},{65,1},{2,66},{66,2},{3,67},{67,3},{4,68},{68... | collective-permute-start | bytes 294920 | tf_op jit(solution)/shard_map/ppermute | solution.py:278

commit v16 on v15

--- a/solution.py
+++ b/solution.py
@@ -208,7 +208,7 @@
             return i ^ 1
         return (i + 1) % n if i % 2 else (i - 1) % n
 
-    moves = ((1, 0, 0), (0, 0, 1), (0, 1, 0), (0, 1, 1))
+    moves = ((1, 0, 0), (0, 1, 0), (0, 0, 1))
     flips, cubes = [[] for _ in moves], []
     for c in range(cores):
         for y in range(rings[0]):
@@ -229,13 +229,13 @@
                                 for d in pairs[2]
                             ]
                         )
-    return cubes, flips[0], flips[1:]
+    return cubes, *flips
 
 
 def local(tokens, weight, grad_out):
     shard, cols = weight.shape
     wide = cols // 2
-    cubes, flip_y, flips = partners([lax.axis_size(name) for name in CHIP])
+    cubes, flip_y, flip_x, flip_z = partners([lax.axis_size(name) for name in CHIP])
     here = ("c", "yl", "xl", "zl", "zh")
     spot = jnp.stack([lax.axis_index(name) for name in here])
     spot = spot.astype(jnp.int32)
@@ -269,13 +269,14 @@
     away = lax.ppermute(away, CHIP, flip_y)
     near, _ = lax.optimization_barrier((near, summed))
     near = near + away
-    output = near[0]
-    for n, flip in enumerate(flips):
-        output = output + lax.ppermute(near[n + 1], CHIP, flip)
+    near = near[:2] + lax.ppermute(near[2:], CHIP, flip_x)
 
     lines = jnp.broadcast_to(summed[None], (lax.axis_size("yh"), shard, wide))
-    half = jnp.sum(lax.all_to_all(lines, "yh", 0, 0), axis=0)
+    lines = lax.all_to_all(lines, "yh", 0, 0)
+    near, lines = lax.optimization_barrier((near, lines))
+    half = jnp.sum(lines, axis=0)
     other = lax.ppermute(half, "c", SWAP)
+    output = near[0] + lax.ppermute(near[1], CHIP, flip_z)
     first = spot[0] == 0
     weight_grad = jnp.concatenate(
         [jnp.where(first, half, other), jnp.where(first, other, half)], axis=1

time: 113 us -> 113 us (level)
  the two profiles are of different devices: /device:TPU:57 before, /device:TPU:11 now
where the time goes in v16:
time: 113 us
  starting transfers between devices  58.9 us (52%)
  waiting for transfers between devices  37.7 us (33%)
  Pallas kernels  11.9 us (11%)
  other arithmetic  2.38 us (2%)
    ppermute x4, starting transfers between devices, local(): gathered.append(lax.ppermute(weight, ('c', 'xh', 'zh'), shift))  17.9 us
    all_to_all x1, starting transfers between devices, local(): packed = lax.all_to_all(packed, CHIP, 0, 0, axis_index_groups=cubes)  12.4 us
    ppermute x4, waiting for transfers between devices, local(): gathered.append(lax.ppermute(weight, ('c', 'xh', 'zh'), shift))  12.2 us
    all_to_all x1, waiting for transfers between devices, local(): term = lax.all_to_all(term.reshape(-1, shard, wide), ('xh', 'zh'), 0, 0)  9.85 us
    all_to_all x1, starting transfers between devices, local(): term = lax.all_to_all(term.reshape(-1, shard, wide), ('xh', 'zh'), 0, 0)  8.54 us
    ppermute x1, waiting for transfers between devices, local(): near = near[:2] + lax.ppermute(near[2:], CHIP, flip_x)  5.48 us
    all_to_all x1, starting transfers between devices, local(): lines = lax.all_to_all(lines, 'yh', 0, 0)  5.42 us
    all_to_all x1, waiting for transfers between devices, local(): lines = lax.all_to_all(lines, 'yh', 0, 0)  4.47 us
  transfers between devices with their start and end apart: 13, of which 8 were waited for; matrix products, arithmetic and copies ran while one was open for 2% of the time, Pallas kernels for 4%

profile of v16, /device:TPU:11, one launch (start us, length us, event | category | flops | bytes accessed | tf_op | source)
XLA Modules:
  0.0 112.6 jit_solution(16114554626914781527)
XLA Ops:
  0.6 3.9 %shard_map.50 = bf16[8,128,1792]{2,1,0:T(8,128)(2,1)} custom-call(bf16[128,12288]{1,0:T(8,128)(2,1)} %t_ref.1, bf16[128,256]{1,0:T(8,128)(2,1)} %g_ref.1), custom_call_target="tpu_custom_call" | custom-call | tf_op jit(solution)/shard_map/pallas_call | solution.py:60
  4.6 12.4 %all-to-all-start = ((bf16[8,128,1792]{2,1,0:T(8,128)(2,1)}), bf16[8,128,1792]{2,1,0:T(8,128)(2,1)}, u32[]{:S(2)}, u32[]{:S(2)}) async-start(bf16[8,128,1792]{2,1,0:T(8,128)(2,1)} %shard_map.50), calls=%async_computation | async-start | bytes 7340032 | tf_op jit(solution)/shard_map/all_to_all | solution.py:244
  17.0 1.9 %collective-permute-start = (bf16[192,256]{1,0:T(8,128)(2,1)S(1)}, bf16[192,256]{1,0:T(8,128)(2,1)S(1)}, u32[]{:S(2)}, u32[]{:S(2)}) collective-permute-start(bf16[192,256]{1,0:T(8,128)(2,1)S(1)} %copy-done), channel_id=1, source_target_pairs={{0,0},{2,2},{4,4},{6,6},{16,80},{18,82},{20,84},{22,86},{64,16},{6... | collective-permute-start | bytes 294920 | tf_op jit(solution)/shard_map/ppermute | solution.py:258
  18.9 1.9 %collective-permute-start.1 = (bf16[192,256]{1,0:T(8,128)(2,1)S(1)}, bf16[192,256]{1,0:T(8,128)(2,1)S(1)}, u32[]{:S(2)}, u32[]{:S(2)}) collective-permute-start(bf16[192,256]{1,0:T(8,128)(2,1)S(1)} %copy-done), channel_id=1, source_target_pairs={{0,2},{2,4},{4,6},{6,0},{16,82},{18,84},{20,86},{22,80},{64,18},{6... | collective-permute-start | bytes 294920 | tf_op jit(solution)/shard_map/ppermute | solution.py:258
  20.8 10.1 %collective-permute-start.2 = (bf16[192,256]{1,0:T(8,128)(2,1)S(1)}, bf16[192,256]{1,0:T(8,128)(2,1)S(1)}, u32[]{:S(2)}, u32[]{:S(2)}) collective-permute-start(bf16[192,256]{1,0:T(8,128)(2,1)S(1)} %copy-done), channel_id=1, source_target_pairs={{0,4},{2,6},{4,0},{6,2},{16,84},{18,86},{20,80},{22,82},{64,20},{6... | collective-permute-start | bytes 294920 | tf_op jit(solution)/shard_map/ppermute | solution.py:258
  30.9 4.0 %collective-permute-start.3 = (bf16[192,256]{1,0:T(8,128)(2,1)S(1)}, bf16[192,256]{1,0:T(8,128)(2,1)S(1)}, u32[]{:S(2)}, u32[]{:S(2)}) collective-permute-start(bf16[192,256]{1,0:T(8,128)(2,1)S(1)} %copy-done), channel_id=1, source_target_pairs={{0,6},{2,0},{4,2},{6,4},{16,86},{18,80},{20,82},{22,84},{64,22},{6... | collective-permute-start | bytes 294920 | tf_op jit(solution)/shard_map/ppermute | solution.py:258
  35.7 7.0 %collective-permute-done.2.refs_2_ = bf16[192,256]{1,0:T(8,128)(2,1)S(1)} collective-permute-done((bf16[192,256]{1,0:T(8,128)(2,1)S(1)}, bf16[192,256]{1,0:T(8,128)(2,1)S(1)}, u32[]{:S(2)}, u32[]{:S(2)}) %collective-permute-start.2) | collective-permute-done | bytes 98336 | tf_op jit(solution)/shard_map/ppermute | solution.py:258
  42.7 4.5 %collective-permute-done.3.refs_3_ = bf16[192,256]{1,0:T(8,128)(2,1)S(1)} collective-permute-done((bf16[192,256]{1,0:T(8,128)(2,1)S(1)}, bf16[192,256]{1,0:T(8,128)(2,1)S(1)}, u32[]{:S(2)}, u32[]{:S(2)}) %collective-permute-start.3) | collective-permute-done | bytes 98336 | tf_op jit(solution)/shard_map/ppermute | solution.py:258
  47.2 1.4 %all-to-all-done.p_ref = bf16[8,128,1792]{2,1,0:T(8,128)(2,1)} async-done(((bf16[8,128,1792]{2,1,0:T(8,128)(2,1)}), bf16[8,128,1792]{2,1,0:T(8,128)(2,1)}, u32[]{:S(2)}, u32[]{:S(2)}) %all-to-all-start) | async-done | bytes 3670048 | tf_op jit(solution)/shard_map/all_to_all | solution.py:244
  48.6 3.8 %shard_map.52 = (f32[1536,128]{1,0:T(8,128)S(1)}, f32[1536,128]{1,0:T(8,128)S(1)}) custom-call(s32[5]{0:T(128)S(1)} %stack.23.spot_ref, bf16[8,128,1792]{2,1,0:T(8,128)(2,1)} %all-to-all-done.p_ref), custom_call_target="tpu_custom_call" | custom-call | tf_op jit(solution)/shard_map/pallas_call | solution.py:111
  52.4 2.5 %collective-permute-start.5 = (f32[1536,128]{1,0:T(8,128)S(1)}, f32[1536,128]{1,0:T(8,128)S(1)}, u32[]{:S(2)}, u32[]{:S(2)}) collective-permute-start(f32[1536,128]{1,0:T(8,128)S(1)} %get-tuple-element.20), channel_id=1, source_target_pairs={{0,64},{64,0},{1,65},{65,1},{2,66},{66,2},{3,67},{67,3},{4,68},{68... | collective-permute-start | bytes 2359304 | tf_op jit(solution)/shard_map/ppermute | solution.py:262
  55.5 1.9 %collective-permute-start.4 = (bf16[4,192,256]{2,1,0:T(8,128)(2,1)S(1)}, bf16[4,192,256]{2,1,0:T(8,128)(2,1)S(1)}, u32[]{:S(2)}, u32[]{:S(2)}) collective-permute-start(bf16[4,192,256]{2,1,0:T(8,128)(2,1)S(1)} %shard_map.51.m_ref), channel_id=1, source_target_pairs={{0,64},{64,0},{1,65},{65,1},{2,66},{66,2},{3,67},{67,3},{4,68},{68... | collective-permute-start | bytes 1179656 | tf_op jit(solution)/shard_map/ppermute | solution.py:264
  57.5 0.8 add_convert_fusion
  58.3 8.5 %all-to-all-start.1 = ((bf16[8,192,128]{2,1,0:T(8,128)(2,1)}), bf16[8,192,128]{2,1,0:T(8,128)(2,1)S(1)}, u32[]{:S(2)}, u32[]{:S(2)}) async-start(bf16[8,192,128]{2,1,0:T(8,128)(2,1)} %bitcast.5), calls=%async_computation.1 | async-start | bytes 786432 | tf_op jit(solution)/shard_map/all_to_all | solution.py:265
  66.8 3.6 %shard_map.53 = (f32[4,128,256]{2,1,0:T(8,128)S(1)}, f32[4,128,256]{2,1,0:T(8,128)S(1)}) custom-call(s32[5]{0:T(128)S(1)} %stack.23.spot_ref, bf16[8,128,1792]{2,1,0:T(8,128)(2,1)} %all-to-all-done.p_ref, bf16[4,192,256]{2,1,0:T(8,128)(2,1)S(1)} %shard_map.51.m_ref, bf16[4,192,256]{2,1,0:T(8,128)(2,1)S(1)} %collective-permute-done.4.r_ref), custom_call_target="tpu_custom_call" | custom-call | tf_op jit(solution)/shard_map/pallas_call | solution.py:180
  70.4 1.9 %collective-permute-start.6 = (f32[4,128,256]{2,1,0:T(8,128)S(1)}, f32[4,128,256]{2,1,0:T(8,128)S(1)}, u32[]{:S(2)}, u32[]{:S(2)}) collective-permute-start(f32[4,128,256]{2,1,0:T(8,128)S(1)} %get-tuple-element.25), channel_id=1, source_target_pairs={{0,32},{1,33},{2,34},{3,35},{4,36},{5,37},{6,38},{7,39},{8,40},{9,... | collective-permute-start | bytes 1572872 | tf_op jit(solution)/shard_map/ppermute | solution.py:269
  72.4 9.8 %all-to-all-done.1 = bf16[8,192,128]{2,1,0:T(8,128)(2,1)S(1)} async-done(((bf16[8,192,128]{2,1,0:T(8,128)(2,1)}), bf16[8,192,128]{2,1,0:T(8,128)(2,1)S(1)}, u32[]{:S(2)}, u32[]{:S(2)}) %all-to-all-start.1) | async-done | bytes 393248 | tf_op jit(solution)/shard_map/all_to_all | solution.py:265
  83.0 5.4 %all-to-all-start.2 = ((f32[4,192,128]{2,1,0:T(8,128)}), f32[4,192,128]{2,1,0:T(8,128)S(1)}, u32[]{:S(2)}, u32[]{:S(2)}) async-start(f32[4,192,128]{2,1,0:T(8,128)} %broadcast_in_dim.2), calls=%async_computation.2 | async-start | bytes 786432 | tf_op jit(solution)/shard_map/all_to_all | solution.py:275
  88.6 1.9 %collective-permute-start.7 = (f32[2,128,256]{2,1,0:T(8,128)S(1)}, f32[2,128,256]{2,1,0:T(8,128)S(1)}, u32[]{:S(2)}, u32[]{:S(2)}) collective-permute-start(f32[2,128,256]{2,1,0:T(8,128)S(1)} %slice.17), channel_id=1, source_target_pairs={{0,8},{1,9},{2,10},{3,11},{4,12},{5,13},{6,14},{7,15},{8,0},{9,1},... | collective-permute-start | bytes 786440 | tf_op jit(solution)/shard_map/ppermute | solution.py:272
  90.5 5.5 %collective-permute-done.7 = f32[2,128,256]{2,1,0:T(8,128)S(1)} collective-permute-done((f32[2,128,256]{2,1,0:T(8,128)S(1)}, f32[2,128,256]{2,1,0:T(8,128)S(1)}, u32[]{:S(2)}, u32[]{:S(2)}) %collective-permute-start.7) | collective-permute-done | bytes 262176 | tf_op jit(solution)/shard_map/ppermute | solution.py:272
  96.0 4.5 %all-to-all-done.2 = f32[4,192,128]{2,1,0:T(8,128)S(1)} async-done(((f32[4,192,128]{2,1,0:T(8,128)}), f32[4,192,128]{2,1,0:T(8,128)S(1)}, u32[]{:S(2)}, u32[]{:S(2)}) %all-to-all-start.2) | async-done | bytes 393248 | tf_op jit(solution)/shard_map/all_to_all | solution.py:275
  100.5 4.5 %collective-permute-start.9 = (f32[192,128]{1,0:T(8,128)S(1)}, f32[192,128]{1,0:T(8,128)S(1)}, u32[]{:S(2)}, u32[]{:S(2)}) collective-permute-start(f32[192,128]{1,0:T(8,128)S(1)} %reduce_sum.19), channel_id=1, source_target_pairs={{0,64},{64,0},{1,65},{65,1},{2,66},{66,2},{3,67},{67,3},{4,68},{68... | collective-permute-start | bytes 294920 | tf_op jit(solution)/shard_map/ppermute | solution.py:278
  105.0 1.9 %collective-permute-start.8 = (f32[128,256]{1,0:T(8,128)S(1)}, f32[128,256]{1,0:T(8,128)S(1)}, u32[]{:S(2)}, u32[]{:S(2)}) collective-permute-start(f32[128,256]{1,0:T(8,128)S(1)} %slice_bitcast_fusion), channel_id=1, source_target_pairs={{0,1},{1,0},{2,3},{3,2},{4,5},{5,4},{6,7},{7,6},{8,9},{9,8},{10,11... | collective-permute-start | bytes 393224 | tf_op jit(solution)/shard_map/ppermute | solution.py:279
  107.7 4.3 %collective-permute-done.8 = f32[128,256]{1,0:T(8,128)S(1)} collective-permute-done((f32[128,256]{1,0:T(8,128)S(1)}, f32[128,256]{1,0:T(8,128)S(1)}, u32[]{:S(2)}, u32[]{:S(2)}) %collective-permute-start.8) | collective-permute-done | bytes 131104 | tf_op jit(solution)/shard_map/ppermute | solution.py:279
  (20 shorter events, 3.7 us)
Async XLA Ops:
  4.5 12.4 %copy-start = (bf16[192,256]{1,0:T(8,128)(2,1)S(1)}, bf16[192,256]{1,0:T(8,128)(2,1)}, u32[]{:S(2)}) copy-start(bf16[192,256]{1,0:T(8,128)(2,1)} %param.4) | copy-start | bytes 294916
  4.6 44.0 %all-to-all-start = ((bf16[8,128,1792]{2,1,0:T(8,128)(2,1)}), bf16[8,128,1792]{2,1,0:T(8,128)(2,1)}, u32[]{:S(2)}, u32[]{:S(2)}) async-start(bf16[8,128,1792]{2,1,0:T(8,128)(2,1)} %shard_map.50), calls=%async_computation | async-start | bytes 7340032 | tf_op jit(solution)/shard_map/all_to_all | solution.py:244
  17.0 18.7 %collective-permute-start = (bf16[192,256]{1,0:T(8,128)(2,1)S(1)}, bf16[192,256]{1,0:T(8,128)(2,1)S(1)}, u32[]{:S(2)}, u32[]{:S(2)}) collective-permute-start(bf16[192,256]{1,0:T(8,128)(2,1)S(1)} %copy-done), channel_id=1, source_target_pairs={{0,0},{2,2},{4,4},{6,6},{16,80},{18,82},{20,84},{22,86},{64,16},{6... | collective-permute-start | bytes 294920 | tf_op jit(solution)/shard_map/ppermute | solution.py:258
  18.9 16.8 %collective-permute-start.1 = (bf16[192,256]{1,0:T(8,128)(2,1)S(1)}, bf16[192,256]{1,0:T(8,128)(2,1)S(1)}, u32[]{:S(2)}, u32[]{:S(2)}) collective-permute-start(bf16[192,256]{1,0:T(8,128)(2,1)S(1)} %copy-done), channel_id=1, source_target_pairs={{0,2},{2,4},{4,6},{6,0},{16,82},{18,84},{20,86},{22,80},{64,18},{6... | collective-permute-start | bytes 294920 | tf_op jit(solution)/shard_map/ppermute | solution.py:258
  20.8 21.9 %collective-permute-start.2 = (bf16[192,256]{1,0:T(8,128)(2,1)S(1)}, bf16[192,256]{1,0:T(8,128)(2,1)S(1)}, u32[]{:S(2)}, u32[]{:S(2)}) collective-permute-start(bf16[192,256]{1,0:T(8,128)(2,1)S(1)} %copy-done), channel_id=1, source_target_pairs={{0,4},{2,6},{4,0},{6,2},{16,84},{18,86},{20,80},{22,82},{64,20},{6... | collective-permute-start | bytes 294920 | tf_op jit(solution)/shard_map/ppermute | solution.py:258
  30.9 16.3 %collective-permute-start.3 = (bf16[192,256]{1,0:T(8,128)(2,1)S(1)}, bf16[192,256]{1,0:T(8,128)(2,1)S(1)}, u32[]{:S(2)}, u32[]{:S(2)}) collective-permute-start(bf16[192,256]{1,0:T(8,128)(2,1)S(1)} %copy-done), channel_id=1, source_target_pairs={{0,6},{2,0},{4,2},{6,4},{16,86},{18,80},{20,82},{22,84},{64,22},{6... | collective-permute-start | bytes 294920 | tf_op jit(solution)/shard_map/ppermute | solution.py:258
  52.4 5.0 %collective-permute-start.5 = (f32[1536,128]{1,0:T(8,128)S(1)}, f32[1536,128]{1,0:T(8,128)S(1)}, u32[]{:S(2)}, u32[]{:S(2)}) collective-permute-start(f32[1536,128]{1,0:T(8,128)S(1)} %get-tuple-element.20), channel_id=1, source_target_pairs={{0,64},{64,0},{1,65},{65,1},{2,66},{66,2},{3,67},{67,3},{4,68},{68... | collective-permute-start | bytes 2359304 | tf_op jit(solution)/shard_map/ppermute | solution.py:262
  55.5 11.3 %collective-permute-start.4 = (bf16[4,192,256]{2,1,0:T(8,128)(2,1)S(1)}, bf16[4,192,256]{2,1,0:T(8,128)(2,1)S(1)}, u32[]{:S(2)}, u32[]{:S(2)}) collective-permute-start(bf16[4,192,256]{2,1,0:T(8,128)(2,1)S(1)} %shard_map.51.m_ref), channel_id=1, source_target_pairs={{0,64},{64,0},{1,65},{65,1},{2,66},{66,2},{3,67},{67,3},{4,68},{68... | collective-permute-start | bytes 1179656 | tf_op jit(solution)/shard_map/ppermute | solution.py:264
  58.3 23.9 %all-to-all-start.1 = ((bf16[8,192,128]{2,1,0:T(8,128)(2,1)}), bf16[8,192,128]{2,1,0:T(8,128)(2,1)S(1)}, u32[]{:S(2)}, u32[]{:S(2)}) async-start(bf16[8,192,128]{2,1,0:T(8,128)(2,1)} %bitcast.5), calls=%async_computation.1 | async-start | bytes 786432 | tf_op jit(solution)/shard_map/all_to_all | solution.py:265
  70.4 18.0 %collective-permute-start.6 = (f32[4,128,256]{2,1,0:T(8,128)S(1)}, f32[4,128,256]{2,1,0:T(8,128)S(1)}, u32[]{:S(2)}, u32[]{:S(2)}) collective-permute-start(f32[4,128,256]{2,1,0:T(8,128)S(1)} %get-tuple-element.25), channel_id=1, source_target_pairs={{0,32},{1,33},{2,34},{3,35},{4,36},{5,37},{6,38},{7,39},{8,40},{9,... | collective-permute-start | bytes 1572872 | tf_op jit(solution)/shard_map/ppermute | solution.py:269
  83.0 17.4 %all-to-all-start.2 = ((f32[4,192,128]{2,1,0:T(8,128)}), f32[4,192,128]{2,1,0:T(8,128)S(1)}, u32[]{:S(2)}, u32[]{:S(2)}) async-start(f32[4,192,128]{2,1,0:T(8,128)} %broadcast_in_dim.2), calls=%async_computation.2 | async-start | bytes 786432 | tf_op jit(solution)/shard_map/all_to_all | solution.py:275
  88.6 7.4 %collective-permute-start.7 = (f32[2,128,256]{2,1,0:T(8,128)S(1)}, f32[2,128,256]{2,1,0:T(8,128)S(1)}, u32[]{:S(2)}, u32[]{:S(2)}) collective-permute-start(f32[2,128,256]{2,1,0:T(8,128)S(1)} %slice.17), channel_id=1, source_target_pairs={{0,8},{1,9},{2,10},{3,11},{4,12},{5,13},{6,14},{7,15},{8,0},{9,1},... | collective-permute-start | bytes 786440 | tf_op jit(solution)/shard_map/ppermute | solution.py:272
  100.5 6.4 %collective-permute-start.9 = (f32[192,128]{1,0:T(8,128)S(1)}, f32[192,128]{1,0:T(8,128)S(1)}, u32[]{:S(2)}, u32[]{:S(2)}) collective-permute-start(f32[192,128]{1,0:T(8,128)S(1)} %reduce_sum.19), channel_id=1, source_target_pairs={{0,64},{64,0},{1,65},{65,1},{2,66},{66,2},{3,67},{67,3},{4,68},{68... | collective-permute-start | bytes 294920 | tf_op jit(solution)/shard_map/ppermute | solution.py:278
  105.0 6.9 %collective-permute-start.8 = (f32[128,256]{1,0:T(8,128)S(1)}, f32[128,256]{1,0:T(8,128)S(1)}, u32[]{:S(2)}, u32[]{:S(2)}) collective-permute-start(f32[128,256]{1,0:T(8,128)S(1)} %slice_bitcast_fusion), channel_id=1, source_target_pairs={{0,1},{1,0},{2,3},{3,2},{4,5},{5,4},{6,7},{7,6},{8,9},{9,8},{10,11... | collective-permute-start | bytes 393224 | tf_op jit(solution)/shard_map/ppermute | solution.py:279

commit v17 on v15

--- a/solution.py
+++ b/solution.py
@@ -156,11 +156,9 @@
         core, yl, xl, zl, zh = (spot_ref[i] for i in range(5))
         own = (yl * 2 + xl) * 2 + zl
         loads = []
-        for flip in range(sharers):
+        for n, flip in enumerate((0, 1, 4, 5, 2, 3, 6, 7)):
             loads.append(
-                pltpu.make_async_copy(
-                    p_ref.at[own ^ flip], stage.at[flip], sems.at[flip]
-                )
+                pltpu.make_async_copy(p_ref.at[own ^ flip], stage.at[n], sems.at[n])
             )
             loads[-1].start()
         for back in range(depth):
@@ -208,7 +206,7 @@
             return i ^ 1
         return (i + 1) % n if i % 2 else (i - 1) % n
 
-    moves = ((1, 0, 0), (0, 0, 1), (0, 1, 0), (0, 1, 1))
+    moves = ((0, 1, 0), (0, 0, 1), (1, 0, 0), (1, 0, 1))
     flips, cubes = [[] for _ in moves], []
     for c in range(cores):
         for y in range(rings[0]):
@@ -235,7 +233,7 @@
 def local(tokens, weight, grad_out):
     shard, cols = weight.shape
     wide = cols // 2
-    cubes, flip_y, flips = partners([lax.axis_size(name) for name in CHIP])
+    cubes, flip_x, flips = partners([lax.axis_size(name) for name in CHIP])
     here = ("c", "yl", "xl", "zl", "zh")
     spot = jnp.stack([lax.axis_index(name) for name in here])
     spot = spot.astype(jnp.int32)
@@ -266,7 +264,7 @@
     summed = jnp.sum(term, axis=0, dtype=jnp.float32)
 
     near, away = project(packed, mine, other, spot)
-    away = lax.ppermute(away, CHIP, flip_y)
+    away = lax.ppermute(away, CHIP, flip_x)
     near, _ = lax.optimization_barrier((near, summed))
     near = near + away
     output = near[0]

time: 113 us -> 107 us (0.947)
  the two profiles are of different devices: /device:TPU:57 before, /device:TPU:1 now
where the time goes in v17:
time: 107 us
  starting transfers between devices  63.9 us (60%)
  waiting for transfers between devices  27 us (25%)
  Pallas kernels  11.9 us (11%)
  other arithmetic  2.34 us (2%)
    all_to_all x1, starting transfers between devices, local(): packed = lax.all_to_all(packed, CHIP, 0, 0, axis_index_groups=cubes)  16.1 us
    ppermute x4, starting transfers between devices, local(): gathered.append(lax.ppermute(weight, ('c', 'xh', 'zh'), shift))  15.3 us
    ppermute x4, waiting for transfers between devices, local(): gathered.append(lax.ppermute(weight, ('c', 'xh', 'zh'), shift))  13.6 us
    ppermute x3, starting transfers between devices, local(): output = output + lax.ppermute(near[n + 1], CHIP, flip)  11.9 us
    ppermute x1, starting transfers between devices, local(): away = lax.ppermute(away, CHIP, flip_x)  5.64 us
    all_to_all x1, starting transfers between devices, local(): half = jnp.sum(lax.all_to_all(lines, 'yh', 0, 0), axis=0)  4.99 us
    all_to_all x1, waiting for transfers between devices, local(): packed = lax.all_to_all(packed, CHIP, 0, 0, axis_index_groups=cubes)  4.47 us
    pallas_call x1, Pallas kernels, pack(): pl.pallas_call(body, in_specs=[pl.BlockSpec(memory_space=pl.ANY)] * 2, ou...  3.89 us
  transfers between devices with their start and end apart: 14, of which 9 were waited for; matrix products, arithmetic and copies ran while one was open for 2% of the time, Pallas kernels for 4%

profile of v17, /device:TPU:1, one launch (start us, length us, event | category | flops | bytes accessed | tf_op | source)
XLA Modules:
  0.0 106.8 jit_solution(3474918157578074069)
XLA Ops:
  0.6 3.9 %shard_map.50 = bf16[8,128,1792]{2,1,0:T(8,128)(2,1)} custom-call(bf16[128,12288]{1,0:T(8,128)(2,1)} %t_ref.1, bf16[128,256]{1,0:T(8,128)(2,1)} %g_ref.1), custom_call_target="tpu_custom_call" | custom-call | tf_op jit(solution)/shard_map/pallas_call | solution.py:60
  4.5 16.1 %all-to-all-start = ((bf16[8,128,1792]{2,1,0:T(8,128)(2,1)}), bf16[8,128,1792]{2,1,0:T(8,128)(2,1)}, u32[]{:S(2)}, u32[]{:S(2)}) async-start(bf16[8,128,1792]{2,1,0:T(8,128)(2,1)} %shard_map.50), calls=%async_computation | async-start | bytes 7340032 | tf_op jit(solution)/shard_map/all_to_all | solution.py:242
  20.7 1.9 %collective-permute-start = (bf16[192,256]{1,0:T(8,128)(2,1)S(1)}, bf16[192,256]{1,0:T(8,128)(2,1)S(1)}, u32[]{:S(2)}, u32[]{:S(2)}) collective-permute-start(bf16[192,256]{1,0:T(8,128)(2,1)S(1)} %copy-done), channel_id=1, source_target_pairs={{0,0},{2,2},{4,4},{6,6},{16,80},{18,82},{20,84},{22,86},{64,16},{6... | collective-permute-start | bytes 294920 | tf_op jit(solution)/shard_map/ppermute | solution.py:256
  22.6 1.9 %collective-permute-start.1 = (bf16[192,256]{1,0:T(8,128)(2,1)S(1)}, bf16[192,256]{1,0:T(8,128)(2,1)S(1)}, u32[]{:S(2)}, u32[]{:S(2)}) collective-permute-start(bf16[192,256]{1,0:T(8,128)(2,1)S(1)} %copy-done), channel_id=1, source_target_pairs={{0,2},{2,4},{4,6},{6,0},{16,82},{18,84},{20,86},{22,80},{64,18},{6... | collective-permute-start | bytes 294920 | tf_op jit(solution)/shard_map/ppermute | solution.py:256
  24.5 7.2 %collective-permute-start.2 = (bf16[192,256]{1,0:T(8,128)(2,1)S(1)}, bf16[192,256]{1,0:T(8,128)(2,1)S(1)}, u32[]{:S(2)}, u32[]{:S(2)}) collective-permute-start(bf16[192,256]{1,0:T(8,128)(2,1)S(1)} %copy-done), channel_id=1, source_target_pairs={{0,4},{2,6},{4,0},{6,2},{16,84},{18,86},{20,80},{22,82},{64,20},{6... | collective-permute-start | bytes 294920 | tf_op jit(solution)/shard_map/ppermute | solution.py:256
  31.7 4.3 %collective-permute-start.3 = (bf16[192,256]{1,0:T(8,128)(2,1)S(1)}, bf16[192,256]{1,0:T(8,128)(2,1)S(1)}, u32[]{:S(2)}, u32[]{:S(2)}) collective-permute-start(bf16[192,256]{1,0:T(8,128)(2,1)S(1)} %copy-done), channel_id=1, source_target_pairs={{0,6},{2,0},{4,2},{6,4},{16,86},{18,80},{20,82},{22,84},{64,22},{6... | collective-permute-start | bytes 294920 | tf_op jit(solution)/shard_map/ppermute | solution.py:256
  36.1 2.9 %collective-permute-done.refs_0_ = bf16[192,256]{1,0:T(8,128)(2,1)S(1)} collective-permute-done((bf16[192,256]{1,0:T(8,128)(2,1)S(1)}, bf16[192,256]{1,0:T(8,128)(2,1)S(1)}, u32[]{:S(2)}, u32[]{:S(2)}) %collective-permute-start) | collective-permute-done | bytes 98336 | tf_op jit(solution)/shard_map/ppermute | solution.py:256
  39.0 6.4 %collective-permute-done.2.refs_2_ = bf16[192,256]{1,0:T(8,128)(2,1)S(1)} collective-permute-done((bf16[192,256]{1,0:T(8,128)(2,1)S(1)}, bf16[192,256]{1,0:T(8,128)(2,1)S(1)}, u32[]{:S(2)}, u32[]{:S(2)}) %collective-permute-start.2) | collective-permute-done | bytes 98336 | tf_op jit(solution)/shard_map/ppermute | solution.py:256
  45.4 4.2 %collective-permute-done.3.refs_3_ = bf16[192,256]{1,0:T(8,128)(2,1)S(1)} collective-permute-done((bf16[192,256]{1,0:T(8,128)(2,1)S(1)}, bf16[192,256]{1,0:T(8,128)(2,1)S(1)}, u32[]{:S(2)}, u32[]{:S(2)}) %collective-permute-start.3) | collective-permute-done | bytes 98336 | tf_op jit(solution)/shard_map/ppermute | solution.py:256
  49.7 4.5 %all-to-all-done.p_ref = bf16[8,128,1792]{2,1,0:T(8,128)(2,1)} async-done(((bf16[8,128,1792]{2,1,0:T(8,128)(2,1)}), bf16[8,128,1792]{2,1,0:T(8,128)(2,1)}, u32[]{:S(2)}, u32[]{:S(2)}) %all-to-all-start) | async-done | bytes 3670048 | tf_op jit(solution)/shard_map/all_to_all | solution.py:242
  54.1 3.8 %shard_map.52 = (f32[1536,128]{1,0:T(8,128)S(1)}, f32[1536,128]{1,0:T(8,128)S(1)}) custom-call(s32[5]{0:T(128)S(1)} %stack.23.spot_ref, bf16[8,128,1792]{2,1,0:T(8,128)(2,1)} %all-to-all-done.p_ref), custom_call_target="tpu_custom_call" | custom-call | tf_op jit(solution)/shard_map/pallas_call | solution.py:111
  58.0 1.9 %collective-permute-start.5 = (f32[1536,128]{1,0:T(8,128)S(1)}, f32[1536,128]{1,0:T(8,128)S(1)}, u32[]{:S(2)}, u32[]{:S(2)}) collective-permute-start(f32[1536,128]{1,0:T(8,128)S(1)} %get-tuple-element.18), channel_id=1, source_target_pairs={{0,64},{64,0},{1,65},{65,1},{2,66},{66,2},{3,67},{67,3},{4,68},{68... | collective-permute-start | bytes 2359304 | tf_op jit(solution)/shard_map/ppermute | solution.py:260
  59.9 2.3 %collective-permute-done.5 = f32[1536,128]{1,0:T(8,128)S(1)} collective-permute-done((f32[1536,128]{1,0:T(8,128)S(1)}, f32[1536,128]{1,0:T(8,128)S(1)}, u32[]{:S(2)}, u32[]{:S(2)}) %collective-permute-start.5) | collective-permute-done | bytes 786464 | tf_op jit(solution)/shard_map/ppermute | solution.py:260
  63.0 3.5 %all-to-all-start.1 = ((bf16[8,192,128]{2,1,0:T(8,128)(2,1)}), bf16[8,192,128]{2,1,0:T(8,128)(2,1)S(1)}, u32[]{:S(2)}, u32[]{:S(2)}) async-start(bf16[8,192,128]{2,1,0:T(8,128)(2,1)} %bitcast.5), calls=%async_computation.1 | async-start | bytes 786432 | tf_op jit(solution)/shard_map/all_to_all | solution.py:263
  67.1 2.6 %collective-permute-start.4 = (bf16[4,192,256]{2,1,0:T(8,128)(2,1)S(1)}, bf16[4,192,256]{2,1,0:T(8,128)(2,1)S(1)}, u32[]{:S(2)}, u32[]{:S(2)}) collective-permute-start(bf16[4,192,256]{2,1,0:T(8,128)(2,1)S(1)} %shard_map.51.m_ref), channel_id=1, source_target_pairs={{0,64},{64,0},{1,65},{65,1},{2,66},{66,2},{3,67},{67,3},{4,68},{68... | collective-permute-start | bytes 1179656 | tf_op jit(solution)/shard_map/ppermute | solution.py:262
  71.0 3.6 %shard_map.53 = (f32[4,128,256]{2,1,0:T(8,128)S(1)}, f32[4,128,256]{2,1,0:T(8,128)S(1)}) custom-call(s32[5]{0:T(128)S(1)} %stack.23.spot_ref, bf16[8,128,1792]{2,1,0:T(8,128)(2,1)} %all-to-all-done.p_ref, bf16[4,192,256]{2,1,0:T(8,128)(2,1)S(1)} %shard_map.51.m_ref, bf16[4,192,256]{2,1,0:T(8,128)(2,1)S(1)} %collective-permute-done.4.r_ref), custom_call_target="tpu_custom_call" | custom-call | tf_op jit(solution)/shard_map/pallas_call | solution.py:178
  74.6 5.6 %collective-permute-start.6 = (f32[4,128,256]{2,1,0:T(8,128)S(1)}, f32[4,128,256]{2,1,0:T(8,128)S(1)}, u32[]{:S(2)}, u32[]{:S(2)}) collective-permute-start(f32[4,128,256]{2,1,0:T(8,128)S(1)} %get-tuple-element.23), channel_id=1, source_target_pairs={{0,8},{1,9},{2,10},{3,11},{4,12},{5,13},{6,14},{7,15},{8,0},{9,1},... | collective-permute-start | bytes 1572872 | tf_op jit(solution)/shard_map/ppermute | solution.py:267
  81.1 5.0 %all-to-all-start.2 = ((f32[4,192,128]{2,1,0:T(8,128)}), f32[4,192,128]{2,1,0:T(8,128)S(1)}, u32[]{:S(2)}, u32[]{:S(2)}) async-start(f32[4,192,128]{2,1,0:T(8,128)} %broadcast_in_dim.2), calls=%async_computation.2 | async-start | bytes 786432 | tf_op jit(solution)/shard_map/all_to_all | solution.py:275
  86.1 1.5 %collective-permute-done.6 = f32[4,128,256]{2,1,0:T(8,128)S(1)} collective-permute-done((f32[4,128,256]{2,1,0:T(8,128)S(1)}, f32[4,128,256]{2,1,0:T(8,128)S(1)}, u32[]{:S(2)}, u32[]{:S(2)}) %collective-permute-start.6) | collective-permute-done | bytes 524320 | tf_op jit(solution)/shard_map/ppermute | solution.py:267
  87.8 4.1 %collective-permute-start.7 = (f32[128,256]{1,0:T(8,128)S(1)}, f32[128,256]{1,0:T(8,128)S(1)}, u32[]{:S(2)}, u32[]{:S(2)}) collective-permute-start(f32[128,256]{1,0:T(8,128)S(1)} %get-tuple-element.24), channel_id=1, source_target_pairs={{0,1},{1,0},{2,3},{3,2},{4,5},{5,4},{6,7},{7,6},{8,9},{9,8},{10,11... | collective-permute-start | bytes 393224 | tf_op jit(solution)/shard_map/ppermute | solution.py:272
  91.9 4.5 %collective-permute-start.8 = (f32[128,256]{1,0:T(8,128)S(1)}, f32[128,256]{1,0:T(8,128)S(1)}, u32[]{:S(2)}, u32[]{:S(2)}) collective-permute-start(f32[128,256]{1,0:T(8,128)S(1)} %get-tuple-element.26), channel_id=1, source_target_pairs={{0,32},{1,33},{2,34},{3,35},{4,36},{5,37},{6,38},{7,39},{8,40},{9,... | collective-permute-start | bytes 393224 | tf_op jit(solution)/shard_map/ppermute | solution.py:272
  96.4 3.3 %collective-permute-start.9 = (f32[128,256]{1,0:T(8,128)S(1)}, f32[128,256]{1,0:T(8,128)S(1)}, u32[]{:S(2)}, u32[]{:S(2)}) collective-permute-start(f32[128,256]{1,0:T(8,128)S(1)} %get-tuple-element.25), channel_id=1, source_target_pairs={{0,33},{1,32},{2,35},{3,34},{4,37},{5,36},{6,39},{7,38},{8,41},{9,... | collective-permute-start | bytes 393224 | tf_op jit(solution)/shard_map/ppermute | solution.py:272
  99.7 1.9 %collective-permute-start.10 = (f32[192,128]{1,0:T(8,128)S(1)}, f32[192,128]{1,0:T(8,128)S(1)}, u32[]{:S(2)}, u32[]{:S(2)}) collective-permute-start(f32[192,128]{1,0:T(8,128)S(1)} %reduce_sum.19), channel_id=1, source_target_pairs={{0,64},{64,0},{1,65},{65,1},{2,66},{66,2},{3,67},{67,3},{4,68},{68... | collective-permute-start | bytes 294920 | tf_op jit(solution)/shard_map/ppermute | solution.py:276
  101.6 3.8 %collective-permute-done.9 = f32[128,256]{1,0:T(8,128)S(1)} collective-permute-done((f32[128,256]{1,0:T(8,128)S(1)}, f32[128,256]{1,0:T(8,128)S(1)}, u32[]{:S(2)}, u32[]{:S(2)}) %collective-permute-start.9) | collective-permute-done | bytes 131104 | tf_op jit(solution)/shard_map/ppermute | solution.py:272
  (20 shorter events, 5.2 us)
Async XLA Ops:
  4.5 16.1 %copy-start = (bf16[192,256]{1,0:T(8,128)(2,1)S(1)}, bf16[192,256]{1,0:T(8,128)(2,1)}, u32[]{:S(2)}) copy-start(bf16[192,256]{1,0:T(8,128)(2,1)} %param.4) | copy-start | bytes 294916
  4.5 49.6 %all-to-all-start = ((bf16[8,128,1792]{2,1,0:T(8,128)(2,1)}), bf16[8,128,1792]{2,1,0:T(8,128)(2,1)}, u32[]{:S(2)}, u32[]{:S(2)}) async-start(bf16[8,128,1792]{2,1,0:T(8,128)(2,1)} %shard_map.50), calls=%async_computation | async-start | bytes 7340032 | tf_op jit(solution)/shard_map/all_to_all | solution.py:242
  20.7 18.4 %collective-permute-start = (bf16[192,256]{1,0:T(8,128)(2,1)S(1)}, bf16[192,256]{1,0:T(8,128)(2,1)S(1)}, u32[]{:S(2)}, u32[]{:S(2)}) collective-permute-start(bf16[192,256]{1,0:T(8,128)(2,1)S(1)} %copy-done), channel_id=1, source_target_pairs={{0,0},{2,2},{4,4},{6,6},{16,80},{18,82},{20,84},{22,86},{64,16},{6... | collective-permute-start | bytes 294920 | tf_op jit(solution)/shard_map/ppermute | solution.py:256
  22.6 16.4 %collective-permute-start.1 = (bf16[192,256]{1,0:T(8,128)(2,1)S(1)}, bf16[192,256]{1,0:T(8,128)(2,1)S(1)}, u32[]{:S(2)}, u32[]{:S(2)}) collective-permute-start(bf16[192,256]{1,0:T(8,128)(2,1)S(1)} %copy-done), channel_id=1, source_target_pairs={{0,2},{2,4},{4,6},{6,0},{16,82},{18,84},{20,86},{22,80},{64,18},{6... | collective-permute-start | bytes 294920 | tf_op jit(solution)/shard_map/ppermute | solution.py:256
  24.5 20.9 %collective-permute-start.2 = (bf16[192,256]{1,0:T(8,128)(2,1)S(1)}, bf16[192,256]{1,0:T(8,128)(2,1)S(1)}, u32[]{:S(2)}, u32[]{:S(2)}) collective-permute-start(bf16[192,256]{1,0:T(8,128)(2,1)S(1)} %copy-done), channel_id=1, source_target_pairs={{0,4},{2,6},{4,0},{6,2},{16,84},{18,86},{20,80},{22,82},{64,20},{6... | collective-permute-start | bytes 294920 | tf_op jit(solution)/shard_map/ppermute | solution.py:256
  31.7 18.0 %collective-permute-start.3 = (bf16[192,256]{1,0:T(8,128)(2,1)S(1)}, bf16[192,256]{1,0:T(8,128)(2,1)S(1)}, u32[]{:S(2)}, u32[]{:S(2)}) collective-permute-start(bf16[192,256]{1,0:T(8,128)(2,1)S(1)} %copy-done), channel_id=1, source_target_pairs={{0,6},{2,0},{4,2},{6,4},{16,86},{18,80},{20,82},{22,84},{64,22},{6... | collective-permute-start | bytes 294920 | tf_op jit(solution)/shard_map/ppermute | solution.py:256
  58.0 4.2 %collective-permute-start.5 = (f32[1536,128]{1,0:T(8,128)S(1)}, f32[1536,128]{1,0:T(8,128)S(1)}, u32[]{:S(2)}, u32[]{:S(2)}) collective-permute-start(f32[1536,128]{1,0:T(8,128)S(1)} %get-tuple-element.18), channel_id=1, source_target_pairs={{0,64},{64,0},{1,65},{65,1},{2,66},{66,2},{3,67},{67,3},{4,68},{68... | collective-permute-start | bytes 2359304 | tf_op jit(solution)/shard_map/ppermute | solution.py:260
  63.0 17.3 %all-to-all-start.1 = ((bf16[8,192,128]{2,1,0:T(8,128)(2,1)}), bf16[8,192,128]{2,1,0:T(8,128)(2,1)S(1)}, u32[]{:S(2)}, u32[]{:S(2)}) async-start(bf16[8,192,128]{2,1,0:T(8,128)(2,1)} %bitcast.5), calls=%async_computation.1 | async-start | bytes 786432 | tf_op jit(solution)/shard_map/all_to_all | solution.py:263
  67.1 3.9 %collective-permute-start.4 = (bf16[4,192,256]{2,1,0:T(8,128)(2,1)S(1)}, bf16[4,192,256]{2,1,0:T(8,128)(2,1)S(1)}, u32[]{:S(2)}, u32[]{:S(2)}) collective-permute-start(bf16[4,192,256]{2,1,0:T(8,128)(2,1)S(1)} %shard_map.51.m_ref), channel_id=1, source_target_pairs={{0,64},{64,0},{1,65},{65,1},{2,66},{66,2},{3,67},{67,3},{4,68},{68... | collective-permute-start | bytes 1179656 | tf_op jit(solution)/shard_map/ppermute | solution.py:262
  74.6 13.1 %collective-permute-start.6 = (f32[4,128,256]{2,1,0:T(8,128)S(1)}, f32[4,128,256]{2,1,0:T(8,128)S(1)}, u32[]{:S(2)}, u32[]{:S(2)}) collective-permute-start(f32[4,128,256]{2,1,0:T(8,128)S(1)} %get-tuple-element.23), channel_id=1, source_target_pairs={{0,8},{1,9},{2,10},{3,11},{4,12},{5,13},{6,14},{7,15},{8,0},{9,1},... | collective-permute-start | bytes 1572872 | tf_op jit(solution)/shard_map/ppermute | solution.py:267
  81.1 18.5 %all-to-all-start.2 = ((f32[4,192,128]{2,1,0:T(8,128)}), f32[4,192,128]{2,1,0:T(8,128)S(1)}, u32[]{:S(2)}, u32[]{:S(2)}) async-start(f32[4,192,128]{2,1,0:T(8,128)} %broadcast_in_dim.2), calls=%async_computation.2 | async-start | bytes 786432 | tf_op jit(solution)/shard_map/all_to_all | solution.py:275
  87.8 13.9 %collective-permute-start.7 = (f32[128,256]{1,0:T(8,128)S(1)}, f32[128,256]{1,0:T(8,128)S(1)}, u32[]{:S(2)}, u32[]{:S(2)}) collective-permute-start(f32[128,256]{1,0:T(8,128)S(1)} %get-tuple-element.24), channel_id=1, source_target_pairs={{0,1},{1,0},{2,3},{3,2},{4,5},{5,4},{6,7},{7,6},{8,9},{9,8},{10,11... | collective-permute-start | bytes 393224 | tf_op jit(solution)/shard_map/ppermute | solution.py:272
  91.9 9.7 %collective-permute-start.8 = (f32[128,256]{1,0:T(8,128)S(1)}, f32[128,256]{1,0:T(8,128)S(1)}, u32[]{:S(2)}, u32[]{:S(2)}) collective-permute-start(f32[128,256]{1,0:T(8,128)S(1)} %get-tuple-element.26), channel_id=1, source_target_pairs={{0,32},{1,33},{2,34},{3,35},{4,36},{5,37},{6,38},{7,39},{8,40},{9,... | collective-permute-start | bytes 393224 | tf_op jit(solution)/shard_map/ppermute | solution.py:272
  96.4 9.0 %collective-permute-start.9 = (f32[128,256]{1,0:T(8,128)S(1)}, f32[128,256]{1,0:T(8,128)S(1)}, u32[]{:S(2)}, u32[]{:S(2)}) collective-permute-start(f32[128,256]{1,0:T(8,128)S(1)} %get-tuple-element.25), channel_id=1, source_target_pairs={{0,33},{1,32},{2,35},{3,34},{4,37},{5,36},{6,39},{7,38},{8,41},{9,... | collective-permute-start | bytes 393224 | tf_op jit(solution)/shard_map/ppermute | solution.py:272
  99.7 6.4 %collective-permute-start.10 = (f32[192,128]{1,0:T(8,128)S(1)}, f32[192,128]{1,0:T(8,128)S(1)}, u32[]{:S(2)}, u32[]{:S(2)}) collective-permute-start(f32[192,128]{1,0:T(8,128)S(1)} %reduce_sum.19), channel_id=1, source_target_pairs={{0,64},{64,0},{1,65},{65,1},{2,66},{66,2},{3,67},{67,3},{4,68},{68... | collective-permute-start | bytes 294920 | tf_op jit(solution)/shard_map/ppermute | solution.py:276

commit v18 on v17

--- a/solution.py
+++ b/solution.py
@@ -260,6 +260,7 @@
     term = (keep + lax.ppermute(send, "c", SWAP)).astype(jnp.bfloat16)
     mine, _ = lax.optimization_barrier((join(gathered), send))
     other = lax.ppermute(mine, "c", SWAP)
+    term, other = lax.optimization_barrier((term, other))
     term = lax.all_to_all(term.reshape(-1, shard, wide), ("xh", "zh"), 0, 0)
     summed = jnp.sum(term, axis=0, dtype=jnp.float32)
 

time: 107 us -> 108 us (level)
    all_to_all x1, waiting for transfers between devices: 0.06 us -> 5.52 us  [local(): term = lax.all_to_all(term.reshape(-1, shard, wide), ('xh', 'zh'), 0, 0)]
    ppermute x1, waiting for transfers between devices: 2.25 us -> 0.01 us  [local(): term = (keep + lax.ppermute(send, 'c', SWAP)).astype(jnp.bfloat16)]
    ppermute x1, waiting for transfers between devices: 1.53 us -> 0.01 us  [local(): away = lax.ppermute(away, CHIP, flip_x)]
    ppermute x3, starting transfers between devices: 11.9 us -> 13.3 us  [local(): output = output + lax.ppermute(near[n + 1], CHIP, flip)]
  transfers between devices with their start and end apart: 14 -> 14, of which waited for: 9 -> 7; matrix products, arithmetic and copies ran while one was open for 2% -> 2% of each run, Pallas kernels for 4% -> 4%
where the time goes in v18:
time: 108 us; the launch traced here: 107 us
  starting transfers between devices  64.4 us (60%)
  waiting for transfers between devices  26.8 us (25%)
  Pallas kernels  11.9 us (11%)
  other arithmetic  2.34 us (2%)
    all_to_all x1, starting transfers between devices, local(): packed = lax.all_to_all(packed, CHIP, 0, 0, axis_index_groups=cubes)  16.1 us
    ppermute x4, starting transfers between devices, local(): gathered.append(lax.ppermute(weight, ('c', 'xh', 'zh'), shift))  15.3 us
    ppermute x4, waiting for transfers between devices, local(): gathered.append(lax.ppermute(weight, ('c', 'xh', 'zh'), shift))  13.6 us
    ppermute x3, starting transfers between devices, local(): output = output + lax.ppermute(near[n + 1], CHIP, flip)  13.3 us
    all_to_all x1, waiting for transfers between devices, local(): term = lax.all_to_all(term.reshape(-1, shard, wide), ('xh', 'zh'), 0, 0)  5.52 us
    ppermute x1, starting transfers between devices, local(): away = lax.ppermute(away, CHIP, flip_x)  5.36 us
    all_to_all x1, waiting for transfers between devices, local(): packed = lax.all_to_all(packed, CHIP, 0, 0, axis_index_groups=cubes)  4.47 us
    all_to_all x1, starting transfers between devices, local(): half = jnp.sum(lax.all_to_all(lines, 'yh', 0, 0), axis=0)  4.27 us
  transfers between devices with their start and end apart: 14, of which 7 were waited for; matrix products, arithmetic and copies ran while one was open for 2% of the time, Pallas kernels for 4%

profile of v18, /device:TPU:1, one launch (start us, length us, event | category | flops | bytes accessed | tf_op | source)
XLA Modules:
  0.0 107.2 jit_solution(5653364939064961086)
XLA Ops:
  0.6 3.9 %shard_map.50 = bf16[8,128,1792]{2,1,0:T(8,128)(2,1)} custom-call(bf16[128,12288]{1,0:T(8,128)(2,1)} %t_ref.1, bf16[128,256]{1,0:T(8,128)(2,1)} %g_ref.1), custom_call_target="tpu_custom_call" | custom-call | tf_op jit(solution)/shard_map/pallas_call | solution.py:60
  4.5 16.1 %all-to-all-start = ((bf16[8,128,1792]{2,1,0:T(8,128)(2,1)}), bf16[8,128,1792]{2,1,0:T(8,128)(2,1)}, u32[]{:S(2)}, u32[]{:S(2)}) async-start(bf16[8,128,1792]{2,1,0:T(8,128)(2,1)} %shard_map.50), calls=%async_computation | async-start | bytes 7340032 | tf_op jit(solution)/shard_map/all_to_all | solution.py:242
  20.7 1.9 %collective-permute-start = (bf16[192,256]{1,0:T(8,128)(2,1)S(1)}, bf16[192,256]{1,0:T(8,128)(2,1)S(1)}, u32[]{:S(2)}, u32[]{:S(2)}) collective-permute-start(bf16[192,256]{1,0:T(8,128)(2,1)S(1)} %copy-done), channel_id=1, source_target_pairs={{0,0},{2,2},{4,4},{6,6},{16,80},{18,82},{20,84},{22,86},{64,16},{6... | collective-permute-start | bytes 294920 | tf_op jit(solution)/shard_map/ppermute | solution.py:256
  22.6 1.9 %collective-permute-start.1 = (bf16[192,256]{1,0:T(8,128)(2,1)S(1)}, bf16[192,256]{1,0:T(8,128)(2,1)S(1)}, u32[]{:S(2)}, u32[]{:S(2)}) collective-permute-start(bf16[192,256]{1,0:T(8,128)(2,1)S(1)} %copy-done), channel_id=1, source_target_pairs={{0,2},{2,4},{4,6},{6,0},{16,82},{18,84},{20,86},{22,80},{64,18},{6... | collective-permute-start | bytes 294920 | tf_op jit(solution)/shard_map/ppermute | solution.py:256
  24.5 7.2 %collective-permute-start.2 = (bf16[192,256]{1,0:T(8,128)(2,1)S(1)}, bf16[192,256]{1,0:T(8,128)(2,1)S(1)}, u32[]{:S(2)}, u32[]{:S(2)}) collective-permute-start(bf16[192,256]{1,0:T(8,128)(2,1)S(1)} %copy-done), channel_id=1, source_target_pairs={{0,4},{2,6},{4,0},{6,2},{16,84},{18,86},{20,80},{22,82},{64,20},{6... | collective-permute-start | bytes 294920 | tf_op jit(solution)/shard_map/ppermute | solution.py:256
  31.7 4.3 %collective-permute-start.3 = (bf16[192,256]{1,0:T(8,128)(2,1)S(1)}, bf16[192,256]{1,0:T(8,128)(2,1)S(1)}, u32[]{:S(2)}, u32[]{:S(2)}) collective-permute-start(bf16[192,256]{1,0:T(8,128)(2,1)S(1)} %copy-done), channel_id=1, source_target_pairs={{0,6},{2,0},{4,2},{6,4},{16,86},{18,80},{20,82},{22,84},{64,22},{6... | collective-permute-start | bytes 294920 | tf_op jit(solution)/shard_map/ppermute | solution.py:256
  36.1 2.9 %collective-permute-done.refs_0_ = bf16[192,256]{1,0:T(8,128)(2,1)S(1)} collective-permute-done((bf16[192,256]{1,0:T(8,128)(2,1)S(1)}, bf16[192,256]{1,0:T(8,128)(2,1)S(1)}, u32[]{:S(2)}, u32[]{:S(2)}) %collective-permute-start) | collective-permute-done | bytes 98336 | tf_op jit(solution)/shard_map/ppermute | solution.py:256
  39.0 6.4 %collective-permute-done.2.refs_2_ = bf16[192,256]{1,0:T(8,128)(2,1)S(1)} collective-permute-done((bf16[192,256]{1,0:T(8,128)(2,1)S(1)}, bf16[192,256]{1,0:T(8,128)(2,1)S(1)}, u32[]{:S(2)}, u32[]{:S(2)}) %collective-permute-start.2) | collective-permute-done | bytes 98336 | tf_op jit(solution)/shard_map/ppermute | solution.py:256
  45.4 4.2 %collective-permute-done.3.refs_3_ = bf16[192,256]{1,0:T(8,128)(2,1)S(1)} collective-permute-done((bf16[192,256]{1,0:T(8,128)(2,1)S(1)}, bf16[192,256]{1,0:T(8,128)(2,1)S(1)}, u32[]{:S(2)}, u32[]{:S(2)}) %collective-permute-start.3) | collective-permute-done | bytes 98336 | tf_op jit(solution)/shard_map/ppermute | solution.py:256
  49.7 4.5 %all-to-all-done.p_ref = bf16[8,128,1792]{2,1,0:T(8,128)(2,1)} async-done(((bf16[8,128,1792]{2,1,0:T(8,128)(2,1)}), bf16[8,128,1792]{2,1,0:T(8,128)(2,1)}, u32[]{:S(2)}, u32[]{:S(2)}) %all-to-all-start) | async-done | bytes 3670048 | tf_op jit(solution)/shard_map/all_to_all | solution.py:242
  54.1 3.8 %shard_map.52 = (f32[1536,128]{1,0:T(8,128)S(1)}, f32[1536,128]{1,0:T(8,128)S(1)}) custom-call(s32[5]{0:T(128)S(1)} %stack.23.spot_ref, bf16[8,128,1792]{2,1,0:T(8,128)(2,1)} %all-to-all-done.p_ref), custom_call_target="tpu_custom_call" | custom-call | tf_op jit(solution)/shard_map/pallas_call | solution.py:111
  58.0 1.9 %collective-permute-start.4 = (f32[1536,128]{1,0:T(8,128)S(1)}, f32[1536,128]{1,0:T(8,128)S(1)}, u32[]{:S(2)}, u32[]{:S(2)}) collective-permute-start(f32[1536,128]{1,0:T(8,128)S(1)} %get-tuple-element.20), channel_id=1, source_target_pairs={{0,64},{64,0},{1,65},{65,1},{2,66},{66,2},{3,67},{67,3},{4,68},{68... | collective-permute-start | bytes 2359304 | tf_op jit(solution)/shard_map/ppermute | solution.py:260
  60.5 2.4 %collective-permute-start.5 = (bf16[4,192,256]{2,1,0:T(8,128)(2,1)S(1)}, bf16[4,192,256]{2,1,0:T(8,128)(2,1)S(1)}, u32[]{:S(2)}, u32[]{:S(2)}) collective-permute-start(bf16[4,192,256]{2,1,0:T(8,128)(2,1)S(1)} %shard_map.51.m_ref), channel_id=1, source_target_pairs={{0,64},{64,0},{1,65},{65,1},{2,66},{66,2},{3,67},{67,3},{4,68},{68... | collective-permute-start | bytes 1179656 | tf_op jit(solution)/shard_map/ppermute | solution.py:262
  62.9 0.8 add_convert_fusion
  64.2 3.8 %all-to-all-start.1 = ((bf16[8,192,128]{2,1,0:T(8,128)(2,1)}), bf16[8,192,128]{2,1,0:T(8,128)(2,1)S(1)}, u32[]{:S(2)}, u32[]{:S(2)}) async-start(bf16[8,192,128]{2,1,0:T(8,128)(2,1)} %bitcast.5), calls=%async_computation.1 | async-start | bytes 786432 | tf_op jit(solution)/shard_map/all_to_all | solution.py:264
  68.0 3.6 %shard_map.53 = (f32[4,128,256]{2,1,0:T(8,128)S(1)}, f32[4,128,256]{2,1,0:T(8,128)S(1)}) custom-call(s32[5]{0:T(128)S(1)} %stack.23.spot_ref, bf16[8,128,1792]{2,1,0:T(8,128)(2,1)} %all-to-all-done.p_ref, bf16[4,192,256]{2,1,0:T(8,128)(2,1)S(1)} %shard_map.51.m_ref, bf16[4,192,256]{2,1,0:T(8,128)(2,1)S(1)} %collective-permute-done.5.r_ref), custom_call_target="tpu_custom_call" | custom-call | tf_op jit(solution)/shard_map/pallas_call | solution.py:178
  71.6 5.4 %collective-permute-start.6 = (f32[4,128,256]{2,1,0:T(8,128)S(1)}, f32[4,128,256]{2,1,0:T(8,128)S(1)}, u32[]{:S(2)}, u32[]{:S(2)}) collective-permute-start(f32[4,128,256]{2,1,0:T(8,128)S(1)} %get-tuple-element.27), channel_id=1, source_target_pairs={{0,8},{1,9},{2,10},{3,11},{4,12},{5,13},{6,14},{7,15},{8,0},{9,1},... | collective-permute-start | bytes 1572872 | tf_op jit(solution)/shard_map/ppermute | solution.py:268
  77.0 5.5 %all-to-all-done.1 = bf16[8,192,128]{2,1,0:T(8,128)(2,1)S(1)} async-done(((bf16[8,192,128]{2,1,0:T(8,128)(2,1)}), bf16[8,192,128]{2,1,0:T(8,128)(2,1)S(1)}, u32[]{:S(2)}, u32[]{:S(2)}) %all-to-all-start.1) | async-done | bytes 393248 | tf_op jit(solution)/shard_map/all_to_all | solution.py:264
  83.3 4.3 %all-to-all-start.2 = ((f32[4,192,128]{2,1,0:T(8,128)}), f32[4,192,128]{2,1,0:T(8,128)S(1)}, u32[]{:S(2)}, u32[]{:S(2)}) async-start(f32[4,192,128]{2,1,0:T(8,128)} %broadcast_in_dim.2), calls=%async_computation.2 | async-start | bytes 786432 | tf_op jit(solution)/shard_map/all_to_all | solution.py:276
  87.7 2.3 %collective-permute-start.7 = (f32[128,256]{1,0:T(8,128)S(1)}, f32[128,256]{1,0:T(8,128)S(1)}, u32[]{:S(2)}, u32[]{:S(2)}) collective-permute-start(f32[128,256]{1,0:T(8,128)S(1)} %get-tuple-element.28), channel_id=1, source_target_pairs={{0,1},{1,0},{2,3},{3,2},{4,5},{5,4},{6,7},{7,6},{8,9},{9,8},{10,11... | collective-permute-start | bytes 393224 | tf_op jit(solution)/shard_map/ppermute | solution.py:273
  90.1 6.7 %collective-permute-start.8 = (f32[128,256]{1,0:T(8,128)S(1)}, f32[128,256]{1,0:T(8,128)S(1)}, u32[]{:S(2)}, u32[]{:S(2)}) collective-permute-start(f32[128,256]{1,0:T(8,128)S(1)} %get-tuple-element.30), channel_id=1, source_target_pairs={{0,32},{1,33},{2,34},{3,35},{4,36},{5,37},{6,38},{7,39},{8,40},{9,... | collective-permute-start | bytes 393224 | tf_op jit(solution)/shard_map/ppermute | solution.py:273
  96.8 4.3 %collective-permute-start.9 = (f32[128,256]{1,0:T(8,128)S(1)}, f32[128,256]{1,0:T(8,128)S(1)}, u32[]{:S(2)}, u32[]{:S(2)}) collective-permute-start(f32[128,256]{1,0:T(8,128)S(1)} %get-tuple-element.29), channel_id=1, source_target_pairs={{0,33},{1,32},{2,35},{3,34},{4,37},{5,36},{6,39},{7,38},{8,41},{9,... | collective-permute-start | bytes 393224 | tf_op jit(solution)/shard_map/ppermute | solution.py:273
  101.1 1.9 %collective-permute-start.10 = (f32[192,128]{1,0:T(8,128)S(1)}, f32[192,128]{1,0:T(8,128)S(1)}, u32[]{:S(2)}, u32[]{:S(2)}) collective-permute-start(f32[192,128]{1,0:T(8,128)S(1)} %reduce_sum.19), channel_id=1, source_target_pairs={{0,64},{64,0},{1,65},{65,1},{2,66},{66,2},{3,67},{67,3},{4,68},{68... | collective-permute-start | bytes 294920 | tf_op jit(solution)/shard_map/ppermute | solution.py:277
  103.1 2.7 %collective-permute-done.9 = f32[128,256]{1,0:T(8,128)S(1)} collective-permute-done((f32[128,256]{1,0:T(8,128)S(1)}, f32[128,256]{1,0:T(8,128)S(1)}, u32[]{:S(2)}, u32[]{:S(2)}) %collective-permute-start.9) | collective-permute-done | bytes 131104 | tf_op jit(solution)/shard_map/ppermute | solution.py:273
  (20 shorter events, 3.5 us)
Async XLA Ops:
  4.5 16.1 %copy-start = (bf16[192,256]{1,0:T(8,128)(2,1)S(1)}, bf16[192,256]{1,0:T(8,128)(2,1)}, u32[]{:S(2)}) copy-start(bf16[192,256]{1,0:T(8,128)(2,1)} %param.4) | copy-start | bytes 294916
  4.5 49.6 %all-to-all-start = ((bf16[8,128,1792]{2,1,0:T(8,128)(2,1)}), bf16[8,128,1792]{2,1,0:T(8,128)(2,1)}, u32[]{:S(2)}, u32[]{:S(2)}) async-start(bf16[8,128,1792]{2,1,0:T(8,128)(2,1)} %shard_map.50), calls=%async_computation | async-start | bytes 7340032 | tf_op jit(solution)/shard_map/all_to_all | solution.py:242
  20.7 18.4 %collective-permute-start = (bf16[192,256]{1,0:T(8,128)(2,1)S(1)}, bf16[192,256]{1,0:T(8,128)(2,1)S(1)}, u32[]{:S(2)}, u32[]{:S(2)}) collective-permute-start(bf16[192,256]{1,0:T(8,128)(2,1)S(1)} %copy-done), channel_id=1, source_target_pairs={{0,0},{2,2},{4,4},{6,6},{16,80},{18,82},{20,84},{22,86},{64,16},{6... | collective-permute-start | bytes 294920 | tf_op jit(solution)/shard_map/ppermute | solution.py:256
  22.6 16.4 %collective-permute-start.1 = (bf16[192,256]{1,0:T(8,128)(2,1)S(1)}, bf16[192,256]{1,0:T(8,128)(2,1)S(1)}, u32[]{:S(2)}, u32[]{:S(2)}) collective-permute-start(bf16[192,256]{1,0:T(8,128)(2,1)S(1)} %copy-done), channel_id=1, source_target_pairs={{0,2},{2,4},{4,6},{6,0},{16,82},{18,84},{20,86},{22,80},{64,18},{6... | collective-permute-start | bytes 294920 | tf_op jit(solution)/shard_map/ppermute | solution.py:256
  24.5 20.9 %collective-permute-start.2 = (bf16[192,256]{1,0:T(8,128)(2,1)S(1)}, bf16[192,256]{1,0:T(8,128)(2,1)S(1)}, u32[]{:S(2)}, u32[]{:S(2)}) collective-permute-start(bf16[192,256]{1,0:T(8,128)(2,1)S(1)} %copy-done), channel_id=1, source_target_pairs={{0,4},{2,6},{4,0},{6,2},{16,84},{18,86},{20,80},{22,82},{64,20},{6... | collective-permute-start | bytes 294920 | tf_op jit(solution)/shard_map/ppermute | solution.py:256
  31.7 18.0 %collective-permute-start.3 = (bf16[192,256]{1,0:T(8,128)(2,1)S(1)}, bf16[192,256]{1,0:T(8,128)(2,1)S(1)}, u32[]{:S(2)}, u32[]{:S(2)}) collective-permute-start(bf16[192,256]{1,0:T(8,128)(2,1)S(1)} %copy-done), channel_id=1, source_target_pairs={{0,6},{2,0},{4,2},{6,4},{16,86},{18,80},{20,82},{22,84},{64,22},{6... | collective-permute-start | bytes 294920 | tf_op jit(solution)/shard_map/ppermute | solution.py:256
  58.0 4.9 %collective-permute-start.4 = (f32[1536,128]{1,0:T(8,128)S(1)}, f32[1536,128]{1,0:T(8,128)S(1)}, u32[]{:S(2)}, u32[]{:S(2)}) collective-permute-start(f32[1536,128]{1,0:T(8,128)S(1)} %get-tuple-element.20), channel_id=1, source_target_pairs={{0,64},{64,0},{1,65},{65,1},{2,66},{66,2},{3,67},{67,3},{4,68},{68... | collective-permute-start | bytes 2359304 | tf_op jit(solution)/shard_map/ppermute | solution.py:260
  60.5 3.7 %collective-permute-start.5 = (bf16[4,192,256]{2,1,0:T(8,128)(2,1)S(1)}, bf16[4,192,256]{2,1,0:T(8,128)(2,1)S(1)}, u32[]{:S(2)}, u32[]{:S(2)}) collective-permute-start(bf16[4,192,256]{2,1,0:T(8,128)(2,1)S(1)} %shard_map.51.m_ref), channel_id=1, source_target_pairs={{0,64},{64,0},{1,65},{65,1},{2,66},{66,2},{3,67},{67,3},{4,68},{68... | collective-permute-start | bytes 1179656 | tf_op jit(solution)/shard_map/ppermute | solution.py:262
  64.2 18.3 %all-to-all-start.1 = ((bf16[8,192,128]{2,1,0:T(8,128)(2,1)}), bf16[8,192,128]{2,1,0:T(8,128)(2,1)S(1)}, u32[]{:S(2)}, u32[]{:S(2)}) async-start(bf16[8,192,128]{2,1,0:T(8,128)(2,1)} %bitcast.5), calls=%async_computation.1 | async-start | bytes 786432 | tf_op jit(solution)/shard_map/all_to_all | solution.py:264
  71.6 16.0 %collective-permute-start.6 = (f32[4,128,256]{2,1,0:T(8,128)S(1)}, f32[4,128,256]{2,1,0:T(8,128)S(1)}, u32[]{:S(2)}, u32[]{:S(2)}) collective-permute-start(f32[4,128,256]{2,1,0:T(8,128)S(1)} %get-tuple-element.27), channel_id=1, source_target_pairs={{0,8},{1,9},{2,10},{3,11},{4,12},{5,13},{6,14},{7,15},{8,0},{9,1},... | collective-permute-start | bytes 1572872 | tf_op jit(solution)/shard_map/ppermute | solution.py:268
  83.3 17.7 %all-to-all-start.2 = ((f32[4,192,128]{2,1,0:T(8,128)}), f32[4,192,128]{2,1,0:T(8,128)S(1)}, u32[]{:S(2)}, u32[]{:S(2)}) async-start(f32[4,192,128]{2,1,0:T(8,128)} %broadcast_in_dim.2), calls=%async_computation.2 | async-start | bytes 786432 | tf_op jit(solution)/shard_map/all_to_all | solution.py:276
  87.7 15.3 %collective-permute-start.7 = (f32[128,256]{1,0:T(8,128)S(1)}, f32[128,256]{1,0:T(8,128)S(1)}, u32[]{:S(2)}, u32[]{:S(2)}) collective-permute-start(f32[128,256]{1,0:T(8,128)S(1)} %get-tuple-element.28), channel_id=1, source_target_pairs={{0,1},{1,0},{2,3},{3,2},{4,5},{5,4},{6,7},{7,6},{8,9},{9,8},{10,11... | collective-permute-start | bytes 393224 | tf_op jit(solution)/shard_map/ppermute | solution.py:273
  90.1 13.0 %collective-permute-start.8 = (f32[128,256]{1,0:T(8,128)S(1)}, f32[128,256]{1,0:T(8,128)S(1)}, u32[]{:S(2)}, u32[]{:S(2)}) collective-permute-start(f32[128,256]{1,0:T(8,128)S(1)} %get-tuple-element.30), channel_id=1, source_target_pairs={{0,32},{1,33},{2,34},{3,35},{4,36},{5,37},{6,38},{7,39},{8,40},{9,... | collective-permute-start | bytes 393224 | tf_op jit(solution)/shard_map/ppermute | solution.py:273
  96.8 9.0 %collective-permute-start.9 = (f32[128,256]{1,0:T(8,128)S(1)}, f32[128,256]{1,0:T(8,128)S(1)}, u32[]{:S(2)}, u32[]{:S(2)}) collective-permute-start(f32[128,256]{1,0:T(8,128)S(1)} %get-tuple-element.29), channel_id=1, source_target_pairs={{0,33},{1,32},{2,35},{3,34},{4,37},{5,36},{6,39},{7,38},{8,41},{9,... | collective-permute-start | bytes 393224 | tf_op jit(solution)/shard_map/ppermute | solution.py:273
  101.1 5.3 %collective-permute-start.10 = (f32[192,128]{1,0:T(8,128)S(1)}, f32[192,128]{1,0:T(8,128)S(1)}, u32[]{:S(2)}, u32[]{:S(2)}) collective-permute-start(f32[192,128]{1,0:T(8,128)S(1)} %reduce_sum.19), channel_id=1, source_target_pairs={{0,64},{64,0},{1,65},{65,1},{2,66},{66,2},{3,67},{67,3},{4,68},{68... | collective-permute-start | bytes 294920 | tf_op jit(solution)/shard_map/ppermute | solution.py:277

commit v19 on v17

--- a/solution.py
+++ b/solution.py
@@ -75,7 +75,7 @@
     sharers, rows, both = packed.shape
     cols = both - part
     wide = cols // 2
-    step = 2
+    step = 4
     steps = sharers // step
 
     def body(spot_ref, p_ref, keep_ref, send_ref, stage, sems):

time: 107 us -> 108 us (level)
  no operation moved by 1% of the time
where the time goes in v19:
time: 108 us; the launch traced here: 107 us
  starting transfers between devices  63.9 us (59%)
  waiting for transfers between devices  27 us (25%)
  Pallas kernels  12.1 us (11%)
  other arithmetic  2.34 us (2%)
    all_to_all x1, starting transfers between devices, local(): packed = lax.all_to_all(packed, CHIP, 0, 0, axis_index_groups=cubes)  16.1 us
    ppermute x4, starting transfers between devices, local(): gathered.append(lax.ppermute(weight, ('c', 'xh', 'zh'), shift))  15.3 us
    ppermute x4, waiting for transfers between devices, local(): gathered.append(lax.ppermute(weight, ('c', 'xh', 'zh'), shift))  13.6 us
    ppermute x3, starting transfers between devices, local(): output = output + lax.ppermute(near[n + 1], CHIP, flip)  11.9 us
    ppermute x1, starting transfers between devices, local(): away = lax.ppermute(away, CHIP, flip_x)  5.64 us
    all_to_all x1, starting transfers between devices, local(): half = jnp.sum(lax.all_to_all(lines, 'yh', 0, 0), axis=0)  4.99 us
    all_to_all x1, waiting for transfers between devices, local(): packed = lax.all_to_all(packed, CHIP, 0, 0, axis_index_groups=cubes)  4.47 us
    pallas_call x1, Pallas kernels, terms(): pl.pallas_call(body, in_specs=[pl.BlockSpec(memory_space=pltpu.SMEM), pl....  4.03 us
  transfers between devices with their start and end apart: 14, of which 9 were waited for; matrix products, arithmetic and copies ran while one was open for 2% of the time, Pallas kernels for 4%

profile of v19, /device:TPU:1, one launch (start us, length us, event | category | flops | bytes accessed | tf_op | source)
XLA Modules:
  0.0 107.0 jit_solution(16411639911721699526)
XLA Ops:
  0.6 3.9 %shard_map.50 = bf16[8,128,1792]{2,1,0:T(8,128)(2,1)} custom-call(bf16[128,12288]{1,0:T(8,128)(2,1)} %t_ref.1, bf16[128,256]{1,0:T(8,128)(2,1)} %g_ref.1), custom_call_target="tpu_custom_call" | custom-call | tf_op jit(solution)/shard_map/pallas_call | solution.py:60
  4.5 16.1 %all-to-all-start = ((bf16[8,128,1792]{2,1,0:T(8,128)(2,1)}), bf16[8,128,1792]{2,1,0:T(8,128)(2,1)}, u32[]{:S(2)}, u32[]{:S(2)}) async-start(bf16[8,128,1792]{2,1,0:T(8,128)(2,1)} %shard_map.50), calls=%async_computation | async-start | bytes 7340032 | tf_op jit(solution)/shard_map/all_to_all | solution.py:242
  20.7 1.9 %collective-permute-start = (bf16[192,256]{1,0:T(8,128)(2,1)S(1)}, bf16[192,256]{1,0:T(8,128)(2,1)S(1)}, u32[]{:S(2)}, u32[]{:S(2)}) collective-permute-start(bf16[192,256]{1,0:T(8,128)(2,1)S(1)} %copy-done), channel_id=1, source_target_pairs={{0,0},{2,2},{4,4},{6,6},{16,80},{18,82},{20,84},{22,86},{64,16},{6... | collective-permute-start | bytes 294920 | tf_op jit(solution)/shard_map/ppermute | solution.py:256
  22.6 1.9 %collective-permute-start.1 = (bf16[192,256]{1,0:T(8,128)(2,1)S(1)}, bf16[192,256]{1,0:T(8,128)(2,1)S(1)}, u32[]{:S(2)}, u32[]{:S(2)}) collective-permute-start(bf16[192,256]{1,0:T(8,128)(2,1)S(1)} %copy-done), channel_id=1, source_target_pairs={{0,2},{2,4},{4,6},{6,0},{16,82},{18,84},{20,86},{22,80},{64,18},{6... | collective-permute-start | bytes 294920 | tf_op jit(solution)/shard_map/ppermute | solution.py:256
  24.5 7.2 %collective-permute-start.2 = (bf16[192,256]{1,0:T(8,128)(2,1)S(1)}, bf16[192,256]{1,0:T(8,128)(2,1)S(1)}, u32[]{:S(2)}, u32[]{:S(2)}) collective-permute-start(bf16[192,256]{1,0:T(8,128)(2,1)S(1)} %copy-done), channel_id=1, source_target_pairs={{0,4},{2,6},{4,0},{6,2},{16,84},{18,86},{20,80},{22,82},{64,20},{6... | collective-permute-start | bytes 294920 | tf_op jit(solution)/shard_map/ppermute | solution.py:256
  31.7 4.3 %collective-permute-start.3 = (bf16[192,256]{1,0:T(8,128)(2,1)S(1)}, bf16[192,256]{1,0:T(8,128)(2,1)S(1)}, u32[]{:S(2)}, u32[]{:S(2)}) collective-permute-start(bf16[192,256]{1,0:T(8,128)(2,1)S(1)} %copy-done), channel_id=1, source_target_pairs={{0,6},{2,0},{4,2},{6,4},{16,86},{18,80},{20,82},{22,84},{64,22},{6... | collective-permute-start | bytes 294920 | tf_op jit(solution)/shard_map/ppermute | solution.py:256
  36.1 2.9 %collective-permute-done.refs_0_ = bf16[192,256]{1,0:T(8,128)(2,1)S(1)} collective-permute-done((bf16[192,256]{1,0:T(8,128)(2,1)S(1)}, bf16[192,256]{1,0:T(8,128)(2,1)S(1)}, u32[]{:S(2)}, u32[]{:S(2)}) %collective-permute-start) | collective-permute-done | bytes 98336 | tf_op jit(solution)/shard_map/ppermute | solution.py:256
  39.0 6.4 %collective-permute-done.2.refs_2_ = bf16[192,256]{1,0:T(8,128)(2,1)S(1)} collective-permute-done((bf16[192,256]{1,0:T(8,128)(2,1)S(1)}, bf16[192,256]{1,0:T(8,128)(2,1)S(1)}, u32[]{:S(2)}, u32[]{:S(2)}) %collective-permute-start.2) | collective-permute-done | bytes 98336 | tf_op jit(solution)/shard_map/ppermute | solution.py:256
  45.4 4.2 %collective-permute-done.3.refs_3_ = bf16[192,256]{1,0:T(8,128)(2,1)S(1)} collective-permute-done((bf16[192,256]{1,0:T(8,128)(2,1)S(1)}, bf16[192,256]{1,0:T(8,128)(2,1)S(1)}, u32[]{:S(2)}, u32[]{:S(2)}) %collective-permute-start.3) | collective-permute-done | bytes 98336 | tf_op jit(solution)/shard_map/ppermute | solution.py:256
  49.7 4.5 %all-to-all-done.p_ref = bf16[8,128,1792]{2,1,0:T(8,128)(2,1)} async-done(((bf16[8,128,1792]{2,1,0:T(8,128)(2,1)}), bf16[8,128,1792]{2,1,0:T(8,128)(2,1)}, u32[]{:S(2)}, u32[]{:S(2)}) %all-to-all-start) | async-done | bytes 3670048 | tf_op jit(solution)/shard_map/all_to_all | solution.py:242
  54.1 4.0 %shard_map.52 = (f32[1536,128]{1,0:T(8,128)S(1)}, f32[1536,128]{1,0:T(8,128)S(1)}) custom-call(s32[5]{0:T(128)S(1)} %stack.23.spot_ref, bf16[8,128,1792]{2,1,0:T(8,128)(2,1)} %all-to-all-done.p_ref), custom_call_target="tpu_custom_call" | custom-call | tf_op jit(solution)/shard_map/pallas_call | solution.py:111
  58.2 1.9 %collective-permute-start.5 = (f32[1536,128]{1,0:T(8,128)S(1)}, f32[1536,128]{1,0:T(8,128)S(1)}, u32[]{:S(2)}, u32[]{:S(2)}) collective-permute-start(f32[1536,128]{1,0:T(8,128)S(1)} %get-tuple-element.18), channel_id=1, source_target_pairs={{0,64},{64,0},{1,65},{65,1},{2,66},{66,2},{3,67},{67,3},{4,68},{68... | collective-permute-start | bytes 2359304 | tf_op jit(solution)/shard_map/ppermute | solution.py:260
  60.1 2.3 %collective-permute-done.5 = f32[1536,128]{1,0:T(8,128)S(1)} collective-permute-done((f32[1536,128]{1,0:T(8,128)S(1)}, f32[1536,128]{1,0:T(8,128)S(1)}, u32[]{:S(2)}, u32[]{:S(2)}) %collective-permute-start.5) | collective-permute-done | bytes 786464 | tf_op jit(solution)/shard_map/ppermute | solution.py:260
  63.2 3.5 %all-to-all-start.1 = ((bf16[8,192,128]{2,1,0:T(8,128)(2,1)}), bf16[8,192,128]{2,1,0:T(8,128)(2,1)S(1)}, u32[]{:S(2)}, u32[]{:S(2)}) async-start(bf16[8,192,128]{2,1,0:T(8,128)(2,1)} %bitcast.5), calls=%async_computation.1 | async-start | bytes 786432 | tf_op jit(solution)/shard_map/all_to_all | solution.py:263
  67.3 2.6 %collective-permute-start.4 = (bf16[4,192,256]{2,1,0:T(8,128)(2,1)S(1)}, bf16[4,192,256]{2,1,0:T(8,128)(2,1)S(1)}, u32[]{:S(2)}, u32[]{:S(2)}) collective-permute-start(bf16[4,192,256]{2,1,0:T(8,128)(2,1)S(1)} %shard_map.51.m_ref), channel_id=1, source_target_pairs={{0,64},{64,0},{1,65},{65,1},{2,66},{66,2},{3,67},{67,3},{4,68},{68... | collective-permute-start | bytes 1179656 | tf_op jit(solution)/shard_map/ppermute | solution.py:262
  71.2 3.6 %shard_map.53 = (f32[4,128,256]{2,1,0:T(8,128)S(1)}, f32[4,128,256]{2,1,0:T(8,128)S(1)}) custom-call(s32[5]{0:T(128)S(1)} %stack.23.spot_ref, bf16[8,128,1792]{2,1,0:T(8,128)(2,1)} %all-to-all-done.p_ref, bf16[4,192,256]{2,1,0:T(8,128)(2,1)S(1)} %shard_map.51.m_ref, bf16[4,192,256]{2,1,0:T(8,128)(2,1)S(1)} %collective-permute-done.4.r_ref), custom_call_target="tpu_custom_call" | custom-call | tf_op jit(solution)/shard_map/pallas_call | solution.py:178
  74.8 5.6 %collective-permute-start.6 = (f32[4,128,256]{2,1,0:T(8,128)S(1)}, f32[4,128,256]{2,1,0:T(8,128)S(1)}, u32[]{:S(2)}, u32[]{:S(2)}) collective-permute-start(f32[4,128,256]{2,1,0:T(8,128)S(1)} %get-tuple-element.23), channel_id=1, source_target_pairs={{0,8},{1,9},{2,10},{3,11},{4,12},{5,13},{6,14},{7,15},{8,0},{9,1},... | collective-permute-start | bytes 1572872 | tf_op jit(solution)/shard_map/ppermute | solution.py:267
  81.3 5.0 %all-to-all-start.2 = ((f32[4,192,128]{2,1,0:T(8,128)}), f32[4,192,128]{2,1,0:T(8,128)S(1)}, u32[]{:S(2)}, u32[]{:S(2)}) async-start(f32[4,192,128]{2,1,0:T(8,128)} %broadcast_in_dim.2), calls=%async_computation.2 | async-start | bytes 786432 | tf_op jit(solution)/shard_map/all_to_all | solution.py:275
  86.3 1.5 %collective-permute-done.6 = f32[4,128,256]{2,1,0:T(8,128)S(1)} collective-permute-done((f32[4,128,256]{2,1,0:T(8,128)S(1)}, f32[4,128,256]{2,1,0:T(8,128)S(1)}, u32[]{:S(2)}, u32[]{:S(2)}) %collective-permute-start.6) | collective-permute-done | bytes 524320 | tf_op jit(solution)/shard_map/ppermute | solution.py:267
  88.0 4.1 %collective-permute-start.7 = (f32[128,256]{1,0:T(8,128)S(1)}, f32[128,256]{1,0:T(8,128)S(1)}, u32[]{:S(2)}, u32[]{:S(2)}) collective-permute-start(f32[128,256]{1,0:T(8,128)S(1)} %get-tuple-element.24), channel_id=1, source_target_pairs={{0,1},{1,0},{2,3},{3,2},{4,5},{5,4},{6,7},{7,6},{8,9},{9,8},{10,11... | collective-permute-start | bytes 393224 | tf_op jit(solution)/shard_map/ppermute | solution.py:272
  92.1 4.5 %collective-permute-start.8 = (f32[128,256]{1,0:T(8,128)S(1)}, f32[128,256]{1,0:T(8,128)S(1)}, u32[]{:S(2)}, u32[]{:S(2)}) collective-permute-start(f32[128,256]{1,0:T(8,128)S(1)} %get-tuple-element.26), channel_id=1, source_target_pairs={{0,32},{1,33},{2,34},{3,35},{4,36},{5,37},{6,38},{7,39},{8,40},{9,... | collective-permute-start | bytes 393224 | tf_op jit(solution)/shard_map/ppermute | solution.py:272
  96.6 3.3 %collective-permute-start.9 = (f32[128,256]{1,0:T(8,128)S(1)}, f32[128,256]{1,0:T(8,128)S(1)}, u32[]{:S(2)}, u32[]{:S(2)}) collective-permute-start(f32[128,256]{1,0:T(8,128)S(1)} %get-tuple-element.25), channel_id=1, source_target_pairs={{0,33},{1,32},{2,35},{3,34},{4,37},{5,36},{6,39},{7,38},{8,41},{9,... | collective-permute-start | bytes 393224 | tf_op jit(solution)/shard_map/ppermute | solution.py:272
  99.9 1.9 %collective-permute-start.10 = (f32[192,128]{1,0:T(8,128)S(1)}, f32[192,128]{1,0:T(8,128)S(1)}, u32[]{:S(2)}, u32[]{:S(2)}) collective-permute-start(f32[192,128]{1,0:T(8,128)S(1)} %reduce_sum.19), channel_id=1, source_target_pairs={{0,64},{64,0},{1,65},{65,1},{2,66},{66,2},{3,67},{67,3},{4,68},{68... | collective-permute-start | bytes 294920 | tf_op jit(solution)/shard_map/ppermute | solution.py:276
  101.8 3.8 %collective-permute-done.9 = f32[128,256]{1,0:T(8,128)S(1)} collective-permute-done((f32[128,256]{1,0:T(8,128)S(1)}, f32[128,256]{1,0:T(8,128)S(1)}, u32[]{:S(2)}, u32[]{:S(2)}) %collective-permute-start.9) | collective-permute-done | bytes 131104 | tf_op jit(solution)/shard_map/ppermute | solution.py:272
  (20 shorter events, 5.2 us)
Async XLA Ops:
  4.5 16.1 %copy-start = (bf16[192,256]{1,0:T(8,128)(2,1)S(1)}, bf16[192,256]{1,0:T(8,128)(2,1)}, u32[]{:S(2)}) copy-start(bf16[192,256]{1,0:T(8,128)(2,1)} %param.4) | copy-start | bytes 294916
  4.5 49.6 %all-to-all-start = ((bf16[8,128,1792]{2,1,0:T(8,128)(2,1)}), bf16[8,128,1792]{2,1,0:T(8,128)(2,1)}, u32[]{:S(2)}, u32[]{:S(2)}) async-start(bf16[8,128,1792]{2,1,0:T(8,128)(2,1)} %shard_map.50), calls=%async_computation | async-start | bytes 7340032 | tf_op jit(solution)/shard_map/all_to_all | solution.py:242
  20.7 18.4 %collective-permute-start = (bf16[192,256]{1,0:T(8,128)(2,1)S(1)}, bf16[192,256]{1,0:T(8,128)(2,1)S(1)}, u32[]{:S(2)}, u32[]{:S(2)}) collective-permute-start(bf16[192,256]{1,0:T(8,128)(2,1)S(1)} %copy-done), channel_id=1, source_target_pairs={{0,0},{2,2},{4,4},{6,6},{16,80},{18,82},{20,84},{22,86},{64,16},{6... | collective-permute-start | bytes 294920 | tf_op jit(solution)/shard_map/ppermute | solution.py:256
  22.6 16.4 %collective-permute-start.1 = (bf16[192,256]{1,0:T(8,128)(2,1)S(1)}, bf16[192,256]{1,0:T(8,128)(2,1)S(1)}, u32[]{:S(2)}, u32[]{:S(2)}) collective-permute-start(bf16[192,256]{1,0:T(8,128)(2,1)S(1)} %copy-done), channel_id=1, source_target_pairs={{0,2},{2,4},{4,6},{6,0},{16,82},{18,84},{20,86},{22,80},{64,18},{6... | collective-permute-start | bytes 294920 | tf_op jit(solution)/shard_map/ppermute | solution.py:256
  24.5 20.9 %collective-permute-start.2 = (bf16[192,256]{1,0:T(8,128)(2,1)S(1)}, bf16[192,256]{1,0:T(8,128)(2,1)S(1)}, u32[]{:S(2)}, u32[]{:S(2)}) collective-permute-start(bf16[192,256]{1,0:T(8,128)(2,1)S(1)} %copy-done), channel_id=1, source_target_pairs={{0,4},{2,6},{4,0},{6,2},{16,84},{18,86},{20,80},{22,82},{64,20},{6... | collective-permute-start | bytes 294920 | tf_op jit(solution)/shard_map/ppermute | solution.py:256
  31.7 18.0 %collective-permute-start.3 = (bf16[192,256]{1,0:T(8,128)(2,1)S(1)}, bf16[192,256]{1,0:T(8,128)(2,1)S(1)}, u32[]{:S(2)}, u32[]{:S(2)}) collective-permute-start(bf16[192,256]{1,0:T(8,128)(2,1)S(1)} %copy-done), channel_id=1, source_target_pairs={{0,6},{2,0},{4,2},{6,4},{16,86},{18,80},{20,82},{22,84},{64,22},{6... | collective-permute-start | bytes 294920 | tf_op jit(solution)/shard_map/ppermute | solution.py:256
  58.2 4.2 %collective-permute-start.5 = (f32[1536,128]{1,0:T(8,128)S(1)}, f32[1536,128]{1,0:T(8,128)S(1)}, u32[]{:S(2)}, u32[]{:S(2)}) collective-permute-start(f32[1536,128]{1,0:T(8,128)S(1)} %get-tuple-element.18), channel_id=1, source_target_pairs={{0,64},{64,0},{1,65},{65,1},{2,66},{66,2},{3,67},{67,3},{4,68},{68... | collective-permute-start | bytes 2359304 | tf_op jit(solution)/shard_map/ppermute | solution.py:260
  63.2 17.3 %all-to-all-start.1 = ((bf16[8,192,128]{2,1,0:T(8,128)(2,1)}), bf16[8,192,128]{2,1,0:T(8,128)(2,1)S(1)}, u32[]{:S(2)}, u32[]{:S(2)}) async-start(bf16[8,192,128]{2,1,0:T(8,128)(2,1)} %bitcast.5), calls=%async_computation.1 | async-start | bytes 786432 | tf_op jit(solution)/shard_map/all_to_all | solution.py:263
  67.3 3.9 %collective-permute-start.4 = (bf16[4,192,256]{2,1,0:T(8,128)(2,1)S(1)}, bf16[4,192,256]{2,1,0:T(8,128)(2,1)S(1)}, u32[]{:S(2)}, u32[]{:S(2)}) collective-permute-start(bf16[4,192,256]{2,1,0:T(8,128)(2,1)S(1)} %shard_map.51.m_ref), channel_id=1, source_target_pairs={{0,64},{64,0},{1,65},{65,1},{2,66},{66,2},{3,67},{67,3},{4,68},{68... | collective-permute-start | bytes 1179656 | tf_op jit(solution)/shard_map/ppermute | solution.py:262
  74.8 13.1 %collective-permute-start.6 = (f32[4,128,256]{2,1,0:T(8,128)S(1)}, f32[4,128,256]{2,1,0:T(8,128)S(1)}, u32[]{:S(2)}, u32[]{:S(2)}) collective-permute-start(f32[4,128,256]{2,1,0:T(8,128)S(1)} %get-tuple-element.23), channel_id=1, source_target_pairs={{0,8},{1,9},{2,10},{3,11},{4,12},{5,13},{6,14},{7,15},{8,0},{9,1},... | collective-permute-start | bytes 1572872 | tf_op jit(solution)/shard_map/ppermute | solution.py:267
  81.3 18.5 %all-to-all-start.2 = ((f32[4,192,128]{2,1,0:T(8,128)}), f32[4,192,128]{2,1,0:T(8,128)S(1)}, u32[]{:S(2)}, u32[]{:S(2)}) async-start(f32[4,192,128]{2,1,0:T(8,128)} %broadcast_in_dim.2), calls=%async_computation.2 | async-start | bytes 786432 | tf_op jit(solution)/shard_map/all_to_all | solution.py:275
  88.0 13.9 %collective-permute-start.7 = (f32[128,256]{1,0:T(8,128)S(1)}, f32[128,256]{1,0:T(8,128)S(1)}, u32[]{:S(2)}, u32[]{:S(2)}) collective-permute-start(f32[128,256]{1,0:T(8,128)S(1)} %get-tuple-element.24), channel_id=1, source_target_pairs={{0,1},{1,0},{2,3},{3,2},{4,5},{5,4},{6,7},{7,6},{8,9},{9,8},{10,11... | collective-permute-start | bytes 393224 | tf_op jit(solution)/shard_map/ppermute | solution.py:272
  92.1 9.7 %collective-permute-start.8 = (f32[128,256]{1,0:T(8,128)S(1)}, f32[128,256]{1,0:T(8,128)S(1)}, u32[]{:S(2)}, u32[]{:S(2)}) collective-permute-start(f32[128,256]{1,0:T(8,128)S(1)} %get-tuple-element.26), channel_id=1, source_target_pairs={{0,32},{1,33},{2,34},{3,35},{4,36},{5,37},{6,38},{7,39},{8,40},{9,... | collective-permute-start | bytes 393224 | tf_op jit(solution)/shard_map/ppermute | solution.py:272
  96.6 9.0 %collective-permute-start.9 = (f32[128,256]{1,0:T(8,128)S(1)}, f32[128,256]{1,0:T(8,128)S(1)}, u32[]{:S(2)}, u32[]{:S(2)}) collective-permute-start(f32[128,256]{1,0:T(8,128)S(1)} %get-tuple-element.25), channel_id=1, source_target_pairs={{0,33},{1,32},{2,35},{3,34},{4,37},{5,36},{6,39},{7,38},{8,41},{9,... | collective-permute-start | bytes 393224 | tf_op jit(solution)/shard_map/ppermute | solution.py:272
  99.9 6.4 %collective-permute-start.10 = (f32[192,128]{1,0:T(8,128)S(1)}, f32[192,128]{1,0:T(8,128)S(1)}, u32[]{:S(2)}, u32[]{:S(2)}) collective-permute-start(f32[192,128]{1,0:T(8,128)S(1)} %reduce_sum.19), channel_id=1, source_target_pairs={{0,64},{64,0},{1,65},{65,1},{2,66},{66,2},{3,67},{67,3},{4,68},{68... | collective-permute-start | bytes 294920 | tf_op jit(solution)/shard_map/ppermute | solution.py:276
